TPU v7x, 768 devices: a whole 4x8x12 slice. The times are simulated.
768 devices in a mesh: dp: 24 (over z_hi, x, core), mp: 32 (over y, z_lo).
Axes of the slice: x: 4, y: 8, z: 12 (z_hi: 3, z_lo: 4; z = z_hi * 4 + z_lo), core: 2. Of those that a mesh axis runs over, the one named last changes fastest.
Arguments:
- query_input: bfloat16 [12288, 4096], P('dp', 'mp'), may hold values from -6 to 6
- key_input: bfloat16 [12288, 4096], P('dp', 'mp'), may hold values from -6 to 6
- value_input: bfloat16 [12288, 4096], P('dp', 'mp'), may hold values from -6 to 6
- query_gain: float32 [128], replicated, may hold values from 0.1 to 1.9
- key_gain: float32 [128], replicated, may hold values from 0.1 to 1.9
- out_weight: bfloat16 [4096, 6144], P('mp', 'dp'), may hold values from -0.09375 to 0.09375
- grad_output: bfloat16 [12288, 6144], P(('dp', 'mp')), may hold values from -24 to 24
Outputs:
- grad_query: bfloat16 [12288, 4096], P('dp', 'mp')
- grad_key: bfloat16 [12288, 4096], P('dp', 'mp')
- grad_value: bfloat16 [12288, 4096], P('dp', 'mp')
- grad_weight: bfloat16 [4096, 6144], P('mp', 'dp')
All inputs are finite; a program needn't handle non-finite values.
Results may differ from a plain program's by a relative error of at most 0.019.
Values may be sent and summed in bfloat16 or wider, within the bound.
No kernel may reach another device: no remote copies, remote signals or barrier semaphores. Data moves between devices by JAX's collectives and lax.ppermute only.
A program may use at most 32 MiB of HBM per device.

v0:
```python
import math

import jax
import jax.numpy as jnp
from jax import lax
from jax.sharding import PartitionSpec as P

DH = 128
PATCH = 256


epsilon = 1e-06


def normalize(inputs, gain):
    inputs = inputs.astype(jnp.float32)
    average = jnp.mean(inputs, axis=-1, keepdims=True)
    centred = inputs - average
    inverse = lax.rsqrt(jnp.mean(centred * centred, axis=-1, keepdims=True) + epsilon)
    unit_rows = centred * inverse
    return (unit_rows, inverse, unit_rows * gain)


def norm_back(gradient, unit_rows, inverse, gain):
    scaled = gradient * gain
    return (
        scaled
        - jnp.mean(scaled, axis=-1, keepdims=True)
        - unit_rows * jnp.mean(scaled * unit_rows, axis=-1, keepdims=True)
    ) * inverse


def shards(query_input, key_input, value_input, query_gain, key_gain, out_weight, grad_output):
    tok_rows, local_width = query_input.shape
    heads_here = local_width // DH
    head_shape = (tok_rows // PATCH, PATCH, heads_here, DH)
    scaling = 1.0 / math.sqrt(DH)
    weight_full = lax.all_gather(out_weight, "dp", axis=1, tiled=True)
    query_unit, query_inv, query_normed = normalize(query_input.reshape(head_shape), query_gain)
    key_unit, key_inv, key_normed = normalize(key_input.reshape(head_shape), key_gain)
    query_low = query_normed.astype(jnp.bfloat16)
    key_low = key_normed.astype(jnp.bfloat16)
    value_four = value_input.reshape(head_shape)
    scores = (
        jnp.einsum("iphd,ikhd->ihpk", query_low, key_low, preferred_element_type=jnp.float32)
        * scaling
    )
    exponent = jnp.exp(scores)
    attention = exponent / jnp.sum(exponent, axis=-1, keepdims=True)
    attention_low = attention.astype(jnp.bfloat16)
    mixed = jnp.einsum(
        "ihpk,ikhd->iphd", attention_low, value_four, preferred_element_type=jnp.float32
    )
    mixed = mixed.astype(jnp.bfloat16).reshape(tok_rows, local_width)
    by_columns = (((1,), (1,)), ((), ()))
    by_rows = (((0,), (0,)), ((), ()))
    gathered = lax.all_gather(grad_output, "mp", axis=0, tiled=True)
    heads_sum = lax.dot_general(
        gathered, weight_full, by_columns, preferred_element_type=jnp.float32
    )
    weight_term = lax.dot_general(mixed, gathered, by_rows, preferred_element_type=jnp.float32)
    grad_heads = heads_sum.astype(jnp.bfloat16).reshape(head_shape)
    grad_value = jnp.einsum(
        "ihpk,iphd->ikhd", attention_low, grad_heads, preferred_element_type=jnp.float32
    ).astype(jnp.bfloat16)
    grad_attention = jnp.einsum(
        "iphd,ikhd->ihpk", grad_heads, value_four, preferred_element_type=jnp.float32
    )
    row_delta = jnp.sum(attention * grad_attention, axis=-1, keepdims=True)
    grad_scores = (attention * (grad_attention - row_delta)).astype(jnp.bfloat16)
    grad_qn = (
        jnp.einsum("ihpk,ikhd->iphd", grad_scores, key_low, preferred_element_type=jnp.float32)
        * scaling
    )
    grad_kn = (
        jnp.einsum("ihpk,iphd->ikhd", grad_scores, query_low, preferred_element_type=jnp.float32)
        * scaling
    )
    grad_query = norm_back(grad_qn, query_unit, query_inv, query_gain).astype(jnp.bfloat16)
    grad_key = norm_back(grad_kn, key_unit, key_inv, key_gain).astype(jnp.bfloat16)
    grad_weight = lax.psum_scatter(
        weight_term.astype(jnp.bfloat16), "dp", scatter_dimension=1, tiled=True
    )
    flat = (tok_rows, local_width)
    return (grad_query.reshape(flat), grad_key.reshape(flat), grad_value.reshape(flat), grad_weight)


def solution(mesh):
    in_specs = (
        P("dp", "mp"),
        P("dp", "mp"),
        P("dp", "mp"),
        P(),
        P(),
        P("mp", "dp"),
        P(("dp", "mp"), None),
    )
    out_specs = (P("dp", "mp"), P("dp", "mp"), P("dp", "mp"), P("mp", "dp"))
    return jax.shard_map(shards, mesh=mesh, in_specs=in_specs, out_specs=out_specs, check_vma=False)
```

profile of v0, /device:TPU:1, one launch (start us, length us, event | category | flops | bytes accessed | tf_op | source)
XLA Modules:
  0.0 417.7 jit_solution(18091547613716907344)
XLA Ops:
  7.2 0.0 copy-start
  7.2 0.0 all-gather.5.cloned.1.call-start
  7.2 0.7 all-gather.5.cloned.1.call-update
  7.9 0.0 all-gather.3.cloned.1.call-start
  8.0 0.7 all-gather.3.cloned.1.call-update
  8.7 0.0 reduce-scatter.2.cloned.1.call-start
  8.7 0.9 convert_element_type.145
  9.6 1.0 convert_reduce_fusion
  10.7 1.1 multiply_reduce_fusion.3
  11.8 0.1 copy.21
  12.0 0.9 convert_element_type.144
  12.9 1.0 convert_reduce_fusion.1
  14.0 1.1 multiply_reduce_fusion.4
  15.1 0.1 copy.20
  15.3 0.7 broadcast_multiply_fusion.7
  15.9 0.8 multiply_convert_fusion.3
  16.7 75.0 %all-gather.5.cloned.1.call-done = bf16[128,6144]{1,0:T(8,128)(2,1)} async-done(((bf16[128,256]{1,0:T(8,128)(2,1)}), bf16[128,6144]{1,0:T(8,128)(2,1)}) %all-gather.5.cloned.1.call-update) | async-done | bytes 1572880 | tf_op jit(solution)/shard_map/all_gather | solution.py:38
  91.7 162.5 %all-gather.3.cloned.1.call-done = bf16[512,6144]{1,0:T(8,128)(2,1)} async-done(((bf16[16,6144]{1,0:T(8,128)(2,1)}), bf16[512,6144]{1,0:T(8,128)(2,1)}) %all-gather.3.cloned.1.call-update) | async-done | bytes 6291472 | tf_op jit(solution)/shard_map/all_gather | solution.py:57
  254.2 5.0 %convolution_convert_fusion.3 = bf16[512,128]{1,0:T(8,128)(2,1)S(1)} fusion(bf16[512,6144]{1,0:T(8,128)(2,1)} %all-gather.3.cloned.1.call-done, bf16[128,6144]{1,0:T(8,128)(2,1)} %all-gather.5.cloned.1.call-done), kind=kOutput, calls=%fused_computation.11 | convolution fusion | flops 805371904 | bytes 7995392 | tf_op jit(solution)/shard_map/dot_general | solution.py:58
  259.3 0.0 copy-done
  259.3 0.2 fusion.14
  259.5 0.4 multiply_reduce_fusion
  259.9 0.3 convolution_convert_fusion.1
  260.2 0.0 copy-start.1
  260.2 5.0 %convolution_convert_fusion = bf16[128,6144]{1,0:T(8,128)(2,1)} fusion(bf16[512,128]{1,0:T(8,128)(2,1)S(1)} %bitcast.56, bf16[512,6144]{1,0:T(8,128)(2,1)} %all-gather.3.cloned.1.call-done), kind=kOutput, calls=%fused_computation | convolution fusion | flops 806092800 | bytes 7995392 | tf_op jit(solution)/shard_map/dot_general | solution.py:61
  265.2 0.0 reduce-scatter.2.cloned.1.call-update
  265.2 0.0 copy-done.1
  265.2 0.1 copy.25
  265.3 0.1 copy.28
  265.5 0.1 multiply_convert_fusion
  265.6 0.2 fusion.13
  265.8 0.1 multiply_convert_fusion.2
  265.9 0.8 copy.26
  266.6 0.2 fusion.12
  266.9 0.1 multiply_convert_fusion.1
  267.0 0.8 copy.29
  267.7 0.2 fusion.5
  268.0 0.8 copy.32
  268.7 142.5 %reduce-scatter.2.cloned.1.call-done = bf16[128,256]{1,0:T(8,128)(2,1)} async-done(((bf16[128,6144]{1,0:T(8,128)(2,1)}), bf16[128,256]{1,0:T(8,128)(2,1)}) %reduce-scatter.2.cloned.1.call-update) | async-done | bytes 65552 | tf_op jit(solution)/shard_map/reduce_scatter | solution.py:81
  (13 shorter events, 0.1 us)
Async XLA Ops:
  7.2 252.1 %copy-start = (bf16[512,128]{1,0:T(8,128)(2,1)S(1)}, bf16[512,128]{1,0:T(8,128)(2,1)}, u32[]{:S(2)}) copy-start(bf16[512,128]{1,0:T(8,128)(2,1)} %param.9) | copy-start | bytes 393220
  7.2 84.5 %all-gather.5.cloned.1.call-start = ((), (), s32[]{:S(2)}) async-start(), calls=%async_computation.2 | async-start | bytes 1638400 | tf_op jit(solution)/shard_map/all_gather | solution.py:38
  7.9 246.3 %all-gather.3.cloned.1.call-start = ((), (), s32[]{:S(2)}) async-start(), calls=%async_computation.1 | async-start | bytes 6488064 | tf_op jit(solution)/shard_map/all_gather | solution.py:57
  8.7 402.5 %reduce-scatter.2.cloned.1.call-start = ((), (), s32[]{:S(2)}) async-start(), calls=%async_computation.3 | async-start | bytes 1638400 | tf_op jit(solution)/shard_map/reduce_scatter | solution.py:81
  260.2 5.0 %copy-start.1 = (f32[128]{0:T(128)S(1)}, f32[128]{0:T(128)}, u32[]{:S(2)}) copy-start(f32[128]{0:T(128)} %param.11) | copy-start | bytes 1540
Sparse Core Ops, SparseCore 0:
  11.9 79.7 all-gather.4
  94.1 160.1 all-gather.2
  265.3 145.8 reduce-scatter.1
where the time goes:
time: 418 us
  waiting for transfers between devices  381 us (91%)
  between operations  13.9 us (3%)
  matrix products  11.5 us (3%)
  other arithmetic  7.86 us (2%)
    all_gather x1, waiting for transfers between devices, shards(): gathered = lax.all_gather(grad_output, 'mp', axis=0, tiled=True)  163 us
    reduce_scatter x1, waiting for transfers between devices, shards(): lax.psum_scatter(weight_term.astype(jnp.bfloat16), 'dp', scatter_dimensio...  142 us
    all_gather x1, waiting for transfers between devices, shards(): weight_full = lax.all_gather(out_weight, 'dp', axis=1, tiled=True)  75 us
  transfers between devices with their start and end apart: 3, of which 3 were waited for; matrix products, arithmetic and copies ran while one was open for 3% of the time, Pallas kernels for 0%

commit v1 on v0

v1 whole, which is shorter than its diff:
```python
import functools
import math

import jax
import jax.numpy as jnp
from jax import lax
from jax.experimental import pallas as pl
from jax.experimental.pallas import tpu as pltpu
from jax.sharding import Mesh
from jax.sharding import PartitionSpec as P

DH = 128
PATCH = 256
IMAGES = 2
TOK = 512
NZ, NX, NC, NY, NL = 3, 4, 2, 8, 4
BLK = 256
WIDE = NZ * NC * BLK
epsilon = 1e-06
F32 = jnp.float32
BF16 = jnp.bfloat16
VMEM_LIMIT = 32 * 1024 * 1024
SCALING = 1.0 / math.sqrt(DH)


def dot(a, b, ca, cb):
    return lax.dot_general(a, b, (((ca,), (cb,)), ((), ())), preferred_element_type=F32)


def normalize(inputs):
    inputs = inputs.astype(F32)
    average = jnp.mean(inputs, axis=-1, keepdims=True)
    centred = inputs - average
    inverse = lax.rsqrt(jnp.mean(centred * centred, axis=-1, keepdims=True) + epsilon)
    return centred * inverse, inverse


def norm_back(gradient, unit_rows, inverse, gain):
    scaled = gradient * gain
    return (
        scaled
        - jnp.mean(scaled, axis=-1, keepdims=True)
        - unit_rows * jnp.mean(scaled * unit_rows, axis=-1, keepdims=True)
    ) * inverse


def forward_kernel(q_ref, k_ref, v_ref, qg_ref, kg_ref, mixed_ref, att_ref):
    for image in range(IMAGES):
        rows = pl.ds(image * PATCH, PATCH)
        query_low = (normalize(q_ref[rows, :])[0] * qg_ref[...]).astype(BF16)
        key_low = (normalize(k_ref[rows, :])[0] * kg_ref[...]).astype(BF16)
        exponent = jnp.exp(dot(query_low, key_low, 1, 1) * SCALING)
        attention = exponent / jnp.sum(exponent, axis=-1, keepdims=True)
        att_ref[image] = attention
        mixed = dot(v_ref[rows, :], attention.astype(BF16), 0, 1)
        mixed_ref[:, rows] = mixed.astype(BF16)


def backward_kernel(
    q_ref, k_ref, v_ref, qg_ref, kg_ref, att_ref, gh_ref, dq_ref, dk_ref, dv_ref
):
    for image in range(IMAGES):
        rows = pl.ds(image * PATCH, PATCH)
        total = gh_ref[0, rows, :].astype(F32)
        for part in range(1, NL):
            total = total + gh_ref[part, rows, :].astype(F32)
        grad_heads = total.astype(BF16)
        query_unit, query_inv = normalize(q_ref[rows, :])
        key_unit, key_inv = normalize(k_ref[rows, :])
        query_low = (query_unit * qg_ref[...]).astype(BF16)
        key_low = (key_unit * kg_ref[...]).astype(BF16)
        attention = att_ref[image]
        dv_ref[rows, :] = dot(attention.astype(BF16), grad_heads, 0, 0).astype(BF16)
        grad_attention = dot(grad_heads, v_ref[rows, :], 1, 1)
        row_delta = jnp.sum(attention * grad_attention, axis=-1, keepdims=True)
        grad_scores = (attention * (grad_attention - row_delta)).astype(BF16)
        grad_qn = dot(grad_scores, key_low, 1, 0) * SCALING
        grad_kn = dot(grad_scores, query_low, 0, 0) * SCALING
        dq_ref[rows, :] = norm_back(grad_qn, query_unit, query_inv, qg_ref[...]).astype(BF16)
        dk_ref[rows, :] = norm_back(grad_kn, key_unit, key_inv, kg_ref[...]).astype(BF16)


def block(ref, zone, core):
    start = pl.multiple_of(lax.rem(zone, NZ) * (NC * BLK) + core * BLK, BLK)
    return ref[:, pl.ds(start, BLK)]


def heads_kernel(g_ref, own_ref, other_ref, out_ref):
    zone, core = lax.axis_index("zh"), lax.axis_index("core")
    total = None
    for ref, side in ((own_ref, core), (other_ref, 1 - core)):
        for step in range(NZ):
            weight = ref[:, step].reshape(NX * DH, BLK)
            term = dot(block(g_ref, zone + NZ - step, side), weight, 1, 1)
            total = term if total is None else total + term
    for head in range(NL):
        out_ref[head] = total[:, head * DH : (head + 1) * DH].astype(BF16)


def weight_kernel(g_ref, mixed_ref, keep_ref, send_ref):
    zone, core = lax.axis_index("zh"), lax.axis_index("core")
    mixed = mixed_ref[...]
    for ref, side in ((send_ref, 1 - core), (keep_ref, core)):
        for step in range(NZ):
            term = dot(mixed, block(g_ref, zone + step, side), 1, 0)
            ref[:, step] = term.reshape(NL, DH, BLK).astype(ref.dtype)


def call(kernel, outs, flops, moved, *operands):
    return pl.pallas_call(
        kernel,
        out_shape=outs,
        in_specs=[pl.BlockSpec(memory_space=pltpu.VMEM)] * len(operands),
        out_specs=jax.tree.map(lambda _: pl.BlockSpec(memory_space=pltpu.VMEM), outs),
        compiler_params=pltpu.CompilerParams(vmem_limit_bytes=VMEM_LIMIT),
        cost_estimate=pl.CostEstimate(flops=flops, bytes_accessed=moved, transcendentals=0),
    )(*operands)


def crossing(shift):
    pairs = []
    for zone in range(NZ):
        for across in range(NX):
            for low in range(NL):
                target = (zone + shift) % NZ
                pairs.append(
                    ((zone * NX + across) * NL + low, (target * NX + low) * NL + across)
                )
    return pairs


def cross(entry, shift):
    return lax.ppermute(entry, ("zh", "x", "zl"), crossing(shift))


def swap_cores(entry):
    return lax.ppermute(entry, "core", [(0, 1), (1, 0)])


def shards(query_input, key_input, value_input, query_gain, key_gain, out_weight, grad_output):
    query_gain = query_gain.reshape(1, DH)
    key_gain = key_gain.reshape(1, DH)
    shape = jax.ShapeDtypeStruct

    rows = grad_output.shape[0]
    pieces = grad_output.reshape(rows, NZ, NL, NC * BLK).transpose(2, 0, 1, 3)
    pieces = pieces.reshape(NL * rows, WIDE)
    exchanged = lax.all_to_all(pieces, "zl", 0, 0, tiled=True)
    gathered = lax.all_gather(exchanged, "y", axis=0, tiled=True)

    moved = jnp.stack([cross(out_weight, shift) for shift in range(NZ)])
    own = lax.all_gather(moved, "x", axis=0)
    other = swap_cores(own)

    mixed, attention = call(
        forward_kernel,
        (shape((DH, TOK), BF16), shape((IMAGES, PATCH, PATCH), F32)),
        2 * 2 * IMAGES * PATCH * PATCH * DH,
        1 << 20,
        query_input,
        key_input,
        value_input,
        query_gain,
        key_gain,
    )
    mixed_all = lax.all_gather(mixed, "zl", axis=0, tiled=True)

    gathered, mixed_all, own, other = lax.optimization_barrier(
        (gathered, mixed_all, own, other)
    )
    keep, send = call(
        weight_kernel,
        (shape((NL, NZ, DH, BLK), F32), shape((NL, NZ, DH, BLK), BF16)),
        2 * TOK * TOK * WIDE,
        5 << 20,
        gathered,
        mixed_all,
    )
    received = swap_cores(send)
    partial = call(
        heads_kernel,
        shape((NL, TOK, DH), BF16),
        2 * TOK * TOK * WIDE,
        4 << 20,
        gathered,
        own,
        other,
    )
    grad_heads = lax.all_to_all(partial, "zl", 0, 0, tiled=True)

    summed = (keep + received.astype(F32)).astype(BF16)
    spread = lax.all_to_all(summed, "x", 0, 0, tiled=True)
    by_zone = sum(spread[part].astype(F32) for part in range(NX)).astype(BF16)
    last = [cross(by_zone[shift], shift) for shift in range(NZ)]
    grad_weight = sum(entry.astype(F32) for entry in last).astype(BF16)

    grad_query, grad_key, grad_value = call(
        backward_kernel,
        (shape((TOK, DH), BF16),) * 3,
        5 * 2 * IMAGES * PATCH * PATCH * DH,
        2 << 20,
        query_input,
        key_input,
        value_input,
        query_gain,
        key_gain,
        attention,
        grad_heads,
    )
    return grad_query, grad_key, grad_value, grad_weight


def solution(mesh):
    axes = ("zh", "x", "core", "y", "zl")
    fine = Mesh(mesh.devices.reshape(NZ, NX, NC, NY, NL), axes)
    tokens, heads = ("zh", "x", "core"), ("y", "zl")
    in_specs = (
        P(tokens, heads),
        P(tokens, heads),
        P(tokens, heads),
        P(),
        P(),
        P(heads, tokens),
        P(tokens + heads, None),
    )
    out_specs = (P(tokens, heads), P(tokens, heads), P(tokens, heads), P(heads, tokens))
    return jax.shard_map(shards, mesh=fine, in_specs=in_specs, out_specs=out_specs, check_vma=False)
```

time: 418 us -> 153 us (0.37)
  the two profiles are of different devices: /device:TPU:1 before, /device:TPU:224 now
where the time goes in v1:
time: 153 us; the launch traced here: 152 us
  starting transfers between devices  46.5 us (30%)
  blocking collectives  40.7 us (27%)
  waiting for transfers between devices  38.1 us (25%)
  between operations  14.3 us (9%)
  Pallas kernels  5.8 us (4%)
  local copies, waits for them, and re-layouts  3.84 us (3%)
  other arithmetic  3.14 us (2%)
    ppermute x6, starting transfers between devices, cross(): return lax.ppermute(entry, ('zh', 'x', 'zl'), crossing(shift))  33.4 us
    ppermute x6, waiting for transfers between devices, cross(): return lax.ppermute(entry, ('zh', 'x', 'zl'), crossing(shift))  23.9 us
    all_gather x1, blocking collectives, shards(): mixed_all = lax.all_gather(mixed, 'zl', axis=0, tiled=True)  16.4 us
    all_gather x1, blocking collectives, shards(): own = lax.all_gather(moved, 'x', axis=0)  14.3 us
    all_to_all x1, waiting for transfers between devices, shards(): spread = lax.all_to_all(summed, 'x', 0, 0, tiled=True)  11.1 us
    all_to_all x1, blocking collectives, shards(): exchanged = lax.all_to_all(pieces, 'zl', 0, 0, tiled=True)  10.1 us
    pallas_call x4, Pallas kernels, call(): pl.pallas_call(kernel, out_shape=outs, in_specs=[pl.BlockSpec(memory_spac...  5.8 us
    all_to_all x1, starting transfers between devices, shards(): grad_heads = lax.all_to_all(partial, 'zl', 0, 0, tiled=True)  5.09 us
  transfers between devices with their start and end apart: 11, of which 7 were waited for; matrix products, arithmetic and copies ran while one was open for 1% of the time, Pallas kernels for 3%

profile of v1, /device:TPU:224, one launch (start us, length us, event | category | flops | bytes accessed | tf_op | source)
XLA Modules:
  0.0 152.4 jit_solution(11927257743960038827)
XLA Ops:
  7.2 0.0 copy-start.9
  7.2 0.0 copy-start.4
  7.2 0.0 copy-start.3
  7.2 0.0 copy-start.2
  7.2 0.0 copy-start.8
  7.2 0.0 copy-start.7
  7.2 0.0 all-gather.3.cloned.1.call-start
  7.3 1.2 reshape.37
  8.5 0.1 copy.15
  8.6 0.3 all_to_all.14
  8.9 10.1 %all_to_all.22 = bf16[4,16,1536]{2,1,0:T(8,128)(2,1)} all-to-all(bf16[4,16,1536]{2,1,0:T(8,128)(2,1)S(1)} %all_to_all.14), channel_id=1, replica_groups=mesh['zh'=3,'x'=4,'core'=2,'y'=8,'zl'=4] {'zl'}, dimensions={0} | all-to-all | bytes 393216 | tf_op jit(solution)/shard_map/all_to_all | solution.py:148
  19.0 0.0 all-gather.3.cloned.1.call-update
  19.0 0.0 copy-done.9
  19.0 6.5 %collective-permute-start = (bf16[128,256]{1,0:T(8,128)(2,1)S(1)}, bf16[128,256]{1,0:T(8,128)(2,1)S(1)}, u32[]{:S(2)}, u32[]{:S(2)}) collective-permute-start(bf16[128,256]{1,0:T(8,128)(2,1)S(1)} %copy-done.9), channel_id=1, source_target_pairs={{0,0},{1,64},{2,128},{3,192},{64,1},{65,65},{66,129},{67,193},{128... | collective-permute-start | bytes 196616 | tf_op jit(solution)/shard_map/ppermute | solution.py:133
  25.5 12.4 %collective-permute-start.2 = (bf16[128,256]{1,0:T(8,128)(2,1)S(1)}, bf16[128,256]{1,0:T(8,128)(2,1)S(1)}, u32[]{:S(2)}, u32[]{:S(2)}) collective-permute-start(bf16[128,256]{1,0:T(8,128)(2,1)S(1)} %copy-done.9), channel_id=1, source_target_pairs={{0,512},{1,576},{2,640},{3,704},{64,513},{65,577},{66,641},{67,705... | collective-permute-start | bytes 196616 | tf_op jit(solution)/shard_map/ppermute | solution.py:133
  37.9 1.9 %collective-permute-start.1 = (bf16[128,256]{1,0:T(8,128)(2,1)S(1)}, bf16[128,256]{1,0:T(8,128)(2,1)S(1)}, u32[]{:S(2)}, u32[]{:S(2)}) collective-permute-start(bf16[128,256]{1,0:T(8,128)(2,1)S(1)} %copy-done.9), channel_id=1, source_target_pairs={{0,256},{1,320},{2,384},{3,448},{64,257},{65,321},{66,385},{67,449... | collective-permute-start | bytes 196616 | tf_op jit(solution)/shard_map/ppermute | solution.py:133
  39.8 0.0 collective-permute-done
  39.8 5.0 %collective-permute-done.2 = bf16[128,256]{1,0:T(8,128)(2,1)S(1)} collective-permute-done((bf16[128,256]{1,0:T(8,128)(2,1)S(1)}, bf16[128,256]{1,0:T(8,128)(2,1)S(1)}, u32[]{:S(2)}, u32[]{:S(2)}) %collective-permute-start.2) | collective-permute-done | bytes 65568 | tf_op jit(solution)/shard_map/ppermute | solution.py:133
  44.8 7.5 %collective-permute-done.1 = bf16[128,256]{1,0:T(8,128)(2,1)S(1)} collective-permute-done((bf16[128,256]{1,0:T(8,128)(2,1)S(1)}, bf16[128,256]{1,0:T(8,128)(2,1)S(1)}, u32[]{:S(2)}, u32[]{:S(2)}) %collective-permute-start.1) | collective-permute-done | bytes 65568 | tf_op jit(solution)/shard_map/ppermute | solution.py:133
  52.4 14.3 %all-gather = bf16[12,128,256]{2,1,0:T(8,128)(2,1)S(1)} all-gather(bf16[3,128,256]{2,1,0:T(8,128)(2,1)S(1)} %pad_maximum_fusion), channel_id=2, replica_groups=mesh['zh'=3,'x'=4,'core'=2,'y'=8,'zl'=4] {'x'}, dimensions={0}, use_global_device_ids=true | all-gather | bytes 983040 | tf_op jit(solution)/shard_map/all_gather | solution.py:152
  66.7 1.9 %collective-permute-start.3 = (bf16[4,3,128,256]{3,2,1,0:T(8,128)(2,1)S(1)}, bf16[4,3,128,256]{3,2,1,0:T(8,128)(2,1)S(1)}, u32[]{:S(2)}, u32[]{:S(2)}) collective-permute-start(bf16[4,3,128,256]{3,2,1,0:T(8,128)(2,1)S(1)} %bitcast.16), channel_id=1, source_target_pairs={{0,32},{32,0},{1,33},{33,1},{2,34},{34,2},{3,35},{35,3},{4,36},{36... | collective-permute-start | bytes 2359304 | tf_op jit(solution)/shard_map/ppermute | solution.py:137
  68.6 0.0 copy-done.4
  68.6 0.0 copy-done.3
  68.6 0.8 shard_map.102
  69.5 0.8 copy-done.5
  70.3 16.4 %all_gather.13.mixed_ref = bf16[512,512]{1,0:T(8,128)(2,1)S(1)} all-gather(bf16[128,512]{1,0:T(8,128)(2,1)S(1)} %get-tuple-element.16), channel_id=1, replica_groups=mesh['zh'=3,'x'=4,'core'=2,'y'=8,'zl'=4] {'zl'}, dimensions={0}, use_global_device_ids=true | all-gather | bytes 655360 | tf_op jit(solution)/shard_map/all_gather | solution.py:166
  86.6 0.0 collective-permute-done.3.other_ref
  86.6 1.4 copy-done
  88.1 1.0 shard_map.105
  89.0 1.9 %collective-permute-start.4 = (bf16[4,3,128,256]{3,2,1,0:T(8,128)(2,1)S(1)}, bf16[4,3,128,256]{3,2,1,0:T(8,128)(2,1)S(1)}, u32[]{:S(2)}, u32[]{:S(2)}) collective-permute-start(bf16[4,3,128,256]{3,2,1,0:T(8,128)(2,1)S(1)} %get-tuple-element.25), channel_id=1, source_target_pairs={{0,32},{32,0},{1,33},{33,1},{2,34},{34,2},{3,35},{35,3},{4,36},{36... | collective-permute-start | bytes 2359304 | tf_op jit(solution)/shard_map/ppermute | solution.py:137
  91.0 2.3 %collective-permute-done.4 = bf16[4,3,128,256]{3,2,1,0:T(8,128)(2,1)S(1)} collective-permute-done((bf16[4,3,128,256]{3,2,1,0:T(8,128)(2,1)S(1)}, bf16[4,3,128,256]{3,2,1,0:T(8,128)(2,1)S(1)}, u32[]{:S(2)}, u32[]{:S(2)}) %collective-permute-start.4) | collective-permute-done | bytes 786464 | tf_op jit(solution)/shard_map/ppermute | solution.py:137
  93.2 1.1 add_convert_fusion
  94.4 4.2 %all-to-all-start.2 = ((bf16[4,3,128,256]{3,2,1,0:T(8,128)(2,1)}), bf16[4,3,128,256]{3,2,1,0:T(8,128)(2,1)}, u32[]{:S(2)}, u32[]{:S(2)}) async-start(bf16[4,3,128,256]{3,2,1,0:T(8,128)(2,1)} %add_convert_fusion), calls=%async_computation.2 | async-start | bytes 1572864 | tf_op jit(solution)/shard_map/all_to_all | solution.py:192
  98.6 0.0 copy-done.1
  98.6 1.8 %shard_map.103 = bf16[4,512,128]{2,1,0:T(8,128)(2,1)} custom-call(bf16[512,1536]{1,0:T(8,128)(2,1)S(1)} %copy-done.1, bf16[4,3,128,256]{3,2,1,0:T(8,128)(2,1)S(1)} %bitcast.17, bf16[4,3,128,256]{3,2,1,0:T(8,128)(2,1)S(1)} %collective-permute-done.3.other_ref), custom_call_target="tpu_custom_call" | custom-call | flops 805306368 | bytes 4194304 | tf_op jit(solution)/shard_map/pallas_call | solution.py:110
  100.4 11.1 %all-to-all-done.2 = bf16[4,3,128,256]{3,2,1,0:T(8,128)(2,1)} async-done(((bf16[4,3,128,256]{3,2,1,0:T(8,128)(2,1)}), bf16[4,3,128,256]{3,2,1,0:T(8,128)(2,1)}, u32[]{:S(2)}, u32[]{:S(2)}) %all-to-all-start.2) | async-done | bytes 786464 | tf_op jit(solution)/shard_map/all_to_all | solution.py:192
  111.5 5.1 %all-to-all-start.1 = ((bf16[4,512,128]{2,1,0:T(8,128)(2,1)}), bf16[4,512,128]{2,1,0:T(8,128)(2,1)S(1)}, u32[]{:S(2)}, u32[]{:S(2)}) async-start(bf16[4,512,128]{2,1,0:T(8,128)(2,1)} %shard_map.103), calls=%async_computation.1 | async-start | bytes 1048576 | tf_op jit(solution)/shard_map/all_to_all | solution.py:189
  116.6 1.3 add_convert_fusion.1
  118.0 2.5 %collective-permute-start.5 = (bf16[128,256]{1,0:T(8,128)(2,1)S(1)}, bf16[128,256]{1,0:T(8,128)(2,1)S(1)}, u32[]{:S(2)}, u32[]{:S(2)}) collective-permute-start(bf16[128,256]{1,0:T(8,128)(2,1)S(1)} %get-tuple-element.26), channel_id=1, source_target_pairs={{0,0},{1,64},{2,128},{3,192},{64,1},{65,65},{66,129},{67,193},{128... | collective-permute-start | bytes 196616 | tf_op jit(solution)/shard_map/ppermute | solution.py:133
  120.5 8.2 %collective-permute-start.7 = (bf16[128,256]{1,0:T(8,128)(2,1)S(1)}, bf16[128,256]{1,0:T(8,128)(2,1)S(1)}, u32[]{:S(2)}, u32[]{:S(2)}) collective-permute-start(bf16[128,256]{1,0:T(8,128)(2,1)S(1)} %get-tuple-element.27), channel_id=1, source_target_pairs={{0,512},{1,576},{2,640},{3,704},{64,513},{65,577},{66,641},{67,705... | collective-permute-start | bytes 196616 | tf_op jit(solution)/shard_map/ppermute | solution.py:133
  128.7 1.9 %collective-permute-start.6 = (bf16[128,256]{1,0:T(8,128)(2,1)S(1)}, bf16[128,256]{1,0:T(8,128)(2,1)S(1)}, u32[]{:S(2)}, u32[]{:S(2)}) collective-permute-start(bf16[128,256]{1,0:T(8,128)(2,1)S(1)} %get-tuple-element.28), channel_id=1, source_target_pairs={{0,256},{1,320},{2,384},{3,448},{64,257},{65,321},{66,385},{67,449... | collective-permute-start | bytes 196616 | tf_op jit(solution)/shard_map/ppermute | solution.py:133
  130.6 0.8 all-to-all-done.1.gh_ref
  131.4 0.0 copy-done.6
  131.4 2.2 %shard_map.104 = (bf16[512,128]{1,0:T(8,128)(2,1)}, bf16[512,128]{1,0:T(8,128)(2,1)}, bf16[512,128]{1,0:T(8,128)(2,1)}) custom-call(bf16[512,128]{1,0:T(8,128)(2,1)S(1)} %copy-done.2, bf16[512,128]{1,0:T(8,128)(2,1)S(1)} %copy-done.3, bf16[512,128]{1,0:T(8,128)(2,1)S(1)} %copy-done.4, f32[1,128]{1,0:T(1,128)S(1)} %bitcast.19, f32[1,128]{1,0:T(1,128)S(1)} %bitcast.21, ...), custom_call_target="tpu_custom_call" | custom-call | flops 167772160 | bytes 2097152 | tf_op jit(solution)/shard_map/pallas_call | solution.py:110
  133.5 0.0 collective-permute-done.5
  133.5 2.8 %collective-permute-done.7 = bf16[128,256]{1,0:T(8,128)(2,1)S(1)} collective-permute-done((bf16[128,256]{1,0:T(8,128)(2,1)S(1)}, bf16[128,256]{1,0:T(8,128)(2,1)S(1)}, u32[]{:S(2)}, u32[]{:S(2)}) %collective-permute-start.7) | collective-permute-done | bytes 65568 | tf_op jit(solution)/shard_map/ppermute | solution.py:133
  136.3 8.6 %collective-permute-done.6 = bf16[128,256]{1,0:T(8,128)(2,1)S(1)} collective-permute-done((bf16[128,256]{1,0:T(8,128)(2,1)S(1)}, bf16[128,256]{1,0:T(8,128)(2,1)S(1)}, u32[]{:S(2)}, u32[]{:S(2)}) %collective-permute-start.6) | collective-permute-done | bytes 65568 | tf_op jit(solution)/shard_map/ppermute | solution.py:133
  144.9 0.7 add_convert_fusion.2
  (10 shorter events, 0.1 us)
Async XLA Ops:
  7.2 11.8 %copy-start.9 = (bf16[128,256]{1,0:T(8,128)(2,1)S(1)}, bf16[128,256]{1,0:T(8,128)(2,1)}, u32[]{:S(2)}) copy-start(bf16[128,256]{1,0:T(8,128)(2,1)} %param.12) | copy-start | bytes 196612
  7.2 61.4 %copy-start.4 = (bf16[512,128]{1,0:T(8,128)(2,1)S(1)}, bf16[512,128]{1,0:T(8,128)(2,1)}, u32[]{:S(2)}) copy-start(bf16[512,128]{1,0:T(8,128)(2,1)} %v_ref.3) | copy-start | bytes 393220
  7.2 61.4 %copy-start.3 = (bf16[512,128]{1,0:T(8,128)(2,1)S(1)}, bf16[512,128]{1,0:T(8,128)(2,1)}, u32[]{:S(2)}) copy-start(bf16[512,128]{1,0:T(8,128)(2,1)} %k_ref.3) | copy-start | bytes 393220
  7.2 61.4 %copy-start.2 = (bf16[512,128]{1,0:T(8,128)(2,1)S(1)}, bf16[512,128]{1,0:T(8,128)(2,1)}, u32[]{:S(2)}) copy-start(bf16[512,128]{1,0:T(8,128)(2,1)} %q_ref.3) | copy-start | bytes 393220
  7.2 61.4 %copy-start.8 = (f32[128]{0:T(128)S(1)}, f32[128]{0:T(128)}, u32[]{:S(2)}) copy-start(f32[128]{0:T(128)} %param.11) | copy-start | bytes 1540
  7.2 61.4 %copy-start.7 = (f32[128]{0:T(128)S(1)}, f32[128]{0:T(128)}, u32[]{:S(2)}) copy-start(f32[128]{0:T(128)} %param.10) | copy-start | bytes 1540
  7.2 79.4 %all-gather.3.cloned.1.call-start = ((), (), s32[]{:S(2)}) async-start(), calls=%async_computation.3 | async-start | bytes 1769472 | tf_op jit(solution)/shard_map/all_gather | solution.py:149
  19.0 20.8 %collective-permute-start = (bf16[128,256]{1,0:T(8,128)(2,1)S(1)}, bf16[128,256]{1,0:T(8,128)(2,1)S(1)}, u32[]{:S(2)}, u32[]{:S(2)}) collective-permute-start(bf16[128,256]{1,0:T(8,128)(2,1)S(1)} %copy-done.9), channel_id=1, source_target_pairs={{0,0},{1,64},{2,128},{3,192},{64,1},{65,65},{66,129},{67,193},{128... | collective-permute-start | bytes 196616 | tf_op jit(solution)/shard_map/ppermute | solution.py:133
  25.5 19.4 %collective-permute-start.2 = (bf16[128,256]{1,0:T(8,128)(2,1)S(1)}, bf16[128,256]{1,0:T(8,128)(2,1)S(1)}, u32[]{:S(2)}, u32[]{:S(2)}) collective-permute-start(bf16[128,256]{1,0:T(8,128)(2,1)S(1)} %copy-done.9), channel_id=1, source_target_pairs={{0,512},{1,576},{2,640},{3,704},{64,513},{65,577},{66,641},{67,705... | collective-permute-start | bytes 196616 | tf_op jit(solution)/shard_map/ppermute | solution.py:133
  37.9 14.5 %collective-permute-start.1 = (bf16[128,256]{1,0:T(8,128)(2,1)S(1)}, bf16[128,256]{1,0:T(8,128)(2,1)S(1)}, u32[]{:S(2)}, u32[]{:S(2)}) collective-permute-start(bf16[128,256]{1,0:T(8,128)(2,1)S(1)} %copy-done.9), channel_id=1, source_target_pairs={{0,256},{1,320},{2,384},{3,448},{64,257},{65,321},{66,385},{67,449... | collective-permute-start | bytes 196616 | tf_op jit(solution)/shard_map/ppermute | solution.py:133
  66.7 20.0 %collective-permute-start.3 = (bf16[4,3,128,256]{3,2,1,0:T(8,128)(2,1)S(1)}, bf16[4,3,128,256]{3,2,1,0:T(8,128)(2,1)S(1)}, u32[]{:S(2)}, u32[]{:S(2)}) collective-permute-start(bf16[4,3,128,256]{3,2,1,0:T(8,128)(2,1)S(1)} %bitcast.16), channel_id=1, source_target_pairs={{0,32},{32,0},{1,33},{33,1},{2,34},{34,2},{3,35},{35,3},{4,36},{36... | collective-permute-start | bytes 2359304 | tf_op jit(solution)/shard_map/ppermute | solution.py:137
  69.5 0.8 copy-start.5
  86.6 1.4 copy-start
  89.0 4.2 %collective-permute-start.4 = (bf16[4,3,128,256]{3,2,1,0:T(8,128)(2,1)S(1)}, bf16[4,3,128,256]{3,2,1,0:T(8,128)(2,1)S(1)}, u32[]{:S(2)}, u32[]{:S(2)}) collective-permute-start(bf16[4,3,128,256]{3,2,1,0:T(8,128)(2,1)S(1)} %get-tuple-element.25), channel_id=1, source_target_pairs={{0,32},{32,0},{1,33},{33,1},{2,34},{34,2},{3,35},{35,3},{4,36},{36... | collective-permute-start | bytes 2359304 | tf_op jit(solution)/shard_map/ppermute | solution.py:137
  93.2 5.4 %copy-start.1 = (bf16[512,1536]{1,0:T(8,128)(2,1)S(1)}, bf16[512,1536]{1,0:T(8,128)(2,1)}, u32[]{:S(2)}) copy-start(bf16[512,1536]{1,0:T(8,128)(2,1)} %all-gather.3.cloned.1.call-done.g_ref) | copy-start | bytes 4718596
  94.4 17.1 %all-to-all-start.2 = ((bf16[4,3,128,256]{3,2,1,0:T(8,128)(2,1)}), bf16[4,3,128,256]{3,2,1,0:T(8,128)(2,1)}, u32[]{:S(2)}, u32[]{:S(2)}) async-start(bf16[4,3,128,256]{3,2,1,0:T(8,128)(2,1)} %add_convert_fusion), calls=%async_computation.2 | async-start | bytes 1572864 | tf_op jit(solution)/shard_map/all_to_all | solution.py:192
  100.4 30.9 %copy-start.6 = (f32[2,256,256]{2,1,0:T(8,128)S(1)}, f32[2,256,256]{2,1,0:T(8,128)}, u32[]{:S(2)}) copy-start(f32[2,256,256]{2,1,0:T(8,128)} %copy-done.5) | copy-start | bytes 1572868
  111.5 19.8 %all-to-all-start.1 = ((bf16[4,512,128]{2,1,0:T(8,128)(2,1)}), bf16[4,512,128]{2,1,0:T(8,128)(2,1)S(1)}, u32[]{:S(2)}, u32[]{:S(2)}) async-start(bf16[4,512,128]{2,1,0:T(8,128)(2,1)} %shard_map.103), calls=%async_computation.1 | async-start | bytes 1048576 | tf_op jit(solution)/shard_map/all_to_all | solution.py:189
  118.0 15.6 %collective-permute-start.5 = (bf16[128,256]{1,0:T(8,128)(2,1)S(1)}, bf16[128,256]{1,0:T(8,128)(2,1)S(1)}, u32[]{:S(2)}, u32[]{:S(2)}) collective-permute-start(bf16[128,256]{1,0:T(8,128)(2,1)S(1)} %get-tuple-element.26), channel_id=1, source_target_pairs={{0,0},{1,64},{2,128},{3,192},{64,1},{65,65},{66,129},{67,193},{128... | collective-permute-start | bytes 196616 | tf_op jit(solution)/shard_map/ppermute | solution.py:133
  120.5 15.8 %collective-permute-start.7 = (bf16[128,256]{1,0:T(8,128)(2,1)S(1)}, bf16[128,256]{1,0:T(8,128)(2,1)S(1)}, u32[]{:S(2)}, u32[]{:S(2)}) collective-permute-start(bf16[128,256]{1,0:T(8,128)(2,1)S(1)} %get-tuple-element.27), channel_id=1, source_target_pairs={{0,512},{1,576},{2,640},{3,704},{64,513},{65,577},{66,641},{67,705... | collective-permute-start | bytes 196616 | tf_op jit(solution)/shard_map/ppermute | solution.py:133
  128.7 16.2 %collective-permute-start.6 = (bf16[128,256]{1,0:T(8,128)(2,1)S(1)}, bf16[128,256]{1,0:T(8,128)(2,1)S(1)}, u32[]{:S(2)}, u32[]{:S(2)}) collective-permute-start(bf16[128,256]{1,0:T(8,128)(2,1)S(1)} %get-tuple-element.28), channel_id=1, source_target_pairs={{0,256},{1,320},{2,384},{3,448},{64,257},{65,321},{66,385},{67,449... | collective-permute-start | bytes 196616 | tf_op jit(solution)/shard_map/ppermute | solution.py:133
Sparse Core Ops, SparseCore 0:
  19.1 47.4 all-gather.2

commit v2 on v1

--- a/solution.py
+++ b/solution.py
@@ -15,7 +15,7 @@
 TOK = 512
 NZ, NX, NC, NY, NL = 3, 4, 2, 8, 4
 BLK = 256
-WIDE = NZ * NC * BLK
+WIDE = NZ * BLK
 epsilon = 1e-06
 F32 = jnp.float32
 BF16 = jnp.bfloat16
@@ -62,7 +62,7 @@
     for image in range(IMAGES):
         rows = pl.ds(image * PATCH, PATCH)
         total = gh_ref[0, rows, :].astype(F32)
-        for part in range(1, NL):
+        for part in range(1, NY):
             total = total + gh_ref[part, rows, :].astype(F32)
         grad_heads = total.astype(BF16)
         query_unit, query_inv = normalize(q_ref[rows, :])
@@ -80,57 +80,78 @@
         dk_ref[rows, :] = norm_back(grad_kn, key_unit, key_inv, kg_ref[...]).astype(BF16)
 
 
-def block(ref, zone, core):
-    start = pl.multiple_of(lax.rem(zone, NZ) * (NC * BLK) + core * BLK, BLK)
-    return ref[:, pl.ds(start, BLK)]
-
-
-def heads_kernel(g_ref, own_ref, other_ref, out_ref):
-    zone, core = lax.axis_index("zh"), lax.axis_index("core")
-    total = None
-    for ref, side in ((own_ref, core), (other_ref, 1 - core)):
+def assemble(g_refs, held_ref):
+    low = lax.axis_index("zl")
+    for step in range(NL):
+        held_ref[low ^ step] = g_refs[step][...]
+
+
+def block(ref, zone):
+    columns = pl.ds(zone * BLK, BLK)
+    parts = [ref[:, line, :, columns].reshape(-1, BLK) for line in range(NY)]
+    return jnp.concatenate(parts, axis=0)
+
+
+def heads_kernel(*refs):
+    g_refs, own_refs, other_refs = refs[:NL], refs[NL : NL + NX], refs[NL + NX : NL + 2 * NX]
+    out_ref, held_ref = refs[-2:]
+    assemble(g_refs, held_ref)
+    here, core, across = (lax.axis_index(name) for name in ("zh", "core", "x"))
+    blocks = [block(held_ref, lax.rem(here + NZ - zone, NZ)) for zone in range(NZ)]
+    for step in range(NX):
+        for part_refs, side in ((own_refs, core), (other_refs, 1 - core)):
+            total = None
+            for zone in range(NZ):
+                term = dot(blocks[zone], part_refs[step][zone], 1, 1)
+                total = term if total is None else total + term
+            head = NC * lax.rem(across + NX - step, NX) + side
+            out_ref[head] = total.astype(BF16)
+
+
+def weight_kernel(*refs):
+    g_refs, mixed_ref = refs[:NL], refs[NL]
+    keep_ref, send_ref, held_ref = refs[-3:]
+    assemble(g_refs, held_ref)
+    here, core, across = (lax.axis_index(name) for name in ("zh", "core", "x"))
+    blocks = [block(held_ref, lax.rem(here + step, NZ)) for step in range(NZ)]
+    for ref, side in ((send_ref, 1 - core), (keep_ref, core)):
+        parts = [mixed_ref[lax.rem(across + step, NX), side] for step in range(NX)]
+        mixed = jnp.concatenate(parts, axis=0)
         for step in range(NZ):
-            weight = ref[:, step].reshape(NX * DH, BLK)
-            term = dot(block(g_ref, zone + NZ - step, side), weight, 1, 1)
-            total = term if total is None else total + term
-    for head in range(NL):
-        out_ref[head] = total[:, head * DH : (head + 1) * DH].astype(BF16)
-
-
-def weight_kernel(g_ref, mixed_ref, keep_ref, send_ref):
-    zone, core = lax.axis_index("zh"), lax.axis_index("core")
-    mixed = mixed_ref[...]
-    for ref, side in ((send_ref, 1 - core), (keep_ref, core)):
-        for step in range(NZ):
-            term = dot(mixed, block(g_ref, zone + step, side), 1, 0)
-            ref[:, step] = term.reshape(NL, DH, BLK).astype(ref.dtype)
-
-
-def call(kernel, outs, flops, moved, *operands):
+            term = dot(mixed, blocks[step], 1, 0)
+            ref[:, step] = term.reshape(NX, DH, BLK).astype(ref.dtype)
+
+
+def call(kernel, outs, flops, moved, operands, scratch=()):
     return pl.pallas_call(
         kernel,
         out_shape=outs,
         in_specs=[pl.BlockSpec(memory_space=pltpu.VMEM)] * len(operands),
         out_specs=jax.tree.map(lambda _: pl.BlockSpec(memory_space=pltpu.VMEM), outs),
+        scratch_shapes=list(scratch),
         compiler_params=pltpu.CompilerParams(vmem_limit_bytes=VMEM_LIMIT),
         cost_estimate=pl.CostEstimate(flops=flops, bytes_accessed=moved, transcendentals=0),
     )(*operands)
 
 
-def crossing(shift):
+def cross(entry, shift):
     pairs = []
     for zone in range(NZ):
-        for across in range(NX):
-            for low in range(NL):
+        for across in range(NX * NC):
+            for line in range(NY):
                 target = (zone + shift) % NZ
                 pairs.append(
-                    ((zone * NX + across) * NL + low, (target * NX + low) * NL + across)
+                    ((zone * NX * NC + across) * NY + line, (target * NX * NC + line) * NY + across)
                 )
-    return pairs
-
-
-def cross(entry, shift):
-    return lax.ppermute(entry, ("zh", "x", "zl"), crossing(shift))
+    return lax.ppermute(entry, ("zh", "x", "core", "y"), pairs)
+
+
+def shifted(entry, axis, size, step):
+    return lax.ppermute(entry, axis, [(at, (at + step) % size) for at in range(size)])
+
+
+def flipped(entry, axis, size, step):
+    return lax.ppermute(entry, axis, [(at, at ^ step) for at in range(size)])
 
 
 def swap_cores(entry):
@@ -141,56 +162,53 @@
     query_gain = query_gain.reshape(1, DH)
     key_gain = key_gain.reshape(1, DH)
     shape = jax.ShapeDtypeStruct
-
-    rows = grad_output.shape[0]
-    pieces = grad_output.reshape(rows, NZ, NL, NC * BLK).transpose(2, 0, 1, 3)
-    pieces = pieces.reshape(NL * rows, WIDE)
-    exchanged = lax.all_to_all(pieces, "zl", 0, 0, tiled=True)
-    gathered = lax.all_gather(exchanged, "y", axis=0, tiled=True)
-
-    moved = jnp.stack([cross(out_weight, shift) for shift in range(NZ)])
-    own = lax.all_gather(moved, "x", axis=0)
-    other = swap_cores(own)
 
     mixed, attention = call(
         forward_kernel,
         (shape((DH, TOK), BF16), shape((IMAGES, PATCH, PATCH), F32)),
         2 * 2 * IMAGES * PATCH * PATCH * DH,
         1 << 20,
-        query_input,
-        key_input,
-        value_input,
-        query_gain,
-        key_gain,
-    )
-    mixed_all = lax.all_gather(mixed, "zl", axis=0, tiled=True)
-
-    gathered, mixed_all, own, other = lax.optimization_barrier(
-        (gathered, mixed_all, own, other)
-    )
+        (query_input, key_input, value_input, query_gain, key_gain),
+    )
+    rows = grad_output.shape[0]
+    pieces = grad_output.reshape(rows, NZ, NY, BLK).transpose(2, 0, 1, 3)
+    pieces = pieces.reshape(NY, rows, WIDE)
+    pieces, mixed = lax.optimization_barrier((pieces, mixed))
+    mixed_all = lax.all_gather(mixed, "y", axis=0, tiled=True)
+    exchanged = lax.all_to_all(pieces, "y", 0, 0, tiled=True)
+    crossed = cross(out_weight, 0)
+    exchanged, crossed = lax.optimization_barrier((exchanged, crossed))
+    zones = [crossed] + [shifted(crossed, "zh", NZ, step) for step in range(1, NZ)]
+    gathered = [exchanged] + [flipped(exchanged, "zl", NL, step) for step in range(1, NL)]
+    zones = jnp.stack(zones)
+    own = [zones] + [shifted(zones, "x", NX, step) for step in range(1, NX)]
+    gathered, mixed_all, own = lax.optimization_barrier((gathered, mixed_all, own))
+    other = [swap_cores(entry) for entry in own]
+
+    half = (NX, NZ, DH, BLK)
+    held = (pltpu.VMEM((NL, NY, rows, WIDE), BF16),)
     keep, send = call(
         weight_kernel,
-        (shape((NL, NZ, DH, BLK), F32), shape((NL, NZ, DH, BLK), BF16)),
-        2 * TOK * TOK * WIDE,
+        (shape(half, F32), shape(half, BF16)),
+        2 * TOK * NY * DH * WIDE,
         5 << 20,
-        gathered,
-        mixed_all,
+        (*gathered, mixed_all.reshape(NX, NC, DH, TOK)),
+        held,
     )
     received = swap_cores(send)
     partial = call(
         heads_kernel,
-        shape((NL, TOK, DH), BF16),
-        2 * TOK * TOK * WIDE,
+        shape((NY, TOK, DH), BF16),
+        2 * TOK * NY * DH * WIDE,
         4 << 20,
-        gathered,
-        own,
-        other,
-    )
-    grad_heads = lax.all_to_all(partial, "zl", 0, 0, tiled=True)
-
-    summed = (keep + received.astype(F32)).astype(BF16)
-    spread = lax.all_to_all(summed, "x", 0, 0, tiled=True)
-    by_zone = sum(spread[part].astype(F32) for part in range(NX)).astype(BF16)
+        (*gathered, *own, *other),
+        held,
+    )
+    grad_heads = lax.all_to_all(partial, "y", 0, 0, tiled=True)
+
+    summed = [(keep[step] + received[step].astype(F32)).astype(BF16) for step in range(NX)]
+    spread = [summed[0]] + [shifted(summed[step], "x", NX, step) for step in range(1, NX)]
+    by_zone = sum(entry.astype(F32) for entry in spread).astype(BF16)
     last = [cross(by_zone[shift], shift) for shift in range(NZ)]
     grad_weight = sum(entry.astype(F32) for entry in last).astype(BF16)
 
@@ -199,13 +217,7 @@
         (shape((TOK, DH), BF16),) * 3,
         5 * 2 * IMAGES * PATCH * PATCH * DH,
         2 << 20,
-        query_input,
-        key_input,
-        value_input,
-        query_gain,
-        key_gain,
-        attention,
-        grad_heads,
+        (query_input, key_input, value_input, query_gain, key_gain, attention, grad_heads),
     )
     return grad_query, grad_key, grad_value, grad_weight
 

time: 153 us -> 167 us (1.092)
  the two profiles are of different devices: /device:TPU:224 before, /device:TPU:96 now
where the time goes in v2:
time: 167 us; the launch traced here: 166 us
  starting transfers between devices  91.3 us (55%)
  waiting for transfers between devices  41.3 us (25%)
  between operations  14.4 us (9%)
  Pallas kernels  9.05 us (5%)
  local copies, waits for them, and re-layouts  7.24 us (4%)
  other arithmetic  2.99 us (2%)
    ppermute x8, starting transfers between devices, shifted(): lax.ppermute(entry, axis, [(at, (at + step) % size) for at in range(size)])  32.4 us
    ppermute x4, starting transfers between devices, cross(): return lax.ppermute(entry, ('zh', 'x', 'core', 'y'), pairs)  23.5 us
    ppermute x8, waiting for transfers between devices, shifted(): lax.ppermute(entry, axis, [(at, (at + step) % size) for at in range(size)])  20.9 us
    ppermute x4, waiting for transfers between devices, cross(): return lax.ppermute(entry, ('zh', 'x', 'core', 'y'), pairs)  20.3 us
    ppermute x5, starting transfers between devices, swap_cores(): return lax.ppermute(entry, 'core', [(0, 1), (1, 0)])  10.6 us
    ppermute x3, starting transfers between devices, flipped(): return lax.ppermute(entry, axis, [(at, at ^ step) for at in range(size)])  10.5 us
    pallas_call x4, Pallas kernels, call(): pl.pallas_call(kernel, out_shape=outs, in_specs=[pl.BlockSpec(memory_spac...  9.05 us
    all_to_all x1, starting transfers between devices, shards(): exchanged = lax.all_to_all(pieces, 'y', 0, 0, tiled=True)  7.22 us
  transfers between devices with their start and end apart: 23, of which 9 were waited for; matrix products, arithmetic and copies ran while one was open for 2% of the time, Pallas kernels for 3%

profile of v2, /device:TPU:96, one launch (start us, length us, event | category | flops | bytes accessed | tf_op | source)
XLA Modules:
  0.0 166.3 jit_solution(2507546893152430808)
XLA Ops:
  7.2 0.0 all-gather.2.cloned.1.call-start
  7.2 1.0 copy.13
  8.2 0.1 copy.15
  8.3 0.9 reshape.40
  9.2 0.9 copy-done
  10.1 0.9 copy-done.2
  11.0 0.9 copy-done.4
  11.9 0.7 copy-done.6
  12.6 0.7 copy-done.8
  13.2 1.5 shard_map.102
  14.7 7.2 %all-to-all-start = ((bf16[8,16,768]{2,1,0:T(8,128)(2,1)}), bf16[8,16,768]{2,1,0:T(8,128)(2,1)S(1)}, u32[]{:S(2)}, u32[]{:S(2)}) async-start(bf16[8,16,768]{2,1,0:T(8,128)(2,1)} %reshape.40), calls=%async_computation | async-start | bytes 393216 | tf_op jit(solution)/shard_map/all_to_all | solution.py:178
  21.9 4.4 %collective-permute-start = (bf16[128,256]{1,0:T(8,128)(2,1)S(1)}, bf16[128,256]{1,0:T(8,128)(2,1)S(1)}, u32[]{:S(2)}, u32[]{:S(2)}) collective-permute-start(bf16[128,256]{1,0:T(8,128)(2,1)S(1)} %copy-done.11), channel_id=1, source_target_pairs={{0,0},{4,32},{8,64},{12,96},{16,128},{20,160},{24,192},{28,224},{3... | collective-permute-start | bytes 196616 | tf_op jit(solution)/shard_map/ppermute | solution.py:146
  26.3 8.4 %collective-permute-done = bf16[128,256]{1,0:T(8,128)(2,1)S(1)} collective-permute-done((bf16[128,256]{1,0:T(8,128)(2,1)S(1)}, bf16[128,256]{1,0:T(8,128)(2,1)S(1)}, u32[]{:S(2)}, u32[]{:S(2)}) %collective-permute-start) | collective-permute-done | bytes 65568 | tf_op jit(solution)/shard_map/ppermute | solution.py:146
  34.8 4.3 %collective-permute-start.3 = (bf16[8,16,768]{2,1,0:T(8,128)(2,1)S(1)}, bf16[8,16,768]{2,1,0:T(8,128)(2,1)S(1)}, u32[]{:S(2)}, u32[]{:S(2)}) collective-permute-start(bf16[8,16,768]{2,1,0:T(8,128)(2,1)S(1)} %all-to-all-done.refs_0_), channel_id=1, source_target_pairs={{0,3},{1,2},{2,1},{3,0},{4,7},{5,6},{6,5},{7,4},{8,11},{9,10},{10,... | collective-permute-start | bytes 589832 | tf_op jit(solution)/shard_map/ppermute | solution.py:154
  39.0 13.3 %collective-permute-start.5 = (bf16[128,256]{1,0:T(8,128)(2,1)S(1)}, bf16[128,256]{1,0:T(8,128)(2,1)S(1)}, u32[]{:S(2)}, u32[]{:S(2)}) collective-permute-start(bf16[128,256]{1,0:T(8,128)(2,1)S(1)} %collective-permute-done), channel_id=1, source_target_pairs={{0,512},{256,0},{512,256},{1,513},{257,1},{513,257},{2,514},{258,2... | collective-permute-start | bytes 196616 | tf_op jit(solution)/shard_map/ppermute | solution.py:150
  52.4 1.9 %collective-permute-start.4 = (bf16[128,256]{1,0:T(8,128)(2,1)S(1)}, bf16[128,256]{1,0:T(8,128)(2,1)S(1)}, u32[]{:S(2)}, u32[]{:S(2)}) collective-permute-start(bf16[128,256]{1,0:T(8,128)(2,1)S(1)} %collective-permute-done), channel_id=1, source_target_pairs={{0,256},{256,512},{512,0},{1,257},{257,513},{513,1},{2,258},{258,5... | collective-permute-start | bytes 196616 | tf_op jit(solution)/shard_map/ppermute | solution.py:150
  54.3 2.8 %collective-permute-start.2 = (bf16[8,16,768]{2,1,0:T(8,128)(2,1)S(1)}, bf16[8,16,768]{2,1,0:T(8,128)(2,1)S(1)}, u32[]{:S(2)}, u32[]{:S(2)}) collective-permute-start(bf16[8,16,768]{2,1,0:T(8,128)(2,1)S(1)} %all-to-all-done.refs_0_), channel_id=1, source_target_pairs={{0,2},{1,3},{2,0},{3,1},{4,6},{5,7},{6,4},{7,5},{8,10},{9,11},{10,... | collective-permute-start | bytes 589832 | tf_op jit(solution)/shard_map/ppermute | solution.py:154
  57.1 3.4 %collective-permute-start.1 = (bf16[8,16,768]{2,1,0:T(8,128)(2,1)S(1)}, bf16[8,16,768]{2,1,0:T(8,128)(2,1)S(1)}, u32[]{:S(2)}, u32[]{:S(2)}) collective-permute-start(bf16[8,16,768]{2,1,0:T(8,128)(2,1)S(1)} %all-to-all-done.refs_0_), channel_id=1, source_target_pairs={{0,1},{1,0},{2,3},{3,2},{4,5},{5,4},{6,7},{7,6},{8,9},{9,8},{10,11... | collective-permute-start | bytes 589832 | tf_op jit(solution)/shard_map/ppermute | solution.py:154
  60.5 7.1 %collective-permute-done.4 = bf16[128,256]{1,0:T(8,128)(2,1)S(1)} collective-permute-done((bf16[128,256]{1,0:T(8,128)(2,1)S(1)}, bf16[128,256]{1,0:T(8,128)(2,1)S(1)}, u32[]{:S(2)}, u32[]{:S(2)}) %collective-permute-start.4) | collective-permute-done | bytes 65568 | tf_op jit(solution)/shard_map/ppermute | solution.py:150
  67.7 1.9 %collective-permute-start.8 = (bf16[3,128,256]{2,1,0:T(8,128)(2,1)S(1)}, bf16[3,128,256]{2,1,0:T(8,128)(2,1)S(1)}, u32[]{:S(2)}, u32[]{:S(2)}) collective-permute-start(bf16[3,128,256]{2,1,0:T(8,128)(2,1)S(1)} %pad_maximum_fusion.refs_4_), channel_id=1, source_target_pairs={{0,192},{64,0},{128,64},{192,128},{1,193},{65,1},{129,65},{193,129... | collective-permute-start | bytes 589832 | tf_op jit(solution)/shard_map/ppermute | solution.py:150
  69.6 1.9 %collective-permute-start.7 = (bf16[3,128,256]{2,1,0:T(8,128)(2,1)S(1)}, bf16[3,128,256]{2,1,0:T(8,128)(2,1)S(1)}, u32[]{:S(2)}, u32[]{:S(2)}) collective-permute-start(bf16[3,128,256]{2,1,0:T(8,128)(2,1)S(1)} %pad_maximum_fusion.refs_4_), channel_id=1, source_target_pairs={{0,128},{64,192},{128,0},{192,64},{1,129},{65,193},{129,1},{193,65... | collective-permute-start | bytes 589832 | tf_op jit(solution)/shard_map/ppermute | solution.py:150
  71.5 3.9 %collective-permute-start.6 = (bf16[3,128,256]{2,1,0:T(8,128)(2,1)S(1)}, bf16[3,128,256]{2,1,0:T(8,128)(2,1)}, u32[]{:S(2)}, u32[]{:S(2)}) collective-permute-start(bf16[3,128,256]{2,1,0:T(8,128)(2,1)S(1)} %pad_maximum_fusion.refs_4_), channel_id=1, source_target_pairs={{0,64},{64,128},{128,192},{192,0},{1,65},{65,129},{129,193},{193,1... | collective-permute-start | bytes 589832 | tf_op jit(solution)/shard_map/ppermute | solution.py:150
  75.5 3.2 %collective-permute-done.7.refs_6_ = bf16[3,128,256]{2,1,0:T(8,128)(2,1)S(1)} collective-permute-done((bf16[3,128,256]{2,1,0:T(8,128)(2,1)S(1)}, bf16[3,128,256]{2,1,0:T(8,128)(2,1)S(1)}, u32[]{:S(2)}, u32[]{:S(2)}) %collective-permute-start.7) | collective-permute-done | bytes 196640 | tf_op jit(solution)/shard_map/ppermute | solution.py:150
  78.7 3.2 %collective-permute-done.6.refs_5_ = bf16[3,128,256]{2,1,0:T(8,128)(2,1)} collective-permute-done((bf16[3,128,256]{2,1,0:T(8,128)(2,1)S(1)}, bf16[3,128,256]{2,1,0:T(8,128)(2,1)}, u32[]{:S(2)}, u32[]{:S(2)}) %collective-permute-start.6) | collective-permute-done | bytes 196640 | tf_op jit(solution)/shard_map/ppermute | solution.py:150
  81.9 1.9 %collective-permute-start.9 = (bf16[3,128,256]{2,1,0:T(8,128)(2,1)S(1)}, bf16[3,128,256]{2,1,0:T(8,128)(2,1)S(1)}, u32[]{:S(2)}, u32[]{:S(2)}) collective-permute-start(bf16[3,128,256]{2,1,0:T(8,128)(2,1)S(1)} %pad_maximum_fusion.refs_4_), channel_id=1, source_target_pairs={{0,32},{32,0},{1,33},{33,1},{2,34},{34,2},{3,35},{35,3},{4,36},{36... | collective-permute-start | bytes 589832 | tf_op jit(solution)/shard_map/ppermute | solution.py:158
  83.8 2.4 %collective-permute-start.10 = (bf16[3,128,256]{2,1,0:T(8,128)(2,1)}, bf16[3,128,256]{2,1,0:T(8,128)(2,1)S(1)}, u32[]{:S(2)}, u32[]{:S(2)}) collective-permute-start(bf16[3,128,256]{2,1,0:T(8,128)(2,1)} %collective-permute-done.6.refs_5_), channel_id=1, source_target_pairs={{0,32},{32,0},{1,33},{33,1},{2,34},{34,2},{3,35},{35,3},{4,36},{36... | collective-permute-start | bytes 589832 | tf_op jit(solution)/shard_map/ppermute | solution.py:158
  86.2 1.9 %collective-permute-start.11 = (bf16[3,128,256]{2,1,0:T(8,128)(2,1)S(1)}, bf16[3,128,256]{2,1,0:T(8,128)(2,1)S(1)}, u32[]{:S(2)}, u32[]{:S(2)}) collective-permute-start(bf16[3,128,256]{2,1,0:T(8,128)(2,1)S(1)} %collective-permute-done.7.refs_6_), channel_id=1, source_target_pairs={{0,32},{32,0},{1,33},{33,1},{2,34},{34,2},{3,35},{35,3},{4,36},{36... | collective-permute-start | bytes 589832 | tf_op jit(solution)/shard_map/ppermute | solution.py:158
  88.1 2.4 %collective-permute-start.12 = (bf16[3,128,256]{2,1,0:T(8,128)(2,1)S(1)}, bf16[3,128,256]{2,1,0:T(8,128)(2,1)S(1)}, u32[]{:S(2)}, u32[]{:S(2)}) collective-permute-start(bf16[3,128,256]{2,1,0:T(8,128)(2,1)S(1)} %collective-permute-done.8.refs_7_), channel_id=1, source_target_pairs={{0,32},{32,0},{1,33},{33,1},{2,34},{34,2},{3,35},{35,3},{4,36},{36... | collective-permute-start | bytes 589832 | tf_op jit(solution)/shard_map/ppermute | solution.py:158
  90.6 1.2 copy-done.10
  91.8 1.7 shard_map.105
  93.4 1.9 %collective-permute-start.13 = (bf16[4,3,128,256]{3,2,1,0:T(8,128)(2,1)}, bf16[4,3,128,256]{3,2,1,0:T(8,128)(2,1)}, u32[]{:S(2)}, u32[]{:S(2)}) collective-permute-start(bf16[4,3,128,256]{3,2,1,0:T(8,128)(2,1)} %get-tuple-element.43), channel_id=1, source_target_pairs={{0,32},{32,0},{1,33},{33,1},{2,34},{34,2},{3,35},{35,3},{4,36},{36... | collective-permute-start | bytes 2359304 | tf_op jit(solution)/shard_map/ppermute | solution.py:158
  95.4 3.8 %shard_map.103 = bf16[8,512,128]{2,1,0:T(8,128)(2,1)} custom-call(bf16[8,16,768]{2,1,0:T(8,128)(2,1)S(1)} %all-to-all-done.refs_0_, bf16[8,16,768]{2,1,0:T(8,128)(2,1)S(1)} %collective-permute-done.1.refs_1_, bf16[8,16,768]{2,1,0:T(8,128)(2,1)S(1)} %collective-permute-done.2.refs_2_, bf16[8,16,768]{2,1,0:T(8,128)(2,1)S(1)} %collective-permute-done.3.refs_3_, ...), custom_call_target="tpu_custom_call" | custom-call | flops 805306368 | bytes 4194304 | tf_op jit(solution)/shard_map/pallas_call | solution.py:126
  99.1 7.2 %all-to-all-start.1 = ((bf16[8,512,128]{2,1,0:T(8,128)(2,1)}), bf16[8,512,128]{2,1,0:T(8,128)(2,1)S(1)}, u32[]{:S(2)}, u32[]{:S(2)}) async-start(bf16[8,512,128]{2,1,0:T(8,128)(2,1)} %shard_map.103), calls=%async_computation.1 | async-start | bytes 2097152 | tf_op jit(solution)/shard_map/all_to_all | solution.py:207
  106.3 1.3 fusion.4
  107.7 2.1 %collective-permute-start.14 = (bf16[3,128,256]{2,1,0:T(8,128)(2,1)S(1)}, bf16[3,128,256]{2,1,0:T(8,128)(2,1)S(1)}, u32[]{:S(2)}, u32[]{:S(2)}) collective-permute-start(bf16[3,128,256]{2,1,0:T(8,128)(2,1)S(1)} %get-tuple-element.44), channel_id=1, source_target_pairs={{0,64},{64,128},{128,192},{192,0},{1,65},{65,129},{129,193},{193,1... | collective-permute-start | bytes 589832 | tf_op jit(solution)/shard_map/ppermute | solution.py:150
  109.7 5.1 %collective-permute-start.16 = (bf16[3,128,256]{2,1,0:T(8,128)(2,1)S(1)}, bf16[3,128,256]{2,1,0:T(8,128)(2,1)S(1)}, u32[]{:S(2)}, u32[]{:S(2)}) collective-permute-start(bf16[3,128,256]{2,1,0:T(8,128)(2,1)S(1)} %get-tuple-element.45), channel_id=1, source_target_pairs={{0,192},{64,0},{128,64},{192,128},{1,193},{65,1},{129,65},{193,129... | collective-permute-start | bytes 589832 | tf_op jit(solution)/shard_map/ppermute | solution.py:150
  114.9 2.2 %collective-permute-start.15 = (bf16[3,128,256]{2,1,0:T(8,128)(2,1)S(1)}, bf16[3,128,256]{2,1,0:T(8,128)(2,1)S(1)}, u32[]{:S(2)}, u32[]{:S(2)}) collective-permute-start(bf16[3,128,256]{2,1,0:T(8,128)(2,1)S(1)} %get-tuple-element.46), channel_id=1, source_target_pairs={{0,128},{64,192},{128,0},{192,64},{1,129},{65,193},{129,1},{193,65... | collective-permute-start | bytes 589832 | tf_op jit(solution)/shard_map/ppermute | solution.py:150
  117.0 0.6 collective-permute-done.14
  117.6 5.4 %collective-permute-done.16 = bf16[3,128,256]{2,1,0:T(8,128)(2,1)S(1)} collective-permute-done((bf16[3,128,256]{2,1,0:T(8,128)(2,1)S(1)}, bf16[3,128,256]{2,1,0:T(8,128)(2,1)S(1)}, u32[]{:S(2)}, u32[]{:S(2)}) %collective-permute-start.16) | collective-permute-done | bytes 196640 | tf_op jit(solution)/shard_map/ppermute | solution.py:150
  123.0 1.4 collective-permute-done.15
  124.4 1.1 fusion.2
  125.5 2.2 %collective-permute-start.17 = (bf16[128,256]{1,0:T(8,128)(2,1)S(1)}, bf16[128,256]{1,0:T(8,128)(2,1)S(1)}, u32[]{:S(2)}, u32[]{:S(2)}) collective-permute-start(bf16[128,256]{1,0:T(8,128)(2,1)S(1)} %get-tuple-element.47), channel_id=1, source_target_pairs={{0,0},{4,32},{8,64},{12,96},{16,128},{20,160},{24,192},{28,224},{3... | collective-permute-start | bytes 196616 | tf_op jit(solution)/shard_map/ppermute | solution.py:146
  127.7 11.6 %collective-permute-start.19 = (bf16[128,256]{1,0:T(8,128)(2,1)S(1)}, bf16[128,256]{1,0:T(8,128)(2,1)S(1)}, u32[]{:S(2)}, u32[]{:S(2)}) collective-permute-start(bf16[128,256]{1,0:T(8,128)(2,1)S(1)} %get-tuple-element.48), channel_id=1, source_target_pairs={{0,512},{4,544},{8,576},{12,608},{16,640},{20,672},{24,704},{28,73... | collective-permute-start | bytes 196616 | tf_op jit(solution)/shard_map/ppermute | solution.py:146
  139.3 5.3 %collective-permute-start.18 = (bf16[128,256]{1,0:T(8,128)(2,1)S(1)}, bf16[128,256]{1,0:T(8,128)(2,1)S(1)}, u32[]{:S(2)}, u32[]{:S(2)}) collective-permute-start(bf16[128,256]{1,0:T(8,128)(2,1)S(1)} %get-tuple-element.49), channel_id=1, source_target_pairs={{0,256},{4,288},{8,320},{12,352},{16,384},{20,416},{24,448},{28,48... | collective-permute-start | bytes 196616 | tf_op jit(solution)/shard_map/ppermute | solution.py:146
  144.7 0.3 collective-permute-done.19
  145.0 11.6 %collective-permute-done.18 = bf16[128,256]{1,0:T(8,128)(2,1)S(1)} collective-permute-done((bf16[128,256]{1,0:T(8,128)(2,1)S(1)}, bf16[128,256]{1,0:T(8,128)(2,1)S(1)}, u32[]{:S(2)}, u32[]{:S(2)}) %collective-permute-start.18) | collective-permute-done | bytes 65568 | tf_op jit(solution)/shard_map/ppermute | solution.py:146
  156.6 0.7 add_convert_fusion.4
  157.3 2.2 %shard_map.104 = (bf16[512,128]{1,0:T(8,128)(2,1)}, bf16[512,128]{1,0:T(8,128)(2,1)}, bf16[512,128]{1,0:T(8,128)(2,1)}) custom-call(bf16[512,128]{1,0:T(8,128)(2,1)S(1)} %copy-done.1, bf16[512,128]{1,0:T(8,128)(2,1)S(1)} %copy-done.3, bf16[512,128]{1,0:T(8,128)(2,1)S(1)} %copy-done.5, f32[1,128]{1,0:T(1,128)S(1)} %bitcast.30, f32[1,128]{1,0:T(1,128)S(1)} %bitcast.32, ...), custom_call_target="tpu_custom_call" | custom-call | flops 167772160 | bytes 2097152 | tf_op jit(solution)/shard_map/pallas_call | solution.py:126
  (35 shorter events, 0.1 us)
Async XLA Ops:
  7.2 14.8 %copy-start.11 = (bf16[128,256]{1,0:T(8,128)(2,1)S(1)}, bf16[128,256]{1,0:T(8,128)(2,1)}, u32[]{:S(2)}) copy-start(bf16[128,256]{1,0:T(8,128)(2,1)} %param.12) | copy-start | bytes 196612
  7.2 74.7 %all-gather.2.cloned.1.call-start = ((), (), s32[]{:S(2)}) async-start(), calls=%async_computation.2 | async-start | bytes 1179648 | tf_op jit(solution)/shard_map/all_gather | solution.py:177
  9.2 0.9 copy-start
  10.1 0.9 copy-start.2
  11.0 0.9 copy-start.4
  11.9 0.7 copy-start.6
  12.6 0.7 copy-start.8
  14.7 20.0 %all-to-all-start = ((bf16[8,16,768]{2,1,0:T(8,128)(2,1)}), bf16[8,16,768]{2,1,0:T(8,128)(2,1)S(1)}, u32[]{:S(2)}, u32[]{:S(2)}) async-start(bf16[8,16,768]{2,1,0:T(8,128)(2,1)} %reshape.40), calls=%async_computation | async-start | bytes 393216 | tf_op jit(solution)/shard_map/all_to_all | solution.py:178
  21.9 12.8 %collective-permute-start = (bf16[128,256]{1,0:T(8,128)(2,1)S(1)}, bf16[128,256]{1,0:T(8,128)(2,1)S(1)}, u32[]{:S(2)}, u32[]{:S(2)}) collective-permute-start(bf16[128,256]{1,0:T(8,128)(2,1)S(1)} %copy-done.11), channel_id=1, source_target_pairs={{0,0},{4,32},{8,64},{12,96},{16,128},{20,160},{24,192},{28,224},{3... | collective-permute-start | bytes 196616 | tf_op jit(solution)/shard_map/ppermute | solution.py:146
  34.8 36.8 %collective-permute-start.3 = (bf16[8,16,768]{2,1,0:T(8,128)(2,1)S(1)}, bf16[8,16,768]{2,1,0:T(8,128)(2,1)S(1)}, u32[]{:S(2)}, u32[]{:S(2)}) collective-permute-start(bf16[8,16,768]{2,1,0:T(8,128)(2,1)S(1)} %all-to-all-done.refs_0_), channel_id=1, source_target_pairs={{0,3},{1,2},{2,1},{3,0},{4,7},{5,6},{6,5},{7,4},{8,11},{9,10},{10,... | collective-permute-start | bytes 589832 | tf_op jit(solution)/shard_map/ppermute | solution.py:154
  39.0 21.5 %collective-permute-start.5 = (bf16[128,256]{1,0:T(8,128)(2,1)S(1)}, bf16[128,256]{1,0:T(8,128)(2,1)S(1)}, u32[]{:S(2)}, u32[]{:S(2)}) collective-permute-start(bf16[128,256]{1,0:T(8,128)(2,1)S(1)} %collective-permute-done), channel_id=1, source_target_pairs={{0,512},{256,0},{512,256},{1,513},{257,1},{513,257},{2,514},{258,2... | collective-permute-start | bytes 196616 | tf_op jit(solution)/shard_map/ppermute | solution.py:150
  52.4 15.3 %collective-permute-start.4 = (bf16[128,256]{1,0:T(8,128)(2,1)S(1)}, bf16[128,256]{1,0:T(8,128)(2,1)S(1)}, u32[]{:S(2)}, u32[]{:S(2)}) collective-permute-start(bf16[128,256]{1,0:T(8,128)(2,1)S(1)} %collective-permute-done), channel_id=1, source_target_pairs={{0,256},{256,512},{512,0},{1,257},{257,513},{513,1},{2,258},{258,5... | collective-permute-start | bytes 196616 | tf_op jit(solution)/shard_map/ppermute | solution.py:150
  54.3 21.2 %collective-permute-start.2 = (bf16[8,16,768]{2,1,0:T(8,128)(2,1)S(1)}, bf16[8,16,768]{2,1,0:T(8,128)(2,1)S(1)}, u32[]{:S(2)}, u32[]{:S(2)}) collective-permute-start(bf16[8,16,768]{2,1,0:T(8,128)(2,1)S(1)} %all-to-all-done.refs_0_), channel_id=1, source_target_pairs={{0,2},{1,3},{2,0},{3,1},{4,6},{5,7},{6,4},{7,5},{8,10},{9,11},{10,... | collective-permute-start | bytes 589832 | tf_op jit(solution)/shard_map/ppermute | solution.py:154
  57.1 18.4 %collective-permute-start.1 = (bf16[8,16,768]{2,1,0:T(8,128)(2,1)S(1)}, bf16[8,16,768]{2,1,0:T(8,128)(2,1)S(1)}, u32[]{:S(2)}, u32[]{:S(2)}) collective-permute-start(bf16[8,16,768]{2,1,0:T(8,128)(2,1)S(1)} %all-to-all-done.refs_0_), channel_id=1, source_target_pairs={{0,1},{1,0},{2,3},{3,2},{4,5},{5,4},{6,7},{7,6},{8,9},{9,8},{10,11... | collective-permute-start | bytes 589832 | tf_op jit(solution)/shard_map/ppermute | solution.py:154
  67.7 7.8 %collective-permute-start.8 = (bf16[3,128,256]{2,1,0:T(8,128)(2,1)S(1)}, bf16[3,128,256]{2,1,0:T(8,128)(2,1)S(1)}, u32[]{:S(2)}, u32[]{:S(2)}) collective-permute-start(bf16[3,128,256]{2,1,0:T(8,128)(2,1)S(1)} %pad_maximum_fusion.refs_4_), channel_id=1, source_target_pairs={{0,192},{64,0},{128,64},{192,128},{1,193},{65,1},{129,65},{193,129... | collective-permute-start | bytes 589832 | tf_op jit(solution)/shard_map/ppermute | solution.py:150
  69.6 9.1 %collective-permute-start.7 = (bf16[3,128,256]{2,1,0:T(8,128)(2,1)S(1)}, bf16[3,128,256]{2,1,0:T(8,128)(2,1)S(1)}, u32[]{:S(2)}, u32[]{:S(2)}) collective-permute-start(bf16[3,128,256]{2,1,0:T(8,128)(2,1)S(1)} %pad_maximum_fusion.refs_4_), channel_id=1, source_target_pairs={{0,128},{64,192},{128,0},{192,64},{1,129},{65,193},{129,1},{193,65... | collective-permute-start | bytes 589832 | tf_op jit(solution)/shard_map/ppermute | solution.py:150
  71.5 10.3 %collective-permute-start.6 = (bf16[3,128,256]{2,1,0:T(8,128)(2,1)S(1)}, bf16[3,128,256]{2,1,0:T(8,128)(2,1)}, u32[]{:S(2)}, u32[]{:S(2)}) collective-permute-start(bf16[3,128,256]{2,1,0:T(8,128)(2,1)S(1)} %pad_maximum_fusion.refs_4_), channel_id=1, source_target_pairs={{0,64},{64,128},{128,192},{192,0},{1,65},{65,129},{129,193},{193,1... | collective-permute-start | bytes 589832 | tf_op jit(solution)/shard_map/ppermute | solution.py:150
  81.9 13.5 %collective-permute-start.9 = (bf16[3,128,256]{2,1,0:T(8,128)(2,1)S(1)}, bf16[3,128,256]{2,1,0:T(8,128)(2,1)S(1)}, u32[]{:S(2)}, u32[]{:S(2)}) collective-permute-start(bf16[3,128,256]{2,1,0:T(8,128)(2,1)S(1)} %pad_maximum_fusion.refs_4_), channel_id=1, source_target_pairs={{0,32},{32,0},{1,33},{33,1},{2,34},{34,2},{3,35},{35,3},{4,36},{36... | collective-permute-start | bytes 589832 | tf_op jit(solution)/shard_map/ppermute | solution.py:158
  83.8 11.6 %collective-permute-start.10 = (bf16[3,128,256]{2,1,0:T(8,128)(2,1)}, bf16[3,128,256]{2,1,0:T(8,128)(2,1)S(1)}, u32[]{:S(2)}, u32[]{:S(2)}) collective-permute-start(bf16[3,128,256]{2,1,0:T(8,128)(2,1)} %collective-permute-done.6.refs_5_), channel_id=1, source_target_pairs={{0,32},{32,0},{1,33},{33,1},{2,34},{34,2},{3,35},{35,3},{4,36},{36... | collective-permute-start | bytes 589832 | tf_op jit(solution)/shard_map/ppermute | solution.py:158
  86.2 9.2 %collective-permute-start.11 = (bf16[3,128,256]{2,1,0:T(8,128)(2,1)S(1)}, bf16[3,128,256]{2,1,0:T(8,128)(2,1)S(1)}, u32[]{:S(2)}, u32[]{:S(2)}) collective-permute-start(bf16[3,128,256]{2,1,0:T(8,128)(2,1)S(1)} %collective-permute-done.7.refs_6_), channel_id=1, source_target_pairs={{0,32},{32,0},{1,33},{33,1},{2,34},{34,2},{3,35},{35,3},{4,36},{36... | collective-permute-start | bytes 589832 | tf_op jit(solution)/shard_map/ppermute | solution.py:158
  88.1 7.2 %collective-permute-start.12 = (bf16[3,128,256]{2,1,0:T(8,128)(2,1)S(1)}, bf16[3,128,256]{2,1,0:T(8,128)(2,1)S(1)}, u32[]{:S(2)}, u32[]{:S(2)}) collective-permute-start(bf16[3,128,256]{2,1,0:T(8,128)(2,1)S(1)} %collective-permute-done.8.refs_7_), channel_id=1, source_target_pairs={{0,32},{32,0},{1,33},{33,1},{2,34},{34,2},{3,35},{35,3},{4,36},{36... | collective-permute-start | bytes 589832 | tf_op jit(solution)/shard_map/ppermute | solution.py:158
  90.5 1.2 copy-start.10
  93.4 12.9 %collective-permute-start.13 = (bf16[4,3,128,256]{3,2,1,0:T(8,128)(2,1)}, bf16[4,3,128,256]{3,2,1,0:T(8,128)(2,1)}, u32[]{:S(2)}, u32[]{:S(2)}) collective-permute-start(bf16[4,3,128,256]{3,2,1,0:T(8,128)(2,1)} %get-tuple-element.43), channel_id=1, source_target_pairs={{0,32},{32,0},{1,33},{33,1},{2,34},{34,2},{3,35},{35,3},{4,36},{36... | collective-permute-start | bytes 2359304 | tf_op jit(solution)/shard_map/ppermute | solution.py:158
  99.1 58.1 %all-to-all-start.1 = ((bf16[8,512,128]{2,1,0:T(8,128)(2,1)}), bf16[8,512,128]{2,1,0:T(8,128)(2,1)S(1)}, u32[]{:S(2)}, u32[]{:S(2)}) async-start(bf16[8,512,128]{2,1,0:T(8,128)(2,1)} %shard_map.103), calls=%async_computation.1 | async-start | bytes 2097152 | tf_op jit(solution)/shard_map/all_to_all | solution.py:207
  107.6 49.7 %copy-start.1 = (bf16[512,128]{1,0:T(8,128)(2,1)S(1)}, bf16[512,128]{1,0:T(8,128)(2,1)}, u32[]{:S(2)}) copy-start(bf16[512,128]{1,0:T(8,128)(2,1)} %q_ref.3) | copy-start | bytes 393220
  107.6 49.7 %copy-start.3 = (bf16[512,128]{1,0:T(8,128)(2,1)S(1)}, bf16[512,128]{1,0:T(8,128)(2,1)}, u32[]{:S(2)}) copy-start(bf16[512,128]{1,0:T(8,128)(2,1)} %k_ref.3) | copy-start | bytes 393220
  107.6 49.7 %copy-start.5 = (bf16[512,128]{1,0:T(8,128)(2,1)S(1)}, bf16[512,128]{1,0:T(8,128)(2,1)}, u32[]{:S(2)}) copy-start(bf16[512,128]{1,0:T(8,128)(2,1)} %v_ref.3) | copy-start | bytes 393220
  107.6 49.7 %copy-start.7 = (f32[128]{0:T(128)S(1)}, f32[128]{0:T(128)}, u32[]{:S(2)}) copy-start(f32[128]{0:T(128)} %param.10) | copy-start | bytes 1540
  107.7 49.7 %copy-start.9 = (f32[128]{0:T(128)S(1)}, f32[128]{0:T(128)}, u32[]{:S(2)}) copy-start(f32[128]{0:T(128)} %param.11) | copy-start | bytes 1540
  107.7 10.0 %collective-permute-start.14 = (bf16[3,128,256]{2,1,0:T(8,128)(2,1)S(1)}, bf16[3,128,256]{2,1,0:T(8,128)(2,1)S(1)}, u32[]{:S(2)}, u32[]{:S(2)}) collective-permute-start(bf16[3,128,256]{2,1,0:T(8,128)(2,1)S(1)} %get-tuple-element.44), channel_id=1, source_target_pairs={{0,64},{64,128},{128,192},{192,0},{1,65},{65,129},{129,193},{193,1... | collective-permute-start | bytes 589832 | tf_op jit(solution)/shard_map/ppermute | solution.py:150
  109.7 13.3 %collective-permute-start.16 = (bf16[3,128,256]{2,1,0:T(8,128)(2,1)S(1)}, bf16[3,128,256]{2,1,0:T(8,128)(2,1)S(1)}, u32[]{:S(2)}, u32[]{:S(2)}) collective-permute-start(bf16[3,128,256]{2,1,0:T(8,128)(2,1)S(1)} %get-tuple-element.45), channel_id=1, source_target_pairs={{0,192},{64,0},{128,64},{192,128},{1,193},{65,1},{129,65},{193,129... | collective-permute-start | bytes 589832 | tf_op jit(solution)/shard_map/ppermute | solution.py:150
  114.9 9.6 %collective-permute-start.15 = (bf16[3,128,256]{2,1,0:T(8,128)(2,1)S(1)}, bf16[3,128,256]{2,1,0:T(8,128)(2,1)S(1)}, u32[]{:S(2)}, u32[]{:S(2)}) collective-permute-start(bf16[3,128,256]{2,1,0:T(8,128)(2,1)S(1)} %get-tuple-element.46), channel_id=1, source_target_pairs={{0,128},{64,192},{128,0},{192,64},{1,129},{65,193},{129,1},{193,65... | collective-permute-start | bytes 589832 | tf_op jit(solution)/shard_map/ppermute | solution.py:150
  125.5 19.2 %collective-permute-start.17 = (bf16[128,256]{1,0:T(8,128)(2,1)S(1)}, bf16[128,256]{1,0:T(8,128)(2,1)S(1)}, u32[]{:S(2)}, u32[]{:S(2)}) collective-permute-start(bf16[128,256]{1,0:T(8,128)(2,1)S(1)} %get-tuple-element.47), channel_id=1, source_target_pairs={{0,0},{4,32},{8,64},{12,96},{16,128},{20,160},{24,192},{28,224},{3... | collective-permute-start | bytes 196616 | tf_op jit(solution)/shard_map/ppermute | solution.py:146
  127.7 17.3 %collective-permute-start.19 = (bf16[128,256]{1,0:T(8,128)(2,1)S(1)}, bf16[128,256]{1,0:T(8,128)(2,1)S(1)}, u32[]{:S(2)}, u32[]{:S(2)}) collective-permute-start(bf16[128,256]{1,0:T(8,128)(2,1)S(1)} %get-tuple-element.48), channel_id=1, source_target_pairs={{0,512},{4,544},{8,576},{12,608},{16,640},{20,672},{24,704},{28,73... | collective-permute-start | bytes 196616 | tf_op jit(solution)/shard_map/ppermute | solution.py:146
  139.3 17.3 %collective-permute-start.18 = (bf16[128,256]{1,0:T(8,128)(2,1)S(1)}, bf16[128,256]{1,0:T(8,128)(2,1)S(1)}, u32[]{:S(2)}, u32[]{:S(2)}) collective-permute-start(bf16[128,256]{1,0:T(8,128)(2,1)S(1)} %get-tuple-element.49), channel_id=1, source_target_pairs={{0,256},{4,288},{8,320},{12,352},{16,384},{20,416},{24,448},{28,48... | collective-permute-start | bytes 196616 | tf_op jit(solution)/shard_map/ppermute | solution.py:146
Sparse Core Ops, SparseCore 0:
  14.8 46.8 all-gather.1

commit v3 on v2

--- a/solution.py
+++ b/solution.py
@@ -44,7 +44,11 @@
     ) * inverse
 
 
-def forward_kernel(q_ref, k_ref, v_ref, qg_ref, kg_ref, mixed_ref, att_ref):
+def forward_kernel(q_ref, k_ref, v_ref, qg_ref, kg_ref, go_ref, mixed_ref, att_ref, cut_ref):
+    for zone in range(NZ):
+        for line in range(NY):
+            source = (zone * NY + line) * BLK
+            cut_ref[line, :, zone * BLK : (zone + 1) * BLK] = go_ref[:, source : source + BLK]
     for image in range(IMAGES):
         rows = pl.ds(image * PATCH, PATCH)
         query_low = (normalize(q_ref[rows, :])[0] * qg_ref[...]).astype(BF16)
@@ -80,40 +84,28 @@
         dk_ref[rows, :] = norm_back(grad_kn, key_unit, key_inv, kg_ref[...]).astype(BF16)
 
 
-def assemble(g_refs, held_ref):
-    low = lax.axis_index("zl")
-    for step in range(NL):
-        held_ref[low ^ step] = g_refs[step][...]
-
-
 def block(ref, zone):
     columns = pl.ds(zone * BLK, BLK)
     parts = [ref[:, line, :, columns].reshape(-1, BLK) for line in range(NY)]
     return jnp.concatenate(parts, axis=0)
 
 
-def heads_kernel(*refs):
-    g_refs, own_refs, other_refs = refs[:NL], refs[NL : NL + NX], refs[NL + NX : NL + 2 * NX]
-    out_ref, held_ref = refs[-2:]
-    assemble(g_refs, held_ref)
+def heads_kernel(g_ref, own_ref, other_ref, out_ref):
+    here, core = lax.axis_index("zh"), lax.axis_index("core")
+    blocks = [block(g_ref, lax.rem(here + NZ - step, NZ)) for step in range(NZ)]
+    for ref, side in ((own_ref, core), (other_ref, 1 - core)):
+        total = None
+        for step in range(NZ):
+            term = dot(blocks[step], ref[:, step].reshape(NX * DH, BLK), 1, 1)
+            total = term if total is None else total + term
+        for across in range(NX):
+            piece = total[:, across * DH : (across + 1) * DH]
+            out_ref[NC * across + side] = piece.astype(BF16)
+
+
+def weight_kernel(g_ref, mixed_ref, keep_ref, send_ref):
     here, core, across = (lax.axis_index(name) for name in ("zh", "core", "x"))
-    blocks = [block(held_ref, lax.rem(here + NZ - zone, NZ)) for zone in range(NZ)]
-    for step in range(NX):
-        for part_refs, side in ((own_refs, core), (other_refs, 1 - core)):
-            total = None
-            for zone in range(NZ):
-                term = dot(blocks[zone], part_refs[step][zone], 1, 1)
-                total = term if total is None else total + term
-            head = NC * lax.rem(across + NX - step, NX) + side
-            out_ref[head] = total.astype(BF16)
-
-
-def weight_kernel(*refs):
-    g_refs, mixed_ref = refs[:NL], refs[NL]
-    keep_ref, send_ref, held_ref = refs[-3:]
-    assemble(g_refs, held_ref)
-    here, core, across = (lax.axis_index(name) for name in ("zh", "core", "x"))
-    blocks = [block(held_ref, lax.rem(here + step, NZ)) for step in range(NZ)]
+    blocks = [block(g_ref, lax.rem(here + step, NZ)) for step in range(NZ)]
     for ref, side in ((send_ref, 1 - core), (keep_ref, core)):
         parts = [mixed_ref[lax.rem(across + step, NX), side] for step in range(NX)]
         mixed = jnp.concatenate(parts, axis=0)
@@ -122,13 +114,12 @@
             ref[:, step] = term.reshape(NX, DH, BLK).astype(ref.dtype)
 
 
-def call(kernel, outs, flops, moved, operands, scratch=()):
+def call(kernel, outs, flops, moved, operands):
     return pl.pallas_call(
         kernel,
         out_shape=outs,
         in_specs=[pl.BlockSpec(memory_space=pltpu.VMEM)] * len(operands),
         out_specs=jax.tree.map(lambda _: pl.BlockSpec(memory_space=pltpu.VMEM), outs),
-        scratch_shapes=list(scratch),
         compiler_params=pltpu.CompilerParams(vmem_limit_bytes=VMEM_LIMIT),
         cost_estimate=pl.CostEstimate(flops=flops, bytes_accessed=moved, transcendentals=0),
     )(*operands)
@@ -150,10 +141,6 @@
     return lax.ppermute(entry, axis, [(at, (at + step) % size) for at in range(size)])
 
 
-def flipped(entry, axis, size, step):
-    return lax.ppermute(entry, axis, [(at, at ^ step) for at in range(size)])
-
-
 def swap_cores(entry):
     return lax.ppermute(entry, "core", [(0, 1), (1, 0)])
 
@@ -163,37 +150,35 @@
     key_gain = key_gain.reshape(1, DH)
     shape = jax.ShapeDtypeStruct
 
-    mixed, attention = call(
+    rows = grad_output.shape[0]
+    mixed, attention, pieces = call(
         forward_kernel,
-        (shape((DH, TOK), BF16), shape((IMAGES, PATCH, PATCH), F32)),
+        (
+            shape((DH, TOK), BF16),
+            shape((IMAGES, PATCH, PATCH), F32),
+            shape((NY, rows, WIDE), BF16),
+        ),
         2 * 2 * IMAGES * PATCH * PATCH * DH,
         1 << 20,
-        (query_input, key_input, value_input, query_gain, key_gain),
-    )
-    rows = grad_output.shape[0]
-    pieces = grad_output.reshape(rows, NZ, NY, BLK).transpose(2, 0, 1, 3)
-    pieces = pieces.reshape(NY, rows, WIDE)
-    pieces, mixed = lax.optimization_barrier((pieces, mixed))
+        (query_input, key_input, value_input, query_gain, key_gain, grad_output),
+    )
     mixed_all = lax.all_gather(mixed, "y", axis=0, tiled=True)
     exchanged = lax.all_to_all(pieces, "y", 0, 0, tiled=True)
-    crossed = cross(out_weight, 0)
+    crossed = jnp.stack([cross(out_weight, shift) for shift in range(NZ)])
     exchanged, crossed = lax.optimization_barrier((exchanged, crossed))
-    zones = [crossed] + [shifted(crossed, "zh", NZ, step) for step in range(1, NZ)]
-    gathered = [exchanged] + [flipped(exchanged, "zl", NL, step) for step in range(1, NL)]
-    zones = jnp.stack(zones)
-    own = [zones] + [shifted(zones, "x", NX, step) for step in range(1, NX)]
+    copies = jnp.broadcast_to(crossed[None], (NX,) + crossed.shape)
+    own = lax.all_to_all(copies, "x", 0, 0, tiled=True)
+    gathered = lax.all_gather(exchanged, "zl", axis=0)
     gathered, mixed_all, own = lax.optimization_barrier((gathered, mixed_all, own))
-    other = [swap_cores(entry) for entry in own]
+    other = swap_cores(own)
 
     half = (NX, NZ, DH, BLK)
-    held = (pltpu.VMEM((NL, NY, rows, WIDE), BF16),)
     keep, send = call(
         weight_kernel,
         (shape(half, F32), shape(half, BF16)),
         2 * TOK * NY * DH * WIDE,
         5 << 20,
-        (*gathered, mixed_all.reshape(NX, NC, DH, TOK)),
-        held,
+        (gathered, mixed_all.reshape(NX, NC, DH, TOK)),
     )
     received = swap_cores(send)
     partial = call(
@@ -201,12 +186,11 @@
         shape((NY, TOK, DH), BF16),
         2 * TOK * NY * DH * WIDE,
         4 << 20,
-        (*gathered, *own, *other),
-        held,
-    )
+        (gathered, own, other),
+    )
+    summed = [(keep[step] + received[step].astype(F32)).astype(BF16) for step in range(NX)]
+    partial, *summed = lax.optimization_barrier((partial, *summed))
     grad_heads = lax.all_to_all(partial, "y", 0, 0, tiled=True)
-
-    summed = [(keep[step] + received[step].astype(F32)).astype(BF16) for step in range(NX)]
     spread = [summed[0]] + [shifted(summed[step], "x", NX, step) for step in range(1, NX)]
     by_zone = sum(entry.astype(F32) for entry in spread).astype(BF16)
     last = [cross(by_zone[shift], shift) for shift in range(NZ)]

time: 167 us -> 158 us (0.946)
  the two profiles are of different devices: /device:TPU:96 before, /device:TPU:22 now
where the time goes in v3:
time: 158 us; the launch traced here: 157 us
  starting transfers between devices  84.1 us (53%)
  waiting for transfers between devices  23.1 us (15%)
  blocking collectives  20.7 us (13%)
  between operations  14.3 us (9%)
  local copies, waits for them, and re-layouts  7.18 us (5%)
  Pallas kernels  6.63 us (4%)
    ppermute x6, starting transfers between devices, cross(): return lax.ppermute(entry, ('zh', 'x', 'core', 'y'), pairs)  50.7 us
    all_gather x1, blocking collectives, shards(): gathered = lax.all_gather(exchanged, 'zl', axis=0)  20.7 us
    ppermute x6, waiting for transfers between devices, cross(): return lax.ppermute(entry, ('zh', 'x', 'core', 'y'), pairs)  15.7 us
    ppermute x3, starting transfers between devices, shifted(): lax.ppermute(entry, axis, [(at, (at + step) % size) for at in range(size)])  8.65 us
    all_to_all x1, starting transfers between devices, shards(): grad_heads = lax.all_to_all(partial, 'y', 0, 0, tiled=True)  8.49 us
    all_to_all x1, starting transfers between devices, shards(): exchanged = lax.all_to_all(pieces, 'y', 0, 0, tiled=True)  7.44 us
    ppermute x3, waiting for transfers between devices, shifted(): lax.ppermute(entry, axis, [(at, (at + step) % size) for at in range(size)])  7.35 us
    pallas_call x4, Pallas kernels, call(): pl.pallas_call(kernel, out_shape=outs, in_specs=[pl.BlockSpec(memory_spac...  6.63 us
  transfers between devices with their start and end apart: 15, of which 6 were waited for; matrix products, arithmetic and copies ran while one was open for 1% of the time, Pallas kernels for 2%

profile of v3, /device:TPU:22, one launch (start us, length us, event | category | flops | bytes accessed | tf_op | source)
XLA Modules:
  0.0 157.0 jit_solution(2980863099190091881)
XLA Ops:
  7.2 0.0 all-gather.3.cloned.1.call-start
  7.2 0.0 copy-start
  7.2 0.9 copy-done
  8.1 0.9 copy-done.2
  9.0 0.9 copy-done.4
  9.9 0.9 copy-done.6
  10.9 0.7 copy-done.7
  11.5 0.7 copy-done.9
  12.2 1.5 shard_map.102
  13.7 0.0 all-gather.3.cloned.1.call-update
  13.7 7.4 %all-to-all-start = ((bf16[8,16,768]{2,1,0:T(8,128)(2,1)}), bf16[8,16,768]{2,1,0:T(8,128)(2,1)S(1)}, u32[]{:S(2)}, u32[]{:S(2)}) async-start(bf16[8,16,768]{2,1,0:T(8,128)(2,1)} %get-tuple-element.23), calls=%async_computation | async-start | bytes 393216 | tf_op jit(solution)/shard_map/all_to_all | solution.py:166
  21.1 6.3 %collective-permute-start = (bf16[128,256]{1,0:T(8,128)(2,1)}, bf16[128,256]{1,0:T(8,128)(2,1)S(1)}, u32[]{:S(2)}, u32[]{:S(2)}) collective-permute-start(bf16[128,256]{1,0:T(8,128)(2,1)} %param.12), channel_id=1, source_target_pairs={{0,0},{4,32},{8,64},{12,96},{16,128},{20,160},{24,192},{28,224},{3... | collective-permute-start | bytes 196616 | tf_op jit(solution)/shard_map/ppermute | solution.py:137
  27.4 14.3 %collective-permute-start.1 = (bf16[128,256]{1,0:T(8,128)(2,1)}, bf16[128,256]{1,0:T(8,128)(2,1)S(1)}, u32[]{:S(2)}, u32[]{:S(2)}) collective-permute-start(bf16[128,256]{1,0:T(8,128)(2,1)} %param.12), channel_id=1, source_target_pairs={{0,256},{4,288},{8,320},{12,352},{16,384},{20,416},{24,448},{28,48... | collective-permute-start | bytes 196616 | tf_op jit(solution)/shard_map/ppermute | solution.py:137
  41.7 5.6 %collective-permute-start.2 = (bf16[128,256]{1,0:T(8,128)(2,1)}, bf16[128,256]{1,0:T(8,128)(2,1)S(1)}, u32[]{:S(2)}, u32[]{:S(2)}) collective-permute-start(bf16[128,256]{1,0:T(8,128)(2,1)} %param.12), channel_id=1, source_target_pairs={{0,512},{4,544},{8,576},{12,608},{16,640},{20,672},{24,704},{28,73... | collective-permute-start | bytes 196616 | tf_op jit(solution)/shard_map/ppermute | solution.py:137
  47.3 0.0 collective-permute-done
  47.3 1.6 %collective-permute-done.1 = bf16[128,256]{1,0:T(8,128)(2,1)S(1)} collective-permute-done((bf16[128,256]{1,0:T(8,128)(2,1)}, bf16[128,256]{1,0:T(8,128)(2,1)S(1)}, u32[]{:S(2)}, u32[]{:S(2)}) %collective-permute-start.1) | collective-permute-done | bytes 65568 | tf_op jit(solution)/shard_map/ppermute | solution.py:137
  48.9 11.0 %collective-permute-done.2 = bf16[128,256]{1,0:T(8,128)(2,1)S(1)} collective-permute-done((bf16[128,256]{1,0:T(8,128)(2,1)}, bf16[128,256]{1,0:T(8,128)(2,1)S(1)}, u32[]{:S(2)}, u32[]{:S(2)}) %collective-permute-start.2) | collective-permute-done | bytes 65568 | tf_op jit(solution)/shard_map/ppermute | solution.py:137
  60.0 0.0 all-to-all-done
  60.0 1.0 broadcast_in_dim.2
  61.0 4.5 %all-to-all-start.1 = ((bf16[4,3,128,256]{3,2,1,0:T(8,128)(2,1)}), bf16[4,3,128,256]{3,2,1,0:T(8,128)(2,1)S(1)}, u32[]{:S(2)}, u32[]{:S(2)}) async-start(bf16[4,3,128,256]{3,2,1,0:T(8,128)(2,1)} %broadcast_in_dim.2), calls=%async_computation.1 | async-start | bytes 1572864 | tf_op jit(solution)/shard_map/all_to_all | solution.py:170
  65.5 20.7 %all-gather = bf16[32,16,768]{2,1,0:T(8,128)(2,1)S(1)} all-gather(bf16[8,16,768]{2,1,0:T(8,128)(2,1)S(1)} %all-to-all-done), channel_id=2, replica_groups=mesh['zh'=3,'x'=4,'core'=2,'y'=8,'zl'=4] {'zl'}, dimensions={0}, use_global_device_ids=true | all-gather | bytes 983040 | tf_op jit(solution)/shard_map/all_gather | solution.py:171
  86.2 1.9 %collective-permute-start.3 = (bf16[4,3,128,256]{3,2,1,0:T(8,128)(2,1)S(1)}, bf16[4,3,128,256]{3,2,1,0:T(8,128)(2,1)S(1)}, u32[]{:S(2)}, u32[]{:S(2)}) collective-permute-start(bf16[4,3,128,256]{3,2,1,0:T(8,128)(2,1)S(1)} %all-to-all-done.1.own_ref), channel_id=1, source_target_pairs={{0,32},{32,0},{1,33},{33,1},{2,34},{34,2},{3,35},{35,3},{4,36},{36... | collective-permute-start | bytes 2359304 | tf_op jit(solution)/shard_map/ppermute | solution.py:145
  88.1 1.2 copy-done.11
  89.3 1.0 shard_map.104
  90.3 2.4 %collective-permute-start.4 = (bf16[4,3,128,256]{3,2,1,0:T(8,128)(2,1)S(1)}, bf16[4,3,128,256]{3,2,1,0:T(8,128)(2,1)S(1)}, u32[]{:S(2)}, u32[]{:S(2)}) collective-permute-start(bf16[4,3,128,256]{3,2,1,0:T(8,128)(2,1)S(1)} %get-tuple-element.31), channel_id=1, source_target_pairs={{0,32},{32,0},{1,33},{33,1},{2,34},{34,2},{3,35},{35,3},{4,36},{36... | collective-permute-start | bytes 2359304 | tf_op jit(solution)/shard_map/ppermute | solution.py:145
  92.8 0.0 collective-permute-done.3.other_ref
  92.8 2.0 %shard_map.103 = bf16[8,512,128]{2,1,0:T(8,128)(2,1)} custom-call(bf16[4,8,16,768]{3,2,1,0:T(8,128)(2,1)S(1)} %bitcast.22, bf16[4,3,128,256]{3,2,1,0:T(8,128)(2,1)S(1)} %all-to-all-done.1.own_ref, bf16[4,3,128,256]{3,2,1,0:T(8,128)(2,1)S(1)} %collective-permute-done.3.other_ref), custom_call_target="tpu_custom_call" | custom-call | flops 805306368 | bytes 4194304 | tf_op jit(solution)/shard_map/pallas_call | solution.py:118
  94.8 0.0 collective-permute-done.4
  94.8 0.2 fusion.3
  95.0 0.0 copy-start.1
  95.0 0.0 copy-start.3
  95.0 0.0 copy-start.5
  95.0 0.0 copy-start.8
  95.0 0.0 copy-start.10
  95.0 8.5 %all-to-all-start.2 = ((bf16[8,512,128]{2,1,0:T(8,128)(2,1)}), bf16[8,512,128]{2,1,0:T(8,128)(2,1)S(1)}, u32[]{:S(2)}, u32[]{:S(2)}) async-start(bf16[8,512,128]{2,1,0:T(8,128)(2,1)} %shard_map.103), calls=%async_computation.2 | async-start | bytes 2097152 | tf_op jit(solution)/shard_map/all_to_all | solution.py:193
  103.5 1.9 %collective-permute-start.5 = (bf16[3,128,256]{2,1,0:T(8,128)(2,1)S(1)}, bf16[3,128,256]{2,1,0:T(8,128)(2,1)S(1)}, u32[]{:S(2)}, u32[]{:S(2)}) collective-permute-start(bf16[3,128,256]{2,1,0:T(8,128)(2,1)S(1)} %get-tuple-element.37), channel_id=1, source_target_pairs={{0,64},{64,128},{128,192},{192,0},{1,65},{65,129},{129,193},{193,1... | collective-permute-start | bytes 589832 | tf_op jit(solution)/shard_map/ppermute | solution.py:141
  105.4 4.8 %collective-permute-start.6 = (bf16[3,128,256]{2,1,0:T(8,128)(2,1)S(1)}, bf16[3,128,256]{2,1,0:T(8,128)(2,1)S(1)}, u32[]{:S(2)}, u32[]{:S(2)}) collective-permute-start(bf16[3,128,256]{2,1,0:T(8,128)(2,1)S(1)} %get-tuple-element.38), channel_id=1, source_target_pairs={{0,128},{64,192},{128,0},{192,64},{1,129},{65,193},{129,1},{193,65... | collective-permute-start | bytes 589832 | tf_op jit(solution)/shard_map/ppermute | solution.py:141
  110.3 1.9 %collective-permute-start.7 = (bf16[3,128,256]{2,1,0:T(8,128)(2,1)S(1)}, bf16[3,128,256]{2,1,0:T(8,128)(2,1)S(1)}, u32[]{:S(2)}, u32[]{:S(2)}) collective-permute-start(bf16[3,128,256]{2,1,0:T(8,128)(2,1)S(1)} %get-tuple-element.39), channel_id=1, source_target_pairs={{0,192},{64,0},{128,64},{192,128},{1,193},{65,1},{129,65},{193,129... | collective-permute-start | bytes 589832 | tf_op jit(solution)/shard_map/ppermute | solution.py:141
  112.2 1.0 collective-permute-done.5
  113.2 2.4 %collective-permute-done.6 = bf16[3,128,256]{2,1,0:T(8,128)(2,1)S(1)} collective-permute-done((bf16[3,128,256]{2,1,0:T(8,128)(2,1)S(1)}, bf16[3,128,256]{2,1,0:T(8,128)(2,1)S(1)}, u32[]{:S(2)}, u32[]{:S(2)}) %collective-permute-start.6) | collective-permute-done | bytes 196640 | tf_op jit(solution)/shard_map/ppermute | solution.py:141
  115.6 3.9 %collective-permute-done.7 = bf16[3,128,256]{2,1,0:T(8,128)(2,1)S(1)} collective-permute-done((bf16[3,128,256]{2,1,0:T(8,128)(2,1)S(1)}, bf16[3,128,256]{2,1,0:T(8,128)(2,1)S(1)}, u32[]{:S(2)}, u32[]{:S(2)}) %collective-permute-start.7) | collective-permute-done | bytes 196640 | tf_op jit(solution)/shard_map/ppermute | solution.py:141
  119.5 0.1 add_convert_fusion
  119.7 4.7 %collective-permute-start.10 = (bf16[128,256]{1,0:T(8,128)(2,1)S(1)}, bf16[128,256]{1,0:T(8,128)(2,1)S(1)}, u32[]{:S(2)}, u32[]{:S(2)}) collective-permute-start(bf16[128,256]{1,0:T(8,128)(2,1)S(1)} %get-tuple-element.45), channel_id=1, source_target_pairs={{0,512},{4,544},{8,576},{12,608},{16,640},{20,672},{24,704},{28,73... | collective-permute-start | bytes 196616 | tf_op jit(solution)/shard_map/ppermute | solution.py:137
  124.4 4.8 %collective-permute-start.8 = (bf16[128,256]{1,0:T(8,128)(2,1)S(1)}, bf16[128,256]{1,0:T(8,128)(2,1)S(1)}, u32[]{:S(2)}, u32[]{:S(2)}) collective-permute-start(bf16[128,256]{1,0:T(8,128)(2,1)S(1)} %get-tuple-element.44), channel_id=1, source_target_pairs={{0,0},{4,32},{8,64},{12,96},{16,128},{20,160},{24,192},{28,224},{3... | collective-permute-start | bytes 196616 | tf_op jit(solution)/shard_map/ppermute | solution.py:137
  129.2 15.0 %collective-permute-start.9 = (bf16[128,256]{1,0:T(8,128)(2,1)S(1)}, bf16[128,256]{1,0:T(8,128)(2,1)S(1)}, u32[]{:S(2)}, u32[]{:S(2)}) collective-permute-start(bf16[128,256]{1,0:T(8,128)(2,1)S(1)} %get-tuple-element.46), channel_id=1, source_target_pairs={{0,256},{4,288},{8,320},{12,352},{16,384},{20,416},{24,448},{28,48... | collective-permute-start | bytes 196616 | tf_op jit(solution)/shard_map/ppermute | solution.py:137
  144.2 3.1 %collective-permute-done.9 = bf16[128,256]{1,0:T(8,128)(2,1)S(1)} collective-permute-done((bf16[128,256]{1,0:T(8,128)(2,1)S(1)}, bf16[128,256]{1,0:T(8,128)(2,1)S(1)}, u32[]{:S(2)}, u32[]{:S(2)}) %collective-permute-start.9) | collective-permute-done | bytes 65568 | tf_op jit(solution)/shard_map/ppermute | solution.py:137
  147.3 0.7 add_convert_fusion.5
  148.0 2.2 %shard_map.105 = (bf16[512,128]{1,0:T(8,128)(2,1)}, bf16[512,128]{1,0:T(8,128)(2,1)}, bf16[512,128]{1,0:T(8,128)(2,1)}) custom-call(bf16[512,128]{1,0:T(8,128)(2,1)S(1)} %copy-done.1, bf16[512,128]{1,0:T(8,128)(2,1)S(1)} %copy-done.3, bf16[512,128]{1,0:T(8,128)(2,1)S(1)} %copy-done.5, f32[1,128]{1,0:T(1,128)S(1)} %bitcast.24, f32[1,128]{1,0:T(1,128)S(1)} %bitcast.26, ...), custom_call_target="tpu_custom_call" | custom-call | flops 167772160 | bytes 2097152 | tf_op jit(solution)/shard_map/pallas_call | solution.py:118
  (18 shorter events, 0.1 us)
Async XLA Ops:
  7.2 79.0 %all-gather.3.cloned.1.call-start = ((), (), s32[]{:S(2)}) async-start(), calls=%async_computation.3 | async-start | bytes 1179648 | tf_op jit(solution)/shard_map/all_gather | solution.py:165
  7.2 0.9 copy-start
  8.1 0.9 copy-start.2
  9.0 0.9 copy-start.4
  9.9 0.9 copy-start.6
  10.9 0.7 copy-start.7
  11.5 0.7 copy-start.9
  13.7 46.3 %all-to-all-start = ((bf16[8,16,768]{2,1,0:T(8,128)(2,1)}), bf16[8,16,768]{2,1,0:T(8,128)(2,1)S(1)}, u32[]{:S(2)}, u32[]{:S(2)}) async-start(bf16[8,16,768]{2,1,0:T(8,128)(2,1)} %get-tuple-element.23), calls=%async_computation | async-start | bytes 393216 | tf_op jit(solution)/shard_map/all_to_all | solution.py:166
  21.1 26.2 %collective-permute-start = (bf16[128,256]{1,0:T(8,128)(2,1)}, bf16[128,256]{1,0:T(8,128)(2,1)S(1)}, u32[]{:S(2)}, u32[]{:S(2)}) collective-permute-start(bf16[128,256]{1,0:T(8,128)(2,1)} %param.12), channel_id=1, source_target_pairs={{0,0},{4,32},{8,64},{12,96},{16,128},{20,160},{24,192},{28,224},{3... | collective-permute-start | bytes 196616 | tf_op jit(solution)/shard_map/ppermute | solution.py:137
  27.4 21.5 %collective-permute-start.1 = (bf16[128,256]{1,0:T(8,128)(2,1)}, bf16[128,256]{1,0:T(8,128)(2,1)S(1)}, u32[]{:S(2)}, u32[]{:S(2)}) collective-permute-start(bf16[128,256]{1,0:T(8,128)(2,1)} %param.12), channel_id=1, source_target_pairs={{0,256},{4,288},{8,320},{12,352},{16,384},{20,416},{24,448},{28,48... | collective-permute-start | bytes 196616 | tf_op jit(solution)/shard_map/ppermute | solution.py:137
  41.7 18.2 %collective-permute-start.2 = (bf16[128,256]{1,0:T(8,128)(2,1)}, bf16[128,256]{1,0:T(8,128)(2,1)S(1)}, u32[]{:S(2)}, u32[]{:S(2)}) collective-permute-start(bf16[128,256]{1,0:T(8,128)(2,1)} %param.12), channel_id=1, source_target_pairs={{0,512},{4,544},{8,576},{12,608},{16,640},{20,672},{24,704},{28,73... | collective-permute-start | bytes 196616 | tf_op jit(solution)/shard_map/ppermute | solution.py:137
  61.0 25.2 %all-to-all-start.1 = ((bf16[4,3,128,256]{3,2,1,0:T(8,128)(2,1)}), bf16[4,3,128,256]{3,2,1,0:T(8,128)(2,1)S(1)}, u32[]{:S(2)}, u32[]{:S(2)}) async-start(bf16[4,3,128,256]{3,2,1,0:T(8,128)(2,1)} %broadcast_in_dim.2), calls=%async_computation.1 | async-start | bytes 1572864 | tf_op jit(solution)/shard_map/all_to_all | solution.py:170
  86.2 6.6 %collective-permute-start.3 = (bf16[4,3,128,256]{3,2,1,0:T(8,128)(2,1)S(1)}, bf16[4,3,128,256]{3,2,1,0:T(8,128)(2,1)S(1)}, u32[]{:S(2)}, u32[]{:S(2)}) collective-permute-start(bf16[4,3,128,256]{3,2,1,0:T(8,128)(2,1)S(1)} %all-to-all-done.1.own_ref), channel_id=1, source_target_pairs={{0,32},{32,0},{1,33},{33,1},{2,34},{34,2},{3,35},{35,3},{4,36},{36... | collective-permute-start | bytes 2359304 | tf_op jit(solution)/shard_map/ppermute | solution.py:145
  88.1 1.2 copy-start.11
  90.3 4.4 %collective-permute-start.4 = (bf16[4,3,128,256]{3,2,1,0:T(8,128)(2,1)S(1)}, bf16[4,3,128,256]{3,2,1,0:T(8,128)(2,1)S(1)}, u32[]{:S(2)}, u32[]{:S(2)}) collective-permute-start(bf16[4,3,128,256]{3,2,1,0:T(8,128)(2,1)S(1)} %get-tuple-element.31), channel_id=1, source_target_pairs={{0,32},{32,0},{1,33},{33,1},{2,34},{34,2},{3,35},{35,3},{4,36},{36... | collective-permute-start | bytes 2359304 | tf_op jit(solution)/shard_map/ppermute | solution.py:145
  95.0 53.0 %copy-start.1 = (bf16[512,128]{1,0:T(8,128)(2,1)S(1)}, bf16[512,128]{1,0:T(8,128)(2,1)}, u32[]{:S(2)}) copy-start(bf16[512,128]{1,0:T(8,128)(2,1)} %q_ref.3) | copy-start | bytes 393220
  95.0 53.0 %copy-start.3 = (bf16[512,128]{1,0:T(8,128)(2,1)S(1)}, bf16[512,128]{1,0:T(8,128)(2,1)}, u32[]{:S(2)}) copy-start(bf16[512,128]{1,0:T(8,128)(2,1)} %k_ref.3) | copy-start | bytes 393220
  95.0 53.0 %copy-start.5 = (bf16[512,128]{1,0:T(8,128)(2,1)S(1)}, bf16[512,128]{1,0:T(8,128)(2,1)}, u32[]{:S(2)}) copy-start(bf16[512,128]{1,0:T(8,128)(2,1)} %v_ref.3) | copy-start | bytes 393220
  95.0 53.0 %copy-start.8 = (f32[128]{0:T(128)S(1)}, f32[128]{0:T(128)}, u32[]{:S(2)}) copy-start(f32[128]{0:T(128)} %param.10) | copy-start | bytes 1540
  95.0 53.0 %copy-start.10 = (f32[128]{0:T(128)S(1)}, f32[128]{0:T(128)}, u32[]{:S(2)}) copy-start(f32[128]{0:T(128)} %param.11) | copy-start | bytes 1540
  95.0 52.9 %all-to-all-start.2 = ((bf16[8,512,128]{2,1,0:T(8,128)(2,1)}), bf16[8,512,128]{2,1,0:T(8,128)(2,1)S(1)}, u32[]{:S(2)}, u32[]{:S(2)}) async-start(bf16[8,512,128]{2,1,0:T(8,128)(2,1)} %shard_map.103), calls=%async_computation.2 | async-start | bytes 2097152 | tf_op jit(solution)/shard_map/all_to_all | solution.py:193
  103.5 9.7 %collective-permute-start.5 = (bf16[3,128,256]{2,1,0:T(8,128)(2,1)S(1)}, bf16[3,128,256]{2,1,0:T(8,128)(2,1)S(1)}, u32[]{:S(2)}, u32[]{:S(2)}) collective-permute-start(bf16[3,128,256]{2,1,0:T(8,128)(2,1)S(1)} %get-tuple-element.37), channel_id=1, source_target_pairs={{0,64},{64,128},{128,192},{192,0},{1,65},{65,129},{129,193},{193,1... | collective-permute-start | bytes 589832 | tf_op jit(solution)/shard_map/ppermute | solution.py:141
  105.4 10.2 %collective-permute-start.6 = (bf16[3,128,256]{2,1,0:T(8,128)(2,1)S(1)}, bf16[3,128,256]{2,1,0:T(8,128)(2,1)S(1)}, u32[]{:S(2)}, u32[]{:S(2)}) collective-permute-start(bf16[3,128,256]{2,1,0:T(8,128)(2,1)S(1)} %get-tuple-element.38), channel_id=1, source_target_pairs={{0,128},{64,192},{128,0},{192,64},{1,129},{65,193},{129,1},{193,65... | collective-permute-start | bytes 589832 | tf_op jit(solution)/shard_map/ppermute | solution.py:141
  110.3 9.3 %collective-permute-start.7 = (bf16[3,128,256]{2,1,0:T(8,128)(2,1)S(1)}, bf16[3,128,256]{2,1,0:T(8,128)(2,1)S(1)}, u32[]{:S(2)}, u32[]{:S(2)}) collective-permute-start(bf16[3,128,256]{2,1,0:T(8,128)(2,1)S(1)} %get-tuple-element.39), channel_id=1, source_target_pairs={{0,192},{64,0},{128,64},{192,128},{1,193},{65,1},{129,65},{193,129... | collective-permute-start | bytes 589832 | tf_op jit(solution)/shard_map/ppermute | solution.py:141
  119.7 24.5 %collective-permute-start.10 = (bf16[128,256]{1,0:T(8,128)(2,1)S(1)}, bf16[128,256]{1,0:T(8,128)(2,1)S(1)}, u32[]{:S(2)}, u32[]{:S(2)}) collective-permute-start(bf16[128,256]{1,0:T(8,128)(2,1)S(1)} %get-tuple-element.45), channel_id=1, source_target_pairs={{0,512},{4,544},{8,576},{12,608},{16,640},{20,672},{24,704},{28,73... | collective-permute-start | bytes 196616 | tf_op jit(solution)/shard_map/ppermute | solution.py:137
  124.4 19.9 %collective-permute-start.8 = (bf16[128,256]{1,0:T(8,128)(2,1)S(1)}, bf16[128,256]{1,0:T(8,128)(2,1)S(1)}, u32[]{:S(2)}, u32[]{:S(2)}) collective-permute-start(bf16[128,256]{1,0:T(8,128)(2,1)S(1)} %get-tuple-element.44), channel_id=1, source_target_pairs={{0,0},{4,32},{8,64},{12,96},{16,128},{20,160},{24,192},{28,224},{3... | collective-permute-start | bytes 196616 | tf_op jit(solution)/shard_map/ppermute | solution.py:137
  129.2 18.1 %collective-permute-start.9 = (bf16[128,256]{1,0:T(8,128)(2,1)S(1)}, bf16[128,256]{1,0:T(8,128)(2,1)S(1)}, u32[]{:S(2)}, u32[]{:S(2)}) collective-permute-start(bf16[128,256]{1,0:T(8,128)(2,1)S(1)} %get-tuple-element.46), channel_id=1, source_target_pairs={{0,256},{4,288},{8,320},{12,352},{16,384},{20,416},{24,448},{28,48... | collective-permute-start | bytes 196616 | tf_op jit(solution)/shard_map/ppermute | solution.py:137
Sparse Core Ops, SparseCore 0:
  13.8 50.9 all-gather.2

commit v4 on v3

--- a/solution.py
+++ b/solution.py
@@ -44,11 +44,16 @@
     ) * inverse
 
 
-def forward_kernel(q_ref, k_ref, v_ref, qg_ref, kg_ref, go_ref, mixed_ref, att_ref, cut_ref):
+def cut_kernel(go_ref, cut_ref):
     for zone in range(NZ):
-        for line in range(NY):
-            source = (zone * NY + line) * BLK
-            cut_ref[line, :, zone * BLK : (zone + 1) * BLK] = go_ref[:, source : source + BLK]
+        for low in range(NL):
+            for core in range(NC):
+                source = ((zone * NL + low) * NC + core) * BLK
+                piece = go_ref[:, source : source + BLK]
+                cut_ref[core * NL + low, :, zone * BLK : (zone + 1) * BLK] = piece
+
+
+def forward_kernel(q_ref, k_ref, v_ref, qg_ref, kg_ref, mixed_ref, att_ref):
     for image in range(IMAGES):
         rows = pl.ds(image * PATCH, PATCH)
         query_low = (normalize(q_ref[rows, :])[0] * qg_ref[...]).astype(BF16)
@@ -66,7 +71,7 @@
     for image in range(IMAGES):
         rows = pl.ds(image * PATCH, PATCH)
         total = gh_ref[0, rows, :].astype(F32)
-        for part in range(1, NY):
+        for part in range(1, NL):
             total = total + gh_ref[part, rows, :].astype(F32)
         grad_heads = total.astype(BF16)
         query_unit, query_inv = normalize(q_ref[rows, :])
@@ -84,34 +89,32 @@
         dk_ref[rows, :] = norm_back(grad_kn, key_unit, key_inv, kg_ref[...]).astype(BF16)
 
 
-def block(ref, zone):
+def block(ref, side, zone):
     columns = pl.ds(zone * BLK, BLK)
-    parts = [ref[:, line, :, columns].reshape(-1, BLK) for line in range(NY)]
-    return jnp.concatenate(parts, axis=0)
-
-
-def heads_kernel(g_ref, own_ref, other_ref, out_ref):
+    return ref[:, pl.ds(side * NL, NL), :, columns].reshape(TOK, BLK)
+
+
+def heads_kernel(g_ref, own_ref, keep_ref, send_ref):
     here, core = lax.axis_index("zh"), lax.axis_index("core")
-    blocks = [block(g_ref, lax.rem(here + NZ - step, NZ)) for step in range(NZ)]
-    for ref, side in ((own_ref, core), (other_ref, 1 - core)):
+    for ref, side in ((send_ref, 1 - core), (keep_ref, core)):
         total = None
         for step in range(NZ):
-            term = dot(blocks[step], ref[:, step].reshape(NX * DH, BLK), 1, 1)
+            rows = block(g_ref, side, lax.rem(here + NZ - step, NZ))
+            term = dot(rows, own_ref[:, step].reshape(NL * DH, BLK), 1, 1)
             total = term if total is None else total + term
-        for across in range(NX):
-            piece = total[:, across * DH : (across + 1) * DH]
-            out_ref[NC * across + side] = piece.astype(BF16)
-
-
-def weight_kernel(g_ref, mixed_ref, keep_ref, send_ref):
-    here, core, across = (lax.axis_index(name) for name in ("zh", "core", "x"))
-    blocks = [block(g_ref, lax.rem(here + step, NZ)) for step in range(NZ)]
-    for ref, side in ((send_ref, 1 - core), (keep_ref, core)):
-        parts = [mixed_ref[lax.rem(across + step, NX), side] for step in range(NX)]
-        mixed = jnp.concatenate(parts, axis=0)
-        for step in range(NZ):
-            term = dot(mixed, blocks[step], 1, 0)
-            ref[:, step] = term.reshape(NX, DH, BLK).astype(ref.dtype)
+        for head in range(NL):
+            ref[head] = total[:, head * DH : (head + 1) * DH].astype(ref.dtype)
+
+
+def weight_kernel(g_ref, own_ref, other_ref, out_ref):
+    here, core = lax.axis_index("zh"), lax.axis_index("core")
+    own = own_ref[...].reshape(NL * DH, TOK)
+    other = other_ref[...].reshape(NL * DH, TOK)
+    for step in range(NZ):
+        zone = lax.rem(here + step, NZ)
+        total = dot(own, block(g_ref, core, zone), 1, 0)
+        total = total + dot(other, block(g_ref, 1 - core, zone), 1, 0)
+        out_ref[:, step] = total.reshape(NL, DH, BLK).astype(BF16)
 
 
 def call(kernel, outs, flops, moved, operands):
@@ -128,17 +131,18 @@
 def cross(entry, shift):
     pairs = []
     for zone in range(NZ):
-        for across in range(NX * NC):
-            for line in range(NY):
+        for across in range(NX):
+            for low in range(NL):
                 target = (zone + shift) % NZ
                 pairs.append(
-                    ((zone * NX * NC + across) * NY + line, (target * NX * NC + line) * NY + across)
+                    ((zone * NX + across) * NL + low, (target * NX + low) * NL + across)
                 )
-    return lax.ppermute(entry, ("zh", "x", "core", "y"), pairs)
-
-
-def shifted(entry, axis, size, step):
-    return lax.ppermute(entry, axis, [(at, (at + step) % size) for at in range(size)])
+    return lax.ppermute(entry, ("zh", "x", "zl"), pairs)
+
+
+def share(entry, axis, size):
+    copies = jnp.broadcast_to(entry[None], (size,) + entry.shape)
+    return lax.all_to_all(copies, axis, 0, 0, tiled=True)
 
 
 def swap_cores(entry):
@@ -151,48 +155,51 @@
     shape = jax.ShapeDtypeStruct
 
     rows = grad_output.shape[0]
-    mixed, attention, pieces = call(
+    groups = NC * NL
+    pieces = call(cut_kernel, shape((groups, rows, WIDE), BF16), 0, 1 << 18, (grad_output,))
+    exchanged = lax.all_to_all(pieces, ("core", "zl"), 0, 0, tiled=True)
+    gathered = lax.all_gather(exchanged, "y", axis=0)
+
+    mixed, attention = call(
         forward_kernel,
-        (
-            shape((DH, TOK), BF16),
-            shape((IMAGES, PATCH, PATCH), F32),
-            shape((NY, rows, WIDE), BF16),
-        ),
+        (shape((DH, TOK), BF16), shape((IMAGES, PATCH, PATCH), F32)),
         2 * 2 * IMAGES * PATCH * PATCH * DH,
         1 << 20,
-        (query_input, key_input, value_input, query_gain, key_gain, grad_output),
-    )
-    mixed_all = lax.all_gather(mixed, "y", axis=0, tiled=True)
-    exchanged = lax.all_to_all(pieces, "y", 0, 0, tiled=True)
-    crossed = jnp.stack([cross(out_weight, shift) for shift in range(NZ)])
-    exchanged, crossed = lax.optimization_barrier((exchanged, crossed))
-    copies = jnp.broadcast_to(crossed[None], (NX,) + crossed.shape)
-    own = lax.all_to_all(copies, "x", 0, 0, tiled=True)
-    gathered = lax.all_gather(exchanged, "zl", axis=0)
-    gathered, mixed_all, own = lax.optimization_barrier((gathered, mixed_all, own))
-    other = swap_cores(own)
-
-    half = (NX, NZ, DH, BLK)
+        (query_input, key_input, value_input, query_gain, key_gain),
+    )
+    exchanged, out_weight, mixed = lax.optimization_barrier((exchanged, out_weight, mixed))
+    mixed_own = share(mixed, "zl", NL)
+    moved = [cross(out_weight, shift) for shift in range(NZ)]
+    mixed_own, *moved = lax.optimization_barrier((mixed_own, *moved))
+    moved = jnp.stack(moved)
+    mixed_other = swap_cores(mixed_own)
+    own = lax.all_gather(moved, "x", axis=0)
+    gathered, mixed_own, mixed_other, own = lax.optimization_barrier(
+        (gathered, mixed_own, mixed_other, own)
+    )
+
+    partial = call(
+        weight_kernel,
+        shape((NL, NZ, DH, BLK), BF16),
+        2 * TOK * NY * DH * WIDE,
+        5 << 20,
+        (gathered, mixed_own, mixed_other),
+    )
+    spread = lax.all_to_all(partial, "x", 0, 0, tiled=True)
+
+    half = (NL, TOK, DH)
     keep, send = call(
-        weight_kernel,
+        heads_kernel,
         (shape(half, F32), shape(half, BF16)),
         2 * TOK * NY * DH * WIDE,
-        5 << 20,
-        (gathered, mixed_all.reshape(NX, NC, DH, TOK)),
+        4 << 20,
+        (gathered, own),
     )
     received = swap_cores(send)
-    partial = call(
-        heads_kernel,
-        shape((NY, TOK, DH), BF16),
-        2 * TOK * NY * DH * WIDE,
-        4 << 20,
-        (gathered, own, other),
-    )
-    summed = [(keep[step] + received[step].astype(F32)).astype(BF16) for step in range(NX)]
-    partial, *summed = lax.optimization_barrier((partial, *summed))
-    grad_heads = lax.all_to_all(partial, "y", 0, 0, tiled=True)
-    spread = [summed[0]] + [shifted(summed[step], "x", NX, step) for step in range(1, NX)]
-    by_zone = sum(entry.astype(F32) for entry in spread).astype(BF16)
+    summed = (keep + received.astype(F32)).astype(BF16)
+    grad_heads = lax.all_to_all(summed, "zl", 0, 0, tiled=True)
+
+    by_zone = sum(spread[part].astype(F32) for part in range(NX)).astype(BF16)
     last = [cross(by_zone[shift], shift) for shift in range(NZ)]
     grad_weight = sum(entry.astype(F32) for entry in last).astype(BF16)
 

time: 158 us -> 150 us (0.949)
  the two profiles are of different devices: /device:TPU:22 before, /device:TPU:39 now
where the time goes in v4:
time: 150 us
  starting transfers between devices  52.8 us (35%)
  waiting for transfers between devices  39.2 us (26%)
  blocking collectives  27 us (18%)
  between operations  14.2 us (9%)
  local copies, waits for them, and re-layouts  7.22 us (5%)
  Pallas kernels  6.41 us (4%)
  other arithmetic  2.75 us (2%)
    ppermute x6, starting transfers between devices, cross(): return lax.ppermute(entry, ('zh', 'x', 'zl'), pairs)  34.6 us
    ppermute x6, waiting for transfers between devices, cross(): return lax.ppermute(entry, ('zh', 'x', 'zl'), pairs)  30.9 us
    all_to_all x1, blocking collectives, shards(): exchanged = lax.all_to_all(pieces, ('core', 'zl'), 0, 0, tiled=True)  15.5 us
    all_gather x1, blocking collectives, shards(): own = lax.all_gather(moved, 'x', axis=0)  11.5 us
    all_to_all x1, waiting for transfers between devices, shards(): spread = lax.all_to_all(partial, 'x', 0, 0, tiled=True)  8.35 us
    ppermute x2, starting transfers between devices, swap_cores(): return lax.ppermute(entry, 'core', [(0, 1), (1, 0)])  7.25 us
    pallas_call x5, Pallas kernels, call(): pl.pallas_call(kernel, out_shape=outs, in_specs=[pl.BlockSpec(memory_spac...  6.41 us
    unnamed x26, local copies, waits for them, and re-layouts  6.37 us
  transfers between devices with their start and end apart: 12, of which 5 were waited for; matrix products, arithmetic and copies ran while one was open for 2% of the time, Pallas kernels for 2%

profile of v4, /device:TPU:39, one launch (start us, length us, event | category | flops | bytes accessed | tf_op | source)
XLA Modules:
  0.0 149.6 jit_solution(6181232506331168851)
XLA Ops:
  7.2 0.0 all-gather.4.cloned.1.call-start
  7.2 0.0 copy-start.7
  7.2 0.9 copy-done.7
  8.2 15.5 %all_to_all.20 = bf16[8,16,768]{2,1,0:T(8,128)(2,1)} all-to-all(bf16[8,16,768]{2,1,0:T(8,128)(2,1)S(1)} %shard_map.103), channel_id=1, replica_groups=mesh['zh'=3,'x'=4,'core'=2,'y'=8,'zl'=4] {'core','zl'}, dimensions={0} | all-to-all | bytes 393216 | tf_op jit(solution)/shard_map/all_to_all | solution.py:160
  23.6 0.0 all-gather.4.cloned.1.call-update
  23.7 0.0 copy-start.1
  23.7 0.9 copy-done.1
  24.6 0.9 copy-done.3
  25.5 0.9 copy-done.5
  26.4 0.7 copy-done.8
  27.0 0.7 copy-done.10
  27.7 0.8 shard_map.102
  28.5 0.8 broadcast_in_dim.2
  29.4 3.5 %all-to-all-start.1 = ((bf16[4,128,512]{2,1,0:T(8,128)(2,1)}), bf16[4,128,512]{2,1,0:T(8,128)(2,1)S(1)}, u32[]{:S(2)}, u32[]{:S(2)}) async-start(bf16[4,128,512]{2,1,0:T(8,128)(2,1)} %broadcast_in_dim.2), calls=%async_computation.1 | async-start | bytes 1048576 | tf_op jit(solution)/shard_map/all_to_all | solution.py:145
  32.8 0.0 copy-done.12
  32.9 5.0 %collective-permute-start = (bf16[128,256]{1,0:T(8,128)(2,1)S(1)}, bf16[128,256]{1,0:T(8,128)(2,1)S(1)}, u32[]{:S(2)}, u32[]{:S(2)}) collective-permute-start(bf16[128,256]{1,0:T(8,128)(2,1)S(1)} %copy-done.12), channel_id=1, source_target_pairs={{0,0},{1,64},{2,128},{3,192},{64,1},{65,65},{66,129},{67,193},{128... | collective-permute-start | bytes 196616 | tf_op jit(solution)/shard_map/ppermute | solution.py:140
  37.9 12.0 %collective-permute-start.1 = (bf16[128,256]{1,0:T(8,128)(2,1)S(1)}, bf16[128,256]{1,0:T(8,128)(2,1)S(1)}, u32[]{:S(2)}, u32[]{:S(2)}) collective-permute-start(bf16[128,256]{1,0:T(8,128)(2,1)S(1)} %copy-done.12), channel_id=1, source_target_pairs={{0,256},{1,320},{2,384},{3,448},{64,257},{65,321},{66,385},{67,449... | collective-permute-start | bytes 196616 | tf_op jit(solution)/shard_map/ppermute | solution.py:140
  49.9 1.9 %collective-permute-start.2 = (bf16[128,256]{1,0:T(8,128)(2,1)S(1)}, bf16[128,256]{1,0:T(8,128)(2,1)S(1)}, u32[]{:S(2)}, u32[]{:S(2)}) collective-permute-start(bf16[128,256]{1,0:T(8,128)(2,1)S(1)} %copy-done.12), channel_id=1, source_target_pairs={{0,512},{1,576},{2,640},{3,704},{64,513},{65,577},{66,641},{67,705... | collective-permute-start | bytes 196616 | tf_op jit(solution)/shard_map/ppermute | solution.py:140
  51.8 0.0 collective-permute-done
  51.9 7.4 %collective-permute-done.1 = bf16[128,256]{1,0:T(8,128)(2,1)S(1)} collective-permute-done((bf16[128,256]{1,0:T(8,128)(2,1)S(1)}, bf16[128,256]{1,0:T(8,128)(2,1)S(1)}, u32[]{:S(2)}, u32[]{:S(2)}) %collective-permute-start.1) | collective-permute-done | bytes 65568 | tf_op jit(solution)/shard_map/ppermute | solution.py:140
  59.3 7.9 %collective-permute-done.2 = bf16[128,256]{1,0:T(8,128)(2,1)S(1)} collective-permute-done((bf16[128,256]{1,0:T(8,128)(2,1)S(1)}, bf16[128,256]{1,0:T(8,128)(2,1)S(1)}, u32[]{:S(2)}, u32[]{:S(2)}) %collective-permute-start.2) | collective-permute-done | bytes 65568 | tf_op jit(solution)/shard_map/ppermute | solution.py:140
  67.1 0.0 all-to-all-done.1.own_ref
  67.1 2.4 %collective-permute-start.3 = (bf16[4,128,512]{2,1,0:T(8,128)(2,1)S(1)}, bf16[4,128,512]{2,1,0:T(8,128)(2,1)S(1)}, u32[]{:S(2)}, u32[]{:S(2)}) collective-permute-start(bf16[4,128,512]{2,1,0:T(8,128)(2,1)S(1)} %all-to-all-done.1.own_ref), channel_id=1, source_target_pairs={{0,32},{32,0},{1,33},{33,1},{2,34},{34,2},{3,35},{35,3},{4,36},{36... | collective-permute-start | bytes 1572872 | tf_op jit(solution)/shard_map/ppermute | solution.py:149
  69.6 11.5 %all-gather.1 = bf16[12,128,256]{2,1,0:T(8,128)(2,1)S(1)} all-gather(bf16[3,128,256]{2,1,0:T(8,128)(2,1)S(1)} %pad_maximum_fusion), channel_id=3, replica_groups=mesh['zh'=3,'x'=4,'core'=2,'y'=8,'zl'=4] {'x'}, dimensions={0}, use_global_device_ids=true | all-gather | bytes 983040 | tf_op jit(solution)/shard_map/all_gather | solution.py:176
  81.1 0.0 collective-permute-done.3.other_ref
  81.1 1.4 copy-done
  82.5 1.5 shard_map.104
  84.0 4.9 %collective-permute-start.4 = (bf16[4,512,128]{2,1,0:T(8,128)(2,1)}, bf16[4,512,128]{2,1,0:T(8,128)(2,1)}, u32[]{:S(2)}, u32[]{:S(2)}) collective-permute-start(bf16[4,512,128]{2,1,0:T(8,128)(2,1)} %get-tuple-element.32), channel_id=1, source_target_pairs={{0,32},{32,0},{1,33},{33,1},{2,34},{34,2},{3,35},{35,3},{4,36},{36... | collective-permute-start | bytes 1572872 | tf_op jit(solution)/shard_map/ppermute | solution.py:149
  88.9 1.9 %shard_map.106 = bf16[4,3,128,256]{3,2,1,0:T(8,128)(2,1)} custom-call(bf16[8,8,16,768]{3,2,1,0:T(8,128)(2,1)S(1)} %bitcast.14, bf16[4,128,512]{2,1,0:T(8,128)(2,1)S(1)} %all-to-all-done.1.own_ref, bf16[4,128,512]{2,1,0:T(8,128)(2,1)S(1)} %collective-permute-done.3.other_ref), custom_call_target="tpu_custom_call" | custom-call | flops 805306368 | bytes 5242880 | tf_op jit(solution)/shard_map/pallas_call | solution.py:121
  90.8 3.9 %all-to-all-start.3 = ((bf16[4,3,128,256]{3,2,1,0:T(8,128)(2,1)}), bf16[4,3,128,256]{3,2,1,0:T(8,128)(2,1)S(1)}, u32[]{:S(2)}, u32[]{:S(2)}) async-start(bf16[4,3,128,256]{3,2,1,0:T(8,128)(2,1)} %shard_map.106), calls=%async_computation.3 | async-start | bytes 1572864 | tf_op jit(solution)/shard_map/all_to_all | solution.py:188
  94.7 0.0 collective-permute-done.4
  94.7 2.0 %add_convert_fusion = bf16[4,512,128]{2,1,0:T(8,128)(2,1)} fusion(f32[4,512,128]{2,1,0:T(8,128)S(1)} %get-tuple-element.31, bf16[4,512,128]{2,1,0:T(8,128)(2,1)} %collective-permute-done.4), kind=kLoop, calls=%fused_computation | loop fusion | flops 786432 | bytes 2097152 | tf_op jit(solution)/shard_map/convert_element_type | solution.py:199
  96.7 0.0 copy-start.11
  96.7 8.4 %all-to-all-done.3 = bf16[4,3,128,256]{3,2,1,0:T(8,128)(2,1)S(1)} async-done(((bf16[4,3,128,256]{3,2,1,0:T(8,128)(2,1)}), bf16[4,3,128,256]{3,2,1,0:T(8,128)(2,1)S(1)}, u32[]{:S(2)}, u32[]{:S(2)}) %all-to-all-start.3) | async-done | bytes 786464 | tf_op jit(solution)/shard_map/all_to_all | solution.py:188
  105.1 3.5 %all-to-all-start.2 = ((bf16[4,512,128]{2,1,0:T(8,128)(2,1)}), bf16[4,512,128]{2,1,0:T(8,128)(2,1)S(1)}, u32[]{:S(2)}, u32[]{:S(2)}) async-start(bf16[4,512,128]{2,1,0:T(8,128)(2,1)} %add_convert_fusion), calls=%async_computation.2 | async-start | bytes 1048576 | tf_op jit(solution)/shard_map/all_to_all | solution.py:200
  108.5 0.1 add_convert_fusion.1
  108.7 6.6 %collective-permute-start.5 = (bf16[128,256]{1,0:T(8,128)(2,1)S(1)}, bf16[128,256]{1,0:T(8,128)(2,1)S(1)}, u32[]{:S(2)}, u32[]{:S(2)}) collective-permute-start(bf16[128,256]{1,0:T(8,128)(2,1)S(1)} %get-tuple-element.38), channel_id=1, source_target_pairs={{0,0},{1,64},{2,128},{3,192},{64,1},{65,65},{66,129},{67,193},{128... | collective-permute-start | bytes 196616 | tf_op jit(solution)/shard_map/ppermute | solution.py:140
  115.3 7.1 %collective-permute-start.6 = (bf16[128,256]{1,0:T(8,128)(2,1)S(1)}, bf16[128,256]{1,0:T(8,128)(2,1)S(1)}, u32[]{:S(2)}, u32[]{:S(2)}) collective-permute-start(bf16[128,256]{1,0:T(8,128)(2,1)S(1)} %get-tuple-element.40), channel_id=1, source_target_pairs={{0,256},{1,320},{2,384},{3,448},{64,257},{65,321},{66,385},{67,449... | collective-permute-start | bytes 196616 | tf_op jit(solution)/shard_map/ppermute | solution.py:140
  122.4 1.9 %collective-permute-start.7 = (bf16[128,256]{1,0:T(8,128)(2,1)S(1)}, bf16[128,256]{1,0:T(8,128)(2,1)S(1)}, u32[]{:S(2)}, u32[]{:S(2)}) collective-permute-start(bf16[128,256]{1,0:T(8,128)(2,1)S(1)} %get-tuple-element.39), channel_id=1, source_target_pairs={{0,512},{1,576},{2,640},{3,704},{64,513},{65,577},{66,641},{67,705... | collective-permute-start | bytes 196616 | tf_op jit(solution)/shard_map/ppermute | solution.py:140
  124.3 0.0 collective-permute-done.5
  124.3 7.3 %collective-permute-done.6 = bf16[128,256]{1,0:T(8,128)(2,1)S(1)} collective-permute-done((bf16[128,256]{1,0:T(8,128)(2,1)S(1)}, bf16[128,256]{1,0:T(8,128)(2,1)S(1)}, u32[]{:S(2)}, u32[]{:S(2)}) %collective-permute-start.6) | collective-permute-done | bytes 65568 | tf_op jit(solution)/shard_map/ppermute | solution.py:140
  131.7 8.2 %collective-permute-done.7 = bf16[128,256]{1,0:T(8,128)(2,1)S(1)} collective-permute-done((bf16[128,256]{1,0:T(8,128)(2,1)S(1)}, bf16[128,256]{1,0:T(8,128)(2,1)S(1)}, u32[]{:S(2)}, u32[]{:S(2)}) %collective-permute-start.7) | collective-permute-done | bytes 65568 | tf_op jit(solution)/shard_map/ppermute | solution.py:140
  139.9 0.7 add_convert_fusion.2
  140.6 0.0 all-to-all-done.2.gh_ref
  140.6 0.0 copy-done.2
  140.6 0.0 copy-done.4
  140.6 0.0 copy-done.6
  140.6 2.2 %shard_map.105 = (bf16[512,128]{1,0:T(8,128)(2,1)}, bf16[512,128]{1,0:T(8,128)(2,1)}, bf16[512,128]{1,0:T(8,128)(2,1)}) custom-call(bf16[512,128]{1,0:T(8,128)(2,1)S(1)} %copy-done.2, bf16[512,128]{1,0:T(8,128)(2,1)S(1)} %copy-done.4, bf16[512,128]{1,0:T(8,128)(2,1)S(1)} %copy-done.6, f32[1,128]{1,0:T(1,128)S(1)} %bitcast.17, f32[1,128]{1,0:T(1,128)S(1)} %bitcast.19, ...), custom_call_target="tpu_custom_call" | custom-call | flops 167772160 | bytes 2097152 | tf_op jit(solution)/shard_map/pallas_call | solution.py:121
  (16 shorter events, 0.1 us)
Async XLA Ops:
  7.2 73.9 %all-gather.4.cloned.1.call-start = ((), (), s32[]{:S(2)}) async-start(), calls=%async_computation.4 | async-start | bytes 1769472 | tf_op jit(solution)/shard_map/all_gather | solution.py:161
  7.2 0.9 copy-start.7
  8.1 24.7 %copy-start.12 = (bf16[128,256]{1,0:T(8,128)(2,1)S(1)}, bf16[128,256]{1,0:T(8,128)(2,1)}, u32[]{:S(2)}) copy-start(bf16[128,256]{1,0:T(8,128)(2,1)} %param.12) | copy-start | bytes 196612
  23.7 0.9 copy-start.1
  24.6 0.9 copy-start.3
  25.5 0.9 copy-start.5
  26.4 0.7 copy-start.8
  27.0 0.7 copy-start.10
  29.4 37.8 %all-to-all-start.1 = ((bf16[4,128,512]{2,1,0:T(8,128)(2,1)}), bf16[4,128,512]{2,1,0:T(8,128)(2,1)S(1)}, u32[]{:S(2)}, u32[]{:S(2)}) async-start(bf16[4,128,512]{2,1,0:T(8,128)(2,1)} %broadcast_in_dim.2), calls=%async_computation.1 | async-start | bytes 1048576 | tf_op jit(solution)/shard_map/all_to_all | solution.py:145
  32.9 19.0 %collective-permute-start = (bf16[128,256]{1,0:T(8,128)(2,1)S(1)}, bf16[128,256]{1,0:T(8,128)(2,1)S(1)}, u32[]{:S(2)}, u32[]{:S(2)}) collective-permute-start(bf16[128,256]{1,0:T(8,128)(2,1)S(1)} %copy-done.12), channel_id=1, source_target_pairs={{0,0},{1,64},{2,128},{3,192},{64,1},{65,65},{66,129},{67,193},{128... | collective-permute-start | bytes 196616 | tf_op jit(solution)/shard_map/ppermute | solution.py:140
  37.9 21.4 %collective-permute-start.1 = (bf16[128,256]{1,0:T(8,128)(2,1)S(1)}, bf16[128,256]{1,0:T(8,128)(2,1)S(1)}, u32[]{:S(2)}, u32[]{:S(2)}) collective-permute-start(bf16[128,256]{1,0:T(8,128)(2,1)S(1)} %copy-done.12), channel_id=1, source_target_pairs={{0,256},{1,320},{2,384},{3,448},{64,257},{65,321},{66,385},{67,449... | collective-permute-start | bytes 196616 | tf_op jit(solution)/shard_map/ppermute | solution.py:140
  49.9 17.2 %collective-permute-start.2 = (bf16[128,256]{1,0:T(8,128)(2,1)S(1)}, bf16[128,256]{1,0:T(8,128)(2,1)S(1)}, u32[]{:S(2)}, u32[]{:S(2)}) collective-permute-start(bf16[128,256]{1,0:T(8,128)(2,1)S(1)} %copy-done.12), channel_id=1, source_target_pairs={{0,512},{1,576},{2,640},{3,704},{64,513},{65,577},{66,641},{67,705... | collective-permute-start | bytes 196616 | tf_op jit(solution)/shard_map/ppermute | solution.py:140
  67.1 13.9 %collective-permute-start.3 = (bf16[4,128,512]{2,1,0:T(8,128)(2,1)S(1)}, bf16[4,128,512]{2,1,0:T(8,128)(2,1)S(1)}, u32[]{:S(2)}, u32[]{:S(2)}) collective-permute-start(bf16[4,128,512]{2,1,0:T(8,128)(2,1)S(1)} %all-to-all-done.1.own_ref), channel_id=1, source_target_pairs={{0,32},{32,0},{1,33},{33,1},{2,34},{34,2},{3,35},{35,3},{4,36},{36... | collective-permute-start | bytes 1572872 | tf_op jit(solution)/shard_map/ppermute | solution.py:149
  81.1 1.4 copy-start
  84.0 10.7 %collective-permute-start.4 = (bf16[4,512,128]{2,1,0:T(8,128)(2,1)}, bf16[4,512,128]{2,1,0:T(8,128)(2,1)}, u32[]{:S(2)}, u32[]{:S(2)}) collective-permute-start(bf16[4,512,128]{2,1,0:T(8,128)(2,1)} %get-tuple-element.32), channel_id=1, source_target_pairs={{0,32},{32,0},{1,33},{33,1},{2,34},{34,2},{3,35},{35,3},{4,36},{36... | collective-permute-start | bytes 1572872 | tf_op jit(solution)/shard_map/ppermute | solution.py:149
  90.8 14.3 %all-to-all-start.3 = ((bf16[4,3,128,256]{3,2,1,0:T(8,128)(2,1)}), bf16[4,3,128,256]{3,2,1,0:T(8,128)(2,1)S(1)}, u32[]{:S(2)}, u32[]{:S(2)}) async-start(bf16[4,3,128,256]{3,2,1,0:T(8,128)(2,1)} %shard_map.106), calls=%async_computation.3 | async-start | bytes 1572864 | tf_op jit(solution)/shard_map/all_to_all | solution.py:188
  96.7 43.9 %copy-start.2 = (bf16[512,128]{1,0:T(8,128)(2,1)S(1)}, bf16[512,128]{1,0:T(8,128)(2,1)}, u32[]{:S(2)}) copy-start(bf16[512,128]{1,0:T(8,128)(2,1)} %q_ref.3) | copy-start | bytes 393220
  96.7 43.9 %copy-start.4 = (bf16[512,128]{1,0:T(8,128)(2,1)S(1)}, bf16[512,128]{1,0:T(8,128)(2,1)}, u32[]{:S(2)}) copy-start(bf16[512,128]{1,0:T(8,128)(2,1)} %k_ref.3) | copy-start | bytes 393220
  96.7 43.9 %copy-start.6 = (bf16[512,128]{1,0:T(8,128)(2,1)S(1)}, bf16[512,128]{1,0:T(8,128)(2,1)}, u32[]{:S(2)}) copy-start(bf16[512,128]{1,0:T(8,128)(2,1)} %v_ref.3) | copy-start | bytes 393220
  96.7 43.9 %copy-start.9 = (f32[128]{0:T(128)S(1)}, f32[128]{0:T(128)}, u32[]{:S(2)}) copy-start(f32[128]{0:T(128)} %param.10) | copy-start | bytes 1540
  96.7 43.9 %copy-start.11 = (f32[128]{0:T(128)S(1)}, f32[128]{0:T(128)}, u32[]{:S(2)}) copy-start(f32[128]{0:T(128)} %param.11) | copy-start | bytes 1540
  105.1 35.5 %all-to-all-start.2 = ((bf16[4,512,128]{2,1,0:T(8,128)(2,1)}), bf16[4,512,128]{2,1,0:T(8,128)(2,1)S(1)}, u32[]{:S(2)}, u32[]{:S(2)}) async-start(bf16[4,512,128]{2,1,0:T(8,128)(2,1)} %add_convert_fusion), calls=%async_computation.2 | async-start | bytes 1048576 | tf_op jit(solution)/shard_map/all_to_all | solution.py:200
  108.7 15.6 %collective-permute-start.5 = (bf16[128,256]{1,0:T(8,128)(2,1)S(1)}, bf16[128,256]{1,0:T(8,128)(2,1)S(1)}, u32[]{:S(2)}, u32[]{:S(2)}) collective-permute-start(bf16[128,256]{1,0:T(8,128)(2,1)S(1)} %get-tuple-element.38), channel_id=1, source_target_pairs={{0,0},{1,64},{2,128},{3,192},{64,1},{65,65},{66,129},{67,193},{128... | collective-permute-start | bytes 196616 | tf_op jit(solution)/shard_map/ppermute | solution.py:140
  115.3 16.4 %collective-permute-start.6 = (bf16[128,256]{1,0:T(8,128)(2,1)S(1)}, bf16[128,256]{1,0:T(8,128)(2,1)S(1)}, u32[]{:S(2)}, u32[]{:S(2)}) collective-permute-start(bf16[128,256]{1,0:T(8,128)(2,1)S(1)} %get-tuple-element.40), channel_id=1, source_target_pairs={{0,256},{1,320},{2,384},{3,448},{64,257},{65,321},{66,385},{67,449... | collective-permute-start | bytes 196616 | tf_op jit(solution)/shard_map/ppermute | solution.py:140
  122.4 17.5 %collective-permute-start.7 = (bf16[128,256]{1,0:T(8,128)(2,1)S(1)}, bf16[128,256]{1,0:T(8,128)(2,1)S(1)}, u32[]{:S(2)}, u32[]{:S(2)}) collective-permute-start(bf16[128,256]{1,0:T(8,128)(2,1)S(1)} %get-tuple-element.39), channel_id=1, source_target_pairs={{0,512},{1,576},{2,640},{3,704},{64,513},{65,577},{66,641},{67,705... | collective-permute-start | bytes 196616 | tf_op jit(solution)/shard_map/ppermute | solution.py:140
Sparse Core Ops, SparseCore 0:
  23.8 40.6 all-gather.3

commit v5 on v4

--- a/solution.py
+++ b/solution.py
@@ -66,13 +66,14 @@
 
 
 def backward_kernel(
-    q_ref, k_ref, v_ref, qg_ref, kg_ref, att_ref, gh_ref, dq_ref, dk_ref, dv_ref
+    q_ref, k_ref, v_ref, qg_ref, kg_ref, att_ref, *refs
 ):
+    gh_refs, (dq_ref, dk_ref, dv_ref) = refs[:NL], refs[NL:]
     for image in range(IMAGES):
         rows = pl.ds(image * PATCH, PATCH)
-        total = gh_ref[0, rows, :].astype(F32)
+        total = gh_refs[0][rows, :].astype(F32)
         for part in range(1, NL):
-            total = total + gh_ref[part, rows, :].astype(F32)
+            total = total + gh_refs[part][rows, :].astype(F32)
         grad_heads = total.astype(BF16)
         query_unit, query_inv = normalize(q_ref[rows, :])
         key_unit, key_inv = normalize(k_ref[rows, :])
@@ -90,31 +91,30 @@
 
 
 def block(ref, side, zone):
-    columns = pl.ds(zone * BLK, BLK)
+    columns = slice(zone * BLK, (zone + 1) * BLK)
     return ref[:, pl.ds(side * NL, NL), :, columns].reshape(TOK, BLK)
 
 
 def heads_kernel(g_ref, own_ref, keep_ref, send_ref):
-    here, core = lax.axis_index("zh"), lax.axis_index("core")
+    core, low = lax.axis_index("core"), lax.axis_index("zl")
     for ref, side in ((send_ref, 1 - core), (keep_ref, core)):
         total = None
-        for step in range(NZ):
-            rows = block(g_ref, side, lax.rem(here + NZ - step, NZ))
-            term = dot(rows, own_ref[:, step].reshape(NL * DH, BLK), 1, 1)
+        for zone in range(NZ):
+            weight = jnp.concatenate([own_ref[zone, low ^ step] for step in range(NL)], axis=0)
+            term = dot(block(g_ref, side, zone), weight, 1, 1)
             total = term if total is None else total + term
-        for head in range(NL):
-            ref[head] = total[:, head * DH : (head + 1) * DH].astype(ref.dtype)
+        for step in range(NL):
+            ref[step] = total[:, step * DH : (step + 1) * DH].astype(ref.dtype)
 
 
 def weight_kernel(g_ref, own_ref, other_ref, out_ref):
-    here, core = lax.axis_index("zh"), lax.axis_index("core")
+    core = lax.axis_index("core")
     own = own_ref[...].reshape(NL * DH, TOK)
     other = other_ref[...].reshape(NL * DH, TOK)
-    for step in range(NZ):
-        zone = lax.rem(here + step, NZ)
+    for zone in range(NZ):
         total = dot(own, block(g_ref, core, zone), 1, 0)
         total = total + dot(other, block(g_ref, 1 - core, zone), 1, 0)
-        out_ref[:, step] = total.reshape(NL, DH, BLK).astype(BF16)
+        out_ref[zone] = total.reshape(NL, DH, BLK).astype(BF16)
 
 
 def call(kernel, outs, flops, moved, operands):
@@ -128,21 +128,13 @@
     )(*operands)
 
 
-def cross(entry, shift):
-    pairs = []
-    for zone in range(NZ):
-        for across in range(NX):
-            for low in range(NL):
-                target = (zone + shift) % NZ
-                pairs.append(
-                    ((zone * NX + across) * NL + low, (target * NX + low) * NL + across)
-                )
-    return lax.ppermute(entry, ("zh", "x", "zl"), pairs)
-
-
-def share(entry, axis, size):
-    copies = jnp.broadcast_to(entry[None], (size,) + entry.shape)
-    return lax.all_to_all(copies, axis, 0, 0, tiled=True)
+def cross(entry):
+    pairs = [(at * NL + low, low * NL + at) for at in range(NX) for low in range(NL)]
+    return lax.ppermute(entry, ("x", "zl"), pairs)
+
+
+def flip(entry, step):
+    return lax.ppermute(entry, "zl", [(at, at ^ step) for at in range(NL)])
 
 
 def swap_cores(entry):
@@ -168,24 +160,24 @@
         (query_input, key_input, value_input, query_gain, key_gain),
     )
     exchanged, out_weight, mixed = lax.optimization_barrier((exchanged, out_weight, mixed))
-    mixed_own = share(mixed, "zl", NL)
-    moved = [cross(out_weight, shift) for shift in range(NZ)]
-    mixed_own, *moved = lax.optimization_barrier((mixed_own, *moved))
-    moved = jnp.stack(moved)
+    zones = NZ * NX
+    crossed = cross(out_weight)
+    copies = jnp.broadcast_to(crossed[None], (zones, DH, BLK))
+    own = lax.all_to_all(copies, ("zh", "x"), 0, 0, tiled=True).reshape(NZ, NX, DH, BLK)
+    mixed_own = lax.all_gather(mixed, "zl", axis=0)
     mixed_other = swap_cores(mixed_own)
-    own = lax.all_gather(moved, "x", axis=0)
     gathered, mixed_own, mixed_other, own = lax.optimization_barrier(
         (gathered, mixed_own, mixed_other, own)
     )
 
     partial = call(
         weight_kernel,
-        shape((NL, NZ, DH, BLK), BF16),
+        shape((NZ, NX, DH, BLK), BF16),
         2 * TOK * NY * DH * WIDE,
         5 << 20,
         (gathered, mixed_own, mixed_other),
     )
-    spread = lax.all_to_all(partial, "x", 0, 0, tiled=True)
+    spread = lax.all_to_all(partial.reshape(zones, DH, BLK), ("zh", "x"), 0, 0, tiled=True)
 
     half = (NL, TOK, DH)
     keep, send = call(
@@ -196,19 +188,17 @@
         (gathered, own),
     )
     received = swap_cores(send)
-    summed = (keep + received.astype(F32)).astype(BF16)
-    grad_heads = lax.all_to_all(summed, "zl", 0, 0, tiled=True)
-
-    by_zone = sum(spread[part].astype(F32) for part in range(NX)).astype(BF16)
-    last = [cross(by_zone[shift], shift) for shift in range(NZ)]
-    grad_weight = sum(entry.astype(F32) for entry in last).astype(BF16)
+    summed = [(keep[step] + received[step].astype(F32)).astype(BF16) for step in range(NL)]
+    grad_heads = [summed[0]] + [flip(summed[step], step) for step in range(1, NL)]
+
+    grad_weight = cross(sum(spread[part].astype(F32) for part in range(zones)).astype(BF16))
 
     grad_query, grad_key, grad_value = call(
         backward_kernel,
         (shape((TOK, DH), BF16),) * 3,
         5 * 2 * IMAGES * PATCH * PATCH * DH,
         2 << 20,
-        (query_input, key_input, value_input, query_gain, key_gain, attention, grad_heads),
+        (query_input, key_input, value_input, query_gain, key_gain, attention, *grad_heads),
     )
     return grad_query, grad_key, grad_value, grad_weight
 

time: 150 us -> 156 us (1.040)
  the two profiles are of different devices: /device:TPU:39 before, /device:TPU:176 now
where the time goes in v5:
time: 156 us
  blocking collectives  48.1 us (31%)
  starting transfers between devices  41.7 us (27%)
  waiting for transfers between devices  36.3 us (23%)
  between operations  14.3 us (9%)
  local copies, waits for them, and re-layouts  7.98 us (5%)
  Pallas kernels  5.88 us (4%)
    all_gather x1, blocking collectives, shards(): mixed_own = lax.all_gather(mixed, 'zl', axis=0)  36.5 us
    all_to_all x1, waiting for transfers between devices, shards(): lax.all_to_all(partial.reshape(zones, DH, BLK), ('zh', 'x'), 0, 0, tiled=...  23.1 us
    all_to_all x1, blocking collectives, shards(): exchanged = lax.all_to_all(pieces, ('core', 'zl'), 0, 0, tiled=True)  11.7 us
    all_to_all x1, starting transfers between devices, shards(): lax.all_to_all(copies, ('zh', 'x'), 0, 0, tiled=True)  11.3 us
    ppermute x3, starting transfers between devices, flip(): return lax.ppermute(entry, 'zl', [(at, at ^ step) for at in range(NL)])  9.81 us
    ppermute x2, waiting for transfers between devices, cross(): return lax.ppermute(entry, ('x', 'zl'), pairs)  9.44 us
    ppermute x2, starting transfers between devices, cross(): return lax.ppermute(entry, ('x', 'zl'), pairs)  8.44 us
    all_to_all x1, starting transfers between devices, shards(): lax.all_to_all(partial.reshape(zones, DH, BLK), ('zh', 'x'), 0, 0, tiled=...  8.21 us
  transfers between devices with their start and end apart: 10, of which 5 were waited for; matrix products, arithmetic and copies ran while one was open for 2% of the time, Pallas kernels for 3%

profile of v5, /device:TPU:176, one launch (start us, length us, event | category | flops | bytes accessed | tf_op | source)
XLA Modules:
  0.0 155.6 jit_solution(3976790979711126471)
XLA Ops:
  7.2 0.0 all-gather.4.cloned.1.call-start
  7.2 0.0 copy-start.8
  7.2 0.9 copy-done.8
  8.2 11.7 %all_to_all.15 = bf16[8,16,768]{2,1,0:T(8,128)(2,1)} all-to-all(bf16[8,16,768]{2,1,0:T(8,128)(2,1)S(1)} %shard_map.103), channel_id=1, replica_groups=mesh['zh'=3,'x'=4,'core'=2,'y'=8,'zl'=4] {'core','zl'}, dimensions={0} | all-to-all | bytes 393216 | tf_op jit(solution)/shard_map/all_to_all | solution.py:152
  19.8 0.0 all-gather.4.cloned.1.call-update
  19.9 0.0 copy-start.2
  19.9 0.9 copy-done.2
  20.8 0.9 copy-done.4
  21.7 0.9 copy-done.6
  22.6 0.7 copy-done.9
  23.2 0.7 copy-done.11
  23.9 0.8 shard_map.102
  24.7 6.5 %collective-permute-start.1 = (bf16[128,256]{1,0:T(8,128)(2,1)}, bf16[128,256]{1,0:T(8,128)(2,1)S(1)}, u32[]{:S(2)}, u32[]{:S(2)}) collective-permute-start(bf16[128,256]{1,0:T(8,128)(2,1)} %param.12), channel_id=1, source_target_pairs={{0,0},{1,64},{2,128},{3,192},{64,1},{65,65},{66,129},{67,193},{128... | collective-permute-start | bytes 196616 | tf_op jit(solution)/shard_map/ppermute | solution.py:133
  31.3 4.1 %collective-permute-done.1 = bf16[128,256]{1,0:T(8,128)(2,1)S(1)} collective-permute-done((bf16[128,256]{1,0:T(8,128)(2,1)}, bf16[128,256]{1,0:T(8,128)(2,1)S(1)}, u32[]{:S(2)}, u32[]{:S(2)}) %collective-permute-start.1) | collective-permute-done | bytes 65568 | tf_op jit(solution)/shard_map/ppermute | solution.py:133
  35.4 1.0 broadcast_in_dim.2
  36.4 11.3 %all-to-all-start.1 = ((bf16[12,128,256]{2,1,0:T(8,128)(2,1)}), bf16[12,128,256]{2,1,0:T(8,128)(2,1)S(1)}, u32[]{:S(2)}, u32[]{:S(2)}) async-start(bf16[12,128,256]{2,1,0:T(8,128)(2,1)} %broadcast_in_dim.2), calls=%async_computation.1 | async-start | bytes 1572864 | tf_op jit(solution)/shard_map/all_to_all | solution.py:166
  47.6 36.5 %all-gather.1 = bf16[512,512]{1,0:T(8,128)(2,1)S(1)} all-gather(bf16[128,512]{1,0:T(8,128)(2,1)S(1)} %get-tuple-element.19), channel_id=3, replica_groups=mesh['zh'=3,'x'=4,'core'=2,'y'=8,'zl'=4] {'zl'}, dimensions={0}, use_global_device_ids=true | all-gather | bytes 655360 | tf_op jit(solution)/shard_map/all_gather | solution.py:167
  84.1 1.9 %collective-permute-start = (bf16[4,128,512]{2,1,0:T(8,128)(2,1)S(1)}, bf16[4,128,512]{2,1,0:T(8,128)(2,1)S(1)}, u32[]{:S(2)}, u32[]{:S(2)}) collective-permute-start(bf16[4,128,512]{2,1,0:T(8,128)(2,1)S(1)} %bitcast.16), channel_id=1, source_target_pairs={{0,32},{32,0},{1,33},{33,1},{2,34},{34,2},{3,35},{35,3},{4,36},{36... | collective-permute-start | bytes 1572872 | tf_op jit(solution)/shard_map/ppermute | solution.py:141
  86.0 1.9 %collective-permute-done.other_ref = bf16[4,128,512]{2,1,0:T(8,128)(2,1)S(1)} collective-permute-done((bf16[4,128,512]{2,1,0:T(8,128)(2,1)S(1)}, bf16[4,128,512]{2,1,0:T(8,128)(2,1)S(1)}, u32[]{:S(2)}, u32[]{:S(2)}) %collective-permute-start) | collective-permute-done | bytes 524320 | tf_op jit(solution)/shard_map/ppermute | solution.py:141
  87.9 0.0 all-to-all-done.1
  87.9 1.4 copy-done
  89.3 1.9 %shard_map.106 = bf16[3,4,128,256]{3,2,1,0:T(8,128)(2,1)} custom-call(bf16[8,8,16,768]{3,2,1,0:T(8,128)(2,1)S(1)} %bitcast.18, bf16[4,128,512]{2,1,0:T(8,128)(2,1)S(1)} %bitcast.17, bf16[4,128,512]{2,1,0:T(8,128)(2,1)S(1)} %collective-permute-done.other_ref), custom_call_target="tpu_custom_call" | custom-call | flops 805306368 | bytes 5242880 | tf_op jit(solution)/shard_map/pallas_call | solution.py:121
  91.2 8.2 %all-to-all-start.2 = ((bf16[12,128,256]{2,1,0:T(8,128)(2,1)}), bf16[12,128,256]{2,1,0:T(8,128)(2,1)}, u32[]{:S(2)}, u32[]{:S(2)}) async-start(bf16[12,128,256]{2,1,0:T(8,128)(2,1)} %bitcast.9), calls=%async_computation.2 | async-start | bytes 1572864 | tf_op jit(solution)/shard_map/all_to_all | solution.py:180
  99.4 0.0 copy-done.1
  99.4 1.0 shard_map.104
  100.4 0.0 copy-start.3
  100.4 0.0 copy-start.5
  100.4 0.0 copy-start.7
  100.5 0.0 copy-start.10
  100.5 0.0 copy-start.12
  100.5 2.1 %collective-permute-start.2 = (bf16[4,512,128]{2,1,0:T(8,128)(2,1)S(1)}, bf16[4,512,128]{2,1,0:T(8,128)(2,1)S(1)}, u32[]{:S(2)}, u32[]{:S(2)}) collective-permute-start(bf16[4,512,128]{2,1,0:T(8,128)(2,1)S(1)} %get-tuple-element.24), channel_id=1, source_target_pairs={{0,32},{32,0},{1,33},{33,1},{2,34},{34,2},{3,35},{35,3},{4,36},{36... | collective-permute-start | bytes 1572872 | tf_op jit(solution)/shard_map/ppermute | solution.py:141
  102.5 1.9 %collective-permute-done.2 = bf16[4,512,128]{2,1,0:T(8,128)(2,1)S(1)} collective-permute-done((bf16[4,512,128]{2,1,0:T(8,128)(2,1)S(1)}, bf16[4,512,128]{2,1,0:T(8,128)(2,1)S(1)}, u32[]{:S(2)}, u32[]{:S(2)}) %collective-permute-start.2) | collective-permute-done | bytes 524320 | tf_op jit(solution)/shard_map/ppermute | solution.py:141
  104.4 0.1 fusion.3
  104.5 2.5 %collective-permute-start.5 = (bf16[512,128]{1,0:T(8,128)(2,1)S(1)}, bf16[512,128]{1,0:T(8,128)(2,1)S(1)}, u32[]{:S(2)}, u32[]{:S(2)}) collective-permute-start(bf16[512,128]{1,0:T(8,128)(2,1)S(1)} %get-tuple-element.30), channel_id=1, source_target_pairs={{0,3},{1,2},{2,1},{3,0},{4,7},{5,6},{6,5},{7,4},{8,11},{9,10},{10,... | collective-permute-start | bytes 393224 | tf_op jit(solution)/shard_map/ppermute | solution.py:137
  107.1 5.3 %collective-permute-start.4 = (bf16[512,128]{1,0:T(8,128)(2,1)S(1)}, bf16[512,128]{1,0:T(8,128)(2,1)S(1)}, u32[]{:S(2)}, u32[]{:S(2)}) collective-permute-start(bf16[512,128]{1,0:T(8,128)(2,1)S(1)} %get-tuple-element.31), channel_id=1, source_target_pairs={{0,2},{1,3},{2,0},{3,1},{4,6},{5,7},{6,4},{7,5},{8,10},{9,11},{10,... | collective-permute-start | bytes 393224 | tf_op jit(solution)/shard_map/ppermute | solution.py:137
  112.5 1.9 %collective-permute-start.3 = (bf16[512,128]{1,0:T(8,128)(2,1)S(1)}, bf16[512,128]{1,0:T(8,128)(2,1)S(1)}, u32[]{:S(2)}, u32[]{:S(2)}) collective-permute-start(bf16[512,128]{1,0:T(8,128)(2,1)S(1)} %get-tuple-element.32), channel_id=1, source_target_pairs={{0,1},{1,0},{2,3},{3,2},{4,5},{5,4},{6,7},{7,6},{8,9},{9,8},{10,11... | collective-permute-start | bytes 393224 | tf_op jit(solution)/shard_map/ppermute | solution.py:137
  114.4 23.1 %all-to-all-done.2 = bf16[12,128,256]{2,1,0:T(8,128)(2,1)} async-done(((bf16[12,128,256]{2,1,0:T(8,128)(2,1)}), bf16[12,128,256]{2,1,0:T(8,128)(2,1)}, u32[]{:S(2)}, u32[]{:S(2)}) %all-to-all-start.2) | async-done | bytes 786464 | tf_op jit(solution)/shard_map/all_to_all | solution.py:180
  137.4 1.3 fusion.4
  138.7 1.9 %collective-permute-start.6 = (bf16[128,256]{1,0:T(8,128)(2,1)S(1)}, bf16[128,256]{1,0:T(8,128)(2,1)S(1)}, u32[]{:S(2)}, u32[]{:S(2)}) collective-permute-start(bf16[128,256]{1,0:T(8,128)(2,1)S(1)} %fusion.4), channel_id=1, source_target_pairs={{0,0},{1,64},{2,128},{3,192},{64,1},{65,65},{66,129},{67,193},{128... | collective-permute-start | bytes 196616 | tf_op jit(solution)/shard_map/ppermute | solution.py:133
  140.6 0.0 collective-permute-done.5.refs_3_
  140.6 0.0 collective-permute-done.4.refs_2_
  140.7 0.0 collective-permute-done.3.refs_1_
  140.7 0.0 copy-done.3
  140.7 0.0 copy-done.5
  140.7 0.0 copy-done.7
  140.7 2.2 %shard_map.105 = (bf16[512,128]{1,0:T(8,128)(2,1)}, bf16[512,128]{1,0:T(8,128)(2,1)}, bf16[512,128]{1,0:T(8,128)(2,1)}) custom-call(bf16[512,128]{1,0:T(8,128)(2,1)S(1)} %copy-done.3, bf16[512,128]{1,0:T(8,128)(2,1)S(1)} %copy-done.5, bf16[512,128]{1,0:T(8,128)(2,1)S(1)} %copy-done.7, f32[1,128]{1,0:T(1,128)S(1)} %bitcast.22, f32[1,128]{1,0:T(1,128)S(1)} %bitcast.24, ...), custom_call_target="tpu_custom_call" | custom-call | flops 167772160 | bytes 2097152 | tf_op jit(solution)/shard_map/pallas_call | solution.py:121
  142.9 5.3 %collective-permute-done.6 = bf16[128,256]{1,0:T(8,128)(2,1)S(1)} collective-permute-done((bf16[128,256]{1,0:T(8,128)(2,1)S(1)}, bf16[128,256]{1,0:T(8,128)(2,1)S(1)}, u32[]{:S(2)}, u32[]{:S(2)}) %collective-permute-start.6) | collective-permute-done | bytes 65568 | tf_op jit(solution)/shard_map/ppermute | solution.py:133
  148.2 0.6 copy.12
  (10 shorter events, 0.0 us)
Async XLA Ops:
  7.2 80.7 %all-gather.4.cloned.1.call-start = ((), (), s32[]{:S(2)}) async-start(), calls=%async_computation.3 | async-start | bytes 1769472 | tf_op jit(solution)/shard_map/all_gather | solution.py:153
  7.2 0.9 copy-start.8
  19.9 0.9 copy-start.2
  20.8 0.9 copy-start.4
  21.7 0.9 copy-start.6
  22.6 0.7 copy-start.9
  23.2 0.7 copy-start.11
  24.7 10.7 %collective-permute-start.1 = (bf16[128,256]{1,0:T(8,128)(2,1)}, bf16[128,256]{1,0:T(8,128)(2,1)S(1)}, u32[]{:S(2)}, u32[]{:S(2)}) collective-permute-start(bf16[128,256]{1,0:T(8,128)(2,1)} %param.12), channel_id=1, source_target_pairs={{0,0},{1,64},{2,128},{3,192},{64,1},{65,65},{66,129},{67,193},{128... | collective-permute-start | bytes 196616 | tf_op jit(solution)/shard_map/ppermute | solution.py:133
  36.4 51.5 %all-to-all-start.1 = ((bf16[12,128,256]{2,1,0:T(8,128)(2,1)}), bf16[12,128,256]{2,1,0:T(8,128)(2,1)S(1)}, u32[]{:S(2)}, u32[]{:S(2)}) async-start(bf16[12,128,256]{2,1,0:T(8,128)(2,1)} %broadcast_in_dim.2), calls=%async_computation.1 | async-start | bytes 1572864 | tf_op jit(solution)/shard_map/all_to_all | solution.py:166
  84.1 3.8 %collective-permute-start = (bf16[4,128,512]{2,1,0:T(8,128)(2,1)S(1)}, bf16[4,128,512]{2,1,0:T(8,128)(2,1)S(1)}, u32[]{:S(2)}, u32[]{:S(2)}) collective-permute-start(bf16[4,128,512]{2,1,0:T(8,128)(2,1)S(1)} %bitcast.16), channel_id=1, source_target_pairs={{0,32},{32,0},{1,33},{33,1},{2,34},{34,2},{3,35},{35,3},{4,36},{36... | collective-permute-start | bytes 1572872 | tf_op jit(solution)/shard_map/ppermute | solution.py:141
  87.9 1.4 copy-start
  91.2 8.2 %copy-start.1 = (bf16[64,16,768]{2,1,0:T(8,128)(2,1)S(1)}, bf16[64,16,768]{2,1,0:T(8,128)(2,1)}, u32[]{:S(2)}) copy-start(bf16[64,16,768]{2,1,0:T(8,128)(2,1)} %all-gather.4.cloned.1.call-done) | copy-start | bytes 4718596
  91.2 46.3 %all-to-all-start.2 = ((bf16[12,128,256]{2,1,0:T(8,128)(2,1)}), bf16[12,128,256]{2,1,0:T(8,128)(2,1)}, u32[]{:S(2)}, u32[]{:S(2)}) async-start(bf16[12,128,256]{2,1,0:T(8,128)(2,1)} %bitcast.9), calls=%async_computation.2 | async-start | bytes 1572864 | tf_op jit(solution)/shard_map/all_to_all | solution.py:180
  100.4 40.3 %copy-start.3 = (bf16[512,128]{1,0:T(8,128)(2,1)S(1)}, bf16[512,128]{1,0:T(8,128)(2,1)}, u32[]{:S(2)}) copy-start(bf16[512,128]{1,0:T(8,128)(2,1)} %q_ref.3) | copy-start | bytes 393220
  100.4 40.3 %copy-start.5 = (bf16[512,128]{1,0:T(8,128)(2,1)S(1)}, bf16[512,128]{1,0:T(8,128)(2,1)}, u32[]{:S(2)}) copy-start(bf16[512,128]{1,0:T(8,128)(2,1)} %k_ref.3) | copy-start | bytes 393220
  100.4 40.2 %copy-start.7 = (bf16[512,128]{1,0:T(8,128)(2,1)S(1)}, bf16[512,128]{1,0:T(8,128)(2,1)}, u32[]{:S(2)}) copy-start(bf16[512,128]{1,0:T(8,128)(2,1)} %v_ref.3) | copy-start | bytes 393220
  100.5 40.2 %copy-start.10 = (f32[128]{0:T(128)S(1)}, f32[128]{0:T(128)}, u32[]{:S(2)}) copy-start(f32[128]{0:T(128)} %param.10) | copy-start | bytes 1540
  100.5 40.2 %copy-start.12 = (f32[128]{0:T(128)S(1)}, f32[128]{0:T(128)}, u32[]{:S(2)}) copy-start(f32[128]{0:T(128)} %param.11) | copy-start | bytes 1540
  100.5 3.9 %collective-permute-start.2 = (bf16[4,512,128]{2,1,0:T(8,128)(2,1)S(1)}, bf16[4,512,128]{2,1,0:T(8,128)(2,1)S(1)}, u32[]{:S(2)}, u32[]{:S(2)}) collective-permute-start(bf16[4,512,128]{2,1,0:T(8,128)(2,1)S(1)} %get-tuple-element.24), channel_id=1, source_target_pairs={{0,32},{32,0},{1,33},{33,1},{2,34},{34,2},{3,35},{35,3},{4,36},{36... | collective-permute-start | bytes 1572872 | tf_op jit(solution)/shard_map/ppermute | solution.py:141
  104.5 36.1 %collective-permute-start.5 = (bf16[512,128]{1,0:T(8,128)(2,1)S(1)}, bf16[512,128]{1,0:T(8,128)(2,1)S(1)}, u32[]{:S(2)}, u32[]{:S(2)}) collective-permute-start(bf16[512,128]{1,0:T(8,128)(2,1)S(1)} %get-tuple-element.30), channel_id=1, source_target_pairs={{0,3},{1,2},{2,1},{3,0},{4,7},{5,6},{6,5},{7,4},{8,11},{9,10},{10,... | collective-permute-start | bytes 393224 | tf_op jit(solution)/shard_map/ppermute | solution.py:137
  107.1 33.6 %collective-permute-start.4 = (bf16[512,128]{1,0:T(8,128)(2,1)S(1)}, bf16[512,128]{1,0:T(8,128)(2,1)S(1)}, u32[]{:S(2)}, u32[]{:S(2)}) collective-permute-start(bf16[512,128]{1,0:T(8,128)(2,1)S(1)} %get-tuple-element.31), channel_id=1, source_target_pairs={{0,2},{1,3},{2,0},{3,1},{4,6},{5,7},{6,4},{7,5},{8,10},{9,11},{10,... | collective-permute-start | bytes 393224 | tf_op jit(solution)/shard_map/ppermute | solution.py:137
  112.5 28.2 %collective-permute-start.3 = (bf16[512,128]{1,0:T(8,128)(2,1)S(1)}, bf16[512,128]{1,0:T(8,128)(2,1)S(1)}, u32[]{:S(2)}, u32[]{:S(2)}) collective-permute-start(bf16[512,128]{1,0:T(8,128)(2,1)S(1)} %get-tuple-element.32), channel_id=1, source_target_pairs={{0,1},{1,0},{2,3},{3,2},{4,5},{5,4},{6,7},{7,6},{8,9},{9,8},{10,11... | collective-permute-start | bytes 393224 | tf_op jit(solution)/shard_map/ppermute | solution.py:137
  138.7 9.5 %collective-permute-start.6 = (bf16[128,256]{1,0:T(8,128)(2,1)S(1)}, bf16[128,256]{1,0:T(8,128)(2,1)S(1)}, u32[]{:S(2)}, u32[]{:S(2)}) collective-permute-start(bf16[128,256]{1,0:T(8,128)(2,1)S(1)} %fusion.4), channel_id=1, source_target_pairs={{0,0},{1,64},{2,128},{3,192},{64,1},{65,65},{66,129},{67,193},{128... | collective-permute-start | bytes 196616 | tf_op jit(solution)/shard_map/ppermute | solution.py:133
Sparse Core Ops, SparseCore 0:
  20.0 47.4 all-gather.3

commit v6 on v5

--- a/solution.py
+++ b/solution.py
@@ -91,7 +91,7 @@
 
 
 def block(ref, side, zone):
-    columns = slice(zone * BLK, (zone + 1) * BLK)
+    columns = pl.ds(zone * BLK, BLK)
     return ref[:, pl.ds(side * NL, NL), :, columns].reshape(TOK, BLK)
 
 
@@ -108,13 +108,16 @@
 
 
 def weight_kernel(g_ref, own_ref, other_ref, out_ref):
-    core = lax.axis_index("core")
-    own = own_ref[...].reshape(NL * DH, TOK)
-    other = other_ref[...].reshape(NL * DH, TOK)
-    for zone in range(NZ):
+    here, core, low = (lax.axis_index(name) for name in ("zh", "core", "zl"))
+    own, other = (
+        jnp.concatenate([ref[low ^ head] for head in range(NL)], axis=0)
+        for ref in (own_ref, other_ref)
+    )
+    for step in range(NZ):
+        zone = lax.rem(here + step, NZ)
         total = dot(own, block(g_ref, core, zone), 1, 0)
         total = total + dot(other, block(g_ref, 1 - core, zone), 1, 0)
-        out_ref[zone] = total.reshape(NL, DH, BLK).astype(BF16)
+        out_ref[:, step] = total.reshape(NL, DH, BLK).astype(BF16)
 
 
 def call(kernel, outs, flops, moved, operands):
@@ -128,9 +131,16 @@
     )(*operands)
 
 
-def cross(entry):
-    pairs = [(at * NL + low, low * NL + at) for at in range(NX) for low in range(NL)]
-    return lax.ppermute(entry, ("x", "zl"), pairs)
+def cross(entry, shift):
+    pairs = []
+    for zone in range(NZ):
+        for across in range(NX):
+            for low in range(NL):
+                target = (zone + shift) % NZ
+                pairs.append(
+                    ((zone * NX + across) * NL + low, (target * NX + low) * NL + across)
+                )
+    return lax.ppermute(entry, ("zh", "x", "zl"), pairs)
 
 
 def flip(entry, step):
@@ -152,6 +162,12 @@
     exchanged = lax.all_to_all(pieces, ("core", "zl"), 0, 0, tiled=True)
     gathered = lax.all_gather(exchanged, "y", axis=0)
 
+    exchanged, out_weight = lax.optimization_barrier((exchanged, out_weight))
+    zones = NZ * NX
+    crossed = cross(out_weight, 0)
+    query_input, crossed = lax.optimization_barrier((query_input, crossed))
+    copies = jnp.broadcast_to(crossed[None], (zones, DH, BLK))
+    own = lax.all_to_all(copies, ("zh", "x"), 0, 0, tiled=True).reshape(NZ, NX, DH, BLK)
     mixed, attention = call(
         forward_kernel,
         (shape((DH, TOK), BF16), shape((IMAGES, PATCH, PATCH), F32)),
@@ -159,25 +175,11 @@
         1 << 20,
         (query_input, key_input, value_input, query_gain, key_gain),
     )
-    exchanged, out_weight, mixed = lax.optimization_barrier((exchanged, out_weight, mixed))
-    zones = NZ * NX
-    crossed = cross(out_weight)
-    copies = jnp.broadcast_to(crossed[None], (zones, DH, BLK))
-    own = lax.all_to_all(copies, ("zh", "x"), 0, 0, tiled=True).reshape(NZ, NX, DH, BLK)
-    mixed_own = lax.all_gather(mixed, "zl", axis=0)
+    mixed_own = jnp.stack([mixed] + [flip(mixed, step) for step in range(1, NL)])
     mixed_other = swap_cores(mixed_own)
     gathered, mixed_own, mixed_other, own = lax.optimization_barrier(
         (gathered, mixed_own, mixed_other, own)
     )
-
-    partial = call(
-        weight_kernel,
-        shape((NZ, NX, DH, BLK), BF16),
-        2 * TOK * NY * DH * WIDE,
-        5 << 20,
-        (gathered, mixed_own, mixed_other),
-    )
-    spread = lax.all_to_all(partial.reshape(zones, DH, BLK), ("zh", "x"), 0, 0, tiled=True)
 
     half = (NL, TOK, DH)
     keep, send = call(
@@ -187,11 +189,23 @@
         4 << 20,
         (gathered, own),
     )
+    gathered, send = lax.optimization_barrier((gathered, send))
+    partial = call(
+        weight_kernel,
+        shape((NL, NZ, DH, BLK), BF16),
+        2 * TOK * NY * DH * WIDE,
+        5 << 20,
+        (gathered, mixed_own, mixed_other),
+    )
+    spread = lax.all_to_all(partial, "x", 0, 0, tiled=True)
     received = swap_cores(send)
     summed = [(keep[step] + received[step].astype(F32)).astype(BF16) for step in range(NL)]
     grad_heads = [summed[0]] + [flip(summed[step], step) for step in range(1, NL)]
 
-    grad_weight = cross(sum(spread[part].astype(F32) for part in range(zones)).astype(BF16))
+    spread, *grad_heads = lax.optimization_barrier((spread, *grad_heads))
+    by_zone = sum(spread[part].astype(F32) for part in range(NX)).astype(BF16)
+    last = [cross(by_zone[shift], shift) for shift in range(NZ)]
+    grad_weight = sum(entry.astype(F32) for entry in last).astype(BF16)
 
     grad_query, grad_key, grad_value = call(
         backward_kernel,

time: 156 us -> 151 us (0.968)
  the two profiles are of different devices: /device:TPU:176 before, /device:TPU:224 now
where the time goes in v6:
time: 151 us; the launch traced here: 150 us
  starting transfers between devices  65.9 us (44%)
  waiting for transfers between devices  47.1 us (31%)
  between operations  14.3 us (9%)
  blocking collectives  9.9 us (7%)
  Pallas kernels  6.34 us (4%)
  local copies, waits for them, and re-layouts  4.18 us (3%)
  other arithmetic  2.68 us (2%)
    ppermute x6, waiting for transfers between devices, flip(): return lax.ppermute(entry, 'zl', [(at, at ^ step) for at in range(NL)])  28.6 us
    ppermute x4, starting transfers between devices, cross(): return lax.ppermute(entry, ('zh', 'x', 'zl'), pairs)  23.4 us
    ppermute x6, starting transfers between devices, flip(): return lax.ppermute(entry, 'zl', [(at, at ^ step) for at in range(NL)])  20.5 us
    ppermute x4, waiting for transfers between devices, cross(): return lax.ppermute(entry, ('zh', 'x', 'zl'), pairs)  15.8 us
    all_to_all x1, starting transfers between devices, shards(): lax.all_to_all(copies, ('zh', 'x'), 0, 0, tiled=True)  13.4 us
    all_to_all x1, blocking collectives, shards(): exchanged = lax.all_to_all(pieces, ('core', 'zl'), 0, 0, tiled=True)  9.9 us
    pallas_call x5, Pallas kernels, call(): pl.pallas_call(kernel, out_shape=outs, in_specs=[pl.BlockSpec(memory_spac...  6.34 us
    all_to_all x1, starting transfers between devices, shards(): spread = lax.all_to_all(partial, 'x', 0, 0, tiled=True)  4.54 us
  transfers between devices with their start and end apart: 15, of which 9 were waited for; matrix products, arithmetic and copies ran while one was open for 2% of the time, Pallas kernels for 3%

profile of v6, /device:TPU:224, one launch (start us, length us, event | category | flops | bytes accessed | tf_op | source)
XLA Modules:
  0.0 150.3 jit_solution(1639156937286352462)
XLA Ops:
  7.2 0.0 all-gather.3.cloned.1.call-start
  7.2 0.9 copy-done.6
  8.2 0.0 copy-start.1
  8.2 0.0 copy-start.2
  8.2 0.0 copy-start.3
  8.2 0.0 copy-start.7
  8.2 0.0 copy-start.8
  8.2 9.9 %all_to_all.15 = bf16[8,16,768]{2,1,0:T(8,128)(2,1)} all-to-all(bf16[8,16,768]{2,1,0:T(8,128)(2,1)S(1)} %shard_map.102), channel_id=1, replica_groups=mesh['zh'=3,'x'=4,'core'=2,'y'=8,'zl'=4] {'core','zl'}, dimensions={0} | all-to-all | bytes 393216 | tf_op jit(solution)/shard_map/all_to_all | solution.py:162
  18.1 0.0 all-gather.3.cloned.1.call-update
  18.1 7.3 %collective-permute-start = (bf16[128,256]{1,0:T(8,128)(2,1)}, bf16[128,256]{1,0:T(8,128)(2,1)S(1)}, u32[]{:S(2)}, u32[]{:S(2)}) collective-permute-start(bf16[128,256]{1,0:T(8,128)(2,1)} %param.12), channel_id=1, source_target_pairs={{0,0},{1,64},{2,128},{3,192},{64,1},{65,65},{66,129},{67,193},{128... | collective-permute-start | bytes 196616 | tf_op jit(solution)/shard_map/ppermute | solution.py:143
  25.4 3.1 %collective-permute-done = bf16[128,256]{1,0:T(8,128)(2,1)S(1)} collective-permute-done((bf16[128,256]{1,0:T(8,128)(2,1)}, bf16[128,256]{1,0:T(8,128)(2,1)S(1)}, u32[]{:S(2)}, u32[]{:S(2)}) %collective-permute-start) | collective-permute-done | bytes 65568 | tf_op jit(solution)/shard_map/ppermute | solution.py:143
  28.5 1.0 broadcast_in_dim.2
  29.5 13.4 %all-to-all-start.1 = ((bf16[12,128,256]{2,1,0:T(8,128)(2,1)}), bf16[12,128,256]{2,1,0:T(8,128)(2,1)S(1)}, u32[]{:S(2)}, u32[]{:S(2)}) async-start(bf16[12,128,256]{2,1,0:T(8,128)(2,1)} %broadcast_in_dim.2), calls=%async_computation.1 | async-start | bytes 1572864 | tf_op jit(solution)/shard_map/all_to_all | solution.py:170
  43.0 0.8 shard_map.103
  43.8 6.0 %collective-permute-start.3 = (bf16[128,512]{1,0:T(8,128)(2,1)S(1)}, bf16[128,512]{1,0:T(8,128)(2,1)S(1)}, u32[]{:S(2)}, u32[]{:S(2)}) collective-permute-start(bf16[128,512]{1,0:T(8,128)(2,1)S(1)} %get-tuple-element.28), channel_id=1, source_target_pairs={{0,3},{1,2},{2,1},{3,0},{4,7},{5,6},{6,5},{7,4},{8,11},{9,10},{10,... | collective-permute-start | bytes 393224 | tf_op jit(solution)/shard_map/ppermute | solution.py:147
  49.9 1.9 %collective-permute-start.2 = (bf16[128,512]{1,0:T(8,128)(2,1)S(1)}, bf16[128,512]{1,0:T(8,128)(2,1)S(1)}, u32[]{:S(2)}, u32[]{:S(2)}) collective-permute-start(bf16[128,512]{1,0:T(8,128)(2,1)S(1)} %get-tuple-element.28), channel_id=1, source_target_pairs={{0,2},{1,3},{2,0},{3,1},{4,6},{5,7},{6,4},{7,5},{8,10},{9,11},{10,... | collective-permute-start | bytes 393224 | tf_op jit(solution)/shard_map/ppermute | solution.py:147
  51.8 2.5 %collective-permute-start.1 = (bf16[128,512]{1,0:T(8,128)(2,1)S(1)}, bf16[128,512]{1,0:T(8,128)(2,1)S(1)}, u32[]{:S(2)}, u32[]{:S(2)}) collective-permute-start(bf16[128,512]{1,0:T(8,128)(2,1)S(1)} %get-tuple-element.28), channel_id=1, source_target_pairs={{0,1},{1,0},{2,3},{3,2},{4,5},{5,4},{6,7},{7,6},{8,9},{9,8},{10,11... | collective-permute-start | bytes 393224 | tf_op jit(solution)/shard_map/ppermute | solution.py:147
  54.3 17.4 %collective-permute-done.3 = bf16[128,512]{1,0:T(8,128)(2,1)S(1)} collective-permute-done((bf16[128,512]{1,0:T(8,128)(2,1)S(1)}, bf16[128,512]{1,0:T(8,128)(2,1)S(1)}, u32[]{:S(2)}, u32[]{:S(2)}) %collective-permute-start.3) | collective-permute-done | bytes 131104 | tf_op jit(solution)/shard_map/ppermute | solution.py:147
  71.6 6.2 %collective-permute-done.2 = bf16[128,512]{1,0:T(8,128)(2,1)S(1)} collective-permute-done((bf16[128,512]{1,0:T(8,128)(2,1)S(1)}, bf16[128,512]{1,0:T(8,128)(2,1)S(1)}, u32[]{:S(2)}, u32[]{:S(2)}) %collective-permute-start.2) | collective-permute-done | bytes 131104 | tf_op jit(solution)/shard_map/ppermute | solution.py:147
  77.8 0.0 collective-permute-done.1
  77.8 0.1 pad_maximum_fusion.own_ref
  77.9 1.9 %collective-permute-start.4 = (bf16[4,128,512]{2,1,0:T(8,128)(2,1)S(1)}, bf16[4,128,512]{2,1,0:T(8,128)(2,1)S(1)}, u32[]{:S(2)}, u32[]{:S(2)}) collective-permute-start(bf16[4,128,512]{2,1,0:T(8,128)(2,1)S(1)} %pad_maximum_fusion.own_ref), channel_id=1, source_target_pairs={{0,32},{32,0},{1,33},{33,1},{2,34},{34,2},{3,35},{35,3},{4,36},{36... | collective-permute-start | bytes 1572872 | tf_op jit(solution)/shard_map/ppermute | solution.py:151
  79.8 1.9 %collective-permute-done.4.other_ref = bf16[4,128,512]{2,1,0:T(8,128)(2,1)S(1)} collective-permute-done((bf16[4,128,512]{2,1,0:T(8,128)(2,1)S(1)}, bf16[4,128,512]{2,1,0:T(8,128)(2,1)S(1)}, u32[]{:S(2)}, u32[]{:S(2)}) %collective-permute-start.4) | collective-permute-done | bytes 524320 | tf_op jit(solution)/shard_map/ppermute | solution.py:151
  81.7 0.8 copy-done.4
  82.5 0.0 all-to-all-done.1
  82.5 1.4 copy-done
  84.0 1.4 shard_map.104
  85.4 2.0 %collective-permute-start.5 = (bf16[4,512,128]{2,1,0:T(8,128)(2,1)}, bf16[4,512,128]{2,1,0:T(8,128)(2,1)}, u32[]{:S(2)}, u32[]{:S(2)}) collective-permute-start(bf16[4,512,128]{2,1,0:T(8,128)(2,1)} %get-tuple-element.37), channel_id=1, source_target_pairs={{0,32},{32,0},{1,33},{33,1},{2,34},{34,2},{3,35},{35,3},{4,36},{36... | collective-permute-start | bytes 1572872 | tf_op jit(solution)/shard_map/ppermute | solution.py:151
  87.4 1.9 %shard_map.105 = bf16[4,3,128,256]{3,2,1,0:T(8,128)(2,1)} custom-call(bf16[8,8,16,768]{3,2,1,0:T(8,128)(2,1)S(1)} %bitcast.23, bf16[4,128,512]{2,1,0:T(8,128)(2,1)S(1)} %pad_maximum_fusion.own_ref, bf16[4,128,512]{2,1,0:T(8,128)(2,1)S(1)} %copy-done.5), custom_call_target="tpu_custom_call" | custom-call | flops 805306368 | bytes 5242880 | tf_op jit(solution)/shard_map/pallas_call | solution.py:124
  89.3 4.5 %all-to-all-start.2 = ((bf16[4,3,128,256]{3,2,1,0:T(8,128)(2,1)}), bf16[4,3,128,256]{3,2,1,0:T(8,128)(2,1)S(1)}, u32[]{:S(2)}, u32[]{:S(2)}) async-start(bf16[4,3,128,256]{3,2,1,0:T(8,128)(2,1)} %shard_map.105), calls=%async_computation.2 | async-start | bytes 1572864 | tf_op jit(solution)/shard_map/all_to_all | solution.py:200
  93.9 0.0 collective-permute-done.5
  93.9 1.9 %fusion.3 = (bf16[512,128]{1,0:T(8,128)(2,1)}, bf16[512,128]{1,0:T(8,128)(2,1)S(1)}, bf16[512,128]{1,0:T(8,128)(2,1)S(1)}, bf16[512,128]{1,0:T(8,128)(2,1)S(1)}) fusion(f32[4,512,128]{2,1,0:T(8,128)S(1)} %get-tuple-element.36, bf16[4,512,128]{2,1,0:T(8,128)(2,1)} %collective-permute-done.5), kind=kLoop, calls=%fused_computation.9 | loop fusion | flops 786432 | bytes 2097152 | tf_op jit(solution)/shard_map/convert_element_type | solution.py:202
  95.7 2.0 %collective-permute-start.8 = (bf16[512,128]{1,0:T(8,128)(2,1)}, bf16[512,128]{1,0:T(8,128)(2,1)S(1)}, u32[]{:S(2)}, u32[]{:S(2)}) collective-permute-start(bf16[512,128]{1,0:T(8,128)(2,1)} %get-tuple-element.46), channel_id=1, source_target_pairs={{0,3},{1,2},{2,1},{3,0},{4,7},{5,6},{6,5},{7,4},{8,11},{9,10},{10,... | collective-permute-start | bytes 393224 | tf_op jit(solution)/shard_map/ppermute | solution.py:147
  97.8 2.4 %collective-permute-start.7 = (bf16[512,128]{1,0:T(8,128)(2,1)S(1)}, bf16[512,128]{1,0:T(8,128)(2,1)S(1)}, u32[]{:S(2)}, u32[]{:S(2)}) collective-permute-start(bf16[512,128]{1,0:T(8,128)(2,1)S(1)} %get-tuple-element.47), channel_id=1, source_target_pairs={{0,2},{1,3},{2,0},{3,1},{4,6},{5,7},{6,4},{7,5},{8,10},{9,11},{10,... | collective-permute-start | bytes 393224 | tf_op jit(solution)/shard_map/ppermute | solution.py:147
  100.2 5.7 %collective-permute-start.6 = (bf16[512,128]{1,0:T(8,128)(2,1)S(1)}, bf16[512,128]{1,0:T(8,128)(2,1)S(1)}, u32[]{:S(2)}, u32[]{:S(2)}) collective-permute-start(bf16[512,128]{1,0:T(8,128)(2,1)S(1)} %get-tuple-element.48), channel_id=1, source_target_pairs={{0,1},{1,0},{2,3},{3,2},{4,5},{5,4},{6,7},{7,6},{8,9},{9,8},{10,11... | collective-permute-start | bytes 393224 | tf_op jit(solution)/shard_map/ppermute | solution.py:147
  105.9 0.8 all-to-all-done.2
  106.7 0.0 collective-permute-done.8.refs_3_
  106.7 4.1 %collective-permute-done.7.refs_2_ = bf16[512,128]{1,0:T(8,128)(2,1)S(1)} collective-permute-done((bf16[512,128]{1,0:T(8,128)(2,1)S(1)}, bf16[512,128]{1,0:T(8,128)(2,1)S(1)}, u32[]{:S(2)}, u32[]{:S(2)}) %collective-permute-start.7) | collective-permute-done | bytes 131104 | tf_op jit(solution)/shard_map/ppermute | solution.py:147
  110.8 0.9 collective-permute-done.6.refs_1_
  111.7 0.1 add_convert_fusion
  111.9 5.9 %collective-permute-start.9 = (bf16[128,256]{1,0:T(8,128)(2,1)S(1)}, bf16[128,256]{1,0:T(8,128)(2,1)S(1)}, u32[]{:S(2)}, u32[]{:S(2)}) collective-permute-start(bf16[128,256]{1,0:T(8,128)(2,1)S(1)} %get-tuple-element.50), channel_id=1, source_target_pairs={{0,0},{1,64},{2,128},{3,192},{64,1},{65,65},{66,129},{67,193},{128... | collective-permute-start | bytes 196616 | tf_op jit(solution)/shard_map/ppermute | solution.py:143
  117.7 8.3 %collective-permute-start.11 = (bf16[128,256]{1,0:T(8,128)(2,1)S(1)}, bf16[128,256]{1,0:T(8,128)(2,1)S(1)}, u32[]{:S(2)}, u32[]{:S(2)}) collective-permute-start(bf16[128,256]{1,0:T(8,128)(2,1)S(1)} %get-tuple-element.51), channel_id=1, source_target_pairs={{0,512},{1,576},{2,640},{3,704},{64,513},{65,577},{66,641},{67,705... | collective-permute-start | bytes 196616 | tf_op jit(solution)/shard_map/ppermute | solution.py:143
  126.1 1.9 %collective-permute-start.10 = (bf16[128,256]{1,0:T(8,128)(2,1)S(1)}, bf16[128,256]{1,0:T(8,128)(2,1)S(1)}, u32[]{:S(2)}, u32[]{:S(2)}) collective-permute-start(bf16[128,256]{1,0:T(8,128)(2,1)S(1)} %get-tuple-element.52), channel_id=1, source_target_pairs={{0,256},{1,320},{2,384},{3,448},{64,257},{65,321},{66,385},{67,449... | collective-permute-start | bytes 196616 | tf_op jit(solution)/shard_map/ppermute | solution.py:143
  128.0 2.2 %shard_map.106 = (bf16[512,128]{1,0:T(8,128)(2,1)}, bf16[512,128]{1,0:T(8,128)(2,1)}, bf16[512,128]{1,0:T(8,128)(2,1)}) custom-call(bf16[512,128]{1,0:T(8,128)(2,1)S(1)} %copy-done.1, bf16[512,128]{1,0:T(8,128)(2,1)S(1)} %copy-done.2, bf16[512,128]{1,0:T(8,128)(2,1)S(1)} %copy-done.3, f32[1,128]{1,0:T(1,128)S(1)} %bitcast.27, f32[1,128]{1,0:T(1,128)S(1)} %bitcast.29, ...), custom_call_target="tpu_custom_call" | custom-call | flops 167772160 | bytes 2097152 | tf_op jit(solution)/shard_map/pallas_call | solution.py:124
  130.2 0.0 collective-permute-done.9
  130.2 1.1 collective-permute-done.11
  131.3 11.5 %collective-permute-done.10 = bf16[128,256]{1,0:T(8,128)(2,1)S(1)} collective-permute-done((bf16[128,256]{1,0:T(8,128)(2,1)S(1)}, bf16[128,256]{1,0:T(8,128)(2,1)S(1)}, u32[]{:S(2)}, u32[]{:S(2)}) %collective-permute-start.10) | collective-permute-done | bytes 65568 | tf_op jit(solution)/shard_map/ppermute | solution.py:143
  142.8 0.7 add_convert_fusion.5
  (13 shorter events, 0.0 us)
Async XLA Ops:
  7.2 75.4 %all-gather.3.cloned.1.call-start = ((), (), s32[]{:S(2)}) async-start(), calls=%async_computation.3 | async-start | bytes 1769472 | tf_op jit(solution)/shard_map/all_gather | solution.py:163
  7.2 0.9 copy-start.6
  8.2 34.8 %copy-start.1 = (bf16[512,128]{1,0:T(8,128)(2,1)S(1)}, bf16[512,128]{1,0:T(8,128)(2,1)}, u32[]{:S(2)}) copy-start(bf16[512,128]{1,0:T(8,128)(2,1)} %q_ref.1) | copy-start | bytes 393220
  8.2 34.8 %copy-start.2 = (bf16[512,128]{1,0:T(8,128)(2,1)S(1)}, bf16[512,128]{1,0:T(8,128)(2,1)}, u32[]{:S(2)}) copy-start(bf16[512,128]{1,0:T(8,128)(2,1)} %k_ref.3) | copy-start | bytes 393220
  8.2 34.8 %copy-start.3 = (bf16[512,128]{1,0:T(8,128)(2,1)S(1)}, bf16[512,128]{1,0:T(8,128)(2,1)}, u32[]{:S(2)}) copy-start(bf16[512,128]{1,0:T(8,128)(2,1)} %v_ref.3) | copy-start | bytes 393220
  8.2 34.8 %copy-start.7 = (f32[128]{0:T(128)S(1)}, f32[128]{0:T(128)}, u32[]{:S(2)}) copy-start(f32[128]{0:T(128)} %param.10) | copy-start | bytes 1540
  8.2 34.8 %copy-start.8 = (f32[128]{0:T(128)S(1)}, f32[128]{0:T(128)}, u32[]{:S(2)}) copy-start(f32[128]{0:T(128)} %param.11) | copy-start | bytes 1540
  18.1 10.4 %collective-permute-start = (bf16[128,256]{1,0:T(8,128)(2,1)}, bf16[128,256]{1,0:T(8,128)(2,1)S(1)}, u32[]{:S(2)}, u32[]{:S(2)}) collective-permute-start(bf16[128,256]{1,0:T(8,128)(2,1)} %param.12), channel_id=1, source_target_pairs={{0,0},{1,64},{2,128},{3,192},{64,1},{65,65},{66,129},{67,193},{128... | collective-permute-start | bytes 196616 | tf_op jit(solution)/shard_map/ppermute | solution.py:143
  29.5 53.0 %all-to-all-start.1 = ((bf16[12,128,256]{2,1,0:T(8,128)(2,1)}), bf16[12,128,256]{2,1,0:T(8,128)(2,1)S(1)}, u32[]{:S(2)}, u32[]{:S(2)}) async-start(bf16[12,128,256]{2,1,0:T(8,128)(2,1)} %broadcast_in_dim.2), calls=%async_computation.1 | async-start | bytes 1572864 | tf_op jit(solution)/shard_map/all_to_all | solution.py:170
  43.8 27.8 %collective-permute-start.3 = (bf16[128,512]{1,0:T(8,128)(2,1)S(1)}, bf16[128,512]{1,0:T(8,128)(2,1)S(1)}, u32[]{:S(2)}, u32[]{:S(2)}) collective-permute-start(bf16[128,512]{1,0:T(8,128)(2,1)S(1)} %get-tuple-element.28), channel_id=1, source_target_pairs={{0,3},{1,2},{2,1},{3,0},{4,7},{5,6},{6,5},{7,4},{8,11},{9,10},{10,... | collective-permute-start | bytes 393224 | tf_op jit(solution)/shard_map/ppermute | solution.py:147
  49.9 28.0 %collective-permute-start.2 = (bf16[128,512]{1,0:T(8,128)(2,1)S(1)}, bf16[128,512]{1,0:T(8,128)(2,1)S(1)}, u32[]{:S(2)}, u32[]{:S(2)}) collective-permute-start(bf16[128,512]{1,0:T(8,128)(2,1)S(1)} %get-tuple-element.28), channel_id=1, source_target_pairs={{0,2},{1,3},{2,0},{3,1},{4,6},{5,7},{6,4},{7,5},{8,10},{9,11},{10,... | collective-permute-start | bytes 393224 | tf_op jit(solution)/shard_map/ppermute | solution.py:147
  51.8 26.1 %collective-permute-start.1 = (bf16[128,512]{1,0:T(8,128)(2,1)S(1)}, bf16[128,512]{1,0:T(8,128)(2,1)S(1)}, u32[]{:S(2)}, u32[]{:S(2)}) collective-permute-start(bf16[128,512]{1,0:T(8,128)(2,1)S(1)} %get-tuple-element.28), channel_id=1, source_target_pairs={{0,1},{1,0},{2,3},{3,2},{4,5},{5,4},{6,7},{7,6},{8,9},{9,8},{10,11... | collective-permute-start | bytes 393224 | tf_op jit(solution)/shard_map/ppermute | solution.py:147
  77.9 3.8 %collective-permute-start.4 = (bf16[4,128,512]{2,1,0:T(8,128)(2,1)S(1)}, bf16[4,128,512]{2,1,0:T(8,128)(2,1)S(1)}, u32[]{:S(2)}, u32[]{:S(2)}) collective-permute-start(bf16[4,128,512]{2,1,0:T(8,128)(2,1)S(1)} %pad_maximum_fusion.own_ref), channel_id=1, source_target_pairs={{0,32},{32,0},{1,33},{33,1},{2,34},{34,2},{3,35},{35,3},{4,36},{36... | collective-permute-start | bytes 1572872 | tf_op jit(solution)/shard_map/ppermute | solution.py:151
  81.7 0.8 copy-start.4
  82.5 1.4 copy-start
  84.0 3.5 %copy-start.5 = (bf16[4,128,512]{2,1,0:T(8,128)(2,1)S(1)}, bf16[4,128,512]{2,1,0:T(8,128)(2,1)}, u32[]{:S(2)}) copy-start(bf16[4,128,512]{2,1,0:T(8,128)(2,1)} %copy-done.4) | copy-start | bytes 1572868
  85.4 8.5 %collective-permute-start.5 = (bf16[4,512,128]{2,1,0:T(8,128)(2,1)}, bf16[4,512,128]{2,1,0:T(8,128)(2,1)}, u32[]{:S(2)}, u32[]{:S(2)}) collective-permute-start(bf16[4,512,128]{2,1,0:T(8,128)(2,1)} %get-tuple-element.37), channel_id=1, source_target_pairs={{0,32},{32,0},{1,33},{33,1},{2,34},{34,2},{3,35},{35,3},{4,36},{36... | collective-permute-start | bytes 1572872 | tf_op jit(solution)/shard_map/ppermute | solution.py:151
  89.3 17.3 %all-to-all-start.2 = ((bf16[4,3,128,256]{3,2,1,0:T(8,128)(2,1)}), bf16[4,3,128,256]{3,2,1,0:T(8,128)(2,1)S(1)}, u32[]{:S(2)}, u32[]{:S(2)}) async-start(bf16[4,3,128,256]{3,2,1,0:T(8,128)(2,1)} %shard_map.105), calls=%async_computation.2 | async-start | bytes 1572864 | tf_op jit(solution)/shard_map/all_to_all | solution.py:200
  95.7 11.0 %collective-permute-start.8 = (bf16[512,128]{1,0:T(8,128)(2,1)}, bf16[512,128]{1,0:T(8,128)(2,1)S(1)}, u32[]{:S(2)}, u32[]{:S(2)}) collective-permute-start(bf16[512,128]{1,0:T(8,128)(2,1)} %get-tuple-element.46), channel_id=1, source_target_pairs={{0,3},{1,2},{2,1},{3,0},{4,7},{5,6},{6,5},{7,4},{8,11},{9,10},{10,... | collective-permute-start | bytes 393224 | tf_op jit(solution)/shard_map/ppermute | solution.py:147
  97.8 13.1 %collective-permute-start.7 = (bf16[512,128]{1,0:T(8,128)(2,1)S(1)}, bf16[512,128]{1,0:T(8,128)(2,1)S(1)}, u32[]{:S(2)}, u32[]{:S(2)}) collective-permute-start(bf16[512,128]{1,0:T(8,128)(2,1)S(1)} %get-tuple-element.47), channel_id=1, source_target_pairs={{0,2},{1,3},{2,0},{3,1},{4,6},{5,7},{6,4},{7,5},{8,10},{9,11},{10,... | collective-permute-start | bytes 393224 | tf_op jit(solution)/shard_map/ppermute | solution.py:147
  100.2 11.6 %collective-permute-start.6 = (bf16[512,128]{1,0:T(8,128)(2,1)S(1)}, bf16[512,128]{1,0:T(8,128)(2,1)S(1)}, u32[]{:S(2)}, u32[]{:S(2)}) collective-permute-start(bf16[512,128]{1,0:T(8,128)(2,1)S(1)} %get-tuple-element.48), channel_id=1, source_target_pairs={{0,1},{1,0},{2,3},{3,2},{4,5},{5,4},{6,7},{7,6},{8,9},{9,8},{10,11... | collective-permute-start | bytes 393224 | tf_op jit(solution)/shard_map/ppermute | solution.py:147
  111.9 18.3 %collective-permute-start.9 = (bf16[128,256]{1,0:T(8,128)(2,1)S(1)}, bf16[128,256]{1,0:T(8,128)(2,1)S(1)}, u32[]{:S(2)}, u32[]{:S(2)}) collective-permute-start(bf16[128,256]{1,0:T(8,128)(2,1)S(1)} %get-tuple-element.50), channel_id=1, source_target_pairs={{0,0},{1,64},{2,128},{3,192},{64,1},{65,65},{66,129},{67,193},{128... | collective-permute-start | bytes 196616 | tf_op jit(solution)/shard_map/ppermute | solution.py:143
  117.7 13.5 %collective-permute-start.11 = (bf16[128,256]{1,0:T(8,128)(2,1)S(1)}, bf16[128,256]{1,0:T(8,128)(2,1)S(1)}, u32[]{:S(2)}, u32[]{:S(2)}) collective-permute-start(bf16[128,256]{1,0:T(8,128)(2,1)S(1)} %get-tuple-element.51), channel_id=1, source_target_pairs={{0,512},{1,576},{2,640},{3,704},{64,513},{65,577},{66,641},{67,705... | collective-permute-start | bytes 196616 | tf_op jit(solution)/shard_map/ppermute | solution.py:143
  126.1 16.7 %collective-permute-start.10 = (bf16[128,256]{1,0:T(8,128)(2,1)S(1)}, bf16[128,256]{1,0:T(8,128)(2,1)S(1)}, u32[]{:S(2)}, u32[]{:S(2)}) collective-permute-start(bf16[128,256]{1,0:T(8,128)(2,1)S(1)} %get-tuple-element.52), channel_id=1, source_target_pairs={{0,256},{1,320},{2,384},{3,448},{64,257},{65,321},{66,385},{67,449... | collective-permute-start | bytes 196616 | tf_op jit(solution)/shard_map/ppermute | solution.py:143
Sparse Core Ops, SparseCore 0:
  18.3 48.3 all-gather.2

commit v7 on v4

--- a/solution.py
+++ b/solution.py
@@ -70,10 +70,7 @@
 ):
     for image in range(IMAGES):
         rows = pl.ds(image * PATCH, PATCH)
-        total = gh_ref[0, rows, :].astype(F32)
-        for part in range(1, NL):
-            total = total + gh_ref[part, rows, :].astype(F32)
-        grad_heads = total.astype(BF16)
+        grad_heads = gh_ref[rows, :]
         query_unit, query_inv = normalize(q_ref[rows, :])
         key_unit, key_inv = normalize(k_ref[rows, :])
         query_low = (query_unit * qg_ref[...]).astype(BF16)
@@ -94,16 +91,16 @@
     return ref[:, pl.ds(side * NL, NL), :, columns].reshape(TOK, BLK)
 
 
-def heads_kernel(g_ref, own_ref, keep_ref, send_ref):
-    here, core = lax.axis_index("zh"), lax.axis_index("core")
-    for ref, side in ((send_ref, 1 - core), (keep_ref, core)):
+def heads_kernel(g_ref, own_ref, out_ref):
+    here = lax.axis_index("zh")
+    for side in range(NC):
         total = None
         for step in range(NZ):
             rows = block(g_ref, side, lax.rem(here + NZ - step, NZ))
             term = dot(rows, own_ref[:, step].reshape(NL * DH, BLK), 1, 1)
             total = term if total is None else total + term
         for head in range(NL):
-            ref[head] = total[:, head * DH : (head + 1) * DH].astype(ref.dtype)
+            out_ref[side * NL + head] = total[:, head * DH : (head + 1) * DH].astype(BF16)
 
 
 def weight_kernel(g_ref, own_ref, other_ref, out_ref):
@@ -167,17 +164,24 @@
         1 << 20,
         (query_input, key_input, value_input, query_gain, key_gain),
     )
-    exchanged, out_weight, mixed = lax.optimization_barrier((exchanged, out_weight, mixed))
+    exchanged, out_weight = lax.optimization_barrier((exchanged, out_weight))
+    moved = [cross(out_weight, shift) for shift in range(NZ)]
+    mixed, *moved = lax.optimization_barrier((mixed, *moved))
     mixed_own = share(mixed, "zl", NL)
-    moved = [cross(out_weight, shift) for shift in range(NZ)]
-    mixed_own, *moved = lax.optimization_barrier((mixed_own, *moved))
-    moved = jnp.stack(moved)
+    own = lax.all_gather(jnp.stack(moved), "x", axis=0)
+    mixed_own, own = lax.optimization_barrier((mixed_own, own))
     mixed_other = swap_cores(mixed_own)
-    own = lax.all_gather(moved, "x", axis=0)
-    gathered, mixed_own, mixed_other, own = lax.optimization_barrier(
-        (gathered, mixed_own, mixed_other, own)
-    )
-
+    gathered, own, mixed_other = lax.optimization_barrier((gathered, own, mixed_other))
+
+    heads = call(
+        heads_kernel,
+        shape((groups, TOK, DH), BF16),
+        2 * TOK * NY * DH * WIDE,
+        4 << 20,
+        (gathered, own),
+    )
+    gathered, heads = lax.optimization_barrier((gathered, heads))
+    grad_heads = lax.psum_scatter(heads, ("core", "zl"), scatter_dimension=0, tiled=True)
     partial = call(
         weight_kernel,
         shape((NL, NZ, DH, BLK), BF16),
@@ -186,19 +190,6 @@
         (gathered, mixed_own, mixed_other),
     )
     spread = lax.all_to_all(partial, "x", 0, 0, tiled=True)
-
-    half = (NL, TOK, DH)
-    keep, send = call(
-        heads_kernel,
-        (shape(half, F32), shape(half, BF16)),
-        2 * TOK * NY * DH * WIDE,
-        4 << 20,
-        (gathered, own),
-    )
-    received = swap_cores(send)
-    summed = (keep + received.astype(F32)).astype(BF16)
-    grad_heads = lax.all_to_all(summed, "zl", 0, 0, tiled=True)
-
     by_zone = sum(spread[part].astype(F32) for part in range(NX)).astype(BF16)
     last = [cross(by_zone[shift], shift) for shift in range(NZ)]
     grad_weight = sum(entry.astype(F32) for entry in last).astype(BF16)
@@ -208,7 +199,7 @@
         (shape((TOK, DH), BF16),) * 3,
         5 * 2 * IMAGES * PATCH * PATCH * DH,
         2 << 20,
-        (query_input, key_input, value_input, query_gain, key_gain, attention, grad_heads),
+        (query_input, key_input, value_input, query_gain, key_gain, attention, grad_heads.reshape(TOK, DH)),
     )
     return grad_query, grad_key, grad_value, grad_weight
 

time: 150 us -> 144 us (0.960)
  the two profiles are of different devices: /device:TPU:39 before, /device:TPU:1 now
where the time goes in v7:
time: 144 us
  blocking collectives  47.3 us (33%)
  starting transfers between devices  36.5 us (25%)
  waiting for transfers between devices  29.1 us (20%)
  between operations  14.2 us (10%)
  local copies, waits for them, and re-layouts  9.96 us (7%)
  Pallas kernels  5.97 us (4%)
    all_to_all x1, blocking collectives, shards(): exchanged = lax.all_to_all(pieces, ('core', 'zl'), 0, 0, tiled=True)  21.2 us
    ppermute x6, starting transfers between devices, cross(): return lax.ppermute(entry, ('zh', 'x', 'zl'), pairs)  20.5 us
    reduce_scatter x1, waiting for transfers between devices, shards(): lax.psum_scatter(heads, ('core', 'zl'), scatter_dimension=0, tiled=True)  18.2 us
    all_to_all x1, blocking collectives, shards(): spread = lax.all_to_all(partial, 'x', 0, 0, tiled=True)  14.4 us
    all_to_all x1, starting transfers between devices, share(): return lax.all_to_all(copies, axis, 0, 0, tiled=True)  12.4 us
    all_gather x1, blocking collectives, shards(): own = lax.all_gather(jnp.stack(moved), 'x', axis=0)  11.6 us
    unnamed x32, local copies, waits for them, and re-layouts  9.11 us
    ppermute x6, waiting for transfers between devices, cross(): return lax.ppermute(entry, ('zh', 'x', 'zl'), pairs)  7.08 us
  transfers between devices with their start and end apart: 10, of which 5 were waited for; matrix products, arithmetic and copies ran while one was open for 1% of the time, Pallas kernels for 1%

profile of v7, /device:TPU:1, one launch (start us, length us, event | category | flops | bytes accessed | tf_op | source)
XLA Modules:
  0.0 143.9 jit_solution(8051501534659283522)
XLA Ops:
  7.2 0.0 all-gather.4.cloned.1.call-start
  7.2 0.0 copy-start.10
  7.2 0.9 copy-done.10
  8.2 21.2 %all_to_all.15 = bf16[8,16,768]{2,1,0:T(8,128)(2,1)} all-to-all(bf16[8,16,768]{2,1,0:T(8,128)(2,1)S(1)} %shard_map.103), channel_id=1, replica_groups=mesh['zh'=3,'x'=4,'core'=2,'y'=8,'zl'=4] {'core','zl'}, dimensions={0} | all-to-all | bytes 393216 | tf_op jit(solution)/shard_map/all_to_all | solution.py:157
  29.4 0.0 all-gather.4.cloned.1.call-update
  29.4 6.7 %collective-permute-start.2 = (bf16[128,256]{1,0:T(8,128)(2,1)}, bf16[128,256]{1,0:T(8,128)(2,1)S(1)}, u32[]{:S(2)}, u32[]{:S(2)}) collective-permute-start(bf16[128,256]{1,0:T(8,128)(2,1)} %param.12), channel_id=1, source_target_pairs={{0,512},{1,576},{2,640},{3,704},{64,513},{65,577},{66,641},{67,705... | collective-permute-start | bytes 196616 | tf_op jit(solution)/shard_map/ppermute | solution.py:137
  36.1 2.5 %collective-permute-start.1 = (bf16[128,256]{1,0:T(8,128)(2,1)}, bf16[128,256]{1,0:T(8,128)(2,1)S(1)}, u32[]{:S(2)}, u32[]{:S(2)}) collective-permute-start(bf16[128,256]{1,0:T(8,128)(2,1)} %param.12), channel_id=1, source_target_pairs={{0,256},{1,320},{2,384},{3,448},{64,257},{65,321},{66,385},{67,449... | collective-permute-start | bytes 196616 | tf_op jit(solution)/shard_map/ppermute | solution.py:137
  38.6 1.5 %collective-permute-start = (bf16[128,256]{1,0:T(8,128)(2,1)}, bf16[128,256]{1,0:T(8,128)(2,1)S(1)}, u32[]{:S(2)}, u32[]{:S(2)}) collective-permute-start(bf16[128,256]{1,0:T(8,128)(2,1)} %param.12), channel_id=1, source_target_pairs={{0,0},{1,64},{2,128},{3,192},{64,1},{65,65},{66,129},{67,193},{128... | collective-permute-start | bytes 196616 | tf_op jit(solution)/shard_map/ppermute | solution.py:137
  40.1 0.9 copy-done.2
  41.0 0.9 copy-done.4
  41.9 0.9 copy-done.6
  42.8 0.7 copy-done.12
  43.5 0.7 copy-done.14
  44.1 0.8 shard_map.102
  45.0 0.0 collective-permute-done.2
  45.0 0.2 collective-permute-done.1
  45.2 0.0 collective-permute-done
  45.2 0.8 broadcast_in_dim.2
  46.1 12.4 %all-to-all-start.1 = ((bf16[4,128,512]{2,1,0:T(8,128)(2,1)}), bf16[4,128,512]{2,1,0:T(8,128)(2,1)S(1)}, u32[]{:S(2)}, u32[]{:S(2)}) async-start(bf16[4,128,512]{2,1,0:T(8,128)(2,1)} %broadcast_in_dim.2), calls=%async_computation.1 | async-start | bytes 1048576 | tf_op jit(solution)/shard_map/all_to_all | solution.py:142
  58.5 0.0 reduce-scatter.2.cloned.1.call-start
  58.5 11.6 %all-gather.1 = bf16[12,128,256]{2,1,0:T(8,128)(2,1)S(1)} all-gather(bf16[3,128,256]{2,1,0:T(8,128)(2,1)S(1)} %pad_maximum_fusion), channel_id=3, replica_groups=mesh['zh'=3,'x'=4,'core'=2,'y'=8,'zl'=4] {'x'}, dimensions={0}, use_global_device_ids=true | all-gather | bytes 983040 | tf_op jit(solution)/shard_map/all_gather | solution.py:171
  70.1 2.3 %all-to-all-done.1.own_ref = bf16[4,128,512]{2,1,0:T(8,128)(2,1)S(1)} async-done(((bf16[4,128,512]{2,1,0:T(8,128)(2,1)}), bf16[4,128,512]{2,1,0:T(8,128)(2,1)S(1)}, u32[]{:S(2)}, u32[]{:S(2)}) %all-to-all-start.1) | async-done | bytes 524320 | tf_op jit(solution)/shard_map/all_to_all | solution.py:142
  72.5 3.5 %collective-permute-start.3 = (bf16[4,128,512]{2,1,0:T(8,128)(2,1)S(1)}, bf16[4,128,512]{2,1,0:T(8,128)(2,1)S(1)}, u32[]{:S(2)}, u32[]{:S(2)}) collective-permute-start(bf16[4,128,512]{2,1,0:T(8,128)(2,1)S(1)} %all-to-all-done.1.own_ref), channel_id=1, source_target_pairs={{0,32},{32,0},{1,33},{33,1},{2,34},{34,2},{3,35},{35,3},{4,36},{36... | collective-permute-start | bytes 1572872 | tf_op jit(solution)/shard_map/ppermute | solution.py:146
  76.0 1.5 %collective-permute-done.3.other_ref = bf16[4,128,512]{2,1,0:T(8,128)(2,1)S(1)} collective-permute-done((bf16[4,128,512]{2,1,0:T(8,128)(2,1)S(1)}, bf16[4,128,512]{2,1,0:T(8,128)(2,1)S(1)}, u32[]{:S(2)}, u32[]{:S(2)}) %collective-permute-start.3) | collective-permute-done | bytes 524320 | tf_op jit(solution)/shard_map/ppermute | solution.py:146
  77.5 0.8 copy-done.8
  78.3 1.4 copy-done
  79.7 2.0 %shard_map.104 = bf16[8,512,128]{2,1,0:T(8,128)(2,1)} custom-call(bf16[8,8,16,768]{3,2,1,0:T(8,128)(2,1)S(1)} %bitcast.14, bf16[4,3,128,256]{3,2,1,0:T(8,128)(2,1)S(1)} %bitcast.16), custom_call_target="tpu_custom_call" | custom-call | flops 805306368 | bytes 4194304 | tf_op jit(solution)/shard_map/pallas_call | solution.py:118
  81.7 0.0 reduce-scatter.2.cloned.1.call-update
  81.7 1.0 copy-done.9
  82.8 1.0 shard_map.106
  83.7 0.0 copy-start.3
  83.8 0.0 copy-start.5
  83.8 0.0 copy-start.7
  83.8 0.0 copy-start.13
  83.8 0.0 copy-start.15
  83.8 14.4 %all_to_all.16 = bf16[4,3,128,256]{3,2,1,0:T(8,128)(2,1)S(1)} all-to-all(bf16[4,3,128,256]{3,2,1,0:T(8,128)(2,1)S(1)} %shard_map.106), channel_id=1, replica_groups=mesh['zh'=3,'x'=4,'core'=2,'y'=8,'zl'=4] {'x'}, dimensions={0} | all-to-all | bytes 1572864 | tf_op jit(solution)/shard_map/all_to_all | solution.py:192
  98.3 0.1 add_convert_fusion
  98.4 0.7 collective-permute-start.4
  99.0 7.0 %collective-permute-start.6 = (bf16[128,256]{1,0:T(8,128)(2,1)S(1)}, bf16[128,256]{1,0:T(8,128)(2,1)S(1)}, u32[]{:S(2)}, u32[]{:S(2)}) collective-permute-start(bf16[128,256]{1,0:T(8,128)(2,1)S(1)} %get-tuple-element.39), channel_id=1, source_target_pairs={{0,512},{1,576},{2,640},{3,704},{64,513},{65,577},{66,641},{67,705... | collective-permute-start | bytes 196616 | tf_op jit(solution)/shard_map/ppermute | solution.py:137
  106.0 2.2 %collective-permute-start.5 = (bf16[128,256]{1,0:T(8,128)(2,1)S(1)}, bf16[128,256]{1,0:T(8,128)(2,1)S(1)}, u32[]{:S(2)}, u32[]{:S(2)}) collective-permute-start(bf16[128,256]{1,0:T(8,128)(2,1)S(1)} %get-tuple-element.40), channel_id=1, source_target_pairs={{0,256},{1,320},{2,384},{3,448},{64,257},{65,321},{66,385},{67,449... | collective-permute-start | bytes 196616 | tf_op jit(solution)/shard_map/ppermute | solution.py:137
  108.3 0.0 collective-permute-done.4
  108.3 0.0 collective-permute-done.6
  108.3 6.8 %collective-permute-done.5 = bf16[128,256]{1,0:T(8,128)(2,1)S(1)} collective-permute-done((bf16[128,256]{1,0:T(8,128)(2,1)S(1)}, bf16[128,256]{1,0:T(8,128)(2,1)S(1)}, u32[]{:S(2)}, u32[]{:S(2)}) %collective-permute-start.5) | collective-permute-done | bytes 65568 | tf_op jit(solution)/shard_map/ppermute | solution.py:137
  115.1 0.7 add_convert_fusion.1
  115.8 18.2 %reduce-scatter.2.cloned.1.call-done = bf16[1,512,128]{2,1,0:T(8,128)(2,1)} async-done(((bf16[8,512,128]{2,1,0:T(8,128)(2,1)}), bf16[1,512,128]{2,1,0:T(8,128)(2,1)}) %reduce-scatter.2.cloned.1.call-update) | async-done | bytes 131088 | tf_op jit(solution)/shard_map/reduce_scatter | solution.py:184
  133.9 0.0 copy-done.5
  134.0 0.9 copy-done.11
  134.9 2.1 %shard_map.105 = (bf16[512,128]{1,0:T(8,128)(2,1)}, bf16[512,128]{1,0:T(8,128)(2,1)}, bf16[512,128]{1,0:T(8,128)(2,1)}) custom-call(bf16[512,128]{1,0:T(8,128)(2,1)S(1)} %copy-done.3, bf16[512,128]{1,0:T(8,128)(2,1)S(1)} %copy-done.5, bf16[512,128]{1,0:T(8,128)(2,1)S(1)} %copy-done.7, f32[1,128]{1,0:T(1,128)S(1)} %bitcast.19, f32[1,128]{1,0:T(1,128)S(1)} %bitcast.21, ...), custom_call_target="tpu_custom_call" | custom-call | flops 167772160 | bytes 2097152 | tf_op jit(solution)/shard_map/pallas_call | solution.py:118
  (19 shorter events, 0.1 us)
Async XLA Ops:
  7.2 71.1 %all-gather.4.cloned.1.call-start = ((), (), s32[]{:S(2)}) async-start(), calls=%async_computation.5 | async-start | bytes 1769472 | tf_op jit(solution)/shard_map/all_gather | solution.py:158
  7.2 0.9 copy-start.10
  29.4 15.6 %collective-permute-start.2 = (bf16[128,256]{1,0:T(8,128)(2,1)}, bf16[128,256]{1,0:T(8,128)(2,1)S(1)}, u32[]{:S(2)}, u32[]{:S(2)}) collective-permute-start(bf16[128,256]{1,0:T(8,128)(2,1)} %param.12), channel_id=1, source_target_pairs={{0,512},{1,576},{2,640},{3,704},{64,513},{65,577},{66,641},{67,705... | collective-permute-start | bytes 196616 | tf_op jit(solution)/shard_map/ppermute | solution.py:137
  36.1 9.1 %collective-permute-start.1 = (bf16[128,256]{1,0:T(8,128)(2,1)}, bf16[128,256]{1,0:T(8,128)(2,1)S(1)}, u32[]{:S(2)}, u32[]{:S(2)}) collective-permute-start(bf16[128,256]{1,0:T(8,128)(2,1)} %param.12), channel_id=1, source_target_pairs={{0,256},{1,320},{2,384},{3,448},{64,257},{65,321},{66,385},{67,449... | collective-permute-start | bytes 196616 | tf_op jit(solution)/shard_map/ppermute | solution.py:137
  38.6 6.6 %collective-permute-start = (bf16[128,256]{1,0:T(8,128)(2,1)}, bf16[128,256]{1,0:T(8,128)(2,1)S(1)}, u32[]{:S(2)}, u32[]{:S(2)}) collective-permute-start(bf16[128,256]{1,0:T(8,128)(2,1)} %param.12), channel_id=1, source_target_pairs={{0,0},{1,64},{2,128},{3,192},{64,1},{65,65},{66,129},{67,193},{128... | collective-permute-start | bytes 196616 | tf_op jit(solution)/shard_map/ppermute | solution.py:137
  40.1 0.9 copy-start.2
  41.0 0.9 copy-start.4
  41.9 0.9 copy-start.6
  42.8 0.7 copy-start.12
  43.5 0.7 copy-start.14
  46.1 26.4 %all-to-all-start.1 = ((bf16[4,128,512]{2,1,0:T(8,128)(2,1)}), bf16[4,128,512]{2,1,0:T(8,128)(2,1)S(1)}, u32[]{:S(2)}, u32[]{:S(2)}) async-start(bf16[4,128,512]{2,1,0:T(8,128)(2,1)} %broadcast_in_dim.2), calls=%async_computation.1 | async-start | bytes 1048576 | tf_op jit(solution)/shard_map/all_to_all | solution.py:142
  58.5 75.5 %reduce-scatter.2.cloned.1.call-start = ((), (), s32[]{:S(2)}) async-start(), calls=%async_computation.4 | async-start | bytes 1179648 | tf_op jit(solution)/shard_map/reduce_scatter | solution.py:184
  72.5 5.0 %collective-permute-start.3 = (bf16[4,128,512]{2,1,0:T(8,128)(2,1)S(1)}, bf16[4,128,512]{2,1,0:T(8,128)(2,1)S(1)}, u32[]{:S(2)}, u32[]{:S(2)}) collective-permute-start(bf16[4,128,512]{2,1,0:T(8,128)(2,1)S(1)} %all-to-all-done.1.own_ref), channel_id=1, source_target_pairs={{0,32},{32,0},{1,33},{33,1},{2,34},{34,2},{3,35},{35,3},{4,36},{36... | collective-permute-start | bytes 1572872 | tf_op jit(solution)/shard_map/ppermute | solution.py:146
  77.5 0.8 copy-start.8
  78.3 1.4 copy-start
  79.7 2.0 %copy-start.1 = (bf16[64,16,768]{2,1,0:T(8,128)(2,1)S(1)}, bf16[64,16,768]{2,1,0:T(8,128)(2,1)}, u32[]{:S(2)}) copy-start(bf16[64,16,768]{2,1,0:T(8,128)(2,1)} %all-gather.4.cloned.1.call-done) | copy-start | bytes 4718596
  81.7 1.0 copy-start.9
  83.7 50.2 %copy-start.3 = (bf16[512,128]{1,0:T(8,128)(2,1)S(1)}, bf16[512,128]{1,0:T(8,128)(2,1)}, u32[]{:S(2)}) copy-start(bf16[512,128]{1,0:T(8,128)(2,1)} %q_ref.3) | copy-start | bytes 393220
  83.8 50.2 %copy-start.5 = (bf16[512,128]{1,0:T(8,128)(2,1)S(1)}, bf16[512,128]{1,0:T(8,128)(2,1)}, u32[]{:S(2)}) copy-start(bf16[512,128]{1,0:T(8,128)(2,1)} %k_ref.3) | copy-start | bytes 393220
  83.8 50.2 %copy-start.7 = (bf16[512,128]{1,0:T(8,128)(2,1)S(1)}, bf16[512,128]{1,0:T(8,128)(2,1)}, u32[]{:S(2)}) copy-start(bf16[512,128]{1,0:T(8,128)(2,1)} %v_ref.3) | copy-start | bytes 393220
  83.8 50.2 %copy-start.13 = (f32[128]{0:T(128)S(1)}, f32[128]{0:T(128)}, u32[]{:S(2)}) copy-start(f32[128]{0:T(128)} %param.10) | copy-start | bytes 1540
  83.8 50.2 %copy-start.15 = (f32[128]{0:T(128)S(1)}, f32[128]{0:T(128)}, u32[]{:S(2)}) copy-start(f32[128]{0:T(128)} %param.11) | copy-start | bytes 1540
  98.4 9.9 %collective-permute-start.4 = (bf16[128,256]{1,0:T(8,128)(2,1)S(1)}, bf16[128,256]{1,0:T(8,128)(2,1)S(1)}, u32[]{:S(2)}, u32[]{:S(2)}) collective-permute-start(bf16[128,256]{1,0:T(8,128)(2,1)S(1)} %get-tuple-element.38), channel_id=1, source_target_pairs={{0,0},{1,64},{2,128},{3,192},{64,1},{65,65},{66,129},{67,193},{128... | collective-permute-start | bytes 196616 | tf_op jit(solution)/shard_map/ppermute | solution.py:137
  99.0 9.2 %collective-permute-start.6 = (bf16[128,256]{1,0:T(8,128)(2,1)S(1)}, bf16[128,256]{1,0:T(8,128)(2,1)S(1)}, u32[]{:S(2)}, u32[]{:S(2)}) collective-permute-start(bf16[128,256]{1,0:T(8,128)(2,1)S(1)} %get-tuple-element.39), channel_id=1, source_target_pairs={{0,512},{1,576},{2,640},{3,704},{64,513},{65,577},{66,641},{67,705... | collective-permute-start | bytes 196616 | tf_op jit(solution)/shard_map/ppermute | solution.py:137
  106.0 9.1 %collective-permute-start.5 = (bf16[128,256]{1,0:T(8,128)(2,1)S(1)}, bf16[128,256]{1,0:T(8,128)(2,1)S(1)}, u32[]{:S(2)}, u32[]{:S(2)}) collective-permute-start(bf16[128,256]{1,0:T(8,128)(2,1)S(1)} %get-tuple-element.40), channel_id=1, source_target_pairs={{0,256},{1,320},{2,384},{3,448},{64,257},{65,321},{66,385},{67,449... | collective-permute-start | bytes 196616 | tf_op jit(solution)/shard_map/ppermute | solution.py:137
  134.0 0.9 copy-start.11
Sparse Core Ops, SparseCore 0:
  29.5 38.6 all-gather.3
  81.8 52.0 reduce-scatter.1

commit v8 on v7

--- a/solution.py
+++ b/solution.py
@@ -19,7 +19,7 @@
 epsilon = 1e-06
 F32 = jnp.float32
 BF16 = jnp.bfloat16
-VMEM_LIMIT = 32 * 1024 * 1024
+VMEM_LIMIT = 12 * 1024 * 1024
 SCALING = 1.0 / math.sqrt(DH)
 
 
@@ -91,16 +91,16 @@
     return ref[:, pl.ds(side * NL, NL), :, columns].reshape(TOK, BLK)
 
 
-def heads_kernel(g_ref, own_ref, out_ref):
-    here = lax.axis_index("zh")
-    for side in range(NC):
+def heads_kernel(g_ref, own_ref, keep_ref, send_ref):
+    here, core = lax.axis_index("zh"), lax.axis_index("core")
+    for ref, side in ((send_ref, 1 - core), (keep_ref, core)):
         total = None
         for step in range(NZ):
             rows = block(g_ref, side, lax.rem(here + NZ - step, NZ))
             term = dot(rows, own_ref[:, step].reshape(NL * DH, BLK), 1, 1)
             total = term if total is None else total + term
         for head in range(NL):
-            out_ref[side * NL + head] = total[:, head * DH : (head + 1) * DH].astype(BF16)
+            ref[head] = total[:, head * DH : (head + 1) * DH].astype(BF16)
 
 
 def weight_kernel(g_ref, own_ref, other_ref, out_ref):
@@ -173,15 +173,16 @@
     mixed_other = swap_cores(mixed_own)
     gathered, own, mixed_other = lax.optimization_barrier((gathered, own, mixed_other))
 
-    heads = call(
+    half = (NL, TOK, DH)
+    keep, send = call(
         heads_kernel,
-        shape((groups, TOK, DH), BF16),
+        (shape(half, BF16), shape(half, BF16)),
         2 * TOK * NY * DH * WIDE,
         4 << 20,
         (gathered, own),
     )
-    gathered, heads = lax.optimization_barrier((gathered, heads))
-    grad_heads = lax.psum_scatter(heads, ("core", "zl"), scatter_dimension=0, tiled=True)
+    gathered, send = lax.optimization_barrier((gathered, send))
+    received = swap_cores(send)
     partial = call(
         weight_kernel,
         shape((NL, NZ, DH, BLK), BF16),
@@ -190,6 +191,8 @@
         (gathered, mixed_own, mixed_other),
     )
     spread = lax.all_to_all(partial, "x", 0, 0, tiled=True)
+    summed = (keep.astype(F32) + received.astype(F32)).astype(BF16)
+    grad_heads = lax.psum_scatter(summed, "zl", scatter_dimension=0, tiled=True)
     by_zone = sum(spread[part].astype(F32) for part in range(NX)).astype(BF16)
     last = [cross(by_zone[shift], shift) for shift in range(NZ)]
     grad_weight = sum(entry.astype(F32) for entry in last).astype(BF16)

time: 144 us -> 141 us (0.979)
  the two profiles are of different devices: /device:TPU:1 before, /device:TPU:128 now
where the time goes in v8:
time: 141 us; the launch traced here: 140 us
  starting transfers between devices  43.4 us (31%)
  waiting for transfers between devices  35.7 us (25%)
  blocking collectives  29.9 us (21%)
  between operations  14.3 us (10%)
  local copies, waits for them, and re-layouts  8.15 us (6%)
  Pallas kernels  5.91 us (4%)
  other arithmetic  2.87 us (2%)
    ppermute x6, starting transfers between devices, cross(): return lax.ppermute(entry, ('zh', 'x', 'zl'), pairs)  31.7 us
    ppermute x6, waiting for transfers between devices, cross(): return lax.ppermute(entry, ('zh', 'x', 'zl'), pairs)  23 us
    all_to_all x1, blocking collectives, shards(): exchanged = lax.all_to_all(pieces, ('core', 'zl'), 0, 0, tiled=True)  16.6 us
    all_gather x1, blocking collectives, shards(): own = lax.all_gather(jnp.stack(moved), 'x', axis=0)  13.3 us
    all_to_all x1, waiting for transfers between devices, shards(): spread = lax.all_to_all(partial, 'x', 0, 0, tiled=True)  10.8 us
    unnamed x26, local copies, waits for them, and re-layouts  7.29 us
    pallas_call x5, Pallas kernels, call(): pl.pallas_call(kernel, out_shape=outs, in_specs=[pl.BlockSpec(memory_spac...  5.91 us
    all_to_all x1, starting transfers between devices, share(): return lax.all_to_all(copies, axis, 0, 0, tiled=True)  4.19 us
  transfers between devices with their start and end apart: 12, of which 5 were waited for; matrix products, arithmetic and copies ran while one was open for 3% of the time, Pallas kernels for 2%

profile of v8, /device:TPU:128, one launch (start us, length us, event | category | flops | bytes accessed | tf_op | source)
XLA Modules:
  0.0 140.2 jit_solution(9405254622821595871)
XLA Ops:
  7.2 0.0 all-gather.4.cloned.1.call-start
  7.2 0.9 copy-done.7
  8.2 16.6 %all_to_all.15 = bf16[8,16,768]{2,1,0:T(8,128)(2,1)} all-to-all(bf16[8,16,768]{2,1,0:T(8,128)(2,1)S(1)} %shard_map.103), channel_id=1, replica_groups=mesh['zh'=3,'x'=4,'core'=2,'y'=8,'zl'=4] {'core','zl'}, dimensions={0} | all-to-all | bytes 393216 | tf_op jit(solution)/shard_map/all_to_all | solution.py:157
  24.7 0.0 all-gather.4.cloned.1.call-update
  24.8 11.0 %collective-permute-start.2 = (bf16[128,256]{1,0:T(8,128)(2,1)}, bf16[128,256]{1,0:T(8,128)(2,1)S(1)}, u32[]{:S(2)}, u32[]{:S(2)}) collective-permute-start(bf16[128,256]{1,0:T(8,128)(2,1)} %param.12), channel_id=1, source_target_pairs={{0,512},{1,576},{2,640},{3,704},{64,513},{65,577},{66,641},{67,705... | collective-permute-start | bytes 196616 | tf_op jit(solution)/shard_map/ppermute | solution.py:137
  35.8 1.9 %collective-permute-start.1 = (bf16[128,256]{1,0:T(8,128)(2,1)}, bf16[128,256]{1,0:T(8,128)(2,1)S(1)}, u32[]{:S(2)}, u32[]{:S(2)}) collective-permute-start(bf16[128,256]{1,0:T(8,128)(2,1)} %param.12), channel_id=1, source_target_pairs={{0,256},{1,320},{2,384},{3,448},{64,257},{65,321},{66,385},{67,449... | collective-permute-start | bytes 196616 | tf_op jit(solution)/shard_map/ppermute | solution.py:137
  37.7 3.3 %collective-permute-start = (bf16[128,256]{1,0:T(8,128)(2,1)}, bf16[128,256]{1,0:T(8,128)(2,1)S(1)}, u32[]{:S(2)}, u32[]{:S(2)}) collective-permute-start(bf16[128,256]{1,0:T(8,128)(2,1)} %param.12), channel_id=1, source_target_pairs={{0,0},{1,64},{2,128},{3,192},{64,1},{65,65},{66,129},{67,193},{128... | collective-permute-start | bytes 196616 | tf_op jit(solution)/shard_map/ppermute | solution.py:137
  41.0 0.0 copy-start.1
  41.0 0.9 copy-done.1
  41.9 0.9 copy-done.3
  42.8 0.9 copy-done.5
  43.7 0.7 copy-done.9
  44.4 0.7 copy-done.11
  45.0 0.8 shard_map.102
  45.8 0.0 collective-permute-done.2
  45.9 6.7 %collective-permute-done.1 = bf16[128,256]{1,0:T(8,128)(2,1)S(1)} collective-permute-done((bf16[128,256]{1,0:T(8,128)(2,1)}, bf16[128,256]{1,0:T(8,128)(2,1)S(1)}, u32[]{:S(2)}, u32[]{:S(2)}) %collective-permute-start.1) | collective-permute-done | bytes 65568 | tf_op jit(solution)/shard_map/ppermute | solution.py:137
  52.6 0.0 collective-permute-done
  52.6 0.8 broadcast_in_dim.2
  53.4 4.2 %all-to-all-start.1 = ((bf16[4,128,512]{2,1,0:T(8,128)(2,1)}), bf16[4,128,512]{2,1,0:T(8,128)(2,1)S(1)}, u32[]{:S(2)}, u32[]{:S(2)}) async-start(bf16[4,128,512]{2,1,0:T(8,128)(2,1)} %broadcast_in_dim.2), calls=%async_computation.1 | async-start | bytes 1048576 | tf_op jit(solution)/shard_map/all_to_all | solution.py:142
  57.7 13.3 %all-gather.1 = bf16[12,128,256]{2,1,0:T(8,128)(2,1)S(1)} all-gather(bf16[3,128,256]{2,1,0:T(8,128)(2,1)S(1)} %pad_maximum_fusion), channel_id=3, replica_groups=mesh['zh'=3,'x'=4,'core'=2,'y'=8,'zl'=4] {'x'}, dimensions={0}, use_global_device_ids=true | all-gather | bytes 983040 | tf_op jit(solution)/shard_map/all_gather | solution.py:171
  71.0 0.0 all-to-all-done.1.own_ref
  71.0 1.9 %collective-permute-start.3 = (bf16[4,128,512]{2,1,0:T(8,128)(2,1)S(1)}, bf16[4,128,512]{2,1,0:T(8,128)(2,1)S(1)}, u32[]{:S(2)}, u32[]{:S(2)}) collective-permute-start(bf16[4,128,512]{2,1,0:T(8,128)(2,1)S(1)} %all-to-all-done.1.own_ref), channel_id=1, source_target_pairs={{0,32},{32,0},{1,33},{33,1},{2,34},{34,2},{3,35},{35,3},{4,36},{36... | collective-permute-start | bytes 1572872 | tf_op jit(solution)/shard_map/ppermute | solution.py:146
  72.9 1.9 %collective-permute-done.3.other_ref = bf16[4,128,512]{2,1,0:T(8,128)(2,1)S(1)} collective-permute-done((bf16[4,128,512]{2,1,0:T(8,128)(2,1)S(1)}, bf16[4,128,512]{2,1,0:T(8,128)(2,1)S(1)}, u32[]{:S(2)}, u32[]{:S(2)}) %collective-permute-start.3) | collective-permute-done | bytes 524320 | tf_op jit(solution)/shard_map/ppermute | solution.py:146
  74.8 1.4 %copy-done = bf16[64,16,768]{2,1,0:T(8,128)(2,1)S(1)} copy-done((bf16[64,16,768]{2,1,0:T(8,128)(2,1)S(1)}, bf16[64,16,768]{2,1,0:T(8,128)(2,1)}, u32[]{:S(2)}) %copy-start) | copy-done | bytes 1572888
  76.2 1.0 shard_map.104
  77.2 2.0 %collective-permute-start.4 = (bf16[4,512,128]{2,1,0:T(8,128)(2,1)S(1)}, bf16[4,512,128]{2,1,0:T(8,128)(2,1)}, u32[]{:S(2)}, u32[]{:S(2)}) collective-permute-start(bf16[4,512,128]{2,1,0:T(8,128)(2,1)S(1)} %get-tuple-element.36), channel_id=1, source_target_pairs={{0,32},{32,0},{1,33},{33,1},{2,34},{34,2},{3,35},{35,3},{4,36},{36... | collective-permute-start | bytes 1572872 | tf_op jit(solution)/shard_map/ppermute | solution.py:146
  79.3 1.9 %shard_map.106 = bf16[4,3,128,256]{3,2,1,0:T(8,128)(2,1)} custom-call(bf16[8,8,16,768]{3,2,1,0:T(8,128)(2,1)S(1)} %bitcast.15, bf16[4,128,512]{2,1,0:T(8,128)(2,1)S(1)} %all-to-all-done.1.own_ref, bf16[4,128,512]{2,1,0:T(8,128)(2,1)S(1)} %collective-permute-done.3.other_ref), custom_call_target="tpu_custom_call" | custom-call | flops 805306368 | bytes 5242880 | tf_op jit(solution)/shard_map/pallas_call | solution.py:118
  81.2 3.5 %all-to-all-start.2 = ((bf16[4,3,128,256]{3,2,1,0:T(8,128)(2,1)}), bf16[4,3,128,256]{3,2,1,0:T(8,128)(2,1)S(1)}, u32[]{:S(2)}, u32[]{:S(2)}) async-start(bf16[4,3,128,256]{3,2,1,0:T(8,128)(2,1)} %shard_map.106), calls=%async_computation.3 | async-start | bytes 1572864 | tf_op jit(solution)/shard_map/all_to_all | solution.py:193
  84.7 0.0 reduce-scatter.2.cloned.1.call-start
  84.7 0.0 collective-permute-done.4
  84.8 0.0 copy-start.2
  84.8 0.0 copy-start.4
  84.8 0.0 copy-start.6
  84.8 0.0 copy-start.10
  84.8 0.0 copy-start.12
  84.8 2.1 %add_convert_fusion = bf16[4,512,128]{2,1,0:T(8,128)(2,1)} fusion(bf16[4,512,128]{2,1,0:T(8,128)(2,1)} %collective-permute-done.4, bf16[4,512,128]{2,1,0:T(8,128)(2,1)S(1)} %get-tuple-element.34), kind=kLoop, calls=%fused_computation | loop fusion | flops 1048576 | bytes 1572864 | tf_op jit(solution)/shard_map/convert_element_type | solution.py:194
  86.9 0.0 reduce-scatter.2.cloned.1.call-update
  86.9 10.8 %all-to-all-done.2 = bf16[4,3,128,256]{3,2,1,0:T(8,128)(2,1)S(1)} async-done(((bf16[4,3,128,256]{3,2,1,0:T(8,128)(2,1)}), bf16[4,3,128,256]{3,2,1,0:T(8,128)(2,1)S(1)}, u32[]{:S(2)}, u32[]{:S(2)}) %all-to-all-start.2) | async-done | bytes 786464 | tf_op jit(solution)/shard_map/all_to_all | solution.py:193
  97.8 0.1 add_convert_fusion.1
  97.9 2.2 %collective-permute-start.5 = (bf16[128,256]{1,0:T(8,128)(2,1)S(1)}, bf16[128,256]{1,0:T(8,128)(2,1)S(1)}, u32[]{:S(2)}, u32[]{:S(2)}) collective-permute-start(bf16[128,256]{1,0:T(8,128)(2,1)S(1)} %get-tuple-element.42), channel_id=1, source_target_pairs={{0,0},{1,64},{2,128},{3,192},{64,1},{65,65},{66,129},{67,193},{128... | collective-permute-start | bytes 196616 | tf_op jit(solution)/shard_map/ppermute | solution.py:137
  100.1 11.4 %collective-permute-start.7 = (bf16[128,256]{1,0:T(8,128)(2,1)S(1)}, bf16[128,256]{1,0:T(8,128)(2,1)S(1)}, u32[]{:S(2)}, u32[]{:S(2)}) collective-permute-start(bf16[128,256]{1,0:T(8,128)(2,1)S(1)} %get-tuple-element.43), channel_id=1, source_target_pairs={{0,512},{1,576},{2,640},{3,704},{64,513},{65,577},{66,641},{67,705... | collective-permute-start | bytes 196616 | tf_op jit(solution)/shard_map/ppermute | solution.py:137
  111.5 1.9 %collective-permute-start.6 = (bf16[128,256]{1,0:T(8,128)(2,1)S(1)}, bf16[128,256]{1,0:T(8,128)(2,1)S(1)}, u32[]{:S(2)}, u32[]{:S(2)}) collective-permute-start(bf16[128,256]{1,0:T(8,128)(2,1)S(1)} %get-tuple-element.44), channel_id=1, source_target_pairs={{0,256},{1,320},{2,384},{3,448},{64,257},{65,321},{66,385},{67,449... | collective-permute-start | bytes 196616 | tf_op jit(solution)/shard_map/ppermute | solution.py:137
  113.4 0.0 collective-permute-done.5
  113.4 6.1 %collective-permute-done.7 = bf16[128,256]{1,0:T(8,128)(2,1)S(1)} collective-permute-done((bf16[128,256]{1,0:T(8,128)(2,1)S(1)}, bf16[128,256]{1,0:T(8,128)(2,1)S(1)}, u32[]{:S(2)}, u32[]{:S(2)}) %collective-permute-start.7) | collective-permute-done | bytes 65568 | tf_op jit(solution)/shard_map/ppermute | solution.py:137
  119.5 10.1 %collective-permute-done.6 = bf16[128,256]{1,0:T(8,128)(2,1)S(1)} collective-permute-done((bf16[128,256]{1,0:T(8,128)(2,1)S(1)}, bf16[128,256]{1,0:T(8,128)(2,1)S(1)}, u32[]{:S(2)}, u32[]{:S(2)}) %collective-permute-start.6) | collective-permute-done | bytes 65568 | tf_op jit(solution)/shard_map/ppermute | solution.py:137
  129.6 0.7 add_convert_fusion.2
  130.3 0.9 copy-done.8
  131.2 2.2 %shard_map.105 = (bf16[512,128]{1,0:T(8,128)(2,1)}, bf16[512,128]{1,0:T(8,128)(2,1)}, bf16[512,128]{1,0:T(8,128)(2,1)}) custom-call(bf16[512,128]{1,0:T(8,128)(2,1)S(1)} %copy-done.2, bf16[512,128]{1,0:T(8,128)(2,1)S(1)} %copy-done.4, bf16[512,128]{1,0:T(8,128)(2,1)S(1)} %copy-done.6, f32[1,128]{1,0:T(1,128)S(1)} %bitcast.19, f32[1,128]{1,0:T(1,128)S(1)} %bitcast.21, ...), custom_call_target="tpu_custom_call" | custom-call | flops 167772160 | bytes 2097152 | tf_op jit(solution)/shard_map/pallas_call | solution.py:118
  (17 shorter events, 0.1 us)
Async XLA Ops:
  7.2 67.6 %all-gather.4.cloned.1.call-start = ((), (), s32[]{:S(2)}) async-start(), calls=%async_computation.5 | async-start | bytes 1769472 | tf_op jit(solution)/shard_map/all_gather | solution.py:158
  7.2 0.9 copy-start.7
  24.8 21.1 %collective-permute-start.2 = (bf16[128,256]{1,0:T(8,128)(2,1)}, bf16[128,256]{1,0:T(8,128)(2,1)S(1)}, u32[]{:S(2)}, u32[]{:S(2)}) collective-permute-start(bf16[128,256]{1,0:T(8,128)(2,1)} %param.12), channel_id=1, source_target_pairs={{0,512},{1,576},{2,640},{3,704},{64,513},{65,577},{66,641},{67,705... | collective-permute-start | bytes 196616 | tf_op jit(solution)/shard_map/ppermute | solution.py:137
  35.8 16.8 %collective-permute-start.1 = (bf16[128,256]{1,0:T(8,128)(2,1)}, bf16[128,256]{1,0:T(8,128)(2,1)S(1)}, u32[]{:S(2)}, u32[]{:S(2)}) collective-permute-start(bf16[128,256]{1,0:T(8,128)(2,1)} %param.12), channel_id=1, source_target_pairs={{0,256},{1,320},{2,384},{3,448},{64,257},{65,321},{66,385},{67,449... | collective-permute-start | bytes 196616 | tf_op jit(solution)/shard_map/ppermute | solution.py:137
  37.7 14.9 %collective-permute-start = (bf16[128,256]{1,0:T(8,128)(2,1)}, bf16[128,256]{1,0:T(8,128)(2,1)S(1)}, u32[]{:S(2)}, u32[]{:S(2)}) collective-permute-start(bf16[128,256]{1,0:T(8,128)(2,1)} %param.12), channel_id=1, source_target_pairs={{0,0},{1,64},{2,128},{3,192},{64,1},{65,65},{66,129},{67,193},{128... | collective-permute-start | bytes 196616 | tf_op jit(solution)/shard_map/ppermute | solution.py:137
  41.0 0.9 copy-start.1
  41.9 0.9 copy-start.3
  42.8 0.9 copy-start.5
  43.7 0.7 copy-start.9
  44.4 0.7 copy-start.11
  53.4 17.6 %all-to-all-start.1 = ((bf16[4,128,512]{2,1,0:T(8,128)(2,1)}), bf16[4,128,512]{2,1,0:T(8,128)(2,1)S(1)}, u32[]{:S(2)}, u32[]{:S(2)}) async-start(bf16[4,128,512]{2,1,0:T(8,128)(2,1)} %broadcast_in_dim.2), calls=%async_computation.1 | async-start | bytes 1048576 | tf_op jit(solution)/shard_map/all_to_all | solution.py:142
  71.0 3.8 %collective-permute-start.3 = (bf16[4,128,512]{2,1,0:T(8,128)(2,1)S(1)}, bf16[4,128,512]{2,1,0:T(8,128)(2,1)S(1)}, u32[]{:S(2)}, u32[]{:S(2)}) collective-permute-start(bf16[4,128,512]{2,1,0:T(8,128)(2,1)S(1)} %all-to-all-done.1.own_ref), channel_id=1, source_target_pairs={{0,32},{32,0},{1,33},{33,1},{2,34},{34,2},{3,35},{35,3},{4,36},{36... | collective-permute-start | bytes 1572872 | tf_op jit(solution)/shard_map/ppermute | solution.py:146
  74.8 1.4 %copy-start = (bf16[64,16,768]{2,1,0:T(8,128)(2,1)S(1)}, bf16[64,16,768]{2,1,0:T(8,128)(2,1)}, u32[]{:S(2)}) copy-start(bf16[64,16,768]{2,1,0:T(8,128)(2,1)} %all-gather.4.cloned.1.call-done) | copy-start | bytes 4718596
  77.2 7.5 %collective-permute-start.4 = (bf16[4,512,128]{2,1,0:T(8,128)(2,1)S(1)}, bf16[4,512,128]{2,1,0:T(8,128)(2,1)}, u32[]{:S(2)}, u32[]{:S(2)}) collective-permute-start(bf16[4,512,128]{2,1,0:T(8,128)(2,1)S(1)} %get-tuple-element.36), channel_id=1, source_target_pairs={{0,32},{32,0},{1,33},{33,1},{2,34},{34,2},{3,35},{35,3},{4,36},{36... | collective-permute-start | bytes 1572872 | tf_op jit(solution)/shard_map/ppermute | solution.py:146
  81.2 16.6 %all-to-all-start.2 = ((bf16[4,3,128,256]{3,2,1,0:T(8,128)(2,1)}), bf16[4,3,128,256]{3,2,1,0:T(8,128)(2,1)S(1)}, u32[]{:S(2)}, u32[]{:S(2)}) async-start(bf16[4,3,128,256]{3,2,1,0:T(8,128)(2,1)} %shard_map.106), calls=%async_computation.3 | async-start | bytes 1572864 | tf_op jit(solution)/shard_map/all_to_all | solution.py:193
  84.7 45.6 %reduce-scatter.2.cloned.1.call-start = ((), (), s32[]{:S(2)}) async-start(), calls=%async_computation.4 | async-start | bytes 655360 | tf_op jit(solution)/shard_map/reduce_scatter | solution.py:195
  84.8 45.5 %copy-start.2 = (bf16[512,128]{1,0:T(8,128)(2,1)S(1)}, bf16[512,128]{1,0:T(8,128)(2,1)}, u32[]{:S(2)}) copy-start(bf16[512,128]{1,0:T(8,128)(2,1)} %q_ref.3) | copy-start | bytes 393220
  84.8 45.5 %copy-start.4 = (bf16[512,128]{1,0:T(8,128)(2,1)S(1)}, bf16[512,128]{1,0:T(8,128)(2,1)}, u32[]{:S(2)}) copy-start(bf16[512,128]{1,0:T(8,128)(2,1)} %k_ref.3) | copy-start | bytes 393220
  84.8 45.5 %copy-start.6 = (bf16[512,128]{1,0:T(8,128)(2,1)S(1)}, bf16[512,128]{1,0:T(8,128)(2,1)}, u32[]{:S(2)}) copy-start(bf16[512,128]{1,0:T(8,128)(2,1)} %v_ref.3) | copy-start | bytes 393220
  84.8 45.5 %copy-start.10 = (f32[128]{0:T(128)S(1)}, f32[128]{0:T(128)}, u32[]{:S(2)}) copy-start(f32[128]{0:T(128)} %param.10) | copy-start | bytes 1540
  84.8 45.5 %copy-start.12 = (f32[128]{0:T(128)S(1)}, f32[128]{0:T(128)}, u32[]{:S(2)}) copy-start(f32[128]{0:T(128)} %param.11) | copy-start | bytes 1540
  97.9 15.5 %collective-permute-start.5 = (bf16[128,256]{1,0:T(8,128)(2,1)S(1)}, bf16[128,256]{1,0:T(8,128)(2,1)S(1)}, u32[]{:S(2)}, u32[]{:S(2)}) collective-permute-start(bf16[128,256]{1,0:T(8,128)(2,1)S(1)} %get-tuple-element.42), channel_id=1, source_target_pairs={{0,0},{1,64},{2,128},{3,192},{64,1},{65,65},{66,129},{67,193},{128... | collective-permute-start | bytes 196616 | tf_op jit(solution)/shard_map/ppermute | solution.py:137
  100.1 19.4 %collective-permute-start.7 = (bf16[128,256]{1,0:T(8,128)(2,1)S(1)}, bf16[128,256]{1,0:T(8,128)(2,1)S(1)}, u32[]{:S(2)}, u32[]{:S(2)}) collective-permute-start(bf16[128,256]{1,0:T(8,128)(2,1)S(1)} %get-tuple-element.43), channel_id=1, source_target_pairs={{0,512},{1,576},{2,640},{3,704},{64,513},{65,577},{66,641},{67,705... | collective-permute-start | bytes 196616 | tf_op jit(solution)/shard_map/ppermute | solution.py:137
  111.5 18.2 %collective-permute-start.6 = (bf16[128,256]{1,0:T(8,128)(2,1)S(1)}, bf16[128,256]{1,0:T(8,128)(2,1)S(1)}, u32[]{:S(2)}, u32[]{:S(2)}) collective-permute-start(bf16[128,256]{1,0:T(8,128)(2,1)S(1)} %get-tuple-element.44), channel_id=1, source_target_pairs={{0,256},{1,320},{2,384},{3,448},{64,257},{65,321},{66,385},{67,449... | collective-permute-start | bytes 196616 | tf_op jit(solution)/shard_map/ppermute | solution.py:137
  130.3 0.9 copy-start.8
Sparse Core Ops, SparseCore 0:
  24.9 45.0 all-gather.3
  88.7 33.7 reduce-scatter.1

commit v9 on v8

--- a/solution.py
+++ b/solution.py
@@ -103,7 +103,10 @@
             ref[head] = total[:, head * DH : (head + 1) * DH].astype(BF16)
 
 
-def weight_kernel(g_ref, own_ref, other_ref, out_ref):
+def weight_kernel(g_ref, own_ref, other_ref, keep_ref, received_ref, out_ref, summed_ref):
+    for head in range(NL):
+        both = keep_ref[head].astype(F32) + received_ref[head].astype(F32)
+        summed_ref[head] = both.astype(BF16)
     here, core = lax.axis_index("zh"), lax.axis_index("core")
     own = own_ref[...].reshape(NL * DH, TOK)
     other = other_ref[...].reshape(NL * DH, TOK)
@@ -155,8 +158,6 @@
     groups = NC * NL
     pieces = call(cut_kernel, shape((groups, rows, WIDE), BF16), 0, 1 << 18, (grad_output,))
     exchanged = lax.all_to_all(pieces, ("core", "zl"), 0, 0, tiled=True)
-    gathered = lax.all_gather(exchanged, "y", axis=0)
-
     mixed, attention = call(
         forward_kernel,
         (shape((DH, TOK), BF16), shape((IMAGES, PATCH, PATCH), F32)),
@@ -164,7 +165,8 @@
         1 << 20,
         (query_input, key_input, value_input, query_gain, key_gain),
     )
-    exchanged, out_weight = lax.optimization_barrier((exchanged, out_weight))
+    exchanged, out_weight, mixed = lax.optimization_barrier((exchanged, out_weight, mixed))
+    gathered = lax.all_gather(exchanged, "y", axis=0)
     moved = [cross(out_weight, shift) for shift in range(NZ)]
     mixed, *moved = lax.optimization_barrier((mixed, *moved))
     mixed_own = share(mixed, "zl", NL)
@@ -181,22 +183,18 @@
         4 << 20,
         (gathered, own),
     )
-    gathered, send = lax.optimization_barrier((gathered, send))
     received = swap_cores(send)
-    partial = call(
+    partial, summed = call(
         weight_kernel,
-        shape((NL, NZ, DH, BLK), BF16),
+        (shape((NL, NZ, DH, BLK), BF16), shape(half, BF16)),
         2 * TOK * NY * DH * WIDE,
         5 << 20,
-        (gathered, mixed_own, mixed_other),
+        (gathered, mixed_own, mixed_other, keep, received),
     )
     spread = lax.all_to_all(partial, "x", 0, 0, tiled=True)
-    summed = (keep.astype(F32) + received.astype(F32)).astype(BF16)
     grad_heads = lax.psum_scatter(summed, "zl", scatter_dimension=0, tiled=True)
     by_zone = sum(spread[part].astype(F32) for part in range(NX)).astype(BF16)
     last = [cross(by_zone[shift], shift) for shift in range(NZ)]
-    grad_weight = sum(entry.astype(F32) for entry in last).astype(BF16)
-
     grad_query, grad_key, grad_value = call(
         backward_kernel,
         (shape((TOK, DH), BF16),) * 3,
@@ -204,6 +202,10 @@
         2 << 20,
         (query_input, key_input, value_input, query_gain, key_gain, attention, grad_heads.reshape(TOK, DH)),
     )
+    grad_query, grad_key, grad_value, *last = lax.optimization_barrier(
+        (grad_query, grad_key, grad_value, *last)
+    )
+    grad_weight = sum(entry.astype(F32) for entry in last).astype(BF16)
     return grad_query, grad_key, grad_value, grad_weight
 
 

time: 141 us -> 143 us (1.014)
  the two profiles are of different devices: /device:TPU:128 before, /device:TPU:1 now
where the time goes in v9:
time: 143 us; the launch traced here: 142 us
  starting transfers between devices  56.2 us (39%)
  waiting for transfers between devices  43.7 us (31%)
  between operations  14.2 us (10%)
  blocking collectives  11.6 us (8%)
  local copies, waits for them, and re-layouts  8.81 us (6%)
  Pallas kernels  6.77 us (5%)
    ppermute x6, starting transfers between devices, cross(): return lax.ppermute(entry, ('zh', 'x', 'zl'), pairs)  20.5 us
    reduce_scatter x1, waiting for transfers between devices, shards(): grad_heads = lax.psum_scatter(summed, 'zl', scatter_dimension=0, tiled=True)  18.7 us
    all_to_all x1, starting transfers between devices, shards(): exchanged = lax.all_to_all(pieces, ('core', 'zl'), 0, 0, tiled=True)  13.8 us
    all_to_all x1, starting transfers between devices, share(): return lax.all_to_all(copies, axis, 0, 0, tiled=True)  12.4 us
    all_gather x1, blocking collectives, shards(): own = lax.all_gather(jnp.stack(moved), 'x', axis=0)  11.6 us
    all_to_all x1, waiting for transfers between devices, shards(): spread = lax.all_to_all(partial, 'x', 0, 0, tiled=True)  11.3 us
    unnamed x28, local copies, waits for them, and re-layouts  7.96 us
    pallas_call x5, Pallas kernels, call(): pl.pallas_call(kernel, out_shape=outs, in_specs=[pl.BlockSpec(memory_spac...  6.77 us
  transfers between devices with their start and end apart: 13, of which 7 were waited for; matrix products, arithmetic and copies ran while one was open for 1% of the time, Pallas kernels for 2%

profile of v9, /device:TPU:1, one launch (start us, length us, event | category | flops | bytes accessed | tf_op | source)
XLA Modules:
  0.0 142.1 jit_solution(18102512574903398778)
XLA Ops:
  7.2 0.9 copy-done.7
  8.1 0.7 shard_map.103
  8.8 13.8 %all-to-all-start = ((bf16[8,16,768]{2,1,0:T(8,128)(2,1)}), bf16[8,16,768]{2,1,0:T(8,128)(2,1)S(1)}, u32[]{:S(2)}, u32[]{:S(2)}) async-start(bf16[8,16,768]{2,1,0:T(8,128)(2,1)} %shard_map.103), calls=%async_computation | async-start | bytes 393216 | tf_op jit(solution)/shard_map/all_to_all | solution.py:160
  22.6 0.9 copy-done.1
  23.5 0.9 copy-done.3
  24.4 0.9 copy-done.5
  25.3 0.7 copy-done.9
  26.0 0.7 copy-done.11
  26.6 0.8 shard_map.102
  27.5 2.8 %all-to-all-done = bf16[8,16,768]{2,1,0:T(8,128)(2,1)S(1)} async-done(((bf16[8,16,768]{2,1,0:T(8,128)(2,1)}), bf16[8,16,768]{2,1,0:T(8,128)(2,1)S(1)}, u32[]{:S(2)}, u32[]{:S(2)}) %all-to-all-start) | async-done | bytes 196640 | tf_op jit(solution)/shard_map/all_to_all | solution.py:160
  30.3 0.7 copy-done.13
  30.9 0.0 all-gather.4.cloned.1.call-update
  31.0 6.5 %collective-permute-start.2 = (bf16[128,256]{1,0:T(8,128)(2,1)}, bf16[128,256]{1,0:T(8,128)(2,1)S(1)}, u32[]{:S(2)}, u32[]{:S(2)}) collective-permute-start(bf16[128,256]{1,0:T(8,128)(2,1)} %param.12), channel_id=1, source_target_pairs={{0,512},{1,576},{2,640},{3,704},{64,513},{65,577},{66,641},{67,705... | collective-permute-start | bytes 196616 | tf_op jit(solution)/shard_map/ppermute | solution.py:140
  37.5 2.7 %collective-permute-start.1 = (bf16[128,256]{1,0:T(8,128)(2,1)}, bf16[128,256]{1,0:T(8,128)(2,1)S(1)}, u32[]{:S(2)}, u32[]{:S(2)}) collective-permute-start(bf16[128,256]{1,0:T(8,128)(2,1)} %param.12), channel_id=1, source_target_pairs={{0,256},{1,320},{2,384},{3,448},{64,257},{65,321},{66,385},{67,449... | collective-permute-start | bytes 196616 | tf_op jit(solution)/shard_map/ppermute | solution.py:140
  40.2 1.5 %collective-permute-start = (bf16[128,256]{1,0:T(8,128)(2,1)}, bf16[128,256]{1,0:T(8,128)(2,1)S(1)}, u32[]{:S(2)}, u32[]{:S(2)}) collective-permute-start(bf16[128,256]{1,0:T(8,128)(2,1)} %param.12), channel_id=1, source_target_pairs={{0,0},{1,64},{2,128},{3,192},{64,1},{65,65},{66,129},{67,193},{128... | collective-permute-start | bytes 196616 | tf_op jit(solution)/shard_map/ppermute | solution.py:140
  41.7 0.0 collective-permute-done.2
  41.7 5.0 %collective-permute-done.1 = bf16[128,256]{1,0:T(8,128)(2,1)S(1)} collective-permute-done((bf16[128,256]{1,0:T(8,128)(2,1)}, bf16[128,256]{1,0:T(8,128)(2,1)S(1)}, u32[]{:S(2)}, u32[]{:S(2)}) %collective-permute-start.1) | collective-permute-done | bytes 65568 | tf_op jit(solution)/shard_map/ppermute | solution.py:140
  46.6 0.0 collective-permute-done
  46.6 0.8 broadcast_in_dim.2
  47.5 12.4 %all-to-all-start.1 = ((bf16[4,128,512]{2,1,0:T(8,128)(2,1)}), bf16[4,128,512]{2,1,0:T(8,128)(2,1)S(1)}, u32[]{:S(2)}, u32[]{:S(2)}) async-start(bf16[4,128,512]{2,1,0:T(8,128)(2,1)} %broadcast_in_dim.2), calls=%async_computation.1 | async-start | bytes 1048576 | tf_op jit(solution)/shard_map/all_to_all | solution.py:145
  59.9 11.6 %all-gather.1 = bf16[12,128,256]{2,1,0:T(8,128)(2,1)S(1)} all-gather(bf16[3,128,256]{2,1,0:T(8,128)(2,1)S(1)} %pad_maximum_fusion), channel_id=3, replica_groups=mesh['zh'=3,'x'=4,'core'=2,'y'=8,'zl'=4] {'x'}, dimensions={0}, use_global_device_ids=true | all-gather | bytes 983040 | tf_op jit(solution)/shard_map/all_gather | solution.py:173
  71.5 2.3 %all-to-all-done.1.own_ref = bf16[4,128,512]{2,1,0:T(8,128)(2,1)S(1)} async-done(((bf16[4,128,512]{2,1,0:T(8,128)(2,1)}), bf16[4,128,512]{2,1,0:T(8,128)(2,1)S(1)}, u32[]{:S(2)}, u32[]{:S(2)}) %all-to-all-start.1) | async-done | bytes 524320 | tf_op jit(solution)/shard_map/all_to_all | solution.py:145
  73.9 3.5 %collective-permute-start.3 = (bf16[4,128,512]{2,1,0:T(8,128)(2,1)S(1)}, bf16[4,128,512]{2,1,0:T(8,128)(2,1)S(1)}, u32[]{:S(2)}, u32[]{:S(2)}) collective-permute-start(bf16[4,128,512]{2,1,0:T(8,128)(2,1)S(1)} %all-to-all-done.1.own_ref), channel_id=1, source_target_pairs={{0,32},{32,0},{1,33},{33,1},{2,34},{34,2},{3,35},{35,3},{4,36},{36... | collective-permute-start | bytes 1572872 | tf_op jit(solution)/shard_map/ppermute | solution.py:149
  77.4 1.5 %collective-permute-done.3.other_ref = bf16[4,128,512]{2,1,0:T(8,128)(2,1)S(1)} collective-permute-done((bf16[4,128,512]{2,1,0:T(8,128)(2,1)S(1)}, bf16[4,128,512]{2,1,0:T(8,128)(2,1)S(1)}, u32[]{:S(2)}, u32[]{:S(2)}) %collective-permute-start.3) | collective-permute-done | bytes 524320 | tf_op jit(solution)/shard_map/ppermute | solution.py:149
  78.9 1.4 copy-done
  80.3 1.0 shard_map.104
  81.3 2.3 %collective-permute-start.4 = (bf16[4,512,128]{2,1,0:T(8,128)(2,1)S(1)}, bf16[4,512,128]{2,1,0:T(8,128)(2,1)S(1)}, u32[]{:S(2)}, u32[]{:S(2)}) collective-permute-start(bf16[4,512,128]{2,1,0:T(8,128)(2,1)S(1)} %get-tuple-element.46), channel_id=1, source_target_pairs={{0,32},{32,0},{1,33},{33,1},{2,34},{34,2},{3,35},{35,3},{4,36},{36... | collective-permute-start | bytes 1572872 | tf_op jit(solution)/shard_map/ppermute | solution.py:149
  83.6 1.5 %collective-permute-done.4.received_ref = bf16[4,512,128]{2,1,0:T(8,128)(2,1)S(1)} collective-permute-done((bf16[4,512,128]{2,1,0:T(8,128)(2,1)S(1)}, bf16[4,512,128]{2,1,0:T(8,128)(2,1)S(1)}, u32[]{:S(2)}, u32[]{:S(2)}) %collective-permute-start.4) | collective-permute-done | bytes 524320 | tf_op jit(solution)/shard_map/ppermute | solution.py:149
  85.1 2.1 %shard_map.105 = (bf16[4,3,128,256]{3,2,1,0:T(8,128)(2,1)}, bf16[4,512,128]{2,1,0:T(8,128)(2,1)}) custom-call(bf16[8,8,16,768]{3,2,1,0:T(8,128)(2,1)S(1)} %bitcast.15, bf16[4,128,512]{2,1,0:T(8,128)(2,1)S(1)} %all-to-all-done.1.own_ref, bf16[4,128,512]{2,1,0:T(8,128)(2,1)S(1)} %collective-permute-done.3.other_ref, ...), custom_call_target="tpu_custom_call" | custom-call | flops 805306368 | bytes 5242880 | tf_op jit(solution)/shard_map/pallas_call | solution.py:121
  87.2 0.0 copy-start.12
  87.2 3.6 %all-to-all-start.2 = ((bf16[4,3,128,256]{3,2,1,0:T(8,128)(2,1)}), bf16[4,3,128,256]{3,2,1,0:T(8,128)(2,1)S(1)}, u32[]{:S(2)}, u32[]{:S(2)}) async-start(bf16[4,3,128,256]{3,2,1,0:T(8,128)(2,1)} %get-tuple-element.51), calls=%async_computation.3 | async-start | bytes 1572864 | tf_op jit(solution)/shard_map/all_to_all | solution.py:194
  90.9 0.0 reduce-scatter.2.cloned.1.call-start
  90.9 0.7 reduce-scatter.2.cloned.1.call-update
  91.6 11.3 %all-to-all-done.2 = bf16[4,3,128,256]{3,2,1,0:T(8,128)(2,1)S(1)} async-done(((bf16[4,3,128,256]{3,2,1,0:T(8,128)(2,1)}), bf16[4,3,128,256]{3,2,1,0:T(8,128)(2,1)S(1)}, u32[]{:S(2)}, u32[]{:S(2)}) %all-to-all-start.2) | async-done | bytes 786464 | tf_op jit(solution)/shard_map/all_to_all | solution.py:194
  102.9 0.1 add_convert_fusion
  103.0 6.3 %collective-permute-start.7 = (bf16[128,256]{1,0:T(8,128)(2,1)S(1)}, bf16[128,256]{1,0:T(8,128)(2,1)S(1)}, u32[]{:S(2)}, u32[]{:S(2)}) collective-permute-start(bf16[128,256]{1,0:T(8,128)(2,1)S(1)} %get-tuple-element.58), channel_id=1, source_target_pairs={{0,512},{1,576},{2,640},{3,704},{64,513},{65,577},{66,641},{67,705... | collective-permute-start | bytes 196616 | tf_op jit(solution)/shard_map/ppermute | solution.py:140
  109.3 2.9 %collective-permute-start.6 = (bf16[128,256]{1,0:T(8,128)(2,1)S(1)}, bf16[128,256]{1,0:T(8,128)(2,1)S(1)}, u32[]{:S(2)}, u32[]{:S(2)}) collective-permute-start(bf16[128,256]{1,0:T(8,128)(2,1)S(1)} %get-tuple-element.59), channel_id=1, source_target_pairs={{0,256},{1,320},{2,384},{3,448},{64,257},{65,321},{66,385},{67,449... | collective-permute-start | bytes 196616 | tf_op jit(solution)/shard_map/ppermute | solution.py:140
  112.2 0.7 collective-permute-start.5
  112.9 18.7 %reduce-scatter.2.cloned.1.call-done = bf16[1,512,128]{2,1,0:T(8,128)(2,1)} async-done(((bf16[4,512,128]{2,1,0:T(8,128)(2,1)}), bf16[1,512,128]{2,1,0:T(8,128)(2,1)}) %reduce-scatter.2.cloned.1.call-update) | async-done | bytes 131088 | tf_op jit(solution)/shard_map/reduce_scatter | solution.py:195
  131.6 0.0 copy-done.10
  131.6 0.0 copy-done.12
  131.6 0.0 copy-start.8
  131.6 0.9 copy-done.8
  132.5 2.1 %shard_map.106 = (bf16[512,128]{1,0:T(8,128)(2,1)}, bf16[512,128]{1,0:T(8,128)(2,1)}, bf16[512,128]{1,0:T(8,128)(2,1)}) custom-call(bf16[512,128]{1,0:T(8,128)(2,1)S(1)} %copy-done.2, bf16[512,128]{1,0:T(8,128)(2,1)S(1)} %copy-done.4, bf16[512,128]{1,0:T(8,128)(2,1)S(1)} %copy-done.6, f32[1,128]{1,0:T(1,128)S(1)} %bitcast.19, f32[1,128]{1,0:T(1,128)S(1)} %bitcast.21, ...), custom_call_target="tpu_custom_call" | custom-call | flops 167772160 | bytes 2097152 | tf_op jit(solution)/shard_map/pallas_call | solution.py:121
  134.6 0.0 collective-permute-done.7
  134.6 0.0 collective-permute-done.6
  134.6 0.0 collective-permute-done.5
  134.6 0.7 add_convert_fusion.1
  (19 shorter events, 0.1 us)
Async XLA Ops:
  7.2 0.9 copy-start.7
  8.8 21.5 %all-to-all-start = ((bf16[8,16,768]{2,1,0:T(8,128)(2,1)}), bf16[8,16,768]{2,1,0:T(8,128)(2,1)S(1)}, u32[]{:S(2)}, u32[]{:S(2)}) async-start(bf16[8,16,768]{2,1,0:T(8,128)(2,1)} %shard_map.103), calls=%async_computation | async-start | bytes 393216 | tf_op jit(solution)/shard_map/all_to_all | solution.py:160
  22.6 56.3 %all-gather.4.cloned.1.call-start = ((), (), s32[]{:S(2)}) async-start(), calls=%async_computation.5 | async-start | bytes 1769472 | tf_op jit(solution)/shard_map/all_gather | solution.py:169
  22.6 0.9 copy-start.1
  23.5 0.9 copy-start.3
  24.4 0.9 copy-start.5
  25.3 0.7 copy-start.9
  26.0 0.7 copy-start.11
  30.3 0.7 copy-start.13
  31.0 10.7 %collective-permute-start.2 = (bf16[128,256]{1,0:T(8,128)(2,1)}, bf16[128,256]{1,0:T(8,128)(2,1)S(1)}, u32[]{:S(2)}, u32[]{:S(2)}) collective-permute-start(bf16[128,256]{1,0:T(8,128)(2,1)} %param.12), channel_id=1, source_target_pairs={{0,512},{1,576},{2,640},{3,704},{64,513},{65,577},{66,641},{67,705... | collective-permute-start | bytes 196616 | tf_op jit(solution)/shard_map/ppermute | solution.py:140
  37.5 9.1 %collective-permute-start.1 = (bf16[128,256]{1,0:T(8,128)(2,1)}, bf16[128,256]{1,0:T(8,128)(2,1)S(1)}, u32[]{:S(2)}, u32[]{:S(2)}) collective-permute-start(bf16[128,256]{1,0:T(8,128)(2,1)} %param.12), channel_id=1, source_target_pairs={{0,256},{1,320},{2,384},{3,448},{64,257},{65,321},{66,385},{67,449... | collective-permute-start | bytes 196616 | tf_op jit(solution)/shard_map/ppermute | solution.py:140
  40.2 6.5 %collective-permute-start = (bf16[128,256]{1,0:T(8,128)(2,1)}, bf16[128,256]{1,0:T(8,128)(2,1)S(1)}, u32[]{:S(2)}, u32[]{:S(2)}) collective-permute-start(bf16[128,256]{1,0:T(8,128)(2,1)} %param.12), channel_id=1, source_target_pairs={{0,0},{1,64},{2,128},{3,192},{64,1},{65,65},{66,129},{67,193},{128... | collective-permute-start | bytes 196616 | tf_op jit(solution)/shard_map/ppermute | solution.py:140
  47.5 26.4 %all-to-all-start.1 = ((bf16[4,128,512]{2,1,0:T(8,128)(2,1)}), bf16[4,128,512]{2,1,0:T(8,128)(2,1)S(1)}, u32[]{:S(2)}, u32[]{:S(2)}) async-start(bf16[4,128,512]{2,1,0:T(8,128)(2,1)} %broadcast_in_dim.2), calls=%async_computation.1 | async-start | bytes 1048576 | tf_op jit(solution)/shard_map/all_to_all | solution.py:145
  73.9 5.0 %collective-permute-start.3 = (bf16[4,128,512]{2,1,0:T(8,128)(2,1)S(1)}, bf16[4,128,512]{2,1,0:T(8,128)(2,1)S(1)}, u32[]{:S(2)}, u32[]{:S(2)}) collective-permute-start(bf16[4,128,512]{2,1,0:T(8,128)(2,1)S(1)} %all-to-all-done.1.own_ref), channel_id=1, source_target_pairs={{0,32},{32,0},{1,33},{33,1},{2,34},{34,2},{3,35},{35,3},{4,36},{36... | collective-permute-start | bytes 1572872 | tf_op jit(solution)/shard_map/ppermute | solution.py:149
  78.9 1.4 copy-start
  81.3 3.8 %collective-permute-start.4 = (bf16[4,512,128]{2,1,0:T(8,128)(2,1)S(1)}, bf16[4,512,128]{2,1,0:T(8,128)(2,1)S(1)}, u32[]{:S(2)}, u32[]{:S(2)}) collective-permute-start(bf16[4,512,128]{2,1,0:T(8,128)(2,1)S(1)} %get-tuple-element.46), channel_id=1, source_target_pairs={{0,32},{32,0},{1,33},{33,1},{2,34},{34,2},{3,35},{35,3},{4,36},{36... | collective-permute-start | bytes 1572872 | tf_op jit(solution)/shard_map/ppermute | solution.py:149
  87.2 44.3 %copy-start.2 = (bf16[512,128]{1,0:T(8,128)(2,1)S(1)}, bf16[512,128]{1,0:T(8,128)(2,1)}, u32[]{:S(2)}) copy-start(bf16[512,128]{1,0:T(8,128)(2,1)} %q_ref.3) | copy-start | bytes 393220
  87.2 44.3 %copy-start.4 = (bf16[512,128]{1,0:T(8,128)(2,1)S(1)}, bf16[512,128]{1,0:T(8,128)(2,1)}, u32[]{:S(2)}) copy-start(bf16[512,128]{1,0:T(8,128)(2,1)} %k_ref.3) | copy-start | bytes 393220
  87.2 44.3 %copy-start.6 = (bf16[512,128]{1,0:T(8,128)(2,1)S(1)}, bf16[512,128]{1,0:T(8,128)(2,1)}, u32[]{:S(2)}) copy-start(bf16[512,128]{1,0:T(8,128)(2,1)} %v_ref.3) | copy-start | bytes 393220
  87.2 44.3 %copy-start.10 = (f32[128]{0:T(128)S(1)}, f32[128]{0:T(128)}, u32[]{:S(2)}) copy-start(f32[128]{0:T(128)} %param.10) | copy-start | bytes 1540
  87.2 44.3 %copy-start.12 = (f32[128]{0:T(128)S(1)}, f32[128]{0:T(128)}, u32[]{:S(2)}) copy-start(f32[128]{0:T(128)} %param.11) | copy-start | bytes 1540
  87.2 15.6 %all-to-all-start.2 = ((bf16[4,3,128,256]{3,2,1,0:T(8,128)(2,1)}), bf16[4,3,128,256]{3,2,1,0:T(8,128)(2,1)S(1)}, u32[]{:S(2)}, u32[]{:S(2)}) async-start(bf16[4,3,128,256]{3,2,1,0:T(8,128)(2,1)} %get-tuple-element.51), calls=%async_computation.3 | async-start | bytes 1572864 | tf_op jit(solution)/shard_map/all_to_all | solution.py:194
  90.9 40.7 %reduce-scatter.2.cloned.1.call-start = ((), (), s32[]{:S(2)}) async-start(), calls=%async_computation.4 | async-start | bytes 655360 | tf_op jit(solution)/shard_map/reduce_scatter | solution.py:195
  103.0 31.6 %collective-permute-start.7 = (bf16[128,256]{1,0:T(8,128)(2,1)S(1)}, bf16[128,256]{1,0:T(8,128)(2,1)S(1)}, u32[]{:S(2)}, u32[]{:S(2)}) collective-permute-start(bf16[128,256]{1,0:T(8,128)(2,1)S(1)} %get-tuple-element.58), channel_id=1, source_target_pairs={{0,512},{1,576},{2,640},{3,704},{64,513},{65,577},{66,641},{67,705... | collective-permute-start | bytes 196616 | tf_op jit(solution)/shard_map/ppermute | solution.py:140
  109.3 25.3 %collective-permute-start.6 = (bf16[128,256]{1,0:T(8,128)(2,1)S(1)}, bf16[128,256]{1,0:T(8,128)(2,1)S(1)}, u32[]{:S(2)}, u32[]{:S(2)}) collective-permute-start(bf16[128,256]{1,0:T(8,128)(2,1)S(1)} %get-tuple-element.59), channel_id=1, source_target_pairs={{0,256},{1,320},{2,384},{3,448},{64,257},{65,321},{66,385},{67,449... | collective-permute-start | bytes 196616 | tf_op jit(solution)/shard_map/ppermute | solution.py:140
  112.2 22.4 %collective-permute-start.5 = (bf16[128,256]{1,0:T(8,128)(2,1)S(1)}, bf16[128,256]{1,0:T(8,128)(2,1)S(1)}, u32[]{:S(2)}, u32[]{:S(2)}) collective-permute-start(bf16[128,256]{1,0:T(8,128)(2,1)S(1)} %get-tuple-element.60), channel_id=1, source_target_pairs={{0,0},{1,64},{2,128},{3,192},{64,1},{65,65},{66,129},{67,193},{128... | collective-permute-start | bytes 196616 | tf_op jit(solution)/shard_map/ppermute | solution.py:140
  131.6 0.9 copy-start.8
Sparse Core Ops, SparseCore 0:
  31.1 38.5 all-gather.3
  94.8 36.6 reduce-scatter.1

commit v10 on v8

--- a/solution.py
+++ b/solution.py
@@ -87,16 +87,16 @@
 
 
 def block(ref, side, zone):
-    columns = pl.ds(zone * BLK, BLK)
+    columns = slice(zone * BLK, (zone + 1) * BLK)
     return ref[:, pl.ds(side * NL, NL), :, columns].reshape(TOK, BLK)
 
 
 def heads_kernel(g_ref, own_ref, keep_ref, send_ref):
-    here, core = lax.axis_index("zh"), lax.axis_index("core")
+    core = lax.axis_index("core")
     for ref, side in ((send_ref, 1 - core), (keep_ref, core)):
         total = None
         for step in range(NZ):
-            rows = block(g_ref, side, lax.rem(here + NZ - step, NZ))
+            rows = block(g_ref, side, step)
             term = dot(rows, own_ref[:, step].reshape(NL * DH, BLK), 1, 1)
             total = term if total is None else total + term
         for head in range(NL):
@@ -104,13 +104,12 @@
 
 
 def weight_kernel(g_ref, own_ref, other_ref, out_ref):
-    here, core = lax.axis_index("zh"), lax.axis_index("core")
+    core = lax.axis_index("core")
     own = own_ref[...].reshape(NL * DH, TOK)
     other = other_ref[...].reshape(NL * DH, TOK)
     for step in range(NZ):
-        zone = lax.rem(here + step, NZ)
-        total = dot(own, block(g_ref, core, zone), 1, 0)
-        total = total + dot(other, block(g_ref, 1 - core, zone), 1, 0)
+        total = dot(own, block(g_ref, core, step), 1, 0)
+        total = total + dot(other, block(g_ref, 1 - core, step), 1, 0)
         out_ref[:, step] = total.reshape(NL, DH, BLK).astype(BF16)
 
 
@@ -125,16 +124,9 @@
     )(*operands)
 
 
-def cross(entry, shift):
-    pairs = []
-    for zone in range(NZ):
-        for across in range(NX):
-            for low in range(NL):
-                target = (zone + shift) % NZ
-                pairs.append(
-                    ((zone * NX + across) * NL + low, (target * NX + low) * NL + across)
-                )
-    return lax.ppermute(entry, ("zh", "x", "zl"), pairs)
+def cross(entry):
+    pairs = [(at * NL + low, low * NL + at) for at in range(NX) for low in range(NL)]
+    return lax.ppermute(entry, ("x", "zl"), pairs)
 
 
 def share(entry, axis, size):
@@ -165,10 +157,10 @@
         (query_input, key_input, value_input, query_gain, key_gain),
     )
     exchanged, out_weight = lax.optimization_barrier((exchanged, out_weight))
-    moved = [cross(out_weight, shift) for shift in range(NZ)]
-    mixed, *moved = lax.optimization_barrier((mixed, *moved))
+    zones = share(cross(out_weight), "zh", NZ)
+    mixed, zones = lax.optimization_barrier((mixed, zones))
     mixed_own = share(mixed, "zl", NL)
-    own = lax.all_gather(jnp.stack(moved), "x", axis=0)
+    own = lax.all_gather(zones, "x", axis=0)
     mixed_own, own = lax.optimization_barrier((mixed_own, own))
     mixed_other = swap_cores(mixed_own)
     gathered, own, mixed_other = lax.optimization_barrier((gathered, own, mixed_other))
@@ -194,8 +186,8 @@
     summed = (keep.astype(F32) + received.astype(F32)).astype(BF16)
     grad_heads = lax.psum_scatter(summed, "zl", scatter_dimension=0, tiled=True)
     by_zone = sum(spread[part].astype(F32) for part in range(NX)).astype(BF16)
-    last = [cross(by_zone[shift], shift) for shift in range(NZ)]
-    grad_weight = sum(entry.astype(F32) for entry in last).astype(BF16)
+    last = lax.all_to_all(by_zone, "zh", 0, 0, tiled=True)
+    grad_weight = cross(sum(last[zone].astype(F32) for zone in range(NZ)).astype(BF16))
 
     grad_query, grad_key, grad_value = call(
         backward_kernel,

time: 141 us -> 140 us (level)
  the two profiles are of different devices: /device:TPU:128 before, /device:TPU:1 now
where the time goes in v10:
time: 140 us; the launch traced here: 139 us
  blocking collectives  45.2 us (32%)
  waiting for transfers between devices  33.7 us (24%)
  starting transfers between devices  32.8 us (23%)
  between operations  14.2 us (10%)
  Pallas kernels  6.28 us (4%)
  local copies, waits for them, and re-layouts  5.52 us (4%)
    all_to_all x1, blocking collectives, shards(): exchanged = lax.all_to_all(pieces, ('core', 'zl'), 0, 0, tiled=True)  21.2 us
    all_to_all x2, starting transfers between devices, share(): return lax.all_to_all(copies, axis, 0, 0, tiled=True)  17.7 us
    reduce_scatter x1, waiting for transfers between devices, shards(): grad_heads = lax.psum_scatter(summed, 'zl', scatter_dimension=0, tiled=True)  13.4 us
    all_gather x1, blocking collectives, shards(): own = lax.all_gather(zones, 'x', axis=0)  12.9 us
    all_to_all x1, waiting for transfers between devices, shards(): spread = lax.all_to_all(partial, 'x', 0, 0, tiled=True)  11.2 us
    all_to_all x1, blocking collectives, shards(): last = lax.all_to_all(by_zone, 'zh', 0, 0, tiled=True)  11.1 us
    ppermute x2, starting transfers between devices, swap_cores(): return lax.ppermute(entry, 'core', [(0, 1), (1, 0)])  9.34 us
    all_to_all x2, waiting for transfers between devices, share(): return lax.all_to_all(copies, axis, 0, 0, tiled=True)  7.52 us
  transfers between devices with their start and end apart: 9, of which 5 were waited for; matrix products, arithmetic and copies ran while one was open for 2% of the time, Pallas kernels for 2%

profile of v10, /device:TPU:1, one launch (start us, length us, event | category | flops | bytes accessed | tf_op | source)
XLA Modules:
  0.0 138.6 jit_solution(6885735036084563084)
XLA Ops:
  7.2 0.0 copy-start.3
  7.2 0.0 copy-start.2
  7.2 0.0 copy-start.1
  7.2 0.0 all-gather.4.cloned.1.call-start
  7.2 0.0 copy-start.4
  7.3 1.0 copy-done.4
  8.3 0.0 copy-start.6
  8.3 0.0 copy-start.7
  8.3 21.2 %all_to_all.25 = bf16[8,16,768]{2,1,0:T(8,128)(2,1)} all-to-all(bf16[8,16,768]{2,1,0:T(8,128)(2,1)S(1)} %shard_map.103), channel_id=1, replica_groups=mesh['zh'=3,'x'=4,'core'=2,'y'=8,'zl'=4] {'core','zl'}, dimensions={0} | all-to-all | bytes 393216 | tf_op jit(solution)/shard_map/all_to_all | solution.py:149
  29.5 0.0 all-gather.4.cloned.1.call-update
  29.5 1.5 %collective-permute-start = (bf16[128,256]{1,0:T(8,128)(2,1)}, bf16[128,256]{1,0:T(8,128)(2,1)S(1)}, u32[]{:S(2)}, u32[]{:S(2)}) collective-permute-start(bf16[128,256]{1,0:T(8,128)(2,1)} %param.12), channel_id=1, source_target_pairs={{0,0},{1,64},{2,128},{3,192},{64,1},{65,65},{66,129},{67,193},{128... | collective-permute-start | bytes 196616 | tf_op jit(solution)/shard_map/ppermute | solution.py:129
  31.0 0.0 collective-permute-done
  31.0 0.7 broadcast_in_dim.4
  31.7 6.0 %all-to-all-start.1 = ((bf16[3,128,256]{2,1,0:T(8,128)(2,1)}), bf16[3,128,256]{2,1,0:T(8,128)(2,1)S(1)}, u32[]{:S(2)}, u32[]{:S(2)}) async-start(bf16[3,128,256]{2,1,0:T(8,128)(2,1)} %broadcast_in_dim.4), calls=%async_computation.1 | async-start | bytes 393216 | tf_op jit(solution)/shard_map/all_to_all | solution.py:134
  37.8 0.0 copy-done.3
  37.8 0.0 copy-done.2
  37.8 0.0 copy-done.1
  37.8 0.0 copy-done.6
  37.8 0.0 copy-done.7
  37.8 0.8 shard_map.102
  38.6 6.5 %all-to-all-done.1 = bf16[3,128,256]{2,1,0:T(8,128)(2,1)S(1)} async-done(((bf16[3,128,256]{2,1,0:T(8,128)(2,1)}), bf16[3,128,256]{2,1,0:T(8,128)(2,1)S(1)}, u32[]{:S(2)}, u32[]{:S(2)}) %all-to-all-start.1) | async-done | bytes 196640 | tf_op jit(solution)/shard_map/all_to_all | solution.py:134
  45.1 0.8 broadcast_in_dim.5
  46.0 11.7 %all-to-all-start.2 = ((bf16[4,128,512]{2,1,0:T(8,128)(2,1)}), bf16[4,128,512]{2,1,0:T(8,128)(2,1)S(1)}, u32[]{:S(2)}, u32[]{:S(2)}) async-start(bf16[4,128,512]{2,1,0:T(8,128)(2,1)} %broadcast_in_dim.5), calls=%async_computation.2 | async-start | bytes 1048576 | tf_op jit(solution)/shard_map/all_to_all | solution.py:134
  57.6 12.9 %all-gather.1 = bf16[12,128,256]{2,1,0:T(8,128)(2,1)S(1)} all-gather(bf16[3,128,256]{2,1,0:T(8,128)(2,1)S(1)} %all-to-all-done.1), channel_id=3, replica_groups=mesh['zh'=3,'x'=4,'core'=2,'y'=8,'zl'=4] {'x'}, dimensions={0}, use_global_device_ids=true | all-gather | bytes 983040 | tf_op jit(solution)/shard_map/all_gather | solution.py:163
  70.5 1.0 all-to-all-done.2.own_ref
  71.5 7.1 %collective-permute-start.1 = (bf16[4,128,512]{2,1,0:T(8,128)(2,1)S(1)}, bf16[4,128,512]{2,1,0:T(8,128)(2,1)S(1)}, u32[]{:S(2)}, u32[]{:S(2)}) collective-permute-start(bf16[4,128,512]{2,1,0:T(8,128)(2,1)S(1)} %all-to-all-done.2.own_ref), channel_id=1, source_target_pairs={{0,32},{32,0},{1,33},{33,1},{2,34},{34,2},{3,35},{35,3},{4,36},{36... | collective-permute-start | bytes 1572872 | tf_op jit(solution)/shard_map/ppermute | solution.py:138
  78.6 1.5 %collective-permute-done.1.other_ref = bf16[4,128,512]{2,1,0:T(8,128)(2,1)S(1)} collective-permute-done((bf16[4,128,512]{2,1,0:T(8,128)(2,1)S(1)}, bf16[4,128,512]{2,1,0:T(8,128)(2,1)S(1)}, u32[]{:S(2)}, u32[]{:S(2)}) %collective-permute-start.1) | collective-permute-done | bytes 524320 | tf_op jit(solution)/shard_map/ppermute | solution.py:138
  80.1 0.0 all-gather.4.cloned.1.call-done
  80.1 0.0 copy-start
  80.1 1.4 %copy-done = bf16[64,16,768]{2,1,0:T(8,128)(2,1)S(1)} copy-done((bf16[64,16,768]{2,1,0:T(8,128)(2,1)S(1)}, bf16[64,16,768]{2,1,0:T(8,128)(2,1)}, u32[]{:S(2)}) %copy-start) | copy-done | bytes 1572888
  81.5 1.4 %shard_map.104 = (bf16[4,512,128]{2,1,0:T(8,128)(2,1)S(1)}, bf16[4,512,128]{2,1,0:T(8,128)(2,1)}) custom-call(bf16[8,8,16,768]{3,2,1,0:T(8,128)(2,1)S(1)} %bitcast.9, bf16[4,3,128,256]{3,2,1,0:T(8,128)(2,1)S(1)} %bitcast.11), custom_call_target="tpu_custom_call" | custom-call | flops 805306368 | bytes 4194304 | tf_op jit(solution)/shard_map/pallas_call | solution.py:117
  82.9 2.3 %collective-permute-start.2 = (bf16[4,512,128]{2,1,0:T(8,128)(2,1)}, bf16[4,512,128]{2,1,0:T(8,128)(2,1)S(1)}, u32[]{:S(2)}, u32[]{:S(2)}) collective-permute-start(bf16[4,512,128]{2,1,0:T(8,128)(2,1)} %get-tuple-element.32), channel_id=1, source_target_pairs={{0,32},{32,0},{1,33},{33,1},{2,34},{34,2},{3,35},{35,3},{4,36},{36... | collective-permute-start | bytes 1572872 | tf_op jit(solution)/shard_map/ppermute | solution.py:138
  85.2 1.9 %shard_map.106 = bf16[4,3,128,256]{3,2,1,0:T(8,128)(2,1)} custom-call(bf16[8,8,16,768]{3,2,1,0:T(8,128)(2,1)S(1)} %bitcast.10, bf16[4,128,512]{2,1,0:T(8,128)(2,1)S(1)} %all-to-all-done.2.own_ref, bf16[4,128,512]{2,1,0:T(8,128)(2,1)S(1)} %collective-permute-done.1.other_ref), custom_call_target="tpu_custom_call" | custom-call | flops 805306368 | bytes 5242880 | tf_op jit(solution)/shard_map/pallas_call | solution.py:117
  87.1 3.5 %all-to-all-start.3 = ((bf16[4,3,128,256]{3,2,1,0:T(8,128)(2,1)}), bf16[4,3,128,256]{3,2,1,0:T(8,128)(2,1)S(1)}, u32[]{:S(2)}, u32[]{:S(2)}) async-start(bf16[4,3,128,256]{3,2,1,0:T(8,128)(2,1)} %shard_map.106), calls=%async_computation.4 | async-start | bytes 1572864 | tf_op jit(solution)/shard_map/all_to_all | solution.py:185
  90.6 0.0 reduce-scatter.2.cloned.1.call-start
  90.7 0.0 collective-permute-done.2
  90.7 0.9 add_convert_fusion
  91.6 0.0 reduce-scatter.2.cloned.1.call-update
  91.6 11.2 %all-to-all-done.3 = bf16[4,3,128,256]{3,2,1,0:T(8,128)(2,1)S(1)} async-done(((bf16[4,3,128,256]{3,2,1,0:T(8,128)(2,1)}), bf16[4,3,128,256]{3,2,1,0:T(8,128)(2,1)S(1)}, u32[]{:S(2)}, u32[]{:S(2)}) %all-to-all-start.3) | async-done | bytes 786464 | tf_op jit(solution)/shard_map/all_to_all | solution.py:185
  102.9 0.1 fusion
  103.0 11.1 %all_to_all.26 = bf16[3,128,256]{2,1,0:T(8,128)(2,1)S(1)} all-to-all(bf16[3,128,256]{2,1,0:T(8,128)(2,1)S(1)} %fusion), channel_id=1, replica_groups=mesh['zh'=3,'x'=4,'core'=2,'y'=8,'zl'=4] {'zh'}, dimensions={0} | all-to-all | bytes 393216 | tf_op jit(solution)/shard_map/all_to_all | solution.py:189
  114.1 0.7 collective-permute-start.3
  114.7 0.0 collective-permute-done.3
  114.7 13.4 %reduce-scatter.2.cloned.1.call-done = bf16[1,512,128]{2,1,0:T(8,128)(2,1)} async-done(((bf16[4,512,128]{2,1,0:T(8,128)(2,1)}), bf16[1,512,128]{2,1,0:T(8,128)(2,1)}) %reduce-scatter.2.cloned.1.call-update) | async-done | bytes 131088 | tf_op jit(solution)/shard_map/reduce_scatter | solution.py:187
  128.1 0.0 copy-start.5
  128.1 0.9 copy-done.5
  129.0 2.1 %shard_map.105 = (bf16[512,128]{1,0:T(8,128)(2,1)}, bf16[512,128]{1,0:T(8,128)(2,1)}, bf16[512,128]{1,0:T(8,128)(2,1)}) custom-call(bf16[512,128]{1,0:T(8,128)(2,1)S(1)} %copy-done.1, bf16[512,128]{1,0:T(8,128)(2,1)S(1)} %copy-done.2, bf16[512,128]{1,0:T(8,128)(2,1)S(1)} %copy-done.3, f32[1,128]{1,0:T(1,128)S(1)} %bitcast.14, f32[1,128]{1,0:T(1,128)S(1)} %bitcast.16, ...), custom_call_target="tpu_custom_call" | custom-call | flops 167772160 | bytes 2097152 | tf_op jit(solution)/shard_map/pallas_call | solution.py:117
  131.2 0.6 copy.12
  (2 shorter events, 0.0 us)
Async XLA Ops:
  7.2 30.6 %copy-start.3 = (bf16[512,128]{1,0:T(8,128)(2,1)S(1)}, bf16[512,128]{1,0:T(8,128)(2,1)}, u32[]{:S(2)}) copy-start(bf16[512,128]{1,0:T(8,128)(2,1)} %v_ref.3) | copy-start | bytes 393220
  7.2 30.6 %copy-start.2 = (bf16[512,128]{1,0:T(8,128)(2,1)S(1)}, bf16[512,128]{1,0:T(8,128)(2,1)}, u32[]{:S(2)}) copy-start(bf16[512,128]{1,0:T(8,128)(2,1)} %k_ref.3) | copy-start | bytes 393220
  7.2 30.6 %copy-start.1 = (bf16[512,128]{1,0:T(8,128)(2,1)S(1)}, bf16[512,128]{1,0:T(8,128)(2,1)}, u32[]{:S(2)}) copy-start(bf16[512,128]{1,0:T(8,128)(2,1)} %q_ref.3) | copy-start | bytes 393220
  7.2 72.9 %all-gather.4.cloned.1.call-start = ((), (), s32[]{:S(2)}) async-start(), calls=%async_computation.7 | async-start | bytes 1769472 | tf_op jit(solution)/shard_map/all_gather | solution.py:150
  7.2 1.0 copy-start.4
  8.3 29.5 %copy-start.6 = (f32[128]{0:T(128)S(1)}, f32[128]{0:T(128)}, u32[]{:S(2)}) copy-start(f32[128]{0:T(128)} %param.10) | copy-start | bytes 1540
  8.3 29.5 %copy-start.7 = (f32[128]{0:T(128)S(1)}, f32[128]{0:T(128)}, u32[]{:S(2)}) copy-start(f32[128]{0:T(128)} %param.11) | copy-start | bytes 1540
  29.5 1.5 %collective-permute-start = (bf16[128,256]{1,0:T(8,128)(2,1)}, bf16[128,256]{1,0:T(8,128)(2,1)S(1)}, u32[]{:S(2)}, u32[]{:S(2)}) collective-permute-start(bf16[128,256]{1,0:T(8,128)(2,1)} %param.12), channel_id=1, source_target_pairs={{0,0},{1,64},{2,128},{3,192},{64,1},{65,65},{66,129},{67,193},{128... | collective-permute-start | bytes 196616 | tf_op jit(solution)/shard_map/ppermute | solution.py:129
  31.7 13.4 %all-to-all-start.1 = ((bf16[3,128,256]{2,1,0:T(8,128)(2,1)}), bf16[3,128,256]{2,1,0:T(8,128)(2,1)S(1)}, u32[]{:S(2)}, u32[]{:S(2)}) async-start(bf16[3,128,256]{2,1,0:T(8,128)(2,1)} %broadcast_in_dim.4), calls=%async_computation.1 | async-start | bytes 393216 | tf_op jit(solution)/shard_map/all_to_all | solution.py:134
  46.0 25.6 %all-to-all-start.2 = ((bf16[4,128,512]{2,1,0:T(8,128)(2,1)}), bf16[4,128,512]{2,1,0:T(8,128)(2,1)S(1)}, u32[]{:S(2)}, u32[]{:S(2)}) async-start(bf16[4,128,512]{2,1,0:T(8,128)(2,1)} %broadcast_in_dim.5), calls=%async_computation.2 | async-start | bytes 1048576 | tf_op jit(solution)/shard_map/all_to_all | solution.py:134
  71.5 8.6 %collective-permute-start.1 = (bf16[4,128,512]{2,1,0:T(8,128)(2,1)S(1)}, bf16[4,128,512]{2,1,0:T(8,128)(2,1)S(1)}, u32[]{:S(2)}, u32[]{:S(2)}) collective-permute-start(bf16[4,128,512]{2,1,0:T(8,128)(2,1)S(1)} %all-to-all-done.2.own_ref), channel_id=1, source_target_pairs={{0,32},{32,0},{1,33},{33,1},{2,34},{34,2},{3,35},{35,3},{4,36},{36... | collective-permute-start | bytes 1572872 | tf_op jit(solution)/shard_map/ppermute | solution.py:138
  80.1 1.4 %copy-start = (bf16[64,16,768]{2,1,0:T(8,128)(2,1)S(1)}, bf16[64,16,768]{2,1,0:T(8,128)(2,1)}, u32[]{:S(2)}) copy-start(bf16[64,16,768]{2,1,0:T(8,128)(2,1)} %all-gather.4.cloned.1.call-done) | copy-start | bytes 4718596
  82.9 7.7 %collective-permute-start.2 = (bf16[4,512,128]{2,1,0:T(8,128)(2,1)}, bf16[4,512,128]{2,1,0:T(8,128)(2,1)S(1)}, u32[]{:S(2)}, u32[]{:S(2)}) collective-permute-start(bf16[4,512,128]{2,1,0:T(8,128)(2,1)} %get-tuple-element.32), channel_id=1, source_target_pairs={{0,32},{32,0},{1,33},{33,1},{2,34},{34,2},{3,35},{35,3},{4,36},{36... | collective-permute-start | bytes 1572872 | tf_op jit(solution)/shard_map/ppermute | solution.py:138
  87.1 15.8 %all-to-all-start.3 = ((bf16[4,3,128,256]{3,2,1,0:T(8,128)(2,1)}), bf16[4,3,128,256]{3,2,1,0:T(8,128)(2,1)S(1)}, u32[]{:S(2)}, u32[]{:S(2)}) async-start(bf16[4,3,128,256]{3,2,1,0:T(8,128)(2,1)} %shard_map.106), calls=%async_computation.4 | async-start | bytes 1572864 | tf_op jit(solution)/shard_map/all_to_all | solution.py:185
  90.6 37.5 %reduce-scatter.2.cloned.1.call-start = ((), (), s32[]{:S(2)}) async-start(), calls=%async_computation.6 | async-start | bytes 655360 | tf_op jit(solution)/shard_map/reduce_scatter | solution.py:187
  114.1 0.7 collective-permute-start.3
  128.1 0.9 copy-start.5
Sparse Core Ops, SparseCore 0:
  29.7 38.6 all-gather.3
  94.6 33.5 reduce-scatter.1

commit v11 on v10

--- a/solution.py
+++ b/solution.py
@@ -157,12 +157,13 @@
         (query_input, key_input, value_input, query_gain, key_gain),
     )
     exchanged, out_weight = lax.optimization_barrier((exchanged, out_weight))
-    zones = share(cross(out_weight), "zh", NZ)
-    mixed, zones = lax.optimization_barrier((mixed, zones))
+    crossed = cross(out_weight)
+    mixed, crossed = lax.optimization_barrier((mixed, crossed))
     mixed_own = share(mixed, "zl", NL)
+    zones = lax.all_gather(crossed, "zh", axis=0)
+    mixed_own, zones = lax.optimization_barrier((mixed_own, zones))
+    mixed_other = swap_cores(mixed_own)
     own = lax.all_gather(zones, "x", axis=0)
-    mixed_own, own = lax.optimization_barrier((mixed_own, own))
-    mixed_other = swap_cores(mixed_own)
     gathered, own, mixed_other = lax.optimization_barrier((gathered, own, mixed_other))
 
     half = (NL, TOK, DH)

time: 140 us -> 145 us (1.036)
  the two profiles are of different devices: /device:TPU:1 before, /device:TPU:168 now
where the time goes in v11:
time: 145 us; the launch traced here: 144 us
  blocking collectives  74.2 us (51%)
  starting transfers between devices  20.7 us (14%)
  waiting for transfers between devices  18.5 us (13%)
  between operations  14.2 us (10%)
  local copies, waits for them, and re-layouts  8.73 us (6%)
  Pallas kernels  5.88 us (4%)
  other arithmetic  2.21 us (2%)
    all_gather x1, blocking collectives, shards(): zones = lax.all_gather(crossed, 'zh', axis=0)  30.9 us
    all_to_all x1, blocking collectives, shards(): last = lax.all_to_all(by_zone, 'zh', 0, 0, tiled=True)  17.5 us
    all_gather x1, blocking collectives, shards(): own = lax.all_gather(zones, 'x', axis=0)  14.1 us
    all_to_all x1, blocking collectives, shards(): exchanged = lax.all_to_all(pieces, ('core', 'zl'), 0, 0, tiled=True)  11.7 us
    all_to_all x1, waiting for transfers between devices, shards(): spread = lax.all_to_all(partial, 'x', 0, 0, tiled=True)  11 us
    ppermute x2, starting transfers between devices, cross(): return lax.ppermute(entry, ('x', 'zl'), pairs)  8.44 us
    unnamed x27, local copies, waits for them, and re-layouts  7.9 us
    ppermute x2, waiting for transfers between devices, cross(): return lax.ppermute(entry, ('x', 'zl'), pairs)  7.54 us
  transfers between devices with their start and end apart: 8, of which 2 were waited for; matrix products, arithmetic and copies ran while one was open for 2% of the time, Pallas kernels for 2%

profile of v11, /device:TPU:168, one launch (start us, length us, event | category | flops | bytes accessed | tf_op | source)
XLA Modules:
  0.0 144.4 jit_solution(14227645737442375707)
XLA Ops:
  7.2 0.0 all-gather.5.cloned.1.call-start
  7.2 0.0 copy-start.7
  7.2 0.9 copy-done.7
  8.2 11.7 %all_to_all.20 = bf16[8,16,768]{2,1,0:T(8,128)(2,1)} all-to-all(bf16[8,16,768]{2,1,0:T(8,128)(2,1)S(1)} %shard_map.103), channel_id=1, replica_groups=mesh['zh'=3,'x'=4,'core'=2,'y'=8,'zl'=4] {'core','zl'}, dimensions={0} | all-to-all | bytes 393216 | tf_op jit(solution)/shard_map/all_to_all | solution.py:149
  19.8 0.0 all-gather.5.cloned.1.call-update
  19.9 6.5 %collective-permute-start = (bf16[128,256]{1,0:T(8,128)(2,1)}, bf16[128,256]{1,0:T(8,128)(2,1)S(1)}, u32[]{:S(2)}, u32[]{:S(2)}) collective-permute-start(bf16[128,256]{1,0:T(8,128)(2,1)} %param.12), channel_id=1, source_target_pairs={{0,0},{1,64},{2,128},{3,192},{64,1},{65,65},{66,129},{67,193},{128... | collective-permute-start | bytes 196616 | tf_op jit(solution)/shard_map/ppermute | solution.py:129
  26.4 0.0 copy-start.1
  26.4 0.9 copy-done.1
  27.3 0.9 copy-done.3
  28.2 0.9 copy-done.5
  29.1 0.7 copy-done.9
  29.8 0.7 copy-done.11
  30.4 0.8 shard_map.102
  31.3 0.0 collective-permute-done
  31.3 0.8 broadcast_in_dim.2
  32.1 4.8 %all-to-all-start.1 = ((bf16[4,128,512]{2,1,0:T(8,128)(2,1)}), bf16[4,128,512]{2,1,0:T(8,128)(2,1)S(1)}, u32[]{:S(2)}, u32[]{:S(2)}) async-start(bf16[4,128,512]{2,1,0:T(8,128)(2,1)} %broadcast_in_dim.2), calls=%async_computation.1 | async-start | bytes 1048576 | tf_op jit(solution)/shard_map/all_to_all | solution.py:134
  36.9 30.9 %all-gather.1 = bf16[384,256]{1,0:T(8,128)(2,1)S(1)} all-gather(bf16[128,256]{1,0:T(8,128)(2,1)S(1)} %collective-permute-done), channel_id=3, replica_groups=mesh['zh'=3,'x'=4,'core'=2,'y'=8,'zl'=4] {'zh'}, dimensions={0}, use_global_device_ids=true | all-gather | bytes 262144 | tf_op jit(solution)/shard_map/all_gather | solution.py:163
  67.8 0.0 all-to-all-done.1.own_ref
  67.8 1.9 %collective-permute-start.1 = (bf16[4,128,512]{2,1,0:T(8,128)(2,1)S(1)}, bf16[4,128,512]{2,1,0:T(8,128)(2,1)S(1)}, u32[]{:S(2)}, u32[]{:S(2)}) collective-permute-start(bf16[4,128,512]{2,1,0:T(8,128)(2,1)S(1)} %all-to-all-done.1.own_ref), channel_id=1, source_target_pairs={{0,32},{32,0},{1,33},{33,1},{2,34},{34,2},{3,35},{35,3},{4,36},{36... | collective-permute-start | bytes 1572872 | tf_op jit(solution)/shard_map/ppermute | solution.py:138
  69.7 14.1 %all-gather.2 = bf16[12,128,256]{2,1,0:T(8,128)(2,1)S(1)} all-gather(bf16[3,128,256]{2,1,0:T(8,128)(2,1)S(1)} %bitcast.18), channel_id=4, replica_groups=mesh['zh'=3,'x'=4,'core'=2,'y'=8,'zl'=4] {'x'}, dimensions={0}, use_global_device_ids=true | all-gather | bytes 983040 | tf_op jit(solution)/shard_map/all_gather | solution.py:166
  83.8 0.0 collective-permute-done.1.other_ref
  83.9 1.4 copy-done
  85.3 1.0 shard_map.104
  86.3 1.9 %collective-permute-start.2 = (bf16[4,512,128]{2,1,0:T(8,128)(2,1)S(1)}, bf16[4,512,128]{2,1,0:T(8,128)(2,1)}, u32[]{:S(2)}, u32[]{:S(2)}) collective-permute-start(bf16[4,512,128]{2,1,0:T(8,128)(2,1)S(1)} %get-tuple-element.32), channel_id=1, source_target_pairs={{0,32},{32,0},{1,33},{33,1},{2,34},{34,2},{3,35},{35,3},{4,36},{36... | collective-permute-start | bytes 1572872 | tf_op jit(solution)/shard_map/ppermute | solution.py:138
  88.2 1.9 %shard_map.106 = bf16[4,3,128,256]{3,2,1,0:T(8,128)(2,1)} custom-call(bf16[8,8,16,768]{3,2,1,0:T(8,128)(2,1)S(1)} %bitcast.11, bf16[4,128,512]{2,1,0:T(8,128)(2,1)S(1)} %all-to-all-done.1.own_ref, bf16[4,128,512]{2,1,0:T(8,128)(2,1)S(1)} %collective-permute-done.1.other_ref), custom_call_target="tpu_custom_call" | custom-call | flops 805306368 | bytes 5242880 | tf_op jit(solution)/shard_map/pallas_call | solution.py:117
  90.1 3.5 %all-to-all-start.2 = ((bf16[4,3,128,256]{3,2,1,0:T(8,128)(2,1)}), bf16[4,3,128,256]{3,2,1,0:T(8,128)(2,1)S(1)}, u32[]{:S(2)}, u32[]{:S(2)}) async-start(bf16[4,3,128,256]{3,2,1,0:T(8,128)(2,1)} %shard_map.106), calls=%async_computation.3 | async-start | bytes 1572864 | tf_op jit(solution)/shard_map/all_to_all | solution.py:186
  93.6 0.0 reduce-scatter.2.cloned.1.call-start
  93.6 0.0 collective-permute-done.2
  93.7 0.0 copy-start.2
  93.7 0.0 copy-start.4
  93.7 0.0 copy-start.6
  93.7 0.0 copy-start.10
  93.7 0.0 copy-start.12
  93.7 2.1 %add_convert_fusion = bf16[4,512,128]{2,1,0:T(8,128)(2,1)} fusion(bf16[4,512,128]{2,1,0:T(8,128)(2,1)} %collective-permute-done.2, bf16[4,512,128]{2,1,0:T(8,128)(2,1)S(1)} %get-tuple-element.30), kind=kLoop, calls=%fused_computation | loop fusion | flops 1048576 | bytes 1572864 | tf_op jit(solution)/shard_map/convert_element_type | solution.py:187
  95.8 0.0 reduce-scatter.2.cloned.1.call-update
  95.8 11.0 %all-to-all-done.2 = bf16[4,3,128,256]{3,2,1,0:T(8,128)(2,1)S(1)} async-done(((bf16[4,3,128,256]{3,2,1,0:T(8,128)(2,1)}), bf16[4,3,128,256]{3,2,1,0:T(8,128)(2,1)S(1)}, u32[]{:S(2)}, u32[]{:S(2)}) %all-to-all-start.2) | async-done | bytes 786464 | tf_op jit(solution)/shard_map/all_to_all | solution.py:186
  106.8 0.1 fusion
  106.9 17.5 %all_to_all.21 = bf16[3,128,256]{2,1,0:T(8,128)(2,1)S(1)} all-to-all(bf16[3,128,256]{2,1,0:T(8,128)(2,1)S(1)} %fusion), channel_id=1, replica_groups=mesh['zh'=3,'x'=4,'core'=2,'y'=8,'zl'=4] {'zh'}, dimensions={0} | all-to-all | bytes 393216 | tf_op jit(solution)/shard_map/all_to_all | solution.py:190
  124.4 1.9 %collective-permute-start.3 = (bf16[128,256]{1,0:T(8,128)(2,1)S(1)}, bf16[128,256]{1,0:T(8,128)(2,1)S(1)}, u32[]{:S(2)}, u32[]{:S(2)}) collective-permute-start(bf16[128,256]{1,0:T(8,128)(2,1)S(1)} %fusion.1), channel_id=1, source_target_pairs={{0,0},{1,64},{2,128},{3,192},{64,1},{65,65},{66,129},{67,193},{128... | collective-permute-start | bytes 196616 | tf_op jit(solution)/shard_map/ppermute | solution.py:129
  126.3 7.5 %collective-permute-done.3 = bf16[128,256]{1,0:T(8,128)(2,1)S(1)} collective-permute-done((bf16[128,256]{1,0:T(8,128)(2,1)S(1)}, bf16[128,256]{1,0:T(8,128)(2,1)S(1)}, u32[]{:S(2)}, u32[]{:S(2)}) %collective-permute-start.3) | collective-permute-done | bytes 65568 | tf_op jit(solution)/shard_map/ppermute | solution.py:129
  133.9 0.0 copy-done.2
  133.9 0.0 copy-done.4
  133.9 0.0 copy-done.6
  133.9 0.0 copy-done.10
  133.9 0.0 copy-done.12
  133.9 0.9 copy-done.8
  134.8 2.1 %shard_map.105 = (bf16[512,128]{1,0:T(8,128)(2,1)}, bf16[512,128]{1,0:T(8,128)(2,1)}, bf16[512,128]{1,0:T(8,128)(2,1)}) custom-call(bf16[512,128]{1,0:T(8,128)(2,1)S(1)} %copy-done.2, bf16[512,128]{1,0:T(8,128)(2,1)S(1)} %copy-done.4, bf16[512,128]{1,0:T(8,128)(2,1)S(1)} %copy-done.6, f32[1,128]{1,0:T(1,128)S(1)} %bitcast.15, f32[1,128]{1,0:T(1,128)S(1)} %bitcast.17, ...), custom_call_target="tpu_custom_call" | custom-call | flops 167772160 | bytes 2097152 | tf_op jit(solution)/shard_map/pallas_call | solution.py:117
  137.0 0.6 copy.12
  (10 shorter events, 0.1 us)
Async XLA Ops:
  7.2 76.7 %all-gather.5.cloned.1.call-start = ((), (), s32[]{:S(2)}) async-start(), calls=%async_computation.6 | async-start | bytes 1769472 | tf_op jit(solution)/shard_map/all_gather | solution.py:150
  7.2 0.9 copy-start.7
  19.9 11.4 %collective-permute-start = (bf16[128,256]{1,0:T(8,128)(2,1)}, bf16[128,256]{1,0:T(8,128)(2,1)S(1)}, u32[]{:S(2)}, u32[]{:S(2)}) collective-permute-start(bf16[128,256]{1,0:T(8,128)(2,1)} %param.12), channel_id=1, source_target_pairs={{0,0},{1,64},{2,128},{3,192},{64,1},{65,65},{66,129},{67,193},{128... | collective-permute-start | bytes 196616 | tf_op jit(solution)/shard_map/ppermute | solution.py:129
  26.4 0.9 copy-start.1
  27.3 0.9 copy-start.3
  28.2 0.9 copy-start.5
  29.1 0.7 copy-start.9
  29.8 0.7 copy-start.11
  32.1 35.7 %all-to-all-start.1 = ((bf16[4,128,512]{2,1,0:T(8,128)(2,1)}), bf16[4,128,512]{2,1,0:T(8,128)(2,1)S(1)}, u32[]{:S(2)}, u32[]{:S(2)}) async-start(bf16[4,128,512]{2,1,0:T(8,128)(2,1)} %broadcast_in_dim.2), calls=%async_computation.1 | async-start | bytes 1048576 | tf_op jit(solution)/shard_map/all_to_all | solution.py:134
  67.8 16.0 %collective-permute-start.1 = (bf16[4,128,512]{2,1,0:T(8,128)(2,1)S(1)}, bf16[4,128,512]{2,1,0:T(8,128)(2,1)S(1)}, u32[]{:S(2)}, u32[]{:S(2)}) collective-permute-start(bf16[4,128,512]{2,1,0:T(8,128)(2,1)S(1)} %all-to-all-done.1.own_ref), channel_id=1, source_target_pairs={{0,32},{32,0},{1,33},{33,1},{2,34},{34,2},{3,35},{35,3},{4,36},{36... | collective-permute-start | bytes 1572872 | tf_op jit(solution)/shard_map/ppermute | solution.py:138
  83.9 1.4 copy-start
  86.3 7.4 %collective-permute-start.2 = (bf16[4,512,128]{2,1,0:T(8,128)(2,1)S(1)}, bf16[4,512,128]{2,1,0:T(8,128)(2,1)}, u32[]{:S(2)}, u32[]{:S(2)}) collective-permute-start(bf16[4,512,128]{2,1,0:T(8,128)(2,1)S(1)} %get-tuple-element.32), channel_id=1, source_target_pairs={{0,32},{32,0},{1,33},{33,1},{2,34},{34,2},{3,35},{35,3},{4,36},{36... | collective-permute-start | bytes 1572872 | tf_op jit(solution)/shard_map/ppermute | solution.py:138
  90.1 16.7 %all-to-all-start.2 = ((bf16[4,3,128,256]{3,2,1,0:T(8,128)(2,1)}), bf16[4,3,128,256]{3,2,1,0:T(8,128)(2,1)S(1)}, u32[]{:S(2)}, u32[]{:S(2)}) async-start(bf16[4,3,128,256]{3,2,1,0:T(8,128)(2,1)} %shard_map.106), calls=%async_computation.3 | async-start | bytes 1572864 | tf_op jit(solution)/shard_map/all_to_all | solution.py:186
  93.6 40.3 %reduce-scatter.2.cloned.1.call-start = ((), (), s32[]{:S(2)}) async-start(), calls=%async_computation.5 | async-start | bytes 655360 | tf_op jit(solution)/shard_map/reduce_scatter | solution.py:188
  93.7 40.2 %copy-start.2 = (bf16[512,128]{1,0:T(8,128)(2,1)S(1)}, bf16[512,128]{1,0:T(8,128)(2,1)}, u32[]{:S(2)}) copy-start(bf16[512,128]{1,0:T(8,128)(2,1)} %q_ref.3) | copy-start | bytes 393220
  93.7 40.2 %copy-start.4 = (bf16[512,128]{1,0:T(8,128)(2,1)S(1)}, bf16[512,128]{1,0:T(8,128)(2,1)}, u32[]{:S(2)}) copy-start(bf16[512,128]{1,0:T(8,128)(2,1)} %k_ref.3) | copy-start | bytes 393220
  93.7 40.2 %copy-start.6 = (bf16[512,128]{1,0:T(8,128)(2,1)S(1)}, bf16[512,128]{1,0:T(8,128)(2,1)}, u32[]{:S(2)}) copy-start(bf16[512,128]{1,0:T(8,128)(2,1)} %v_ref.3) | copy-start | bytes 393220
  93.7 40.2 %copy-start.10 = (f32[128]{0:T(128)S(1)}, f32[128]{0:T(128)}, u32[]{:S(2)}) copy-start(f32[128]{0:T(128)} %param.10) | copy-start | bytes 1540
  93.7 40.2 %copy-start.12 = (f32[128]{0:T(128)S(1)}, f32[128]{0:T(128)}, u32[]{:S(2)}) copy-start(f32[128]{0:T(128)} %param.11) | copy-start | bytes 1540
  124.4 9.5 %collective-permute-start.3 = (bf16[128,256]{1,0:T(8,128)(2,1)S(1)}, bf16[128,256]{1,0:T(8,128)(2,1)S(1)}, u32[]{:S(2)}, u32[]{:S(2)}) collective-permute-start(bf16[128,256]{1,0:T(8,128)(2,1)S(1)} %fusion.1), channel_id=1, source_target_pairs={{0,0},{1,64},{2,128},{3,192},{64,1},{65,65},{66,129},{67,193},{128... | collective-permute-start | bytes 196616 | tf_op jit(solution)/shard_map/ppermute | solution.py:129
  133.9 0.9 copy-start.8
Sparse Core Ops, SparseCore 0:
  20.0 48.0 all-gather.4
  97.5 29.1 reduce-scatter.1

commit v12 on v10

--- a/solution.py
+++ b/solution.py
@@ -147,7 +147,6 @@
     groups = NC * NL
     pieces = call(cut_kernel, shape((groups, rows, WIDE), BF16), 0, 1 << 18, (grad_output,))
     exchanged = lax.all_to_all(pieces, ("core", "zl"), 0, 0, tiled=True)
-    gathered = lax.all_gather(exchanged, "y", axis=0)
 
     mixed, attention = call(
         forward_kernel,
@@ -156,8 +155,9 @@
         1 << 20,
         (query_input, key_input, value_input, query_gain, key_gain),
     )
-    exchanged, out_weight = lax.optimization_barrier((exchanged, out_weight))
-    zones = share(cross(out_weight), "zh", NZ)
+    exchanged, crossed = lax.optimization_barrier((exchanged, cross(out_weight)))
+    gathered = lax.all_gather(exchanged, "y", axis=0)
+    zones = share(crossed, "zh", NZ)
     mixed, zones = lax.optimization_barrier((mixed, zones))
     mixed_own = share(mixed, "zl", NL)
     own = lax.all_gather(zones, "x", axis=0)

time: 140 us -> 141 us (level)
  the two profiles are of different devices: /device:TPU:1 before, /device:TPU:128 now
where the time goes in v12:
time: 141 us; the launch traced here: 140 us
  waiting for transfers between devices  42.2 us (30%)
  blocking collectives  35.4 us (25%)
  starting transfers between devices  34.4 us (24%)
  between operations  14.1 us (10%)
  Pallas kernels  6.97 us (5%)
  local copies, waits for them, and re-layouts  6.13 us (4%)
    all_to_all x1, blocking collectives, shards(): last = lax.all_to_all(by_zone, 'zh', 0, 0, tiled=True)  21.4 us
    ppermute x2, waiting for transfers between devices, cross(): return lax.ppermute(entry, ('x', 'zl'), pairs)  15.3 us
    all_gather x1, blocking collectives, shards(): own = lax.all_gather(zones, 'x', axis=0)  13.9 us
    all_to_all x1, waiting for transfers between devices, shards(): spread = lax.all_to_all(partial, 'x', 0, 0, tiled=True)  12 us
    all_to_all x2, starting transfers between devices, share(): return lax.all_to_all(copies, axis, 0, 0, tiled=True)  11.5 us
    all_to_all x1, starting transfers between devices, shards(): exchanged = lax.all_to_all(pieces, ('core', 'zl'), 0, 0, tiled=True)  11.1 us
    all_to_all x2, waiting for transfers between devices, share(): return lax.all_to_all(copies, axis, 0, 0, tiled=True)  8.92 us
    pallas_call x5, Pallas kernels, call(): pl.pallas_call(kernel, out_shape=outs, in_specs=[pl.BlockSpec(memory_spac...  6.97 us
  transfers between devices with their start and end apart: 10, of which 6 were waited for; matrix products, arithmetic and copies ran while one was open for 2% of the time, Pallas kernels for 2%

profile of v12, /device:TPU:128, one launch (start us, length us, event | category | flops | bytes accessed | tf_op | source)
XLA Modules:
  0.0 140.3 jit_solution(3773047152281961544)
XLA Ops:
  7.2 0.0 copy-start.3
  7.2 0.0 copy-start.2
  7.2 0.0 copy-start.1
  7.2 0.0 copy-start.4
  7.2 1.0 copy-done.4
  8.2 0.0 copy-start.6
  8.2 0.0 copy-start.7
  8.2 0.7 shard_map.103
  8.9 11.1 %all-to-all-start = ((bf16[8,16,768]{2,1,0:T(8,128)(2,1)}), bf16[8,16,768]{2,1,0:T(8,128)(2,1)S(1)}, u32[]{:S(2)}, u32[]{:S(2)}) async-start(bf16[8,16,768]{2,1,0:T(8,128)(2,1)} %shard_map.103), calls=%async_computation | async-start | bytes 393216 | tf_op jit(solution)/shard_map/all_to_all | solution.py:149
  19.9 0.0 all-gather.4.cloned.1.call-start
  19.9 1.9 %collective-permute-start = (bf16[128,256]{1,0:T(8,128)(2,1)}, bf16[128,256]{1,0:T(8,128)(2,1)S(1)}, u32[]{:S(2)}, u32[]{:S(2)}) collective-permute-start(bf16[128,256]{1,0:T(8,128)(2,1)} %param.12), channel_id=1, source_target_pairs={{0,0},{1,64},{2,128},{3,192},{64,1},{65,65},{66,129},{67,193},{128... | collective-permute-start | bytes 196616 | tf_op jit(solution)/shard_map/ppermute | solution.py:129
  21.8 7.7 %collective-permute-done = bf16[128,256]{1,0:T(8,128)(2,1)S(1)} collective-permute-done((bf16[128,256]{1,0:T(8,128)(2,1)}, bf16[128,256]{1,0:T(8,128)(2,1)S(1)}, u32[]{:S(2)}, u32[]{:S(2)}) %collective-permute-start) | collective-permute-done | bytes 65568 | tf_op jit(solution)/shard_map/ppermute | solution.py:129
  29.6 0.0 all-to-all-done
  29.6 0.7 copy-done.8
  30.3 0.0 all-gather.4.cloned.1.call-update
  30.3 0.7 broadcast_in_dim.4
  31.0 7.3 %all-to-all-start.1 = ((bf16[3,128,256]{2,1,0:T(8,128)(2,1)}), bf16[3,128,256]{2,1,0:T(8,128)(2,1)S(1)}, u32[]{:S(2)}, u32[]{:S(2)}) async-start(bf16[3,128,256]{2,1,0:T(8,128)(2,1)} %broadcast_in_dim.4), calls=%async_computation.1 | async-start | bytes 393216 | tf_op jit(solution)/shard_map/all_to_all | solution.py:134
  38.3 0.0 copy-done.3
  38.3 0.0 copy-done.2
  38.3 0.0 copy-done.1
  38.3 0.0 copy-done.6
  38.3 0.0 copy-done.7
  38.3 0.8 shard_map.102
  39.1 8.9 %all-to-all-done.1 = bf16[3,128,256]{2,1,0:T(8,128)(2,1)S(1)} async-done(((bf16[3,128,256]{2,1,0:T(8,128)(2,1)}), bf16[3,128,256]{2,1,0:T(8,128)(2,1)S(1)}, u32[]{:S(2)}, u32[]{:S(2)}) %all-to-all-start.1) | async-done | bytes 196640 | tf_op jit(solution)/shard_map/all_to_all | solution.py:134
  48.1 0.8 broadcast_in_dim.5
  48.9 4.2 %all-to-all-start.2 = ((bf16[4,128,512]{2,1,0:T(8,128)(2,1)}), bf16[4,128,512]{2,1,0:T(8,128)(2,1)S(1)}, u32[]{:S(2)}, u32[]{:S(2)}) async-start(bf16[4,128,512]{2,1,0:T(8,128)(2,1)} %broadcast_in_dim.5), calls=%async_computation.2 | async-start | bytes 1048576 | tf_op jit(solution)/shard_map/all_to_all | solution.py:134
  53.1 13.9 %all-gather.1 = bf16[12,128,256]{2,1,0:T(8,128)(2,1)S(1)} all-gather(bf16[3,128,256]{2,1,0:T(8,128)(2,1)S(1)} %all-to-all-done.1), channel_id=3, replica_groups=mesh['zh'=3,'x'=4,'core'=2,'y'=8,'zl'=4] {'x'}, dimensions={0}, use_global_device_ids=true | all-gather | bytes 983040 | tf_op jit(solution)/shard_map/all_gather | solution.py:163
  67.0 0.0 all-to-all-done.2.own_ref
  67.0 1.9 %collective-permute-start.1 = (bf16[4,128,512]{2,1,0:T(8,128)(2,1)S(1)}, bf16[4,128,512]{2,1,0:T(8,128)(2,1)S(1)}, u32[]{:S(2)}, u32[]{:S(2)}) collective-permute-start(bf16[4,128,512]{2,1,0:T(8,128)(2,1)S(1)} %all-to-all-done.2.own_ref), channel_id=1, source_target_pairs={{0,32},{32,0},{1,33},{33,1},{2,34},{34,2},{3,35},{35,3},{4,36},{36... | collective-permute-start | bytes 1572872 | tf_op jit(solution)/shard_map/ppermute | solution.py:138
  69.0 1.9 %collective-permute-done.1.other_ref = bf16[4,128,512]{2,1,0:T(8,128)(2,1)S(1)} collective-permute-done((bf16[4,128,512]{2,1,0:T(8,128)(2,1)S(1)}, bf16[4,128,512]{2,1,0:T(8,128)(2,1)S(1)}, u32[]{:S(2)}, u32[]{:S(2)}) %collective-permute-start.1) | collective-permute-done | bytes 524320 | tf_op jit(solution)/shard_map/ppermute | solution.py:138
  70.8 4.1 %all-gather.4.cloned.1.call-done = bf16[64,16,768]{2,1,0:T(8,128)(2,1)} async-done(((bf16[8,16,768]{2,1,0:T(8,128)(2,1)}), bf16[64,16,768]{2,1,0:T(8,128)(2,1)}) %all-gather.4.cloned.1.call-update) | async-done | bytes 1572880 | tf_op jit(solution)/shard_map/all_gather | solution.py:159
  74.9 1.4 %copy-done = bf16[64,16,768]{2,1,0:T(8,128)(2,1)S(1)} copy-done((bf16[64,16,768]{2,1,0:T(8,128)(2,1)S(1)}, bf16[64,16,768]{2,1,0:T(8,128)(2,1)}, u32[]{:S(2)}) %copy-start) | copy-done | bytes 1572888
  76.3 1.4 %shard_map.104 = (bf16[4,512,128]{2,1,0:T(8,128)(2,1)S(1)}, bf16[4,512,128]{2,1,0:T(8,128)(2,1)}) custom-call(bf16[8,8,16,768]{3,2,1,0:T(8,128)(2,1)S(1)} %bitcast.9, bf16[4,3,128,256]{3,2,1,0:T(8,128)(2,1)S(1)} %bitcast.11), custom_call_target="tpu_custom_call" | custom-call | flops 805306368 | bytes 4194304 | tf_op jit(solution)/shard_map/pallas_call | solution.py:117
  77.7 1.9 %collective-permute-start.2 = (bf16[4,512,128]{2,1,0:T(8,128)(2,1)}, bf16[4,512,128]{2,1,0:T(8,128)(2,1)S(1)}, u32[]{:S(2)}, u32[]{:S(2)}) collective-permute-start(bf16[4,512,128]{2,1,0:T(8,128)(2,1)} %get-tuple-element.34), channel_id=1, source_target_pairs={{0,32},{32,0},{1,33},{33,1},{2,34},{34,2},{3,35},{35,3},{4,36},{36... | collective-permute-start | bytes 1572872 | tf_op jit(solution)/shard_map/ppermute | solution.py:138
  79.7 1.9 %shard_map.106 = bf16[4,3,128,256]{3,2,1,0:T(8,128)(2,1)} custom-call(bf16[8,8,16,768]{3,2,1,0:T(8,128)(2,1)S(1)} %bitcast.10, bf16[4,128,512]{2,1,0:T(8,128)(2,1)S(1)} %all-to-all-done.2.own_ref, bf16[4,128,512]{2,1,0:T(8,128)(2,1)S(1)} %collective-permute-done.1.other_ref), custom_call_target="tpu_custom_call" | custom-call | flops 805306368 | bytes 5242880 | tf_op jit(solution)/shard_map/pallas_call | solution.py:117
  81.5 4.2 %all-to-all-start.3 = ((bf16[4,3,128,256]{3,2,1,0:T(8,128)(2,1)}), bf16[4,3,128,256]{3,2,1,0:T(8,128)(2,1)S(1)}, u32[]{:S(2)}, u32[]{:S(2)}) async-start(bf16[4,3,128,256]{3,2,1,0:T(8,128)(2,1)} %shard_map.106), calls=%async_computation.4 | async-start | bytes 1572864 | tf_op jit(solution)/shard_map/all_to_all | solution.py:185
  85.8 0.0 reduce-scatter.2.cloned.1.call-start
  85.8 0.0 collective-permute-done.2
  85.8 1.0 add_convert_fusion
  86.8 0.0 reduce-scatter.2.cloned.1.call-update
  86.8 12.0 %all-to-all-done.3 = bf16[4,3,128,256]{3,2,1,0:T(8,128)(2,1)S(1)} async-done(((bf16[4,3,128,256]{3,2,1,0:T(8,128)(2,1)}), bf16[4,3,128,256]{3,2,1,0:T(8,128)(2,1)S(1)}, u32[]{:S(2)}, u32[]{:S(2)}) %all-to-all-start.3) | async-done | bytes 786464 | tf_op jit(solution)/shard_map/all_to_all | solution.py:185
  98.7 0.1 fusion
  98.8 21.4 %all_to_all.25 = bf16[3,128,256]{2,1,0:T(8,128)(2,1)S(1)} all-to-all(bf16[3,128,256]{2,1,0:T(8,128)(2,1)S(1)} %fusion), channel_id=1, replica_groups=mesh['zh'=3,'x'=4,'core'=2,'y'=8,'zl'=4] {'zh'}, dimensions={0} | all-to-all | bytes 393216 | tf_op jit(solution)/shard_map/all_to_all | solution.py:189
  120.3 1.9 %collective-permute-start.3 = (bf16[128,256]{1,0:T(8,128)(2,1)S(1)}, bf16[128,256]{1,0:T(8,128)(2,1)S(1)}, u32[]{:S(2)}, u32[]{:S(2)}) collective-permute-start(bf16[128,256]{1,0:T(8,128)(2,1)S(1)} %fusion.1), channel_id=1, source_target_pairs={{0,0},{1,64},{2,128},{3,192},{64,1},{65,65},{66,129},{67,193},{128... | collective-permute-start | bytes 196616 | tf_op jit(solution)/shard_map/ppermute | solution.py:129
  122.2 7.5 %collective-permute-done.3 = bf16[128,256]{1,0:T(8,128)(2,1)S(1)} collective-permute-done((bf16[128,256]{1,0:T(8,128)(2,1)S(1)}, bf16[128,256]{1,0:T(8,128)(2,1)S(1)}, u32[]{:S(2)}, u32[]{:S(2)}) %collective-permute-start.3) | collective-permute-done | bytes 65568 | tf_op jit(solution)/shard_map/ppermute | solution.py:129
  129.7 0.9 copy-done.5
  130.7 2.1 %shard_map.105 = (bf16[512,128]{1,0:T(8,128)(2,1)}, bf16[512,128]{1,0:T(8,128)(2,1)}, bf16[512,128]{1,0:T(8,128)(2,1)}) custom-call(bf16[512,128]{1,0:T(8,128)(2,1)S(1)} %copy-done.1, bf16[512,128]{1,0:T(8,128)(2,1)S(1)} %copy-done.2, bf16[512,128]{1,0:T(8,128)(2,1)S(1)} %copy-done.3, f32[1,128]{1,0:T(1,128)S(1)} %bitcast.14, f32[1,128]{1,0:T(1,128)S(1)} %bitcast.16, ...), custom_call_target="tpu_custom_call" | custom-call | flops 167772160 | bytes 2097152 | tf_op jit(solution)/shard_map/pallas_call | solution.py:117
  132.8 0.6 copy.12
  (5 shorter events, 0.0 us)
Async XLA Ops:
  7.2 31.1 %copy-start.3 = (bf16[512,128]{1,0:T(8,128)(2,1)S(1)}, bf16[512,128]{1,0:T(8,128)(2,1)}, u32[]{:S(2)}) copy-start(bf16[512,128]{1,0:T(8,128)(2,1)} %v_ref.3) | copy-start | bytes 393220
  7.2 31.1 %copy-start.2 = (bf16[512,128]{1,0:T(8,128)(2,1)S(1)}, bf16[512,128]{1,0:T(8,128)(2,1)}, u32[]{:S(2)}) copy-start(bf16[512,128]{1,0:T(8,128)(2,1)} %k_ref.3) | copy-start | bytes 393220
  7.2 31.1 %copy-start.1 = (bf16[512,128]{1,0:T(8,128)(2,1)S(1)}, bf16[512,128]{1,0:T(8,128)(2,1)}, u32[]{:S(2)}) copy-start(bf16[512,128]{1,0:T(8,128)(2,1)} %q_ref.3) | copy-start | bytes 393220
  7.2 1.0 copy-start.4
  8.2 30.1 %copy-start.6 = (f32[128]{0:T(128)S(1)}, f32[128]{0:T(128)}, u32[]{:S(2)}) copy-start(f32[128]{0:T(128)} %param.10) | copy-start | bytes 1540
  8.2 30.1 %copy-start.7 = (f32[128]{0:T(128)S(1)}, f32[128]{0:T(128)}, u32[]{:S(2)}) copy-start(f32[128]{0:T(128)} %param.11) | copy-start | bytes 1540
  8.9 20.7 %all-to-all-start = ((bf16[8,16,768]{2,1,0:T(8,128)(2,1)}), bf16[8,16,768]{2,1,0:T(8,128)(2,1)S(1)}, u32[]{:S(2)}, u32[]{:S(2)}) async-start(bf16[8,16,768]{2,1,0:T(8,128)(2,1)} %shard_map.103), calls=%async_computation | async-start | bytes 393216 | tf_op jit(solution)/shard_map/all_to_all | solution.py:149
  19.9 55.0 %all-gather.4.cloned.1.call-start = ((), (), s32[]{:S(2)}) async-start(), calls=%async_computation.7 | async-start | bytes 1769472 | tf_op jit(solution)/shard_map/all_gather | solution.py:159
  19.9 9.7 %collective-permute-start = (bf16[128,256]{1,0:T(8,128)(2,1)}, bf16[128,256]{1,0:T(8,128)(2,1)S(1)}, u32[]{:S(2)}, u32[]{:S(2)}) collective-permute-start(bf16[128,256]{1,0:T(8,128)(2,1)} %param.12), channel_id=1, source_target_pairs={{0,0},{1,64},{2,128},{3,192},{64,1},{65,65},{66,129},{67,193},{128... | collective-permute-start | bytes 196616 | tf_op jit(solution)/shard_map/ppermute | solution.py:129
  29.6 0.7 copy-start.8
  31.0 17.1 %all-to-all-start.1 = ((bf16[3,128,256]{2,1,0:T(8,128)(2,1)}), bf16[3,128,256]{2,1,0:T(8,128)(2,1)S(1)}, u32[]{:S(2)}, u32[]{:S(2)}) async-start(bf16[3,128,256]{2,1,0:T(8,128)(2,1)} %broadcast_in_dim.4), calls=%async_computation.1 | async-start | bytes 393216 | tf_op jit(solution)/shard_map/all_to_all | solution.py:134
  48.9 18.1 %all-to-all-start.2 = ((bf16[4,128,512]{2,1,0:T(8,128)(2,1)}), bf16[4,128,512]{2,1,0:T(8,128)(2,1)S(1)}, u32[]{:S(2)}, u32[]{:S(2)}) async-start(bf16[4,128,512]{2,1,0:T(8,128)(2,1)} %broadcast_in_dim.5), calls=%async_computation.2 | async-start | bytes 1048576 | tf_op jit(solution)/shard_map/all_to_all | solution.py:134
  67.0 3.8 %collective-permute-start.1 = (bf16[4,128,512]{2,1,0:T(8,128)(2,1)S(1)}, bf16[4,128,512]{2,1,0:T(8,128)(2,1)S(1)}, u32[]{:S(2)}, u32[]{:S(2)}) collective-permute-start(bf16[4,128,512]{2,1,0:T(8,128)(2,1)S(1)} %all-to-all-done.2.own_ref), channel_id=1, source_target_pairs={{0,32},{32,0},{1,33},{33,1},{2,34},{34,2},{3,35},{35,3},{4,36},{36... | collective-permute-start | bytes 1572872 | tf_op jit(solution)/shard_map/ppermute | solution.py:138
  74.9 1.4 %copy-start = (bf16[64,16,768]{2,1,0:T(8,128)(2,1)S(1)}, bf16[64,16,768]{2,1,0:T(8,128)(2,1)}, u32[]{:S(2)}) copy-start(bf16[64,16,768]{2,1,0:T(8,128)(2,1)} %all-gather.4.cloned.1.call-done) | copy-start | bytes 4718596
  77.7 8.0 %collective-permute-start.2 = (bf16[4,512,128]{2,1,0:T(8,128)(2,1)}, bf16[4,512,128]{2,1,0:T(8,128)(2,1)S(1)}, u32[]{:S(2)}, u32[]{:S(2)}) collective-permute-start(bf16[4,512,128]{2,1,0:T(8,128)(2,1)} %get-tuple-element.34), channel_id=1, source_target_pairs={{0,32},{32,0},{1,33},{33,1},{2,34},{34,2},{3,35},{35,3},{4,36},{36... | collective-permute-start | bytes 1572872 | tf_op jit(solution)/shard_map/ppermute | solution.py:138
  81.5 17.2 %all-to-all-start.3 = ((bf16[4,3,128,256]{3,2,1,0:T(8,128)(2,1)}), bf16[4,3,128,256]{3,2,1,0:T(8,128)(2,1)S(1)}, u32[]{:S(2)}, u32[]{:S(2)}) async-start(bf16[4,3,128,256]{3,2,1,0:T(8,128)(2,1)} %shard_map.106), calls=%async_computation.4 | async-start | bytes 1572864 | tf_op jit(solution)/shard_map/all_to_all | solution.py:185
  85.8 44.0 %reduce-scatter.2.cloned.1.call-start = ((), (), s32[]{:S(2)}) async-start(), calls=%async_computation.6 | async-start | bytes 655360 | tf_op jit(solution)/shard_map/reduce_scatter | solution.py:187
  120.3 9.5 %collective-permute-start.3 = (bf16[128,256]{1,0:T(8,128)(2,1)S(1)}, bf16[128,256]{1,0:T(8,128)(2,1)S(1)}, u32[]{:S(2)}, u32[]{:S(2)}) collective-permute-start(bf16[128,256]{1,0:T(8,128)(2,1)S(1)} %fusion.1), channel_id=1, source_target_pairs={{0,0},{1,64},{2,128},{3,192},{64,1},{65,65},{66,129},{67,193},{128... | collective-permute-start | bytes 196616 | tf_op jit(solution)/shard_map/ppermute | solution.py:129
  129.7 0.9 copy-start.5
Sparse Core Ops, SparseCore 0:
  30.4 44.4 all-gather.3
  89.7 34.4 reduce-scatter.1

commit v13 on v10

--- a/solution.py
+++ b/solution.py
@@ -65,12 +65,14 @@
         mixed_ref[:, rows] = mixed.astype(BF16)
 
 
-def backward_kernel(
-    q_ref, k_ref, v_ref, qg_ref, kg_ref, att_ref, gh_ref, dq_ref, dk_ref, dv_ref
-):
+def backward_kernel(q_ref, k_ref, v_ref, qg_ref, kg_ref, att_ref, *refs):
+    gh_refs, (dq_ref, dk_ref, dv_ref) = refs[:NL], refs[NL:]
     for image in range(IMAGES):
         rows = pl.ds(image * PATCH, PATCH)
-        grad_heads = gh_ref[rows, :]
+        total = gh_refs[0][rows, :].astype(F32)
+        for part in range(1, NL):
+            total = total + gh_refs[part][rows, :].astype(F32)
+        grad_heads = total.astype(BF16)
         query_unit, query_inv = normalize(q_ref[rows, :])
         key_unit, key_inv = normalize(k_ref[rows, :])
         query_low = (query_unit * qg_ref[...]).astype(BF16)
@@ -92,15 +94,15 @@
 
 
 def heads_kernel(g_ref, own_ref, keep_ref, send_ref):
-    core = lax.axis_index("core")
+    core, low = lax.axis_index("core"), lax.axis_index("zl")
     for ref, side in ((send_ref, 1 - core), (keep_ref, core)):
         total = None
-        for step in range(NZ):
-            rows = block(g_ref, side, step)
-            term = dot(rows, own_ref[:, step].reshape(NL * DH, BLK), 1, 1)
+        for zone in range(NZ):
+            weight = jnp.concatenate([own_ref[low ^ step, zone] for step in range(NL)], axis=0)
+            term = dot(block(g_ref, side, zone), weight, 1, 1)
             total = term if total is None else total + term
-        for head in range(NL):
-            ref[head] = total[:, head * DH : (head + 1) * DH].astype(BF16)
+        for step in range(NL):
+            ref[step] = total[:, step * DH : (step + 1) * DH].astype(BF16)
 
 
 def weight_kernel(g_ref, own_ref, other_ref, out_ref):
@@ -129,6 +131,10 @@
     return lax.ppermute(entry, ("x", "zl"), pairs)
 
 
+def flip(entry, step):
+    return lax.ppermute(entry, "zl", [(at, at ^ step) for at in range(NL)])
+
+
 def share(entry, axis, size):
     copies = jnp.broadcast_to(entry[None], (size,) + entry.shape)
     return lax.all_to_all(copies, axis, 0, 0, tiled=True)
@@ -183,8 +189,10 @@
         (gathered, mixed_own, mixed_other),
     )
     spread = lax.all_to_all(partial, "x", 0, 0, tiled=True)
-    summed = (keep.astype(F32) + received.astype(F32)).astype(BF16)
-    grad_heads = lax.psum_scatter(summed, "zl", scatter_dimension=0, tiled=True)
+    summed = [
+        (keep[step].astype(F32) + received[step].astype(F32)).astype(BF16) for step in range(NL)
+    ]
+    grad_heads = [summed[0]] + [flip(summed[step], step) for step in range(1, NL)]
     by_zone = sum(spread[part].astype(F32) for part in range(NX)).astype(BF16)
     last = lax.all_to_all(by_zone, "zh", 0, 0, tiled=True)
     grad_weight = cross(sum(last[zone].astype(F32) for zone in range(NZ)).astype(BF16))
@@ -194,7 +202,7 @@
         (shape((TOK, DH), BF16),) * 3,
         5 * 2 * IMAGES * PATCH * PATCH * DH,
         2 << 20,
-        (query_input, key_input, value_input, query_gain, key_gain, attention, grad_heads.reshape(TOK, DH)),
+        (query_input, key_input, value_input, query_gain, key_gain, attention, *grad_heads),
     )
     return grad_query, grad_key, grad_value, grad_weight
 

time: 140 us -> 141 us (level)
  starting transfers between devices: 32.8 us -> 46.7 us
  blocking collectives: 45.2 us -> 34.1 us
  waiting for transfers between devices: 33.7 us -> 30.6 us
    reduce_scatter x1 -> x0, waiting for transfers between devices: 13.4 us -> none  [shards(): grad_heads = lax.psum_scatter(summed, 'zl', scatter_dimension=0, tiled=True)]
    ppermute x0 -> x3, waiting for transfers between devices: none -> 11.8 us  [flip(): return lax.ppermute(entry, 'zl', [(at, at ^ step) for at in range(NL)])]
    all_to_all x1 -> x0, blocking collectives: 11.1 us -> none  [shards(): last = lax.all_to_all(by_zone, 'zh', 0, 0, tiled=True)]
    ppermute x0 -> x3, starting transfers between devices: none -> 9.45 us  [flip(): return lax.ppermute(entry, 'zl', [(at, at ^ step) for at in range(NL)])]
    all_to_all x0 -> x1, starting transfers between devices: none -> 3.83 us  [shards(): last = lax.all_to_all(by_zone, 'zh', 0, 0, tiled=True)]
    add x1, other arithmetic: 0.1 us -> 2 us  [shards(): by_zone = sum((spread[part].astype(F32) for part in range(NX))).astype(BF16)]
    all_to_all x1, waiting for transfers between devices: 11.2 us -> 9.8 us  [shards(): spread = lax.all_to_all(partial, 'x', 0, 0, tiled=True)]
    unnamed x17 -> x19, local copies, waits for them, and re-layouts: 3.98 us -> 3.87 us
  transfers between devices with their start and end apart: 9 -> 12, of which waited for: 5 -> 6; matrix products, arithmetic and copies ran while one was open for 2% -> 3% of each run, Pallas kernels for 2% -> 2%
where the time goes in v13:
time: 141 us; the launch traced here: 139 us
  starting transfers between devices  46.7 us (33%)
  blocking collectives  34.1 us (24%)
  waiting for transfers between devices  30.6 us (22%)
  between operations  14.2 us (10%)
  Pallas kernels  5.94 us (4%)
  local copies, waits for them, and re-layouts  5.43 us (4%)
  other arithmetic  2.17 us (2%)
    all_to_all x1, blocking collectives, shards(): exchanged = lax.all_to_all(pieces, ('core', 'zl'), 0, 0, tiled=True)  21.2 us
    all_to_all x2, starting transfers between devices, share(): return lax.all_to_all(copies, axis, 0, 0, tiled=True)  17.7 us
    all_gather x1, blocking collectives, shards(): own = lax.all_gather(zones, 'x', axis=0)  12.8 us
    ppermute x3, waiting for transfers between devices, flip(): return lax.ppermute(entry, 'zl', [(at, at ^ step) for at in range(NL)])  11.8 us
    all_to_all x1, waiting for transfers between devices, shards(): spread = lax.all_to_all(partial, 'x', 0, 0, tiled=True)  9.8 us
    ppermute x3, starting transfers between devices, flip(): return lax.ppermute(entry, 'zl', [(at, at ^ step) for at in range(NL)])  9.45 us
    ppermute x2, starting transfers between devices, swap_cores(): return lax.ppermute(entry, 'core', [(0, 1), (1, 0)])  9.35 us
    all_to_all x2, waiting for transfers between devices, share(): return lax.all_to_all(copies, axis, 0, 0, tiled=True)  7.53 us
  transfers between devices with their start and end apart: 12, of which 6 were waited for; matrix products, arithmetic and copies ran while one was open for 3% of the time, Pallas kernels for 2%

profile of v13, /device:TPU:1, one launch (start us, length us, event | category | flops | bytes accessed | tf_op | source)
XLA Modules:
  0.0 139.2 jit_solution(3334315772779290955)
XLA Ops:
  7.2 0.0 copy-start.3
  7.2 0.0 copy-start.2
  7.2 0.0 copy-start.1
  7.2 0.0 all-gather.4.cloned.1.call-start
  7.2 0.0 copy-start.4
  7.3 1.0 copy-done.4
  8.3 21.2 %all_to_all.25 = bf16[8,16,768]{2,1,0:T(8,128)(2,1)} all-to-all(bf16[8,16,768]{2,1,0:T(8,128)(2,1)S(1)} %shard_map.103), channel_id=1, replica_groups=mesh['zh'=3,'x'=4,'core'=2,'y'=8,'zl'=4] {'core','zl'}, dimensions={0} | all-to-all | bytes 393216 | tf_op jit(solution)/shard_map/all_to_all | solution.py:155
  29.5 0.0 all-gather.4.cloned.1.call-update
  29.5 1.5 %collective-permute-start = (bf16[128,256]{1,0:T(8,128)(2,1)}, bf16[128,256]{1,0:T(8,128)(2,1)S(1)}, u32[]{:S(2)}, u32[]{:S(2)}) collective-permute-start(bf16[128,256]{1,0:T(8,128)(2,1)} %param.12), channel_id=1, source_target_pairs={{0,0},{1,64},{2,128},{3,192},{64,1},{65,65},{66,129},{67,193},{128... | collective-permute-start | bytes 196616 | tf_op jit(solution)/shard_map/ppermute | solution.py:131
  31.0 0.0 collective-permute-done
  31.0 0.7 broadcast_in_dim.4
  31.8 6.0 %all-to-all-start.1 = ((bf16[3,128,256]{2,1,0:T(8,128)(2,1)}), bf16[3,128,256]{2,1,0:T(8,128)(2,1)S(1)}, u32[]{:S(2)}, u32[]{:S(2)}) async-start(bf16[3,128,256]{2,1,0:T(8,128)(2,1)} %broadcast_in_dim.4), calls=%async_computation.1 | async-start | bytes 393216 | tf_op jit(solution)/shard_map/all_to_all | solution.py:140
  37.8 0.0 copy-done.3
  37.8 0.0 copy-done.2
  37.8 0.0 copy-done.1
  37.8 0.0 copy-done.5
  37.8 0.8 shard_map.102
  38.7 6.5 %all-to-all-done.1 = bf16[3,128,256]{2,1,0:T(8,128)(2,1)S(1)} async-done(((bf16[3,128,256]{2,1,0:T(8,128)(2,1)}), bf16[3,128,256]{2,1,0:T(8,128)(2,1)S(1)}, u32[]{:S(2)}, u32[]{:S(2)}) %all-to-all-start.1) | async-done | bytes 196640 | tf_op jit(solution)/shard_map/all_to_all | solution.py:140
  45.1 0.8 broadcast_in_dim.5
  46.0 11.7 %all-to-all-start.2 = ((bf16[4,128,512]{2,1,0:T(8,128)(2,1)}), bf16[4,128,512]{2,1,0:T(8,128)(2,1)S(1)}, u32[]{:S(2)}, u32[]{:S(2)}) async-start(bf16[4,128,512]{2,1,0:T(8,128)(2,1)} %broadcast_in_dim.5), calls=%async_computation.2 | async-start | bytes 1048576 | tf_op jit(solution)/shard_map/all_to_all | solution.py:140
  57.6 12.8 %all-gather.1 = bf16[12,128,256]{2,1,0:T(8,128)(2,1)S(1)} all-gather(bf16[3,128,256]{2,1,0:T(8,128)(2,1)S(1)} %all-to-all-done.1), channel_id=3, replica_groups=mesh['zh'=3,'x'=4,'core'=2,'y'=8,'zl'=4] {'x'}, dimensions={0}, use_global_device_ids=true | all-gather | bytes 983040 | tf_op jit(solution)/shard_map/all_gather | solution.py:169
  70.5 1.1 all-to-all-done.2.own_ref
  71.5 7.1 %collective-permute-start.1 = (bf16[4,128,512]{2,1,0:T(8,128)(2,1)S(1)}, bf16[4,128,512]{2,1,0:T(8,128)(2,1)S(1)}, u32[]{:S(2)}, u32[]{:S(2)}) collective-permute-start(bf16[4,128,512]{2,1,0:T(8,128)(2,1)S(1)} %all-to-all-done.2.own_ref), channel_id=1, source_target_pairs={{0,32},{32,0},{1,33},{33,1},{2,34},{34,2},{3,35},{35,3},{4,36},{36... | collective-permute-start | bytes 1572872 | tf_op jit(solution)/shard_map/ppermute | solution.py:144
  78.6 1.5 %collective-permute-done.1.other_ref = bf16[4,128,512]{2,1,0:T(8,128)(2,1)S(1)} collective-permute-done((bf16[4,128,512]{2,1,0:T(8,128)(2,1)S(1)}, bf16[4,128,512]{2,1,0:T(8,128)(2,1)S(1)}, u32[]{:S(2)}, u32[]{:S(2)}) %collective-permute-start.1) | collective-permute-done | bytes 524320 | tf_op jit(solution)/shard_map/ppermute | solution.py:144
  80.1 1.4 %copy-done = bf16[64,16,768]{2,1,0:T(8,128)(2,1)S(1)} copy-done((bf16[64,16,768]{2,1,0:T(8,128)(2,1)S(1)}, bf16[64,16,768]{2,1,0:T(8,128)(2,1)}, u32[]{:S(2)}) %copy-start) | copy-done | bytes 1572888
  81.6 1.0 shard_map.104
  82.6 0.0 copy-start.7
  82.6 0.8 copy-done.7
  83.4 1.9 %shard_map.106 = bf16[4,3,128,256]{3,2,1,0:T(8,128)(2,1)} custom-call(bf16[8,8,16,768]{3,2,1,0:T(8,128)(2,1)S(1)} %bitcast.17, bf16[4,128,512]{2,1,0:T(8,128)(2,1)S(1)} %all-to-all-done.2.own_ref, bf16[4,128,512]{2,1,0:T(8,128)(2,1)S(1)} %collective-permute-done.1.other_ref), custom_call_target="tpu_custom_call" | custom-call | flops 805306368 | bytes 5242880 | tf_op jit(solution)/shard_map/pallas_call | solution.py:119
  85.3 4.2 %all-to-all-start.3 = ((bf16[4,3,128,256]{3,2,1,0:T(8,128)(2,1)}), bf16[4,3,128,256]{3,2,1,0:T(8,128)(2,1)}, u32[]{:S(2)}, u32[]{:S(2)}) async-start(bf16[4,3,128,256]{3,2,1,0:T(8,128)(2,1)} %shard_map.106), calls=%async_computation.3 | async-start | bytes 1572864 | tf_op jit(solution)/shard_map/all_to_all | solution.py:191
  89.5 0.0 copy-done.8
  89.5 2.3 %collective-permute-start.2 = (bf16[4,512,128]{2,1,0:T(8,128)(2,1)S(1)}, bf16[4,512,128]{2,1,0:T(8,128)(2,1)S(1)}, u32[]{:S(2)}, u32[]{:S(2)}) collective-permute-start(bf16[4,512,128]{2,1,0:T(8,128)(2,1)S(1)} %copy-done.8), channel_id=1, source_target_pairs={{0,32},{32,0},{1,33},{33,1},{2,34},{34,2},{3,35},{35,3},{4,36},{36... | collective-permute-start | bytes 1572872 | tf_op jit(solution)/shard_map/ppermute | solution.py:144
  91.8 9.8 %all-to-all-done.3 = bf16[4,3,128,256]{3,2,1,0:T(8,128)(2,1)} async-done(((bf16[4,3,128,256]{3,2,1,0:T(8,128)(2,1)}), bf16[4,3,128,256]{3,2,1,0:T(8,128)(2,1)}, u32[]{:S(2)}, u32[]{:S(2)}) %all-to-all-start.3) | async-done | bytes 786464 | tf_op jit(solution)/shard_map/all_to_all | solution.py:191
  101.6 2.0 %fusion = bf16[3,128,256]{2,1,0:T(8,128)(2,1)} fusion(bf16[4,3,128,256]{3,2,1,0:T(8,128)(2,1)} %all-to-all-done.3), kind=kLoop, calls=%fused_computation.5 | loop fusion | flops 786432 | bytes 983040 | tf_op jit(solution)/shard_map/add | solution.py:196
  103.6 3.8 %all-to-all-start.4 = ((bf16[3,128,256]{2,1,0:T(8,128)(2,1)}), bf16[3,128,256]{2,1,0:T(8,128)(2,1)S(1)}, u32[]{:S(2)}, u32[]{:S(2)}) async-start(bf16[3,128,256]{2,1,0:T(8,128)(2,1)} %fusion), calls=%async_computation.4 | async-start | bytes 393216 | tf_op jit(solution)/shard_map/all_to_all | solution.py:197
  107.4 0.0 collective-permute-done.2
  107.4 0.1 fusion.4
  107.6 5.3 %collective-permute-start.5 = (bf16[512,128]{1,0:T(8,128)(2,1)S(1)}, bf16[512,128]{1,0:T(8,128)(2,1)S(1)}, u32[]{:S(2)}, u32[]{:S(2)}) collective-permute-start(bf16[512,128]{1,0:T(8,128)(2,1)S(1)} %get-tuple-element.38), channel_id=1, source_target_pairs={{0,3},{1,2},{2,1},{3,0},{4,7},{5,6},{6,5},{7,4},{8,11},{9,10},{10,... | collective-permute-start | bytes 393224 | tf_op jit(solution)/shard_map/ppermute | solution.py:135
  112.9 1.9 %collective-permute-start.4 = (bf16[512,128]{1,0:T(8,128)(2,1)S(1)}, bf16[512,128]{1,0:T(8,128)(2,1)S(1)}, u32[]{:S(2)}, u32[]{:S(2)}) collective-permute-start(bf16[512,128]{1,0:T(8,128)(2,1)S(1)} %get-tuple-element.39), channel_id=1, source_target_pairs={{0,2},{1,3},{2,0},{3,1},{4,6},{5,7},{6,4},{7,5},{8,10},{9,11},{10,... | collective-permute-start | bytes 393224 | tf_op jit(solution)/shard_map/ppermute | solution.py:135
  114.9 2.2 %collective-permute-start.3 = (bf16[512,128]{1,0:T(8,128)(2,1)S(1)}, bf16[512,128]{1,0:T(8,128)(2,1)S(1)}, u32[]{:S(2)}, u32[]{:S(2)}) collective-permute-start(bf16[512,128]{1,0:T(8,128)(2,1)S(1)} %get-tuple-element.40), channel_id=1, source_target_pairs={{0,1},{1,0},{2,3},{3,2},{4,5},{5,4},{6,7},{7,6},{8,9},{9,8},{10,11... | collective-permute-start | bytes 393224 | tf_op jit(solution)/shard_map/ppermute | solution.py:135
  117.1 0.0 all-to-all-done.4
  117.1 0.7 collective-permute-start.6
  117.8 3.2 %collective-permute-done.5.refs_3_ = bf16[512,128]{1,0:T(8,128)(2,1)S(1)} collective-permute-done((bf16[512,128]{1,0:T(8,128)(2,1)S(1)}, bf16[512,128]{1,0:T(8,128)(2,1)S(1)}, u32[]{:S(2)}, u32[]{:S(2)}) %collective-permute-start.5) | collective-permute-done | bytes 131104 | tf_op jit(solution)/shard_map/ppermute | solution.py:135
  120.9 8.6 %collective-permute-done.4.refs_2_ = bf16[512,128]{1,0:T(8,128)(2,1)S(1)} collective-permute-done((bf16[512,128]{1,0:T(8,128)(2,1)S(1)}, bf16[512,128]{1,0:T(8,128)(2,1)S(1)}, u32[]{:S(2)}, u32[]{:S(2)}) %collective-permute-start.4) | collective-permute-done | bytes 131104 | tf_op jit(solution)/shard_map/ppermute | solution.py:135
  129.5 0.0 collective-permute-done.3.refs_1_
  129.5 2.2 %shard_map.105 = (bf16[512,128]{1,0:T(8,128)(2,1)}, bf16[512,128]{1,0:T(8,128)(2,1)}, bf16[512,128]{1,0:T(8,128)(2,1)}) custom-call(bf16[512,128]{1,0:T(8,128)(2,1)S(1)} %copy-done.1, bf16[512,128]{1,0:T(8,128)(2,1)S(1)} %copy-done.2, bf16[512,128]{1,0:T(8,128)(2,1)S(1)} %copy-done.3, f32[1,128]{1,0:T(1,128)S(1)} %bitcast.20, f32[1,128]{1,0:T(1,128)S(1)} %bitcast.22, ...), custom_call_target="tpu_custom_call" | custom-call | flops 167772160 | bytes 2097152 | tf_op jit(solution)/shard_map/pallas_call | solution.py:119
  131.7 0.0 collective-permute-done.6
  131.7 0.6 copy.12
  (8 shorter events, 0.1 us)
Async XLA Ops:
  7.2 30.6 %copy-start.3 = (bf16[512,128]{1,0:T(8,128)(2,1)S(1)}, bf16[512,128]{1,0:T(8,128)(2,1)}, u32[]{:S(2)}) copy-start(bf16[512,128]{1,0:T(8,128)(2,1)} %v_ref.3) | copy-start | bytes 393220
  7.2 30.6 %copy-start.2 = (bf16[512,128]{1,0:T(8,128)(2,1)S(1)}, bf16[512,128]{1,0:T(8,128)(2,1)}, u32[]{:S(2)}) copy-start(bf16[512,128]{1,0:T(8,128)(2,1)} %k_ref.3) | copy-start | bytes 393220
  7.2 30.6 %copy-start.1 = (bf16[512,128]{1,0:T(8,128)(2,1)S(1)}, bf16[512,128]{1,0:T(8,128)(2,1)}, u32[]{:S(2)}) copy-start(bf16[512,128]{1,0:T(8,128)(2,1)} %q_ref.3) | copy-start | bytes 393220
  7.2 72.9 %all-gather.4.cloned.1.call-start = ((), (), s32[]{:S(2)}) async-start(), calls=%async_computation.5 | async-start | bytes 1769472 | tf_op jit(solution)/shard_map/all_gather | solution.py:156
  7.2 1.0 copy-start.4
  8.3 29.5 %copy-start.5 = (f32[128]{0:T(128)S(1)}, f32[128]{0:T(128)}, u32[]{:S(2)}) copy-start(f32[128]{0:T(128)} %param.10) | copy-start | bytes 1540
  8.3 29.5 %copy-start.6 = (f32[128]{0:T(128)S(1)}, f32[128]{0:T(128)}, u32[]{:S(2)}) copy-start(f32[128]{0:T(128)} %param.11) | copy-start | bytes 1540
  29.5 1.5 %collective-permute-start = (bf16[128,256]{1,0:T(8,128)(2,1)}, bf16[128,256]{1,0:T(8,128)(2,1)S(1)}, u32[]{:S(2)}, u32[]{:S(2)}) collective-permute-start(bf16[128,256]{1,0:T(8,128)(2,1)} %param.12), channel_id=1, source_target_pairs={{0,0},{1,64},{2,128},{3,192},{64,1},{65,65},{66,129},{67,193},{128... | collective-permute-start | bytes 196616 | tf_op jit(solution)/shard_map/ppermute | solution.py:131
  31.8 13.4 %all-to-all-start.1 = ((bf16[3,128,256]{2,1,0:T(8,128)(2,1)}), bf16[3,128,256]{2,1,0:T(8,128)(2,1)S(1)}, u32[]{:S(2)}, u32[]{:S(2)}) async-start(bf16[3,128,256]{2,1,0:T(8,128)(2,1)} %broadcast_in_dim.4), calls=%async_computation.1 | async-start | bytes 393216 | tf_op jit(solution)/shard_map/all_to_all | solution.py:140
  46.0 25.6 %all-to-all-start.2 = ((bf16[4,128,512]{2,1,0:T(8,128)(2,1)}), bf16[4,128,512]{2,1,0:T(8,128)(2,1)S(1)}, u32[]{:S(2)}, u32[]{:S(2)}) async-start(bf16[4,128,512]{2,1,0:T(8,128)(2,1)} %broadcast_in_dim.5), calls=%async_computation.2 | async-start | bytes 1048576 | tf_op jit(solution)/shard_map/all_to_all | solution.py:140
  71.5 8.6 %collective-permute-start.1 = (bf16[4,128,512]{2,1,0:T(8,128)(2,1)S(1)}, bf16[4,128,512]{2,1,0:T(8,128)(2,1)S(1)}, u32[]{:S(2)}, u32[]{:S(2)}) collective-permute-start(bf16[4,128,512]{2,1,0:T(8,128)(2,1)S(1)} %all-to-all-done.2.own_ref), channel_id=1, source_target_pairs={{0,32},{32,0},{1,33},{33,1},{2,34},{34,2},{3,35},{35,3},{4,36},{36... | collective-permute-start | bytes 1572872 | tf_op jit(solution)/shard_map/ppermute | solution.py:144
  80.1 1.4 %copy-start = (bf16[64,16,768]{2,1,0:T(8,128)(2,1)S(1)}, bf16[64,16,768]{2,1,0:T(8,128)(2,1)}, u32[]{:S(2)}) copy-start(bf16[64,16,768]{2,1,0:T(8,128)(2,1)} %all-gather.4.cloned.1.call-done) | copy-start | bytes 4718596
  82.6 0.8 copy-start.7
  83.4 6.1 %copy-start.8 = (bf16[4,512,128]{2,1,0:T(8,128)(2,1)S(1)}, bf16[4,512,128]{2,1,0:T(8,128)(2,1)}, u32[]{:S(2)}) copy-start(bf16[4,512,128]{2,1,0:T(8,128)(2,1)} %copy-done.7) | copy-start | bytes 1572868
  85.3 16.3 %all-to-all-start.3 = ((bf16[4,3,128,256]{3,2,1,0:T(8,128)(2,1)}), bf16[4,3,128,256]{3,2,1,0:T(8,128)(2,1)}, u32[]{:S(2)}, u32[]{:S(2)}) async-start(bf16[4,3,128,256]{3,2,1,0:T(8,128)(2,1)} %shard_map.106), calls=%async_computation.3 | async-start | bytes 1572864 | tf_op jit(solution)/shard_map/all_to_all | solution.py:191
  89.5 17.9 %collective-permute-start.2 = (bf16[4,512,128]{2,1,0:T(8,128)(2,1)S(1)}, bf16[4,512,128]{2,1,0:T(8,128)(2,1)S(1)}, u32[]{:S(2)}, u32[]{:S(2)}) collective-permute-start(bf16[4,512,128]{2,1,0:T(8,128)(2,1)S(1)} %copy-done.8), channel_id=1, source_target_pairs={{0,32},{32,0},{1,33},{33,1},{2,34},{34,2},{3,35},{35,3},{4,36},{36... | collective-permute-start | bytes 1572872 | tf_op jit(solution)/shard_map/ppermute | solution.py:144
  103.6 13.5 %all-to-all-start.4 = ((bf16[3,128,256]{2,1,0:T(8,128)(2,1)}), bf16[3,128,256]{2,1,0:T(8,128)(2,1)S(1)}, u32[]{:S(2)}, u32[]{:S(2)}) async-start(bf16[3,128,256]{2,1,0:T(8,128)(2,1)} %fusion), calls=%async_computation.4 | async-start | bytes 393216 | tf_op jit(solution)/shard_map/all_to_all | solution.py:197
  107.6 13.4 %collective-permute-start.5 = (bf16[512,128]{1,0:T(8,128)(2,1)S(1)}, bf16[512,128]{1,0:T(8,128)(2,1)S(1)}, u32[]{:S(2)}, u32[]{:S(2)}) collective-permute-start(bf16[512,128]{1,0:T(8,128)(2,1)S(1)} %get-tuple-element.38), channel_id=1, source_target_pairs={{0,3},{1,2},{2,1},{3,0},{4,7},{5,6},{6,5},{7,4},{8,11},{9,10},{10,... | collective-permute-start | bytes 393224 | tf_op jit(solution)/shard_map/ppermute | solution.py:135
  112.9 16.6 %collective-permute-start.4 = (bf16[512,128]{1,0:T(8,128)(2,1)S(1)}, bf16[512,128]{1,0:T(8,128)(2,1)S(1)}, u32[]{:S(2)}, u32[]{:S(2)}) collective-permute-start(bf16[512,128]{1,0:T(8,128)(2,1)S(1)} %get-tuple-element.39), channel_id=1, source_target_pairs={{0,2},{1,3},{2,0},{3,1},{4,6},{5,7},{6,4},{7,5},{8,10},{9,11},{10,... | collective-permute-start | bytes 393224 | tf_op jit(solution)/shard_map/ppermute | solution.py:135
  114.9 14.7 %collective-permute-start.3 = (bf16[512,128]{1,0:T(8,128)(2,1)S(1)}, bf16[512,128]{1,0:T(8,128)(2,1)S(1)}, u32[]{:S(2)}, u32[]{:S(2)}) collective-permute-start(bf16[512,128]{1,0:T(8,128)(2,1)S(1)} %get-tuple-element.40), channel_id=1, source_target_pairs={{0,1},{1,0},{2,3},{3,2},{4,5},{5,4},{6,7},{7,6},{8,9},{9,8},{10,11... | collective-permute-start | bytes 393224 | tf_op jit(solution)/shard_map/ppermute | solution.py:135
  117.1 14.6 %collective-permute-start.6 = (bf16[128,256]{1,0:T(8,128)(2,1)S(1)}, bf16[128,256]{1,0:T(8,128)(2,1)S(1)}, u32[]{:S(2)}, u32[]{:S(2)}) collective-permute-start(bf16[128,256]{1,0:T(8,128)(2,1)S(1)} %fusion.5), channel_id=1, source_target_pairs={{0,0},{1,64},{2,128},{3,192},{64,1},{65,65},{66,129},{67,193},{128... | collective-permute-start | bytes 196616 | tf_op jit(solution)/shard_map/ppermute | solution.py:131
Sparse Core Ops, SparseCore 0:
  29.7 38.6 all-gather.3

commit v14 on v13

--- a/solution.py
+++ b/solution.py
@@ -193,6 +193,7 @@
         (keep[step].astype(F32) + received[step].astype(F32)).astype(BF16) for step in range(NL)
     ]
     grad_heads = [summed[0]] + [flip(summed[step], step) for step in range(1, NL)]
+    spread, *grad_heads = lax.optimization_barrier((spread, *grad_heads))
     by_zone = sum(spread[part].astype(F32) for part in range(NX)).astype(BF16)
     last = lax.all_to_all(by_zone, "zh", 0, 0, tiled=True)
     grad_weight = cross(sum(last[zone].astype(F32) for zone in range(NZ)).astype(BF16))

time: 141 us -> 142 us (level)
  the two profiles are of different devices: /device:TPU:1 before, /device:TPU:28 now
where the time goes in v14:
time: 142 us; the launch traced here: 141 us
  blocking collectives  43.3 us (30%)
  starting transfers between devices  40.3 us (28%)
  waiting for transfers between devices  31.4 us (22%)
  between operations  14.2 us (10%)
  Pallas kernels  6.33 us (4%)
  local copies, waits for them, and re-layouts  4.61 us (3%)
    all_to_all x2, starting transfers between devices, share(): return lax.all_to_all(copies, axis, 0, 0, tiled=True)  16.1 us
    all_to_all x1, blocking collectives, shards(): exchanged = lax.all_to_all(pieces, ('core', 'zl'), 0, 0, tiled=True)  15.1 us
    all_to_all x1, blocking collectives, shards(): last = lax.all_to_all(by_zone, 'zh', 0, 0, tiled=True)  15.1 us
    ppermute x2, waiting for transfers between devices, cross(): return lax.ppermute(entry, ('x', 'zl'), pairs)  14.9 us
    all_gather x1, blocking collectives, shards(): own = lax.all_gather(zones, 'x', axis=0)  13.1 us
    ppermute x3, starting transfers between devices, flip(): return lax.ppermute(entry, 'zl', [(at, at ^ step) for at in range(NL)])  10.1 us
    all_to_all x2, waiting for transfers between devices, share(): return lax.all_to_all(copies, axis, 0, 0, tiled=True)  7.52 us
    ppermute x3, waiting for transfers between devices, flip(): return lax.ppermute(entry, 'zl', [(at, at ^ step) for at in range(NL)])  7.09 us
  transfers between devices with their start and end apart: 11, of which 5 were waited for; matrix products, arithmetic and copies ran while one was open for 2% of the time, Pallas kernels for 3%

profile of v14, /device:TPU:28, one launch (start us, length us, event | category | flops | bytes accessed | tf_op | source)
XLA Modules:
  0.0 141.4 jit_solution(11401409679394922217)
XLA Ops:
  7.2 0.0 copy-start.3
  7.2 0.0 copy-start.2
  7.2 0.0 copy-start.1
  7.2 0.0 all-gather.4.cloned.1.call-start
  7.2 0.0 copy-start.4
  7.3 1.0 copy-done.4
  8.3 0.0 copy-start.5
  8.3 0.0 copy-start.6
  8.3 15.1 %all_to_all.25 = bf16[8,16,768]{2,1,0:T(8,128)(2,1)} all-to-all(bf16[8,16,768]{2,1,0:T(8,128)(2,1)S(1)} %shard_map.103), channel_id=1, replica_groups=mesh['zh'=3,'x'=4,'core'=2,'y'=8,'zl'=4] {'core','zl'}, dimensions={0} | all-to-all | bytes 393216 | tf_op jit(solution)/shard_map/all_to_all | solution.py:155
  23.4 0.0 all-gather.4.cloned.1.call-update
  23.4 2.6 %collective-permute-start = (bf16[128,256]{1,0:T(8,128)(2,1)}, bf16[128,256]{1,0:T(8,128)(2,1)S(1)}, u32[]{:S(2)}, u32[]{:S(2)}) collective-permute-start(bf16[128,256]{1,0:T(8,128)(2,1)} %param.12), channel_id=1, source_target_pairs={{0,0},{1,64},{2,128},{3,192},{64,1},{65,65},{66,129},{67,193},{128... | collective-permute-start | bytes 196616 | tf_op jit(solution)/shard_map/ppermute | solution.py:131
  26.0 8.4 %collective-permute-done = bf16[128,256]{1,0:T(8,128)(2,1)S(1)} collective-permute-done((bf16[128,256]{1,0:T(8,128)(2,1)}, bf16[128,256]{1,0:T(8,128)(2,1)S(1)}, u32[]{:S(2)}, u32[]{:S(2)}) %collective-permute-start) | collective-permute-done | bytes 65568 | tf_op jit(solution)/shard_map/ppermute | solution.py:131
  34.5 0.7 broadcast_in_dim.4
  35.2 12.6 %all-to-all-start.1 = ((bf16[3,128,256]{2,1,0:T(8,128)(2,1)}), bf16[3,128,256]{2,1,0:T(8,128)(2,1)S(1)}, u32[]{:S(2)}, u32[]{:S(2)}) async-start(bf16[3,128,256]{2,1,0:T(8,128)(2,1)} %broadcast_in_dim.4), calls=%async_computation.1 | async-start | bytes 393216 | tf_op jit(solution)/shard_map/all_to_all | solution.py:140
  47.8 0.0 copy-done.3
  47.8 0.0 copy-done.2
  47.8 0.0 copy-done.1
  47.8 0.0 copy-done.5
  47.8 0.0 copy-done.6
  47.8 0.8 shard_map.102
  48.6 7.5 %all-to-all-done.1 = bf16[3,128,256]{2,1,0:T(8,128)(2,1)S(1)} async-done(((bf16[3,128,256]{2,1,0:T(8,128)(2,1)}), bf16[3,128,256]{2,1,0:T(8,128)(2,1)S(1)}, u32[]{:S(2)}, u32[]{:S(2)}) %all-to-all-start.1) | async-done | bytes 196640 | tf_op jit(solution)/shard_map/all_to_all | solution.py:140
  56.2 0.8 broadcast_in_dim.5
  57.0 3.5 %all-to-all-start.2 = ((bf16[4,128,512]{2,1,0:T(8,128)(2,1)}), bf16[4,128,512]{2,1,0:T(8,128)(2,1)S(1)}, u32[]{:S(2)}, u32[]{:S(2)}) async-start(bf16[4,128,512]{2,1,0:T(8,128)(2,1)} %broadcast_in_dim.5), calls=%async_computation.2 | async-start | bytes 1048576 | tf_op jit(solution)/shard_map/all_to_all | solution.py:140
  60.5 13.1 %all-gather.1 = bf16[12,128,256]{2,1,0:T(8,128)(2,1)S(1)} all-gather(bf16[3,128,256]{2,1,0:T(8,128)(2,1)S(1)} %all-to-all-done.1), channel_id=3, replica_groups=mesh['zh'=3,'x'=4,'core'=2,'y'=8,'zl'=4] {'x'}, dimensions={0}, use_global_device_ids=true | all-gather | bytes 983040 | tf_op jit(solution)/shard_map/all_gather | solution.py:169
  73.6 0.0 all-to-all-done.2.own_ref
  73.6 1.9 %collective-permute-start.1 = (bf16[4,128,512]{2,1,0:T(8,128)(2,1)S(1)}, bf16[4,128,512]{2,1,0:T(8,128)(2,1)S(1)}, u32[]{:S(2)}, u32[]{:S(2)}) collective-permute-start(bf16[4,128,512]{2,1,0:T(8,128)(2,1)S(1)} %all-to-all-done.2.own_ref), channel_id=1, source_target_pairs={{0,32},{32,0},{1,33},{33,1},{2,34},{34,2},{3,35},{35,3},{4,36},{36... | collective-permute-start | bytes 1572872 | tf_op jit(solution)/shard_map/ppermute | solution.py:144
  75.5 1.9 %collective-permute-done.1.other_ref = bf16[4,128,512]{2,1,0:T(8,128)(2,1)S(1)} collective-permute-done((bf16[4,128,512]{2,1,0:T(8,128)(2,1)S(1)}, bf16[4,128,512]{2,1,0:T(8,128)(2,1)S(1)}, u32[]{:S(2)}, u32[]{:S(2)}) %collective-permute-start.1) | collective-permute-done | bytes 524320 | tf_op jit(solution)/shard_map/ppermute | solution.py:144
  77.4 0.0 all-gather.4.cloned.1.call-done
  77.4 1.4 copy-done
  78.8 1.4 %shard_map.104 = (bf16[4,512,128]{2,1,0:T(8,128)(2,1)S(1)}, bf16[4,512,128]{2,1,0:T(8,128)(2,1)}) custom-call(bf16[8,8,16,768]{3,2,1,0:T(8,128)(2,1)S(1)} %bitcast.16, bf16[4,3,128,256]{3,2,1,0:T(8,128)(2,1)S(1)} %bitcast.18), custom_call_target="tpu_custom_call" | custom-call | flops 805306368 | bytes 4194304 | tf_op jit(solution)/shard_map/pallas_call | solution.py:119
  80.3 2.0 %collective-permute-start.2 = (bf16[4,512,128]{2,1,0:T(8,128)(2,1)}, bf16[4,512,128]{2,1,0:T(8,128)(2,1)}, u32[]{:S(2)}, u32[]{:S(2)}) collective-permute-start(bf16[4,512,128]{2,1,0:T(8,128)(2,1)} %get-tuple-element.39), channel_id=1, source_target_pairs={{0,32},{32,0},{1,33},{33,1},{2,34},{34,2},{3,35},{35,3},{4,36},{36... | collective-permute-start | bytes 1572872 | tf_op jit(solution)/shard_map/ppermute | solution.py:144
  82.3 1.9 %shard_map.105 = bf16[4,3,128,256]{3,2,1,0:T(8,128)(2,1)} custom-call(bf16[8,8,16,768]{3,2,1,0:T(8,128)(2,1)S(1)} %bitcast.17, bf16[4,128,512]{2,1,0:T(8,128)(2,1)S(1)} %all-to-all-done.2.own_ref, bf16[4,128,512]{2,1,0:T(8,128)(2,1)S(1)} %collective-permute-done.1.other_ref), custom_call_target="tpu_custom_call" | custom-call | flops 805306368 | bytes 5242880 | tf_op jit(solution)/shard_map/pallas_call | solution.py:119
  84.2 5.5 %all-to-all-start.3 = ((bf16[4,3,128,256]{3,2,1,0:T(8,128)(2,1)}), bf16[4,3,128,256]{3,2,1,0:T(8,128)(2,1)S(1)}, u32[]{:S(2)}, u32[]{:S(2)}) async-start(bf16[4,3,128,256]{3,2,1,0:T(8,128)(2,1)} %shard_map.105), calls=%async_computation.3 | async-start | bytes 1572864 | tf_op jit(solution)/shard_map/all_to_all | solution.py:191
  89.7 0.0 collective-permute-done.2
  89.7 1.2 fusion.4
  91.0 5.4 %collective-permute-start.5 = (bf16[512,128]{1,0:T(8,128)(2,1)S(1)}, bf16[512,128]{1,0:T(8,128)(2,1)S(1)}, u32[]{:S(2)}, u32[]{:S(2)}) collective-permute-start(bf16[512,128]{1,0:T(8,128)(2,1)S(1)} %get-tuple-element.48), channel_id=1, source_target_pairs={{0,3},{1,2},{2,1},{3,0},{4,7},{5,6},{6,5},{7,4},{8,11},{9,10},{10,... | collective-permute-start | bytes 393224 | tf_op jit(solution)/shard_map/ppermute | solution.py:135
  96.4 1.9 %collective-permute-start.4 = (bf16[512,128]{1,0:T(8,128)(2,1)S(1)}, bf16[512,128]{1,0:T(8,128)(2,1)S(1)}, u32[]{:S(2)}, u32[]{:S(2)}) collective-permute-start(bf16[512,128]{1,0:T(8,128)(2,1)S(1)} %get-tuple-element.49), channel_id=1, source_target_pairs={{0,2},{1,3},{2,0},{3,1},{4,6},{5,7},{6,4},{7,5},{8,10},{9,11},{10,... | collective-permute-start | bytes 393224 | tf_op jit(solution)/shard_map/ppermute | solution.py:135
  98.3 2.8 %collective-permute-start.3 = (bf16[512,128]{1,0:T(8,128)(2,1)S(1)}, bf16[512,128]{1,0:T(8,128)(2,1)S(1)}, u32[]{:S(2)}, u32[]{:S(2)}) collective-permute-start(bf16[512,128]{1,0:T(8,128)(2,1)S(1)} %get-tuple-element.50), channel_id=1, source_target_pairs={{0,1},{1,0},{2,3},{3,2},{4,5},{5,4},{6,7},{7,6},{8,9},{9,8},{10,11... | collective-permute-start | bytes 393224 | tf_op jit(solution)/shard_map/ppermute | solution.py:135
  101.1 0.0 all-to-all-done.3
  101.1 0.0 collective-permute-done.5.refs_3_
  101.1 7.1 %collective-permute-done.4.refs_2_ = bf16[512,128]{1,0:T(8,128)(2,1)S(1)} collective-permute-done((bf16[512,128]{1,0:T(8,128)(2,1)S(1)}, bf16[512,128]{1,0:T(8,128)(2,1)S(1)}, u32[]{:S(2)}, u32[]{:S(2)}) %collective-permute-start.4) | collective-permute-done | bytes 131104 | tf_op jit(solution)/shard_map/ppermute | solution.py:135
  108.2 0.0 collective-permute-done.3.refs_1_
  108.2 0.1 fusion
  108.3 15.1 %all_to_all.26 = bf16[3,128,256]{2,1,0:T(8,128)(2,1)S(1)} all-to-all(bf16[3,128,256]{2,1,0:T(8,128)(2,1)S(1)} %fusion), channel_id=1, replica_groups=mesh['zh'=3,'x'=4,'core'=2,'y'=8,'zl'=4] {'zh'}, dimensions={0} | all-to-all | bytes 393216 | tf_op jit(solution)/shard_map/all_to_all | solution.py:198
  123.4 1.9 %collective-permute-start.6 = (bf16[128,256]{1,0:T(8,128)(2,1)S(1)}, bf16[128,256]{1,0:T(8,128)(2,1)S(1)}, u32[]{:S(2)}, u32[]{:S(2)}) collective-permute-start(bf16[128,256]{1,0:T(8,128)(2,1)S(1)} %fusion.5), channel_id=1, source_target_pairs={{0,0},{1,64},{2,128},{3,192},{64,1},{65,65},{66,129},{67,193},{128... | collective-permute-start | bytes 196616 | tf_op jit(solution)/shard_map/ppermute | solution.py:131
  125.3 2.2 %shard_map.106 = (bf16[512,128]{1,0:T(8,128)(2,1)}, bf16[512,128]{1,0:T(8,128)(2,1)}, bf16[512,128]{1,0:T(8,128)(2,1)}) custom-call(bf16[512,128]{1,0:T(8,128)(2,1)S(1)} %copy-done.1, bf16[512,128]{1,0:T(8,128)(2,1)S(1)} %copy-done.2, bf16[512,128]{1,0:T(8,128)(2,1)S(1)} %copy-done.3, f32[1,128]{1,0:T(1,128)S(1)} %bitcast.20, f32[1,128]{1,0:T(1,128)S(1)} %bitcast.22, ...), custom_call_target="tpu_custom_call" | custom-call | flops 167772160 | bytes 2097152 | tf_op jit(solution)/shard_map/pallas_call | solution.py:119
  127.5 6.4 %collective-permute-done.6 = bf16[128,256]{1,0:T(8,128)(2,1)S(1)} collective-permute-done((bf16[128,256]{1,0:T(8,128)(2,1)S(1)}, bf16[128,256]{1,0:T(8,128)(2,1)S(1)}, u32[]{:S(2)}, u32[]{:S(2)}) %collective-permute-start.6) | collective-permute-done | bytes 65568 | tf_op jit(solution)/shard_map/ppermute | solution.py:131
  133.9 0.6 copy.12
  (3 shorter events, 0.0 us)
Async XLA Ops:
  7.2 40.6 %copy-start.3 = (bf16[512,128]{1,0:T(8,128)(2,1)S(1)}, bf16[512,128]{1,0:T(8,128)(2,1)}, u32[]{:S(2)}) copy-start(bf16[512,128]{1,0:T(8,128)(2,1)} %v_ref.3) | copy-start | bytes 393220
  7.2 40.6 %copy-start.2 = (bf16[512,128]{1,0:T(8,128)(2,1)S(1)}, bf16[512,128]{1,0:T(8,128)(2,1)}, u32[]{:S(2)}) copy-start(bf16[512,128]{1,0:T(8,128)(2,1)} %k_ref.3) | copy-start | bytes 393220
  7.2 40.6 %copy-start.1 = (bf16[512,128]{1,0:T(8,128)(2,1)S(1)}, bf16[512,128]{1,0:T(8,128)(2,1)}, u32[]{:S(2)}) copy-start(bf16[512,128]{1,0:T(8,128)(2,1)} %q_ref.3) | copy-start | bytes 393220
  7.2 70.2 %all-gather.4.cloned.1.call-start = ((), (), s32[]{:S(2)}) async-start(), calls=%async_computation.5 | async-start | bytes 1769472 | tf_op jit(solution)/shard_map/all_gather | solution.py:156
  7.2 1.0 copy-start.4
  8.3 39.5 %copy-start.5 = (f32[128]{0:T(128)S(1)}, f32[128]{0:T(128)}, u32[]{:S(2)}) copy-start(f32[128]{0:T(128)} %param.10) | copy-start | bytes 1540
  8.3 39.5 %copy-start.6 = (f32[128]{0:T(128)S(1)}, f32[128]{0:T(128)}, u32[]{:S(2)}) copy-start(f32[128]{0:T(128)} %param.11) | copy-start | bytes 1540
  23.4 11.0 %collective-permute-start = (bf16[128,256]{1,0:T(8,128)(2,1)}, bf16[128,256]{1,0:T(8,128)(2,1)S(1)}, u32[]{:S(2)}, u32[]{:S(2)}) collective-permute-start(bf16[128,256]{1,0:T(8,128)(2,1)} %param.12), channel_id=1, source_target_pairs={{0,0},{1,64},{2,128},{3,192},{64,1},{65,65},{66,129},{67,193},{128... | collective-permute-start | bytes 196616 | tf_op jit(solution)/shard_map/ppermute | solution.py:131
  35.2 21.0 %all-to-all-start.1 = ((bf16[3,128,256]{2,1,0:T(8,128)(2,1)}), bf16[3,128,256]{2,1,0:T(8,128)(2,1)S(1)}, u32[]{:S(2)}, u32[]{:S(2)}) async-start(bf16[3,128,256]{2,1,0:T(8,128)(2,1)} %broadcast_in_dim.4), calls=%async_computation.1 | async-start | bytes 393216 | tf_op jit(solution)/shard_map/all_to_all | solution.py:140
  57.0 16.6 %all-to-all-start.2 = ((bf16[4,128,512]{2,1,0:T(8,128)(2,1)}), bf16[4,128,512]{2,1,0:T(8,128)(2,1)S(1)}, u32[]{:S(2)}, u32[]{:S(2)}) async-start(bf16[4,128,512]{2,1,0:T(8,128)(2,1)} %broadcast_in_dim.5), calls=%async_computation.2 | async-start | bytes 1048576 | tf_op jit(solution)/shard_map/all_to_all | solution.py:140
  73.6 3.8 %collective-permute-start.1 = (bf16[4,128,512]{2,1,0:T(8,128)(2,1)S(1)}, bf16[4,128,512]{2,1,0:T(8,128)(2,1)S(1)}, u32[]{:S(2)}, u32[]{:S(2)}) collective-permute-start(bf16[4,128,512]{2,1,0:T(8,128)(2,1)S(1)} %all-to-all-done.2.own_ref), channel_id=1, source_target_pairs={{0,32},{32,0},{1,33},{33,1},{2,34},{34,2},{3,35},{35,3},{4,36},{36... | collective-permute-start | bytes 1572872 | tf_op jit(solution)/shard_map/ppermute | solution.py:144
  77.4 1.4 copy-start
  80.3 9.5 %collective-permute-start.2 = (bf16[4,512,128]{2,1,0:T(8,128)(2,1)}, bf16[4,512,128]{2,1,0:T(8,128)(2,1)}, u32[]{:S(2)}, u32[]{:S(2)}) collective-permute-start(bf16[4,512,128]{2,1,0:T(8,128)(2,1)} %get-tuple-element.39), channel_id=1, source_target_pairs={{0,32},{32,0},{1,33},{33,1},{2,34},{34,2},{3,35},{35,3},{4,36},{36... | collective-permute-start | bytes 1572872 | tf_op jit(solution)/shard_map/ppermute | solution.py:144
  84.2 16.9 %all-to-all-start.3 = ((bf16[4,3,128,256]{3,2,1,0:T(8,128)(2,1)}), bf16[4,3,128,256]{3,2,1,0:T(8,128)(2,1)S(1)}, u32[]{:S(2)}, u32[]{:S(2)}) async-start(bf16[4,3,128,256]{3,2,1,0:T(8,128)(2,1)} %shard_map.105), calls=%async_computation.3 | async-start | bytes 1572864 | tf_op jit(solution)/shard_map/all_to_all | solution.py:191
  91.0 10.1 %collective-permute-start.5 = (bf16[512,128]{1,0:T(8,128)(2,1)S(1)}, bf16[512,128]{1,0:T(8,128)(2,1)S(1)}, u32[]{:S(2)}, u32[]{:S(2)}) collective-permute-start(bf16[512,128]{1,0:T(8,128)(2,1)S(1)} %get-tuple-element.48), channel_id=1, source_target_pairs={{0,3},{1,2},{2,1},{3,0},{4,7},{5,6},{6,5},{7,4},{8,11},{9,10},{10,... | collective-permute-start | bytes 393224 | tf_op jit(solution)/shard_map/ppermute | solution.py:135
  96.4 11.8 %collective-permute-start.4 = (bf16[512,128]{1,0:T(8,128)(2,1)S(1)}, bf16[512,128]{1,0:T(8,128)(2,1)S(1)}, u32[]{:S(2)}, u32[]{:S(2)}) collective-permute-start(bf16[512,128]{1,0:T(8,128)(2,1)S(1)} %get-tuple-element.49), channel_id=1, source_target_pairs={{0,2},{1,3},{2,0},{3,1},{4,6},{5,7},{6,4},{7,5},{8,10},{9,11},{10,... | collective-permute-start | bytes 393224 | tf_op jit(solution)/shard_map/ppermute | solution.py:135
  98.3 9.9 %collective-permute-start.3 = (bf16[512,128]{1,0:T(8,128)(2,1)S(1)}, bf16[512,128]{1,0:T(8,128)(2,1)S(1)}, u32[]{:S(2)}, u32[]{:S(2)}) collective-permute-start(bf16[512,128]{1,0:T(8,128)(2,1)S(1)} %get-tuple-element.50), channel_id=1, source_target_pairs={{0,1},{1,0},{2,3},{3,2},{4,5},{5,4},{6,7},{7,6},{8,9},{9,8},{10,11... | collective-permute-start | bytes 393224 | tf_op jit(solution)/shard_map/ppermute | solution.py:135
  123.4 10.5 %collective-permute-start.6 = (bf16[128,256]{1,0:T(8,128)(2,1)S(1)}, bf16[128,256]{1,0:T(8,128)(2,1)S(1)}, u32[]{:S(2)}, u32[]{:S(2)}) collective-permute-start(bf16[128,256]{1,0:T(8,128)(2,1)S(1)} %fusion.5), channel_id=1, source_target_pairs={{0,0},{1,64},{2,128},{3,192},{64,1},{65,65},{66,129},{67,193},{128... | collective-permute-start | bytes 196616 | tf_op jit(solution)/shard_map/ppermute | solution.py:131
Sparse Core Ops, SparseCore 0:
  23.5 47.4 all-gather.3

commit v15 on v10

--- a/solution.py
+++ b/solution.py
@@ -163,7 +163,7 @@
     own = lax.all_gather(zones, "x", axis=0)
     mixed_own, own = lax.optimization_barrier((mixed_own, own))
     mixed_other = swap_cores(mixed_own)
-    gathered, own, mixed_other = lax.optimization_barrier((gathered, own, mixed_other))
+    gathered, own = lax.optimization_barrier((gathered, own))
 
     half = (NL, TOK, DH)
     keep, send = call(

time: 140 us -> 138 us (0.986)
    ppermute x2, waiting for transfers between devices: 1.52 us -> 0.01 us  [swap_cores(): return lax.ppermute(entry, 'core', [(0, 1), (1, 0)])]
  transfers between devices with their start and end apart: 9 -> 9, of which waited for: 5 -> 4; matrix products, arithmetic and copies ran while one was open for 2% -> 2% of each run, Pallas kernels for 2% -> 3%
where the time goes in v15:
time: 138 us; the launch traced here: 137 us
  blocking collectives  45.1 us (33%)
  starting transfers between devices  32.4 us (23%)
  waiting for transfers between devices  32.4 us (23%)
  between operations  14.2 us (10%)
  Pallas kernels  6.28 us (5%)
  local copies, waits for them, and re-layouts  5.51 us (4%)
    all_to_all x1, blocking collectives, shards(): exchanged = lax.all_to_all(pieces, ('core', 'zl'), 0, 0, tiled=True)  21.2 us
    all_to_all x2, starting transfers between devices, share(): return lax.all_to_all(copies, axis, 0, 0, tiled=True)  17.7 us
    reduce_scatter x1, waiting for transfers between devices, shards(): grad_heads = lax.psum_scatter(summed, 'zl', scatter_dimension=0, tiled=True)  14 us
    all_gather x1, blocking collectives, shards(): own = lax.all_gather(zones, 'x', axis=0)  12.9 us
    all_to_all x1, blocking collectives, shards(): last = lax.all_to_all(by_zone, 'zh', 0, 0, tiled=True)  11 us
    all_to_all x1, waiting for transfers between devices, shards(): spread = lax.all_to_all(partial, 'x', 0, 0, tiled=True)  10.8 us
    ppermute x2, starting transfers between devices, swap_cores(): return lax.ppermute(entry, 'core', [(0, 1), (1, 0)])  8.98 us
    all_to_all x2, waiting for transfers between devices, share(): return lax.all_to_all(copies, axis, 0, 0, tiled=True)  7.52 us
  transfers between devices with their start and end apart: 9, of which 4 were waited for; matrix products, arithmetic and copies ran while one was open for 2% of the time, Pallas kernels for 3%

profile of v15, /device:TPU:1, one launch (start us, length us, event | category | flops | bytes accessed | tf_op | source)
XLA Modules:
  0.0 137.0 jit_solution(14423227917751856266)
XLA Ops:
  7.2 0.0 copy-start.3
  7.2 0.0 copy-start.2
  7.2 0.0 copy-start.1
  7.2 0.0 all-gather.4.cloned.1.call-start
  7.2 0.0 copy-start.4
  7.3 1.0 copy-done.4
  8.3 0.0 copy-start.6
  8.3 0.0 copy-start.7
  8.3 21.2 %all_to_all.25 = bf16[8,16,768]{2,1,0:T(8,128)(2,1)} all-to-all(bf16[8,16,768]{2,1,0:T(8,128)(2,1)S(1)} %shard_map.103), channel_id=1, replica_groups=mesh['zh'=3,'x'=4,'core'=2,'y'=8,'zl'=4] {'core','zl'}, dimensions={0} | all-to-all | bytes 393216 | tf_op jit(solution)/shard_map/all_to_all | solution.py:149
  29.5 0.0 all-gather.4.cloned.1.call-update
  29.5 1.5 %collective-permute-start = (bf16[128,256]{1,0:T(8,128)(2,1)}, bf16[128,256]{1,0:T(8,128)(2,1)S(1)}, u32[]{:S(2)}, u32[]{:S(2)}) collective-permute-start(bf16[128,256]{1,0:T(8,128)(2,1)} %param.12), channel_id=1, source_target_pairs={{0,0},{1,64},{2,128},{3,192},{64,1},{65,65},{66,129},{67,193},{128... | collective-permute-start | bytes 196616 | tf_op jit(solution)/shard_map/ppermute | solution.py:129
  31.0 0.0 collective-permute-done
  31.0 0.7 broadcast_in_dim.4
  31.7 6.0 %all-to-all-start.1 = ((bf16[3,128,256]{2,1,0:T(8,128)(2,1)}), bf16[3,128,256]{2,1,0:T(8,128)(2,1)S(1)}, u32[]{:S(2)}, u32[]{:S(2)}) async-start(bf16[3,128,256]{2,1,0:T(8,128)(2,1)} %broadcast_in_dim.4), calls=%async_computation.1 | async-start | bytes 393216 | tf_op jit(solution)/shard_map/all_to_all | solution.py:134
  37.8 0.0 copy-done.3
  37.8 0.0 copy-done.2
  37.8 0.0 copy-done.1
  37.8 0.0 copy-done.6
  37.8 0.0 copy-done.7
  37.8 0.8 shard_map.102
  38.6 6.5 %all-to-all-done.1 = bf16[3,128,256]{2,1,0:T(8,128)(2,1)S(1)} async-done(((bf16[3,128,256]{2,1,0:T(8,128)(2,1)}), bf16[3,128,256]{2,1,0:T(8,128)(2,1)S(1)}, u32[]{:S(2)}, u32[]{:S(2)}) %all-to-all-start.1) | async-done | bytes 196640 | tf_op jit(solution)/shard_map/all_to_all | solution.py:134
  45.1 0.8 broadcast_in_dim.5
  46.0 11.7 %all-to-all-start.2 = ((bf16[4,128,512]{2,1,0:T(8,128)(2,1)}), bf16[4,128,512]{2,1,0:T(8,128)(2,1)S(1)}, u32[]{:S(2)}, u32[]{:S(2)}) async-start(bf16[4,128,512]{2,1,0:T(8,128)(2,1)} %broadcast_in_dim.5), calls=%async_computation.2 | async-start | bytes 1048576 | tf_op jit(solution)/shard_map/all_to_all | solution.py:134
  57.6 12.9 %all-gather.1 = bf16[12,128,256]{2,1,0:T(8,128)(2,1)S(1)} all-gather(bf16[3,128,256]{2,1,0:T(8,128)(2,1)S(1)} %all-to-all-done.1), channel_id=3, replica_groups=mesh['zh'=3,'x'=4,'core'=2,'y'=8,'zl'=4] {'x'}, dimensions={0}, use_global_device_ids=true | all-gather | bytes 983040 | tf_op jit(solution)/shard_map/all_gather | solution.py:163
  70.5 1.0 all-to-all-done.2.own_ref
  71.5 7.1 %collective-permute-start.2 = (bf16[4,128,512]{2,1,0:T(8,128)(2,1)S(1)}, bf16[4,128,512]{2,1,0:T(8,128)(2,1)S(1)}, u32[]{:S(2)}, u32[]{:S(2)}) collective-permute-start(bf16[4,128,512]{2,1,0:T(8,128)(2,1)S(1)} %all-to-all-done.2.own_ref), channel_id=1, source_target_pairs={{0,32},{32,0},{1,33},{33,1},{2,34},{34,2},{3,35},{35,3},{4,36},{36... | collective-permute-start | bytes 1572872 | tf_op jit(solution)/shard_map/ppermute | solution.py:138
  78.6 0.0 all-gather.4.cloned.1.call-done
  78.6 0.0 copy-start
  78.6 1.4 %copy-done = bf16[64,16,768]{2,1,0:T(8,128)(2,1)S(1)} copy-done((bf16[64,16,768]{2,1,0:T(8,128)(2,1)S(1)}, bf16[64,16,768]{2,1,0:T(8,128)(2,1)}, u32[]{:S(2)}) %copy-start) | copy-done | bytes 1572888
  80.0 1.4 %shard_map.104 = (bf16[4,512,128]{2,1,0:T(8,128)(2,1)S(1)}, bf16[4,512,128]{2,1,0:T(8,128)(2,1)}) custom-call(bf16[8,8,16,768]{3,2,1,0:T(8,128)(2,1)S(1)} %bitcast.9, bf16[4,3,128,256]{3,2,1,0:T(8,128)(2,1)S(1)} %bitcast.11), custom_call_target="tpu_custom_call" | custom-call | flops 805306368 | bytes 4194304 | tf_op jit(solution)/shard_map/pallas_call | solution.py:117
  81.5 1.9 %collective-permute-start.1 = (bf16[4,512,128]{2,1,0:T(8,128)(2,1)}, bf16[4,512,128]{2,1,0:T(8,128)(2,1)S(1)}, u32[]{:S(2)}, u32[]{:S(2)}) collective-permute-start(bf16[4,512,128]{2,1,0:T(8,128)(2,1)} %get-tuple-element.30), channel_id=1, source_target_pairs={{0,32},{32,0},{1,33},{33,1},{2,34},{34,2},{3,35},{35,3},{4,36},{36... | collective-permute-start | bytes 1572872 | tf_op jit(solution)/shard_map/ppermute | solution.py:138
  83.4 0.0 collective-permute-done.2.other_ref
  83.4 1.9 %shard_map.106 = bf16[4,3,128,256]{3,2,1,0:T(8,128)(2,1)} custom-call(bf16[8,8,16,768]{3,2,1,0:T(8,128)(2,1)S(1)} %bitcast.10, bf16[4,128,512]{2,1,0:T(8,128)(2,1)S(1)} %all-to-all-done.2.own_ref, bf16[4,128,512]{2,1,0:T(8,128)(2,1)S(1)} %collective-permute-done.2.other_ref), custom_call_target="tpu_custom_call" | custom-call | flops 805306368 | bytes 5242880 | tf_op jit(solution)/shard_map/pallas_call | solution.py:117
  85.3 3.5 %all-to-all-start.3 = ((bf16[4,3,128,256]{3,2,1,0:T(8,128)(2,1)}), bf16[4,3,128,256]{3,2,1,0:T(8,128)(2,1)S(1)}, u32[]{:S(2)}, u32[]{:S(2)}) async-start(bf16[4,3,128,256]{3,2,1,0:T(8,128)(2,1)} %shard_map.106), calls=%async_computation.4 | async-start | bytes 1572864 | tf_op jit(solution)/shard_map/all_to_all | solution.py:185
  88.8 0.0 reduce-scatter.2.cloned.1.call-start
  88.8 0.0 collective-permute-done.1
  88.8 0.9 add_convert_fusion
  89.8 0.0 reduce-scatter.2.cloned.1.call-update
  89.8 10.8 %all-to-all-done.3 = bf16[4,3,128,256]{3,2,1,0:T(8,128)(2,1)S(1)} async-done(((bf16[4,3,128,256]{3,2,1,0:T(8,128)(2,1)}), bf16[4,3,128,256]{3,2,1,0:T(8,128)(2,1)S(1)}, u32[]{:S(2)}, u32[]{:S(2)}) %all-to-all-start.3) | async-done | bytes 786464 | tf_op jit(solution)/shard_map/all_to_all | solution.py:185
  100.6 0.1 fusion
  100.7 11.0 %all_to_all.26 = bf16[3,128,256]{2,1,0:T(8,128)(2,1)S(1)} all-to-all(bf16[3,128,256]{2,1,0:T(8,128)(2,1)S(1)} %fusion), channel_id=1, replica_groups=mesh['zh'=3,'x'=4,'core'=2,'y'=8,'zl'=4] {'zh'}, dimensions={0} | all-to-all | bytes 393216 | tf_op jit(solution)/shard_map/all_to_all | solution.py:189
  111.8 0.7 collective-permute-start.3
  112.5 0.0 collective-permute-done.3
  112.5 14.0 %reduce-scatter.2.cloned.1.call-done = bf16[1,512,128]{2,1,0:T(8,128)(2,1)} async-done(((bf16[4,512,128]{2,1,0:T(8,128)(2,1)}), bf16[1,512,128]{2,1,0:T(8,128)(2,1)}) %reduce-scatter.2.cloned.1.call-update) | async-done | bytes 131088 | tf_op jit(solution)/shard_map/reduce_scatter | solution.py:187
  126.5 0.0 copy-start.5
  126.5 0.9 copy-done.5
  127.4 2.1 %shard_map.105 = (bf16[512,128]{1,0:T(8,128)(2,1)}, bf16[512,128]{1,0:T(8,128)(2,1)}, bf16[512,128]{1,0:T(8,128)(2,1)}) custom-call(bf16[512,128]{1,0:T(8,128)(2,1)S(1)} %copy-done.1, bf16[512,128]{1,0:T(8,128)(2,1)S(1)} %copy-done.2, bf16[512,128]{1,0:T(8,128)(2,1)S(1)} %copy-done.3, f32[1,128]{1,0:T(1,128)S(1)} %bitcast.14, f32[1,128]{1,0:T(1,128)S(1)} %bitcast.16, ...), custom_call_target="tpu_custom_call" | custom-call | flops 167772160 | bytes 2097152 | tf_op jit(solution)/shard_map/pallas_call | solution.py:117
  129.5 0.6 copy.12
  (2 shorter events, 0.0 us)
Async XLA Ops:
  7.2 30.6 %copy-start.3 = (bf16[512,128]{1,0:T(8,128)(2,1)S(1)}, bf16[512,128]{1,0:T(8,128)(2,1)}, u32[]{:S(2)}) copy-start(bf16[512,128]{1,0:T(8,128)(2,1)} %v_ref.3) | copy-start | bytes 393220
  7.2 30.6 %copy-start.2 = (bf16[512,128]{1,0:T(8,128)(2,1)S(1)}, bf16[512,128]{1,0:T(8,128)(2,1)}, u32[]{:S(2)}) copy-start(bf16[512,128]{1,0:T(8,128)(2,1)} %k_ref.3) | copy-start | bytes 393220
  7.2 30.6 %copy-start.1 = (bf16[512,128]{1,0:T(8,128)(2,1)S(1)}, bf16[512,128]{1,0:T(8,128)(2,1)}, u32[]{:S(2)}) copy-start(bf16[512,128]{1,0:T(8,128)(2,1)} %q_ref.3) | copy-start | bytes 393220
  7.2 71.4 %all-gather.4.cloned.1.call-start = ((), (), s32[]{:S(2)}) async-start(), calls=%async_computation.7 | async-start | bytes 1769472 | tf_op jit(solution)/shard_map/all_gather | solution.py:150
  7.2 1.0 copy-start.4
  8.3 29.5 %copy-start.6 = (f32[128]{0:T(128)S(1)}, f32[128]{0:T(128)}, u32[]{:S(2)}) copy-start(f32[128]{0:T(128)} %param.10) | copy-start | bytes 1540
  8.3 29.5 %copy-start.7 = (f32[128]{0:T(128)S(1)}, f32[128]{0:T(128)}, u32[]{:S(2)}) copy-start(f32[128]{0:T(128)} %param.11) | copy-start | bytes 1540
  29.5 1.5 %collective-permute-start = (bf16[128,256]{1,0:T(8,128)(2,1)}, bf16[128,256]{1,0:T(8,128)(2,1)S(1)}, u32[]{:S(2)}, u32[]{:S(2)}) collective-permute-start(bf16[128,256]{1,0:T(8,128)(2,1)} %param.12), channel_id=1, source_target_pairs={{0,0},{1,64},{2,128},{3,192},{64,1},{65,65},{66,129},{67,193},{128... | collective-permute-start | bytes 196616 | tf_op jit(solution)/shard_map/ppermute | solution.py:129
  31.7 13.4 %all-to-all-start.1 = ((bf16[3,128,256]{2,1,0:T(8,128)(2,1)}), bf16[3,128,256]{2,1,0:T(8,128)(2,1)S(1)}, u32[]{:S(2)}, u32[]{:S(2)}) async-start(bf16[3,128,256]{2,1,0:T(8,128)(2,1)} %broadcast_in_dim.4), calls=%async_computation.1 | async-start | bytes 393216 | tf_op jit(solution)/shard_map/all_to_all | solution.py:134
  46.0 25.6 %all-to-all-start.2 = ((bf16[4,128,512]{2,1,0:T(8,128)(2,1)}), bf16[4,128,512]{2,1,0:T(8,128)(2,1)S(1)}, u32[]{:S(2)}, u32[]{:S(2)}) async-start(bf16[4,128,512]{2,1,0:T(8,128)(2,1)} %broadcast_in_dim.5), calls=%async_computation.2 | async-start | bytes 1048576 | tf_op jit(solution)/shard_map/all_to_all | solution.py:134
  71.5 11.9 %collective-permute-start.2 = (bf16[4,128,512]{2,1,0:T(8,128)(2,1)S(1)}, bf16[4,128,512]{2,1,0:T(8,128)(2,1)S(1)}, u32[]{:S(2)}, u32[]{:S(2)}) collective-permute-start(bf16[4,128,512]{2,1,0:T(8,128)(2,1)S(1)} %all-to-all-done.2.own_ref), channel_id=1, source_target_pairs={{0,32},{32,0},{1,33},{33,1},{2,34},{34,2},{3,35},{35,3},{4,36},{36... | collective-permute-start | bytes 1572872 | tf_op jit(solution)/shard_map/ppermute | solution.py:138
  78.6 1.4 %copy-start = (bf16[64,16,768]{2,1,0:T(8,128)(2,1)S(1)}, bf16[64,16,768]{2,1,0:T(8,128)(2,1)}, u32[]{:S(2)}) copy-start(bf16[64,16,768]{2,1,0:T(8,128)(2,1)} %all-gather.4.cloned.1.call-done) | copy-start | bytes 4718596
  81.5 7.4 %collective-permute-start.1 = (bf16[4,512,128]{2,1,0:T(8,128)(2,1)}, bf16[4,512,128]{2,1,0:T(8,128)(2,1)S(1)}, u32[]{:S(2)}, u32[]{:S(2)}) collective-permute-start(bf16[4,512,128]{2,1,0:T(8,128)(2,1)} %get-tuple-element.30), channel_id=1, source_target_pairs={{0,32},{32,0},{1,33},{33,1},{2,34},{34,2},{3,35},{35,3},{4,36},{36... | collective-permute-start | bytes 1572872 | tf_op jit(solution)/shard_map/ppermute | solution.py:138
  85.3 15.4 %all-to-all-start.3 = ((bf16[4,3,128,256]{3,2,1,0:T(8,128)(2,1)}), bf16[4,3,128,256]{3,2,1,0:T(8,128)(2,1)S(1)}, u32[]{:S(2)}, u32[]{:S(2)}) async-start(bf16[4,3,128,256]{3,2,1,0:T(8,128)(2,1)} %shard_map.106), calls=%async_computation.4 | async-start | bytes 1572864 | tf_op jit(solution)/shard_map/all_to_all | solution.py:185
  88.8 37.7 %reduce-scatter.2.cloned.1.call-start = ((), (), s32[]{:S(2)}) async-start(), calls=%async_computation.6 | async-start | bytes 655360 | tf_op jit(solution)/shard_map/reduce_scatter | solution.py:187
  111.8 0.7 collective-permute-start.3
  126.5 0.9 copy-start.5
Sparse Core Ops, SparseCore 0:
  29.7 38.6 all-gather.3
  92.7 33.7 reduce-scatter.1
